TPU v7x, 768 devices: a whole 4x8x12 slice. The times are simulated.
768 devices in a mesh: dp: 12 (over z), mp: 64 (over y, x, core).
Axes of the slice: x: 4, y: 8, z: 12, core: 2. Of those that a mesh axis runs over, the one named last changes fastest.
Arguments:
- inputs: float32 [1536, 8192], P('dp', 'mp'), may hold values from -6 to 6
- block_weights: float32 [2432, 128, 128], P('mp'), may hold values from -0.21875 to 0.21875
- block_list: int32 [2432, 2], P('mp'), may hold values from -1 to 63, as said below
- grad_act: float32 [1536, 32768], P('dp', 'mp'), may hold values from -6 to 6
Outputs:
- act: float32 [1536, 32768], P('dp', 'mp')
- grad_inputs: float32 [1536, 8192], P('dp', 'mp')
- grad_weights: float32 [2432, 128, 128], P('mp')
Inputs may be any that keep to these rules, and one draw needn't show every extreme that they name: `block_list`: rows s * 38 to s * 38 + 37 belong to index s of mp. A live slot holds a row block below 64 and a local column block below 4; the live slots of one index name distinct cells, and come before its empty slots, which hold -1 in both entries. Each index has 12 to 38 live slots; some index has all 38 live.
All inputs are finite; a program needn't handle non-finite values.
Results may differ from a plain program's by a relative error of at most 0.0056.
Values may be sent and summed in bfloat16 or wider, within the bound.
No kernel may reach another device: no remote copies, remote signals or barrier semaphores. Data moves between devices by JAX's collectives and lax.ppermute only.
A program may use at most 32 MiB of HBM per device.

v0:
```python
import jax
import jax.numpy as jnp
from jax import lax
from jax.sharding import PartitionSpec as P

BS = 128


def gelu_parts(pre):
    inner = 0.7978845608 * (pre + 0.044715 * pre * pre * pre)
    tanh_val = jnp.tanh(inner)
    value = 0.5 * pre * (1.0 + tanh_val)
    slope = 0.5 * (1.0 + tanh_val) + 0.5 * pre * (1.0 - tanh_val * tanh_val) * 0.7978845608 * (
        1.0 + 3.0 * 0.044715 * pre * pre
    )
    return (value, slope)


def sum_weights(wgrad_local):
    return lax.psum(wgrad_local, "dp")


def row_table(grow, livef, nblocks):
    blocks = jnp.arange(nblocks, dtype=jnp.int32)
    return (grow[:, None] == blocks[None, :]).astype(jnp.float32) * livef[:, None]


def local(inputs, block_weights, block_list, grad_act):
    tokens = inputs.shape[0]
    slots = block_weights.shape[0]
    col_blocks = grad_act.shape[1] // BS
    full_width = inputs.shape[1] * lax.axis_size("mp")
    row_ids = block_list[:, 0]
    col_ids = block_list[:, 1]
    livef = (row_ids >= 0).astype(jnp.float32)
    grow = jnp.maximum(row_ids, 0)
    gcol = jnp.maximum(col_ids, 0)
    positions = grow[:, None] * BS + jnp.arange(BS, dtype=jnp.int32)[None, :]
    flat_pos = positions.reshape(-1)
    xb = inputs.astype(jnp.bfloat16)
    wb = block_weights.astype(jnp.bfloat16)
    col_hot = (gcol[:, None] == jnp.arange(col_blocks, dtype=jnp.int32)[None, :]).astype(
        jnp.float32
    ) * livef[:, None]
    whole = lax.all_gather(xb, "mp", axis=1, tiled=True)
    selected = jnp.take(whole, flat_pos, axis=1).reshape(tokens, slots, BS)
    products = jnp.einsum("tsk,skl->tsl", selected, wb, preferred_element_type=jnp.float32)
    pre = jnp.einsum("tsl,sc->tcl", products, col_hot, precision=lax.Precision.HIGHEST).reshape(
        tokens, col_blocks * BS
    )
    act, slope = gelu_parts(pre)
    dpre = (grad_act * slope).astype(jnp.bfloat16)
    dsel = jnp.take(dpre.reshape(tokens, col_blocks, BS), gcol, axis=1)
    back = jnp.einsum("tsl,skl->tsk", dsel, wb, preferred_element_type=jnp.float32)
    hot_all = row_table(grow, livef, full_width // BS)
    term = jnp.einsum("tsk,sb->tbk", back, hot_all, precision=lax.Precision.HIGHEST).reshape(
        tokens, full_width
    )
    grad_x = lax.psum_scatter(term, "mp", scatter_dimension=1, tiled=True)
    local_grad = jnp.einsum("tsk,tsl->skl", selected, dsel, preferred_element_type=jnp.float32)
    grad_w = sum_weights(local_grad * livef[:, None, None])
    return (act, grad_x, grad_w)


def solution(mesh):
    in_specs = (P("dp", "mp"), P("mp", None, None), P("mp", None), P("dp", "mp"))
    out_specs = (P("dp", "mp"), P("dp", "mp"), P("mp", None, None))
    return jax.shard_map(local, mesh=mesh, in_specs=in_specs, out_specs=out_specs, check_vma=False)
```

profile of v0, /device:TPU:6, one launch (start us, length us, event | category | flops | bytes accessed | tf_op | source)
XLA Modules:
  0.0 426.0 jit_solution(2022472535180447518)
XLA Ops:
  7.2 0.0 all-gather.2.cloned.1.call-start
  7.2 1.6 copy.9
  8.8 0.0 all-gather.2.cloned.1.call-update
  8.8 0.0 all-reduce.2.cloned.1.call-start
  8.8 1.1 copy.19
  9.9 1.3 maximum_bitcast_fusion
  11.2 0.1 fusion.23
  11.3 0.1 fusion.27
  11.4 1.3 compare_bitcast_fusion
  12.6 0.1 fusion.26
  12.7 93.5 %all-gather.2.cloned.1.call-done = bf16[128,8192]{0,1:T(8,128)(2,1)} async-done(((bf16[128,128]{0,1:T(8,128)(2,1)}), bf16[128,8192]{0,1:T(8,128)(2,1)}) %all-gather.2.cloned.1.call-update) | async-done | bytes 2097168 | tf_op jit(solution)/shard_map/all_gather | solution.py:45
  106.2 11.8 %gather_fusion = bf16[4864,128]{1,0:T(8,128)(2,1)} fusion(bf16[128,8192]{0,1:T(8,128)(2,1)} %all-gather.2.cloned.1.call-done, s32[5120]{0:T(1024)S(1)} %pad_clamp_fusion), kind=kCustom, calls=%fused_computation | custom fusion | bytes 2509824 | tf_op jit(solution)/shard_map/jit(_take)/gather | solution.py:46
  118.1 0.0 copy-done
  118.1 2.5 convolution_bitcast_fusion.1
  120.6 2.8 fusion.6
  123.4 0.1 copy.24
  123.6 0.2 fusion.19
  123.8 0.1 copy.20
  123.9 0.0 copy-start.2
  123.9 1.8 gather_fusion.1
  125.7 4.1 convolution_multiply_fusion
  129.8 0.0 all-reduce.2.cloned.1.call-update
  129.9 0.0 copy-start.1
  129.9 0.2 reduce-scatter.2.cloned.1.call-start
  130.1 2.3 convolution_bitcast_fusion
  132.4 5.0 %fusion = f32[64,128,128]{2,0,1:T(8,128)S(1)} fusion(f32[128,38,128]{2,0,1:T(8,128)S(1)} %convolution_bitcast_fusion, f32[38]{0:T(128)S(1)} %get-tuple-element.12, s32[38]{0:T(128)S(1)} %copy-done.1), kind=kOutput, calls=%fused_computation.3 | convolution fusion | flops 478155520 | bytes 6684976 | tf_op jit(solution)/shard_map/tsk,sb->tbk/dot_general | solution.py:56
  137.4 5.2 %copy.35 = f32[16,8,64,128]{3,1,2,0:T(8,128)} copy(f32[16,8,64,128]{3,2,1,0:T(8,128)S(1)} %bitcast.55) | data formatting | bytes 8388608
  142.6 0.0 reduce-scatter.2.cloned.1.call-update
  142.6 0.8 copy.22
  143.5 109.3 %all-reduce.2.cloned.1.call-done = f32[38,128,128]{2,1,0:T(8,128)} async-done(((f32[38,128,128]{2,1,0:T(8,128)}), f32[38,128,128]{2,1,0:T(8,128)}) %all-reduce.2.cloned.1.call-update) | async-done | bytes 2490384 | tf_op jit(solution)/shard_map/psum | solution.py:20
  252.8 163.3 %reduce-scatter.2.cloned.1.call-done = f32[128,128]{1,0:T(8,128)} async-done(((f32[128,8192]{1,0:T(8,128)}), f32[128,128]{1,0:T(8,128)}) %reduce-scatter.2.cloned.1.call-update) | async-done | bytes 65552 | tf_op jit(solution)/shard_map/reduce_scatter | solution.py:59
  416.1 3.4 copy.37
  (5 shorter events, 0.0 us)
Async XLA Ops:
  7.2 99.0 %all-gather.2.cloned.1.call-start = ((), (), s32[]{:S(2)}) async-start(), calls=%async_computation.1 | async-start | bytes 2129920 | tf_op jit(solution)/shard_map/all_gather | solution.py:45
  8.8 244.0 %all-reduce.2.cloned.1.call-start = ((), (), s32[]{:S(2)}) async-start(), calls=%async_computation.3 | async-start | bytes 4980736 | tf_op jit(solution)/shard_map/psum | solution.py:20
  106.2 11.8 %copy-start = (f32[38,128,128]{2,1,0:T(8,128)S(1)}, f32[38,128,128]{2,1,0:T(8,128)}, u32[]{:S(2)}) copy-start(f32[38,128,128]{2,1,0:T(8,128)} %param.5) | copy-start | bytes 7471108
  123.9 1.8 copy-start.2
  129.9 2.6 copy-start.1
  129.9 286.2 %reduce-scatter.2.cloned.1.call-start = ((), (), s32[]{:S(2)}) async-start(), calls=%async_computation.2 | async-start | bytes 4259840 | tf_op jit(solution)/shard_map/reduce_scatter | solution.py:59
Sparse Core Ops, SparseCore 0:
  12.5 93.6 all-gather.1
  130.0 122.8 all-reduce.1
  259.5 156.4 reduce-scatter.1
where the time goes:
time: 427 us; the launch traced here: 426 us
  waiting for transfers between devices  366 us (86%)
  local copies, waits for them, and re-layouts  26.1 us (6%)
  matrix products  16.7 us (4%)
  between operations  13.8 us (3%)
    reduce_scatter x1, waiting for transfers between devices, local(): grad_x = lax.psum_scatter(term, 'mp', scatter_dimension=1, tiled=True)  163 us
    psum x1, waiting for transfers between devices, sum_weights(): return lax.psum(wgrad_local, 'dp')  109 us
    all_gather x1, waiting for transfers between devices, local(): whole = lax.all_gather(xb, 'mp', axis=1, tiled=True)  93.5 us
    unnamed x11, local copies, waits for them, and re-layouts  12.1 us
    gather x1, local copies, waits for them, and re-layouts, local(): selected = jnp.take(whole, flat_pos, axis=1).reshape(tokens, slots, BS)  11.8 us
  transfers between devices with their start and end apart: 3, of which 3 were waited for; matrix products, arithmetic and copies ran while one was open for 4% of the time, Pallas kernels for 0%

commit v1 on v0

v1 whole, which is shorter than its diff:
```python
import jax
import jax.numpy as jnp
from jax import lax
from jax.experimental import pallas as pl
from jax.experimental.pallas import tpu as pltpu
from jax.sharding import PartitionSpec as P

BS = 128
NY, NX, NC = 8, 4, 2
NZ = 12
HALF = NY * NX
Y_GROUPS = [[(y * NX + x) * NC + c for y in range(NY)] for x in range(NX) for c in range(NC)]
X_GROUPS = [[(y * NX + x) * NC + c for x in range(NX)] for y in range(NY) for c in range(NC)]
CORE_SWAP = [(i, i ^ 1) for i in range(HALF * NC)]
Z_NEAR = [[3 * i + j for j in range(3)] for i in range(4)]
Z_FAR = [[3 * i + j for i in range(4)] for j in range(3)]
F32, BF16 = jnp.float32, jnp.bfloat16


def gelu_parts(pre):
    inner = 0.7978845608 * (pre + 0.044715 * pre * pre * pre)
    tanh_val = jnp.tanh(inner)
    value = 0.5 * pre * (1.0 + tanh_val)
    slope = 0.5 * (1.0 + tanh_val) + 0.5 * pre * (1.0 - tanh_val * tanh_val) * 0.7978845608 * (
        1.0 + 3.0 * 0.044715 * pre * pre
    )
    return value, slope


def dot(a, b, dims):
    return lax.dot_general(a, b, (dims, ((), ())), preferred_element_type=F32)


def block_kernel(idx_ref, col_ref, live_ref, own_ref, sib_ref, w_ref, g_ref,
                 act_ref, gx_own_ref, gx_sib_ref, gw_ref, x_ref, prod_ref, pre_ref, dpre_ref, gx_ref):
    slots = w_ref.shape[0]
    col_blocks = pre_ref.shape[0]
    x_ref[:HALF] = own_ref[...]
    x_ref[HALF:] = sib_ref[...]
    pre_ref[...] = jnp.zeros_like(pre_ref)
    for s in range(slots):
        prod_ref[s] = dot(x_ref[idx_ref[s]], w_ref[s], ((1,), (0,)))
    for s in range(slots):
        pre_ref[col_ref[s]] += prod_ref[s]
    for c in range(col_blocks):
        value, slope = gelu_parts(pre_ref[c])
        lanes = slice(c * BS, (c + 1) * BS)
        act_ref[:, lanes] = value
        dpre_ref[c] = (g_ref[:, lanes] * slope).astype(BF16)
    for s in range(slots):
        wgrad = dot(x_ref[idx_ref[s]], dpre_ref[col_ref[s]], ((0,), (0,)))
        gw_ref[s] = (wgrad * live_ref[s]).astype(BF16)
    gw_ref[slots] = jnp.zeros((BS, BS), BF16)
    gx_ref[...] = jnp.zeros_like(gx_ref)
    for s in range(slots):
        prod_ref[s] = dot(dpre_ref[col_ref[s]], w_ref[s], ((1,), (1,)))
    for s in range(slots):
        gx_ref[idx_ref[s]] += prod_ref[s]
    gx_own_ref[...] = gx_ref[:HALF].astype(BF16)
    gx_sib_ref[...] = gx_ref[HALF:].astype(BF16)


def run_blocks(idx, col, live, own, sib, wb, grad_act):
    slots = wb.shape[0]
    tokens, hidden = grad_act.shape
    smem = pl.BlockSpec(memory_space=pltpu.SMEM)
    vmem = pl.BlockSpec(memory_space=pltpu.VMEM)
    return pl.pallas_call(
        block_kernel,
        out_shape=(
            jax.ShapeDtypeStruct((tokens, hidden), F32),
            jax.ShapeDtypeStruct((HALF, tokens, BS), BF16),
            jax.ShapeDtypeStruct((HALF, tokens, BS), BF16),
            jax.ShapeDtypeStruct((slots + 1, BS, BS), BF16),
        ),
        in_specs=[smem] * 3 + [vmem] * 4,
        out_specs=(vmem,) * 4,
        scratch_shapes=[
            pltpu.VMEM((2 * HALF, tokens, BS), BF16),
            pltpu.VMEM((slots, tokens, BS), F32),
            pltpu.VMEM((hidden // BS, tokens, BS), F32),
            pltpu.VMEM((hidden // BS, tokens, BS), BF16),
            pltpu.VMEM((2 * HALF, tokens, BS), F32),
        ],
        compiler_params=pltpu.CompilerParams(vmem_limit_bytes=40 << 20),
    )(idx, col, live, own, sib, wb, grad_act)


def swap(x, axis, groups):
    return lax.all_to_all(x, axis, 0, 0, tiled=True, axis_index_groups=groups)


def total(x):
    return jnp.sum(x.astype(F32), axis=0)


def local(inputs, block_weights, block_list, grad_act):
    tokens = inputs.shape[0]
    slots = block_weights.shape[0]
    row_ids, col_ids = block_list[:, 0], block_list[:, 1]
    live = (row_ids >= 0).astype(F32)
    row = jnp.maximum(row_ids, 0)
    col = jnp.maximum(col_ids, 0)
    core = lax.axis_index("mp") % NC
    idx = ((row % NC) ^ core) * HALF + ((row // NC) % NX) * NY + row // (NC * NX)
    xb = inputs.astype(BF16)
    wb = (block_weights * live[:, None, None]).astype(BF16)

    by_y = swap(jnp.broadcast_to(xb[None], (NY, tokens, BS)), "mp", Y_GROUPS)
    by_xy = swap(jnp.broadcast_to(by_y[None], (NX, NY, tokens, BS)), "mp", X_GROUPS)
    own = by_xy.reshape(HALF, tokens, BS)
    sib = lax.ppermute(own, "mp", CORE_SWAP)

    act, gx_own, gx_sib, gw = run_blocks(idx, col, live, own, sib, wb, grad_act)

    rows = gw.shape[0] * BS
    near = swap(gw.reshape(3, rows // 3, BS), "dp", Z_NEAR)
    near = total(near).astype(BF16)
    far = swap(near.reshape(4, rows // NZ, BS), "dp", Z_FAR)
    mine = total(far).astype(BF16)
    whole = lax.all_gather(mine, "dp", axis=0, tiled=False)
    whole = whole.reshape(4, 3, rows // NZ, BS).swapaxes(0, 1)
    grad_w = whole.reshape(rows // BS, BS, BS)[:slots].astype(F32)

    gx = (gx_own.astype(F32) + lax.ppermute(gx_sib, "mp", CORE_SWAP).astype(F32)).astype(BF16)
    gx = swap(gx.reshape(NX, NY, tokens, BS), "mp", X_GROUPS)
    gx = swap(total(gx).astype(BF16), "mp", Y_GROUPS)
    grad_x = total(gx)
    return act, grad_x, grad_w


def solution(mesh):
    in_specs = (P("dp", "mp"), P("mp", None, None), P("mp", None), P("dp", "mp"))
    out_specs = (P("dp", "mp"), P("dp", "mp"), P("mp", None, None))
    return jax.shard_map(local, mesh=mesh, in_specs=in_specs, out_specs=out_specs, check_vma=False)
```

time: 427 us -> 177 us (0.41)
  waiting for transfers between devices: 366 us -> 40.3 us
  blocking collectives: 0 us -> 88.1 us
  local copies, waits for them, and re-layouts: 26.1 us -> 2.63 us
  starting transfers between devices: 0.3 us -> 18.5 us
  matrix products: 16.7 us -> 0 us
  other arithmetic: 2.96 us -> 8.82 us
    reduce_scatter x1 -> x0, waiting for transfers between devices: 163 us -> none  [local(): grad_x = lax.psum_scatter(term, 'mp', scatter_dimension=1, tiled=True)]
    psum x1 -> x0, waiting for transfers between devices: 109 us -> none  [sum_weights(): return lax.psum(wgrad_local, 'dp')]
    all_to_all x0 -> x5, blocking collectives: none -> 88.1 us  [swap(): return lax.all_to_all(x, axis, 0, 0, tiled=True, axis_index_groups=groups)]
    all_gather x1, waiting for transfers between devices: 93.5 us -> 25.5 us  [local(): whole = lax.all_gather(mine, 'dp', axis=0, tiled=False)]
    dot_general x5 -> x0, matrix products: 16.7 us -> none  [the longest x1 4.96 us: local(): jnp.einsum('tsk,sb->tbk', back, hot_all, precision=lax.Precision.HIGHEST)]
    all_to_all x0 -> x1, starting transfers between devices: none -> 14.5 us  [swap(): return lax.all_to_all(x, axis, 0, 0, tiled=True, axis_index_groups=groups)]
    all_to_all x0 -> x1, waiting for transfers between devices: none -> 14.2 us  [swap(): return lax.all_to_all(x, axis, 0, 0, tiled=True, axis_index_groups=groups)]
    gather x2 -> x0, local copies, waits for them, and re-layouts: 13.7 us -> none  [the longest x1 11.8 us: local(): selected = jnp.take(whole, flat_pos, axis=1).reshape(tokens, slots, BS)]
  transfers between devices with their start and end apart: 3 -> 4, of which waited for: 3 -> 3; matrix products, arithmetic and copies ran while one was open for 4% -> 3% of each run, Pallas kernels for 0% -> 0%
where the time goes in v1:
time: 177 us; the launch traced here: 176 us
  blocking collectives  88.1 us (50%)
  waiting for transfers between devices  40.3 us (23%)
  starting transfers between devices  18.5 us (10%)
  between operations  14.1 us (8%)
  other arithmetic  8.82 us (5%)
  Pallas kernels  3.73 us (2%)
  local copies, waits for them, and re-layouts  2.63 us (1%)
    all_to_all x5, blocking collectives, swap(): return lax.all_to_all(x, axis, 0, 0, tiled=True, axis_index_groups=groups)  88.1 us
    all_gather x1, waiting for transfers between devices, local(): whole = lax.all_gather(mine, 'dp', axis=0, tiled=False)  25.5 us
    all_to_all x1, starting transfers between devices, swap(): return lax.all_to_all(x, axis, 0, 0, tiled=True, axis_index_groups=groups)  14.5 us
    all_to_all x1, waiting for transfers between devices, swap(): return lax.all_to_all(x, axis, 0, 0, tiled=True, axis_index_groups=groups)  14.2 us
    pallas_call x1, Pallas kernels, run_blocks(): pl.pallas_call(block_kernel, out_shape=(jax.ShapeDtypeStruct((tokens, hid...  3.73 us
  transfers between devices with their start and end apart: 4, of which 3 were waited for; matrix products, arithmetic and copies ran while one was open for 3% of the time, Pallas kernels for 0%

profile of v1, /device:TPU:6, one launch (start us, length us, event | category | flops | bytes accessed | tf_op | source)
XLA Modules:
  0.0 176.1 jit_solution(15524047337636560468)
XLA Ops:
  7.2 0.8 convert_element_type.34
  8.0 0.0 copy-start.3
  8.0 18.8 %all_to_all.30 = bf16[8,128,128]{2,1,0:T(8,128)(2,1)S(1)} all-to-all(bf16[8,128,128]{2,1,0:T(8,128)(2,1)S(1)} %broadcast_in_dim.4), channel_id=1, replica_groups={{0,8,16,24,32,40,48,56},{1,9,17,25,33,41,49,57},{2,10,18,26,34,42,50,58..., dimensions={0} | all-to-all | bytes 524288 | tf_op jit(solution)/shard_map/all_to_all | solution.py:90
  26.8 0.2 broadcast_in_dim.5
  27.1 15.8 %all_to_all.31 = bf16[4,8,128,128]{3,2,1,0:T(8,128)(2,1)S(1)} all-to-all(bf16[4,8,128,128]{3,2,1,0:T(8,128)(2,1)S(1)} %broadcast_in_dim.5), channel_id=1, replica_groups={{0,2,4,6},{1,3,5,7},{8,10,12,14},{9,11,13,15},{16,18,20,22},{17,19,21,2..., dimensions={0} | all-to-all | bytes 2097152 | tf_op jit(solution)/shard_map/all_to_all | solution.py:90
  42.9 0.0 copy-start
  42.9 2.0 %collective-permute-start = (bf16[32,128,128]{2,1,0:T(8,128)(2,1)S(1)}, bf16[32,128,128]{2,1,0:T(8,128)(2,1)S(1)}, u32[]{:S(2)}, u32[]{:S(2)}) collective-permute-start(bf16[32,128,128]{2,1,0:T(8,128)(2,1)S(1)} %bitcast.37), channel_id=1, source_target_pairs={{0,1},{1,0},{2,3},{3,2},{4,5},{5,4},{6,7},{7,6},{8,9},{9,8},{10,11... | collective-permute-start | bytes 3145736 | tf_op jit(solution)/shard_map/ppermute | solution.py:112
  44.9 0.0 copy-done.3
  45.0 2.0 %multiply_convert_fusion.w_ref = bf16[38,128,128]{2,1,0:T(8,128)(2,1)S(1)} fusion(f32[38,128,128]{2,1,0:T(8,128)} %param.5, f32[38]{0:T(128)S(1)} %fusion.7.live_ref), kind=kLoop, calls=%fused_computation | loop fusion | flops 1245184 | bytes 3735704 | tf_op jit(solution)/shard_map/convert_element_type | solution.py:107
  47.0 0.6 collective-permute-done.sib_ref
  47.5 0.0 copy-done
  47.6 3.7 %shard_map.67 = (f32[128,512]{1,0:T(8,128)}, bf16[32,128,128]{2,1,0:T(8,128)(2,1)S(1)}, bf16[32,128,128]{2,1,0:T(8,128)(2,1)S(1)}, bf16[39,128,128]{2,1,0:T(8,128)(2,1)S(1)}) custom-call(s32[38]{0:T(128)S(1)} %fusion.5.idx_ref, s32[38]{0:T(128)S(1)} %maximum_bitcast_fusion.col_ref, f32[38]{0:T(128)S(1)} %fusion.7.live_ref, ...), custom_call_target="tpu_custom_call" | custom-call | tf_op jit(solution)/shard_map/pallas_call | solution.py:68
  51.3 0.0 copy-start.1
  51.3 1.0 copy-done.1
  52.3 26.8 %all_to_all.32 = bf16[3,1664,128]{2,1,0:T(8,128)(2,1)S(1)} all-to-all(bf16[3,1664,128]{2,1,0:T(8,128)(2,1)S(1)} %bitcast.39), channel_id=1, replica_groups={{0,64,128},{192,256,320},{384,448,512},{576,640,704},{1,65,129},{193,25..., dimensions={0} | all-to-all | bytes 2555904 | tf_op jit(solution)/shard_map/all_to_all | solution.py:90
  79.1 1.1 reduce_sum.47
  80.2 14.5 %all-to-all-start.5 = ((bf16[4,416,128]{2,1,0:T(8,128)(2,1)}), bf16[4,416,128]{2,1,0:T(8,128)(2,1)S(1)}, u32[]{:S(2)}, u32[]{:S(2)}) async-start(bf16[4,416,128]{2,1,0:T(8,128)(2,1)} %bitcast.42), calls=%async_computation.5 | async-start | bytes 851968 | tf_op jit(solution)/shard_map/all_to_all | solution.py:90
  94.7 0.0 all-gather.3.cloned.1.call-start
  94.7 0.0 copy-done.2
  94.7 1.9 %collective-permute-start.1 = (bf16[32,128,128]{2,1,0:T(8,128)(2,1)S(1)}, bf16[32,128,128]{2,1,0:T(8,128)(2,1)}, u32[]{:S(2)}, u32[]{:S(2)}) collective-permute-start(bf16[32,128,128]{2,1,0:T(8,128)(2,1)S(1)} %copy-done.2), channel_id=1, source_target_pairs={{0,1},{1,0},{2,3},{3,2},{4,5},{5,4},{6,7},{7,6},{8,9},{9,8},{10,11... | collective-permute-start | bytes 3145736 | tf_op jit(solution)/shard_map/ppermute | solution.py:125
  96.6 14.2 %all-to-all-done.5 = bf16[4,416,128]{2,1,0:T(8,128)(2,1)S(1)} async-done(((bf16[4,416,128]{2,1,0:T(8,128)(2,1)}), bf16[4,416,128]{2,1,0:T(8,128)(2,1)S(1)}, u32[]{:S(2)}, u32[]{:S(2)}) %all-to-all-start.5) | async-done | bytes 426016 | tf_op jit(solution)/shard_map/all_to_all | solution.py:90
  110.8 0.7 reduce_sum.48
  111.5 0.0 all-gather.3.cloned.1.call-update
  111.5 0.0 collective-permute-done.1
  111.5 1.6 add_convert_fusion
  113.1 13.3 %all_to_all.33 = bf16[4,8,128,128]{3,2,1,0:T(8,128)(2,1)S(1)} all-to-all(bf16[4,8,128,128]{3,2,1,0:T(8,128)(2,1)S(1)} %bitcast.41), channel_id=1, replica_groups={{0,2,4,6},{1,3,5,7},{8,10,12,14},{9,11,13,15},{16,18,20,22},{17,19,21,2..., dimensions={0} | all-to-all | bytes 2097152 | tf_op jit(solution)/shard_map/all_to_all | solution.py:90
  126.4 0.2 reduce_sum.45
  126.6 13.3 %all_to_all.34 = bf16[8,128,128]{2,1,0:T(8,128)(2,1)S(1)} all-to-all(bf16[8,128,128]{2,1,0:T(8,128)(2,1)S(1)} %reduce_sum.45), channel_id=1, replica_groups={{0,8,16,24,32,40,48,56},{1,9,17,25,33,41,49,57},{2,10,18,26,34,42,50,58..., dimensions={0} | all-to-all | bytes 524288 | tf_op jit(solution)/shard_map/all_to_all | solution.py:90
  140.0 0.7 convert_reduce_fusion
  140.6 25.5 %all-gather.3.cloned.1.call-done = bf16[4992,128]{1,0:T(8,128)(2,1)} async-done(((bf16[416,128]{1,0:T(8,128)(2,1)}), bf16[4992,128]{1,0:T(8,128)(2,1)}) %all-gather.3.cloned.1.call-update) | async-done | bytes 1277968 | tf_op jit(solution)/shard_map/all_gather | solution.py:121
  166.1 1.4 copy.8
  167.5 1.7 slice_convert_fusion
  (5 shorter events, 0.1 us)
Async XLA Ops:
  8.0 36.9 %copy-start.3 = (s32[38,2]{0,1:T(2,128)S(1)}, s32[38,2]{0,1:T(2,128)}, u32[]{:S(2)}) copy-start(s32[38,2]{0,1:T(2,128)} %param.6) | copy-start | bytes 916
  42.9 4.7 %copy-start = (f32[128,512]{1,0:T(8,128)S(1)}, f32[128,512]{1,0:T(8,128)}, u32[]{:S(2)}) copy-start(f32[128,512]{1,0:T(8,128)} %g_ref.1) | copy-start | bytes 786436
  42.9 4.7 %collective-permute-start = (bf16[32,128,128]{2,1,0:T(8,128)(2,1)S(1)}, bf16[32,128,128]{2,1,0:T(8,128)(2,1)S(1)}, u32[]{:S(2)}, u32[]{:S(2)}) collective-permute-start(bf16[32,128,128]{2,1,0:T(8,128)(2,1)S(1)} %bitcast.37), channel_id=1, source_target_pairs={{0,1},{1,0},{2,3},{3,2},{4,5},{5,4},{6,7},{7,6},{8,9},{9,8},{10,11... | collective-permute-start | bytes 3145736 | tf_op jit(solution)/shard_map/ppermute | solution.py:112
  51.3 1.0 copy-start.1
  52.3 42.4 %copy-start.2 = (bf16[32,128,128]{2,1,0:T(8,128)(2,1)S(1)}, bf16[32,128,128]{2,1,0:T(8,128)(2,1)}, u32[]{:S(2)}) copy-start(bf16[32,128,128]{2,1,0:T(8,128)(2,1)} %copy-done.1) | copy-start | bytes 3145732
  80.2 30.6 %all-to-all-start.5 = ((bf16[4,416,128]{2,1,0:T(8,128)(2,1)}), bf16[4,416,128]{2,1,0:T(8,128)(2,1)S(1)}, u32[]{:S(2)}, u32[]{:S(2)}) async-start(bf16[4,416,128]{2,1,0:T(8,128)(2,1)} %bitcast.42), calls=%async_computation.5 | async-start | bytes 851968 | tf_op jit(solution)/shard_map/all_to_all | solution.py:90
  94.7 71.4 %all-gather.3.cloned.1.call-start = ((), (), s32[]{:S(2)}) async-start(), calls=%async_computation.6 | async-start | bytes 1384448 | tf_op jit(solution)/shard_map/all_gather | solution.py:121
  94.7 16.8 %collective-permute-start.1 = (bf16[32,128,128]{2,1,0:T(8,128)(2,1)S(1)}, bf16[32,128,128]{2,1,0:T(8,128)(2,1)}, u32[]{:S(2)}, u32[]{:S(2)}) collective-permute-start(bf16[32,128,128]{2,1,0:T(8,128)(2,1)S(1)} %copy-done.2), channel_id=1, source_target_pairs={{0,1},{1,0},{2,3},{3,2},{4,5},{5,4},{6,7},{7,6},{8,9},{9,8},{10,11... | collective-permute-start | bytes 3145736 | tf_op jit(solution)/shard_map/ppermute | solution.py:125
Sparse Core Ops, SparseCore 0:
  111.6 54.4 all-gather.2

commit v2 on v1

--- a/solution.py
+++ b/solution.py
@@ -12,8 +12,8 @@
 Y_GROUPS = [[(y * NX + x) * NC + c for y in range(NY)] for x in range(NX) for c in range(NC)]
 X_GROUPS = [[(y * NX + x) * NC + c for x in range(NX)] for y in range(NY) for c in range(NC)]
 CORE_SWAP = [(i, i ^ 1) for i in range(HALF * NC)]
-Z_NEAR = [[3 * i + j for j in range(3)] for i in range(4)]
-Z_FAR = [[3 * i + j for i in range(4)] for j in range(3)]
+CHUNK = 416
+SPLIT = 208
 F32, BF16 = jnp.float32, jnp.bfloat16
 
 
@@ -31,8 +31,9 @@
     return lax.dot_general(a, b, (dims, ((), ())), preferred_element_type=F32)
 
 
-def block_kernel(idx_ref, col_ref, live_ref, own_ref, sib_ref, w_ref, g_ref,
-                 act_ref, gx_own_ref, gx_sib_ref, gw_ref, x_ref, prod_ref, pre_ref, dpre_ref, gx_ref):
+def block_kernel(idx_ref, col_ref, live_ref, rel_ref, own_ref, sib_ref, w_ref, g_ref,
+                 act_ref, gx_own_ref, gx_sib_ref, keep_ref, up1_ref, down1_ref, up2_ref, down2_ref,
+                 x_ref, prod_ref, pre_ref, dpre_ref, gx_ref, gw_ref):
     slots = w_ref.shape[0]
     col_blocks = pre_ref.shape[0]
     x_ref[:HALF] = own_ref[...]
@@ -49,8 +50,21 @@
         dpre_ref[c] = (g_ref[:, lanes] * slope).astype(BF16)
     for s in range(slots):
         wgrad = dot(x_ref[idx_ref[s]], dpre_ref[col_ref[s]], ((0,), (0,)))
-        gw_ref[s] = (wgrad * live_ref[s]).astype(BF16)
-    gw_ref[slots] = jnp.zeros((BS, BS), BF16)
+        wgrad = (wgrad * live_ref[s]).astype(BF16)
+        done = 0
+        while done < BS:
+            chunk, at = divmod(s * BS + done, CHUNK)
+            size = min(BS - done, CHUNK - at)
+            gw_ref[rel_ref[chunk], at:at + size] = wgrad[done:done + size]
+            done += size
+    chunk, at = divmod(slots * BS, CHUNK)
+    gw_ref[rel_ref[chunk], at:] = jnp.zeros((CHUNK - at, BS), BF16)
+    for i in range(3):
+        keep_ref[i] = gw_ref[4 * i]
+        up1_ref[i] = gw_ref[4 * i + 1]
+        down1_ref[i] = gw_ref[(4 * i + 11) % NZ]
+        up2_ref[i] = gw_ref[4 * i + 2, :SPLIT]
+        down2_ref[i] = gw_ref[(4 * i + 10) % NZ, SPLIT:]
     gx_ref[...] = jnp.zeros_like(gx_ref)
     for s in range(slots):
         prod_ref[s] = dot(dpre_ref[col_ref[s]], w_ref[s], ((1,), (1,)))
@@ -60,7 +74,44 @@
     gx_sib_ref[...] = gx_ref[HALF:].astype(BF16)
 
 
-def run_blocks(idx, col, live, own, sib, wb, grad_act):
+def near_kernel(after_ref, keep_ref, a_ref, b_ref, c_ref, d_ref, stay_ref, up_ref, down_ref):
+    for i, out in enumerate((stay_ref, up_ref, down_ref)):
+        part = keep_ref[i].astype(F32) + a_ref[i].astype(F32) + b_ref[i].astype(F32)
+        out[:SPLIT] = (part[:SPLIT] + c_ref[i].astype(F32)).astype(BF16)
+        out[SPLIT:] = (part[SPLIT:] + d_ref[i].astype(F32)).astype(BF16)
+
+
+def far_kernel(after_ref, stay_ref, a_ref, b_ref, out_ref):
+    out_ref[...] = (stay_ref[...].astype(F32) + a_ref[...].astype(F32) + b_ref[...].astype(F32)).astype(BF16)
+
+
+def three_kernel(k0_ref, k4_ref, k8_ref, all_ref, low_ref, high_ref):
+    for i, part in enumerate((k0_ref, k4_ref, k8_ref)):
+        all_ref[i] = part[...]
+        low_ref[i] = part[:SPLIT]
+        high_ref[i] = part[SPLIT:]
+
+
+def x_sum_kernel(after_ref, in_ref, out_ref):
+    out_ref[...] = jnp.sum(in_ref[...].astype(F32), axis=0).astype(BF16)
+
+
+def whole_kernel(rel_ref, after_ref, k0_ref, k4_ref, k8_ref, low1_ref, high1_ref, low2_ref, high2_ref, out_ref, gw_ref):
+    gw_ref[0] = k0_ref[...]
+    gw_ref[4] = k4_ref[...]
+    gw_ref[8] = k8_ref[...]
+    for i in range(3):
+        gw_ref[(4 * i + 11) % NZ] = low1_ref[i]
+        gw_ref[4 * i + 1] = high1_ref[i]
+        gw_ref[(4 * i + 10) % NZ, :SPLIT] = low2_ref[i]
+        gw_ref[4 * i + 2, SPLIT:] = high2_ref[i]
+    rows = out_ref.shape[0]
+    for j in range(NZ):
+        size = min(CHUNK, rows - j * CHUNK)
+        out_ref[j * CHUNK:j * CHUNK + size] = gw_ref[rel_ref[j], :size].astype(F32)
+
+
+def run_blocks(idx, col, live, rel, own, sib, wb, grad_act):
     slots = wb.shape[0]
     tokens, hidden = grad_act.shape
     smem = pl.BlockSpec(memory_space=pltpu.SMEM)
@@ -71,19 +122,20 @@
             jax.ShapeDtypeStruct((tokens, hidden), F32),
             jax.ShapeDtypeStruct((HALF, tokens, BS), BF16),
             jax.ShapeDtypeStruct((HALF, tokens, BS), BF16),
-            jax.ShapeDtypeStruct((slots + 1, BS, BS), BF16),
-        ),
-        in_specs=[smem] * 3 + [vmem] * 4,
-        out_specs=(vmem,) * 4,
+        ) + (jax.ShapeDtypeStruct((3, CHUNK, BS), BF16),) * 3
+        + (jax.ShapeDtypeStruct((3, SPLIT, BS), BF16),) * 2,
+        in_specs=[smem] * 4 + [vmem] * 4,
+        out_specs=(vmem,) * 8,
         scratch_shapes=[
             pltpu.VMEM((2 * HALF, tokens, BS), BF16),
             pltpu.VMEM((slots, tokens, BS), F32),
             pltpu.VMEM((hidden // BS, tokens, BS), F32),
             pltpu.VMEM((hidden // BS, tokens, BS), BF16),
             pltpu.VMEM((2 * HALF, tokens, BS), F32),
+            pltpu.VMEM((NZ, CHUNK, BS), BF16),
         ],
         compiler_params=pltpu.CompilerParams(vmem_limit_bytes=40 << 20),
-    )(idx, col, live, own, sib, wb, grad_act)
+    )(idx, col, live, rel, own, sib, wb, grad_act)
 
 
 def swap(x, axis, groups):
@@ -92,6 +144,56 @@
 
 def total(x):
     return jnp.sum(x.astype(F32), axis=0)
+
+
+def shift(x, by):
+    return lax.ppermute(x, "dp", [(i, (i + by) % NZ) for i in range(NZ)])
+
+
+def call(kernel, ins, outs, after=None):
+    vmem = pl.BlockSpec(memory_space=pltpu.VMEM)
+    first = () if after is None else (after,)
+    return pl.pallas_call(
+        kernel,
+        out_shape=outs,
+        in_specs=[pl.BlockSpec(memory_space=pl.ANY)] * len(first) + [vmem] * len(ins),
+        out_specs=jax.tree.map(lambda _: vmem, outs),
+        compiler_params=pltpu.CompilerParams(vmem_limit_bytes=20 << 20),
+    )(*first, *ins)
+
+
+def reduce_gradients(gx_own, gx_sib, keep, up1, down1, up2, down2, rel, slots):
+    tokens = gx_own.shape[1]
+    one = jax.ShapeDtypeStruct((CHUNK, BS), BF16)
+    half = jax.ShapeDtypeStruct((3, SPLIT, BS), BF16)
+    parts = shift(up1, 1), shift(down1, -1), shift(up2, 2), shift(down2, -2)
+    gx_sib = lax.ppermute(gx_sib, "mp", CORE_SWAP)
+    gx = (gx_own.astype(F32) + gx_sib.astype(F32)).astype(BF16)
+    stay, up, down = call(near_kernel, (keep, *parts), (one,) * 3, gx)
+
+    far = shift(up, 4), shift(down, -4)
+    gx = swap(gx.reshape(NX, NY, tokens, BS), "mp", X_GROUPS)
+    mine = call(far_kernel, (stay, *far), one, gx)
+
+    k8, k4 = shift(mine, 4), shift(mine, -4)
+    three, low, high = call(
+        three_kernel, (mine, k4, k8), (jax.ShapeDtypeStruct((3, CHUNK, BS), BF16), half, half)
+    )
+
+    low1, high1, low2, high2 = shift(three, 1), shift(three, -1), shift(low, 2), shift(high, -2)
+    gx = call(x_sum_kernel, (gx,), jax.ShapeDtypeStruct((NY, tokens, BS), BF16), three)
+    grad_x = total(swap(gx, "mp", Y_GROUPS))
+    smem = pl.BlockSpec(memory_space=pltpu.SMEM)
+    vmem = pl.BlockSpec(memory_space=pltpu.VMEM)
+    grad_w = pl.pallas_call(
+        whole_kernel,
+        out_shape=jax.ShapeDtypeStruct((slots * BS, BS), F32),
+        in_specs=[smem, pl.BlockSpec(memory_space=pl.ANY)] + [vmem] * 7,
+        out_specs=vmem,
+        scratch_shapes=[pltpu.VMEM((NZ, CHUNK, BS), BF16)],
+        compiler_params=pltpu.CompilerParams(vmem_limit_bytes=40 << 20),
+    )(rel, grad_x, mine, k4, k8, low1, high1, low2, high2)
+    return grad_x, grad_w.reshape(slots, BS, BS)
 
 
 def local(inputs, block_weights, block_list, grad_act):
@@ -111,21 +213,11 @@
     own = by_xy.reshape(HALF, tokens, BS)
     sib = lax.ppermute(own, "mp", CORE_SWAP)
 
-    act, gx_own, gx_sib, gw = run_blocks(idx, col, live, own, sib, wb, grad_act)
-
-    rows = gw.shape[0] * BS
-    near = swap(gw.reshape(3, rows // 3, BS), "dp", Z_NEAR)
-    near = total(near).astype(BF16)
-    far = swap(near.reshape(4, rows // NZ, BS), "dp", Z_FAR)
-    mine = total(far).astype(BF16)
-    whole = lax.all_gather(mine, "dp", axis=0, tiled=False)
-    whole = whole.reshape(4, 3, rows // NZ, BS).swapaxes(0, 1)
-    grad_w = whole.reshape(rows // BS, BS, BS)[:slots].astype(F32)
-
-    gx = (gx_own.astype(F32) + lax.ppermute(gx_sib, "mp", CORE_SWAP).astype(F32)).astype(BF16)
-    gx = swap(gx.reshape(NX, NY, tokens, BS), "mp", X_GROUPS)
-    gx = swap(total(gx).astype(BF16), "mp", Y_GROUPS)
-    grad_x = total(gx)
+    rel = (jnp.arange(NZ, dtype=jnp.int32) + NZ - lax.axis_index("dp")) % NZ
+    act, gx_own, gx_sib, keep, up1, down1, up2, down2 = run_blocks(
+        idx, col, live, rel, own, sib, wb, grad_act
+    )
+    grad_x, grad_w = reduce_gradients(gx_own, gx_sib, keep, up1, down1, up2, down2, rel, slots)
     return act, grad_x, grad_w
 
 

time: 177 us -> 157 us (0.89); the launches traced: 176 us -> 154 us
  blocking collectives: 88.1 us -> 18.8 us
  starting transfers between devices: 18.5 us -> 79.8 us
  between operations: 14.1 us -> 0.84 us
  other arithmetic: 8.82 us -> 4.25 us
  Pallas kernels: 3.73 us -> 7.18 us
  waiting for transfers between devices: 40.3 us -> 42.1 us
    all_to_all x5 -> x1, blocking collectives: 88.1 us -> 18.8 us  [swap(): return lax.all_to_all(x, axis, 0, 0, tiled=True, axis_index_groups=groups)]
    ppermute x1 -> x13, starting transfers between devices: 1.92 us -> 61.7 us  [the longest x12 59.7 us: shift(): return lax.ppermute(x, 'dp', [(i, (i + by) % NZ) for i in range(NZ)])]
    ppermute x1 -> x13, waiting for transfers between devices: 0.01 us -> 32.6 us  [the longest x12 30.1 us: shift(): return lax.ppermute(x, 'dp', [(i, (i + by) % NZ) for i in range(NZ)])]
    all_gather x1 -> x0, waiting for transfers between devices: 25.5 us -> none  [local(): whole = lax.all_gather(mine, 'dp', axis=0, tiled=False)]
    all_to_all x1 -> x3, waiting for transfers between devices: 14.2 us -> 8.93 us  [swap(): return lax.all_to_all(x, axis, 0, 0, tiled=True, axis_index_groups=groups)]
    pallas_call x0 -> x5, Pallas kernels: none -> 3.36 us  [the longest x1 2.24 us: reduce_gradients(): pl.pallas_call(whole_kernel, out_shape=jax.ShapeDtypeStruct((slots * BS,...]
    reduce_sum x4 -> x1, other arithmetic: 2.65 us -> 0.04 us  [total(): return jnp.sum(x.astype(F32), axis=0)]
    convert_element_type x2 -> x1, other arithmetic: 3.32 us -> 1.34 us  [reduce_gradients(): gx = (gx_own.astype(F32) + gx_sib.astype(F32)).astype(BF16)]
  transfers between devices with their start and end apart: 4 -> 17, of which waited for: 3 -> 11; matrix products, arithmetic and copies ran while one was open for 3% -> 1% of each run, Pallas kernels for 0% -> 0%
where the time goes in v2:
time: 157 us; the launch traced here: 154 us
  starting transfers between devices  79.8 us (51%)
  waiting for transfers between devices  42.1 us (27%)
  blocking collectives  18.8 us (12%)
  Pallas kernels  7.18 us (5%)
  other arithmetic  4.25 us (3%)
    ppermute x12, starting transfers between devices, shift(): return lax.ppermute(x, 'dp', [(i, (i + by) % NZ) for i in range(NZ)])  59.7 us
    ppermute x12, waiting for transfers between devices, shift(): return lax.ppermute(x, 'dp', [(i, (i + by) % NZ) for i in range(NZ)])  30.1 us
    all_to_all x1, blocking collectives, swap(): return lax.all_to_all(x, axis, 0, 0, tiled=True, axis_index_groups=groups)  18.8 us
    all_to_all x3, starting transfers between devices, swap(): return lax.all_to_all(x, axis, 0, 0, tiled=True, axis_index_groups=groups)  16.2 us
    all_to_all x3, waiting for transfers between devices, swap(): return lax.all_to_all(x, axis, 0, 0, tiled=True, axis_index_groups=groups)  8.93 us
    pallas_call x1, Pallas kernels, run_blocks(): pl.pallas_call(block_kernel, out_shape=(jax.ShapeDtypeStruct((tokens, hid...  3.81 us
  transfers between devices with their start and end apart: 17, of which 11 were waited for; matrix products, arithmetic and copies ran while one was open for 1% of the time, Pallas kernels for 0%

profile of v2, /device:TPU:6, one launch (start us, length us, event | category | flops | bytes accessed | tf_op | source)
XLA Modules:
  0.0 154.2 jit_solution(13307856263667017242)
XLA Ops:
  1.5 18.8 %all_to_all.20 = bf16[8,128,128]{2,1,0:T(8,128)(2,1)S(1)} all-to-all(bf16[8,128,128]{2,1,0:T(8,128)(2,1)S(1)} %broadcast_in_dim.4), channel_id=1, replica_groups={{0,8,16,24,32,40,48,56},{1,9,17,25,33,41,49,57},{2,10,18,26,34,42,50,58..., dimensions={0} | all-to-all | bytes 524288 | tf_op jit(solution)/shard_map/all_to_all | solution.py:142
  20.3 1.2 broadcast_in_dim.5
  21.5 7.2 %all-to-all-start.1 = ((bf16[4,8,128,128]{3,2,1,0:T(8,128)(2,1)}), bf16[4,8,128,128]{3,2,1,0:T(8,128)(2,1)S(1)}, u32[]{:S(2)}, u32[]{:S(2)}) async-start(bf16[4,8,128,128]{3,2,1,0:T(8,128)(2,1)} %broadcast_in_dim.5), calls=%async_computation.1 | async-start | bytes 2097152 | tf_op jit(solution)/shard_map/all_to_all | solution.py:142
  28.7 8.9 %all-to-all-done.1 = bf16[4,8,128,128]{3,2,1,0:T(8,128)(2,1)S(1)} async-done(((bf16[4,8,128,128]{3,2,1,0:T(8,128)(2,1)}), bf16[4,8,128,128]{3,2,1,0:T(8,128)(2,1)S(1)}, u32[]{:S(2)}, u32[]{:S(2)}) %all-to-all-start.1) | async-done | bytes 1048608 | tf_op jit(solution)/shard_map/all_to_all | solution.py:142
  37.7 1.9 %collective-permute-start = (bf16[32,128,128]{2,1,0:T(8,128)(2,1)S(1)}, bf16[32,128,128]{2,1,0:T(8,128)(2,1)S(1)}, u32[]{:S(2)}, u32[]{:S(2)}) collective-permute-start(bf16[32,128,128]{2,1,0:T(8,128)(2,1)S(1)} %bitcast.32), channel_id=1, source_target_pairs={{0,1},{1,0},{2,3},{3,2},{4,5},{5,4},{6,7},{7,6},{8,9},{9,8},{10,11... | collective-permute-start | bytes 3145736 | tf_op jit(solution)/shard_map/ppermute | solution.py:214
  39.7 2.0 %multiply_convert_fusion.w_ref = bf16[38,128,128]{2,1,0:T(8,128)(2,1)S(1)} fusion(f32[38,128,128]{2,1,0:T(8,128)} %param.5, f32[38]{0:T(128)S(1)} %fusion.7.live_ref), kind=kLoop, calls=%fused_computation | loop fusion | flops 1245184 | bytes 3735704 | tf_op jit(solution)/shard_map/convert_element_type | solution.py:209
  42.2 3.8 %shard_map.67 = (f32[128,512]{1,0:T(8,128)}, bf16[32,128,128]{2,1,0:T(8,128)(2,1)S(1)}, bf16[32,128,128]{2,1,0:T(8,128)(2,1)S(1)}, bf16[3,416,128]{2,1,0:T(8,128...) custom-call(s32[38]{0:T(128)S(1)} %fusion.5.idx_ref, ...), custom_call_target="tpu_custom_call" | custom-call | tf_op jit(solution)/shard_map/pallas_call | solution.py:119
  46.0 2.0 %collective-permute-start.1 = (bf16[32,128,128]{2,1,0:T(8,128)(2,1)S(1)}, bf16[32,128,128]{2,1,0:T(8,128)(2,1)S(1)}, u32[]{:S(2)}, u32[]{:S(2)}) collective-permute-start(bf16[32,128,128]{2,1,0:T(8,128)(2,1)S(1)} %get-tuple-element.19), channel_id=1, source_target_pairs={{0,1},{1,0},{2,3},{3,2},{4,5},{5,4},{6,7},{7,6},{8,9},{9,8},{10,11... | collective-permute-start | bytes 3145736 | tf_op jit(solution)/shard_map/ppermute | solution.py:170
  48.1 2.5 %collective-permute-done.1 = bf16[32,128,128]{2,1,0:T(8,128)(2,1)S(1)} collective-permute-done((bf16[32,128,128]{2,1,0:T(8,128)(2,1)S(1)}, bf16[32,128,128]{2,1,0:T(8,128)(2,1)S(1)}, u32[]{:S(2)}, u32[]{:S(2)}) %collective-permute-start.1) | collective-permute-done | bytes 1048608 | tf_op jit(solution)/shard_map/ppermute | solution.py:170
  50.6 1.3 add_convert_fusion.after_ref
  51.9 5.6 %all-to-all-start.2 = ((bf16[4,8,128,128]{3,2,1,0:T(8,128)(2,1)}), bf16[4,8,128,128]{3,2,1,0:T(8,128)(2,1)S(1)}, u32[]{:S(2)}, u32[]{:S(2)}) async-start(bf16[4,8,128,128]{3,2,1,0:T(8,128)(2,1)} %bitcast.8), calls=%async_computation.2 | async-start | bytes 2097152 | tf_op jit(solution)/shard_map/all_to_all | solution.py:142
  57.5 4.3 %collective-permute-start.2 = (bf16[3,416,128]{2,1,0:T(8,128)(2,1)S(1)}, bf16[3,416,128]{2,1,0:T(8,128)(2,1)S(1)}, u32[]{:S(2)}, u32[]{:S(2)}) collective-permute-start(bf16[3,416,128]{2,1,0:T(8,128)(2,1)S(1)} %get-tuple-element.21), channel_id=1, source_target_pairs={{0,64},{64,128},{128,192},{192,256},{256,320},{320,384},{384,448},... | collective-permute-start | bytes 958472 | tf_op jit(solution)/shard_map/ppermute | solution.py:150
  61.8 12.2 %collective-permute-start.3 = (bf16[3,416,128]{2,1,0:T(8,128)(2,1)S(1)}, bf16[3,416,128]{2,1,0:T(8,128)(2,1)S(1)}, u32[]{:S(2)}, u32[]{:S(2)}) collective-permute-start(bf16[3,416,128]{2,1,0:T(8,128)(2,1)S(1)} %get-tuple-element.22), channel_id=1, source_target_pairs={{0,704},{64,0},{128,64},{192,128},{256,192},{320,256},{384,320},{4... | collective-permute-start | bytes 958472 | tf_op jit(solution)/shard_map/ppermute | solution.py:150
  74.0 1.9 %collective-permute-start.4 = (bf16[3,208,128]{2,1,0:T(8,128)(2,1)S(1)}, bf16[3,208,128]{2,1,0:T(8,128)(2,1)S(1)}, u32[]{:S(2)}, u32[]{:S(2)}) collective-permute-start(bf16[3,208,128]{2,1,0:T(8,128)(2,1)S(1)} %get-tuple-element.23), channel_id=1, source_target_pairs={{0,128},{64,192},{128,256},{192,320},{256,384},{320,448},{384,512}... | collective-permute-start | bytes 479240 | tf_op jit(solution)/shard_map/ppermute | solution.py:150
  75.9 6.0 %collective-permute-start.5 = (bf16[3,208,128]{2,1,0:T(8,128)(2,1)S(1)}, bf16[3,208,128]{2,1,0:T(8,128)(2,1)S(1)}, u32[]{:S(2)}, u32[]{:S(2)}) collective-permute-start(bf16[3,208,128]{2,1,0:T(8,128)(2,1)S(1)} %get-tuple-element.24), channel_id=1, source_target_pairs={{0,640},{64,704},{128,0},{192,64},{256,128},{320,192},{384,256},{4... | collective-permute-start | bytes 479240 | tf_op jit(solution)/shard_map/ppermute | solution.py:150
  81.9 4.0 %collective-permute-done.4.c_ref = bf16[3,208,128]{2,1,0:T(8,128)(2,1)S(1)} collective-permute-done((bf16[3,208,128]{2,1,0:T(8,128)(2,1)S(1)}, bf16[3,208,128]{2,1,0:T(8,128)(2,1)S(1)}, u32[]{:S(2)}, u32[]{:S(2)}) %collective-permute-start.4) | collective-permute-done | bytes 159776 | tf_op jit(solution)/shard_map/ppermute | solution.py:150
  85.9 2.2 %collective-permute-done.5.d_ref = bf16[3,208,128]{2,1,0:T(8,128)(2,1)S(1)} collective-permute-done((bf16[3,208,128]{2,1,0:T(8,128)(2,1)S(1)}, bf16[3,208,128]{2,1,0:T(8,128)(2,1)S(1)}, u32[]{:S(2)}, u32[]{:S(2)}) %collective-permute-start.5) | collective-permute-done | bytes 159776 | tf_op jit(solution)/shard_map/ppermute | solution.py:150
  88.3 5.1 %collective-permute-start.6 = (bf16[416,128]{1,0:T(8,128)(2,1)S(1)}, bf16[416,128]{1,0:T(8,128)(2,1)S(1)}, u32[]{:S(2)}, u32[]{:S(2)}) collective-permute-start(bf16[416,128]{1,0:T(8,128)(2,1)S(1)} %get-tuple-element.26), channel_id=1, source_target_pairs={{0,256},{64,320},{128,384},{192,448},{256,512},{320,576},{384,640}... | collective-permute-start | bytes 319496 | tf_op jit(solution)/shard_map/ppermute | solution.py:150
  93.3 4.7 %collective-permute-start.7 = (bf16[416,128]{1,0:T(8,128)(2,1)S(1)}, bf16[416,128]{1,0:T(8,128)(2,1)S(1)}, u32[]{:S(2)}, u32[]{:S(2)}) collective-permute-start(bf16[416,128]{1,0:T(8,128)(2,1)S(1)} %get-tuple-element.27), channel_id=1, source_target_pairs={{0,512},{64,576},{128,640},{192,704},{256,0},{320,64},{384,128},{4... | collective-permute-start | bytes 319496 | tf_op jit(solution)/shard_map/ppermute | solution.py:150
  98.0 4.0 %collective-permute-done.6.a_ref = bf16[416,128]{1,0:T(8,128)(2,1)S(1)} collective-permute-done((bf16[416,128]{1,0:T(8,128)(2,1)S(1)}, bf16[416,128]{1,0:T(8,128)(2,1)S(1)}, u32[]{:S(2)}, u32[]{:S(2)}) %collective-permute-start.6) | collective-permute-done | bytes 106528 | tf_op jit(solution)/shard_map/ppermute | solution.py:150
  102.0 5.0 %collective-permute-done.7.b_ref = bf16[416,128]{1,0:T(8,128)(2,1)S(1)} collective-permute-done((bf16[416,128]{1,0:T(8,128)(2,1)S(1)}, bf16[416,128]{1,0:T(8,128)(2,1)S(1)}, u32[]{:S(2)}, u32[]{:S(2)}) %collective-permute-start.7) | collective-permute-done | bytes 106528 | tf_op jit(solution)/shard_map/ppermute | solution.py:150
  107.0 6.4 %collective-permute-start.9 = (bf16[416,128]{1,0:T(8,128)(2,1)S(1)}, bf16[416,128]{1,0:T(8,128)(2,1)S(1)}, u32[]{:S(2)}, u32[]{:S(2)}) collective-permute-start(bf16[416,128]{1,0:T(8,128)(2,1)S(1)} %shard_map.69.k0_ref), channel_id=1, source_target_pairs={{0,256},{64,320},{128,384},{192,448},{256,512},{320,576},{384,640}... | collective-permute-start | bytes 319496 | tf_op jit(solution)/shard_map/ppermute | solution.py:150
  113.4 3.4 %collective-permute-start.8 = (bf16[416,128]{1,0:T(8,128)(2,1)S(1)}, bf16[416,128]{1,0:T(8,128)(2,1)S(1)}, u32[]{:S(2)}, u32[]{:S(2)}) collective-permute-start(bf16[416,128]{1,0:T(8,128)(2,1)S(1)} %shard_map.69.k0_ref), channel_id=1, source_target_pairs={{0,512},{64,576},{128,640},{192,704},{256,0},{320,64},{384,128},{4... | collective-permute-start | bytes 319496 | tf_op jit(solution)/shard_map/ppermute | solution.py:150
  116.8 3.5 %collective-permute-done.9.k8_ref = bf16[416,128]{1,0:T(8,128)(2,1)S(1)} collective-permute-done((bf16[416,128]{1,0:T(8,128)(2,1)S(1)}, bf16[416,128]{1,0:T(8,128)(2,1)S(1)}, u32[]{:S(2)}, u32[]{:S(2)}) %collective-permute-start.9) | collective-permute-done | bytes 106528 | tf_op jit(solution)/shard_map/ppermute | solution.py:150
  120.3 4.5 %collective-permute-done.8.k4_ref = bf16[416,128]{1,0:T(8,128)(2,1)S(1)} collective-permute-done((bf16[416,128]{1,0:T(8,128)(2,1)S(1)}, bf16[416,128]{1,0:T(8,128)(2,1)S(1)}, u32[]{:S(2)}, u32[]{:S(2)}) %collective-permute-start.8) | collective-permute-done | bytes 106528 | tf_op jit(solution)/shard_map/ppermute | solution.py:150
  125.7 3.4 %all-to-all-start.3 = ((bf16[8,128,128]{2,1,0:T(8,128)(2,1)}), bf16[8,128,128]{2,1,0:T(8,128)(2,1)S(1)}, u32[]{:S(2)}, u32[]{:S(2)}) async-start(bf16[8,128,128]{2,1,0:T(8,128)(2,1)} %shard_map.71), calls=%async_computation.3 | async-start | bytes 524288 | tf_op jit(solution)/shard_map/all_to_all | solution.py:142
  129.1 4.6 %collective-permute-start.11 = (bf16[3,416,128]{2,1,0:T(8,128)(2,1)S(1)}, bf16[3,416,128]{2,1,0:T(8,128)(2,1)S(1)}, u32[]{:S(2)}, u32[]{:S(2)}) collective-permute-start(bf16[3,416,128]{2,1,0:T(8,128)(2,1)S(1)} %get-tuple-element.28.after_ref), channel_id=1, source_target_pairs={{0,704},{64,0},{128,64},{192,128},{256,192},{320,256},{384,320},{4... | collective-permute-start | bytes 958472 | tf_op jit(solution)/shard_map/ppermute | solution.py:150
  133.7 1.9 %collective-permute-start.10 = (bf16[3,416,128]{2,1,0:T(8,128)(2,1)S(1)}, bf16[3,416,128]{2,1,0:T(8,128)(2,1)S(1)}, u32[]{:S(2)}, u32[]{:S(2)}) collective-permute-start(bf16[3,416,128]{2,1,0:T(8,128)(2,1)S(1)} %get-tuple-element.28.after_ref), channel_id=1, source_target_pairs={{0,64},{64,128},{128,192},{192,256},{256,320},{320,384},{384,448},... | collective-permute-start | bytes 958472 | tf_op jit(solution)/shard_map/ppermute | solution.py:150
  135.7 7.3 %collective-permute-start.12 = (bf16[3,208,128]{2,1,0:T(8,128)(2,1)S(1)}, bf16[3,208,128]{2,1,0:T(8,128)(2,1)S(1)}, u32[]{:S(2)}, u32[]{:S(2)}) collective-permute-start(bf16[3,208,128]{2,1,0:T(8,128)(2,1)S(1)} %get-tuple-element.29), channel_id=1, source_target_pairs={{0,128},{64,192},{128,256},{192,320},{256,384},{320,448},{384,512}... | collective-permute-start | bytes 479240 | tf_op jit(solution)/shard_map/ppermute | solution.py:150
  143.0 1.9 %collective-permute-start.13 = (bf16[3,208,128]{2,1,0:T(8,128)(2,1)S(1)}, bf16[3,208,128]{2,1,0:T(8,128)(2,1)S(1)}, u32[]{:S(2)}, u32[]{:S(2)}) collective-permute-start(bf16[3,208,128]{2,1,0:T(8,128)(2,1)S(1)} %get-tuple-element.30), channel_id=1, source_target_pairs={{0,640},{64,704},{128,0},{192,64},{256,128},{320,192},{384,256},{4... | collective-permute-start | bytes 479240 | tf_op jit(solution)/shard_map/ppermute | solution.py:150
  145.0 6.5 %collective-permute-done.12.low2_ref = bf16[3,208,128]{2,1,0:T(8,128)(2,1)S(1)} collective-permute-done((bf16[3,208,128]{2,1,0:T(8,128)(2,1)S(1)}, bf16[3,208,128]{2,1,0:T(8,128)(2,1)S(1)}, u32[]{:S(2)}, u32[]{:S(2)}) %collective-permute-start.12) | collective-permute-done | bytes 159776 | tf_op jit(solution)/shard_map/ppermute | solution.py:150
  152.0 2.2 %shard_map.72 = f32[4864,128]{1,0:T(8,128)} custom-call(s32[12]{0:T(128)S(1)} %and_select_fusion.rel_ref, f32[128,128]{1,0:T(8,128)S(1)} %convert_reduce_fusion.after_ref, bf16[416,128]{1,0:T(8,128)(2,1)S(1)} %shard_map.69.k0_ref, bf16[416,128]{1,0:T(8,128)(2,1)S(1)} %collective-permute-done.8.k4_ref, bf16[416,128]{1,0:T(8,128)(2,1)S(1)} %collective-permute-done.9.k8_ref, ...), custom_call_target="tpu_custom_call" | custom-call | tf_op jit(solution)/shard_map/pallas_call | solution.py:188
  (25 shorter events, 3.2 us)
Async XLA Ops:
  0.6 39.0 %copy-start.2 = (s32[38,2]{0,1:T(2,128)S(1)}, s32[38,2]{0,1:T(2,128)}, u32[]{:S(2)}) copy-start(s32[38,2]{0,1:T(2,128)} %param.6) | copy-start | bytes 916
  21.5 20.7 %copy-start.1 = (f32[128,512]{1,0:T(8,128)S(1)}, f32[128,512]{1,0:T(8,128)}, u32[]{:S(2)}) copy-start(f32[128,512]{1,0:T(8,128)} %g_ref.1) | copy-start | bytes 786436
  21.5 16.1 %all-to-all-start.1 = ((bf16[4,8,128,128]{3,2,1,0:T(8,128)(2,1)}), bf16[4,8,128,128]{3,2,1,0:T(8,128)(2,1)S(1)}, u32[]{:S(2)}, u32[]{:S(2)}) async-start(bf16[4,8,128,128]{3,2,1,0:T(8,128)(2,1)} %broadcast_in_dim.5), calls=%async_computation.1 | async-start | bytes 2097152 | tf_op jit(solution)/shard_map/all_to_all | solution.py:142
  37.7 4.5 %collective-permute-start = (bf16[32,128,128]{2,1,0:T(8,128)(2,1)S(1)}, bf16[32,128,128]{2,1,0:T(8,128)(2,1)S(1)}, u32[]{:S(2)}, u32[]{:S(2)}) collective-permute-start(bf16[32,128,128]{2,1,0:T(8,128)(2,1)S(1)} %bitcast.32), channel_id=1, source_target_pairs={{0,1},{1,0},{2,3},{3,2},{4,5},{5,4},{6,7},{7,6},{8,9},{9,8},{10,11... | collective-permute-start | bytes 3145736 | tf_op jit(solution)/shard_map/ppermute | solution.py:214
  46.0 4.5 %collective-permute-start.1 = (bf16[32,128,128]{2,1,0:T(8,128)(2,1)S(1)}, bf16[32,128,128]{2,1,0:T(8,128)(2,1)S(1)}, u32[]{:S(2)}, u32[]{:S(2)}) collective-permute-start(bf16[32,128,128]{2,1,0:T(8,128)(2,1)S(1)} %get-tuple-element.19), channel_id=1, source_target_pairs={{0,1},{1,0},{2,3},{3,2},{4,5},{5,4},{6,7},{7,6},{8,9},{9,8},{10,11... | collective-permute-start | bytes 3145736 | tf_op jit(solution)/shard_map/ppermute | solution.py:170
  51.9 55.1 %all-to-all-start.2 = ((bf16[4,8,128,128]{3,2,1,0:T(8,128)(2,1)}), bf16[4,8,128,128]{3,2,1,0:T(8,128)(2,1)S(1)}, u32[]{:S(2)}, u32[]{:S(2)}) async-start(bf16[4,8,128,128]{3,2,1,0:T(8,128)(2,1)} %bitcast.8), calls=%async_computation.2 | async-start | bytes 2097152 | tf_op jit(solution)/shard_map/all_to_all | solution.py:142
  57.5 30.6 %collective-permute-start.2 = (bf16[3,416,128]{2,1,0:T(8,128)(2,1)S(1)}, bf16[3,416,128]{2,1,0:T(8,128)(2,1)S(1)}, u32[]{:S(2)}, u32[]{:S(2)}) collective-permute-start(bf16[3,416,128]{2,1,0:T(8,128)(2,1)S(1)} %get-tuple-element.21), channel_id=1, source_target_pairs={{0,64},{64,128},{128,192},{192,256},{256,320},{320,384},{384,448},... | collective-permute-start | bytes 958472 | tf_op jit(solution)/shard_map/ppermute | solution.py:150
  61.8 26.3 %collective-permute-start.3 = (bf16[3,416,128]{2,1,0:T(8,128)(2,1)S(1)}, bf16[3,416,128]{2,1,0:T(8,128)(2,1)S(1)}, u32[]{:S(2)}, u32[]{:S(2)}) collective-permute-start(bf16[3,416,128]{2,1,0:T(8,128)(2,1)S(1)} %get-tuple-element.22), channel_id=1, source_target_pairs={{0,704},{64,0},{128,64},{192,128},{256,192},{320,256},{384,320},{4... | collective-permute-start | bytes 958472 | tf_op jit(solution)/shard_map/ppermute | solution.py:150
  74.0 11.9 %collective-permute-start.4 = (bf16[3,208,128]{2,1,0:T(8,128)(2,1)S(1)}, bf16[3,208,128]{2,1,0:T(8,128)(2,1)S(1)}, u32[]{:S(2)}, u32[]{:S(2)}) collective-permute-start(bf16[3,208,128]{2,1,0:T(8,128)(2,1)S(1)} %get-tuple-element.23), channel_id=1, source_target_pairs={{0,128},{64,192},{128,256},{192,320},{256,384},{320,448},{384,512}... | collective-permute-start | bytes 479240 | tf_op jit(solution)/shard_map/ppermute | solution.py:150
  75.9 12.2 %collective-permute-start.5 = (bf16[3,208,128]{2,1,0:T(8,128)(2,1)S(1)}, bf16[3,208,128]{2,1,0:T(8,128)(2,1)S(1)}, u32[]{:S(2)}, u32[]{:S(2)}) collective-permute-start(bf16[3,208,128]{2,1,0:T(8,128)(2,1)S(1)} %get-tuple-element.24), channel_id=1, source_target_pairs={{0,640},{64,704},{128,0},{192,64},{256,128},{320,192},{384,256},{4... | collective-permute-start | bytes 479240 | tf_op jit(solution)/shard_map/ppermute | solution.py:150
  88.3 13.7 %collective-permute-start.6 = (bf16[416,128]{1,0:T(8,128)(2,1)S(1)}, bf16[416,128]{1,0:T(8,128)(2,1)S(1)}, u32[]{:S(2)}, u32[]{:S(2)}) collective-permute-start(bf16[416,128]{1,0:T(8,128)(2,1)S(1)} %get-tuple-element.26), channel_id=1, source_target_pairs={{0,256},{64,320},{128,384},{192,448},{256,512},{320,576},{384,640}... | collective-permute-start | bytes 319496 | tf_op jit(solution)/shard_map/ppermute | solution.py:150
  93.3 13.6 %collective-permute-start.7 = (bf16[416,128]{1,0:T(8,128)(2,1)S(1)}, bf16[416,128]{1,0:T(8,128)(2,1)S(1)}, u32[]{:S(2)}, u32[]{:S(2)}) collective-permute-start(bf16[416,128]{1,0:T(8,128)(2,1)S(1)} %get-tuple-element.27), channel_id=1, source_target_pairs={{0,512},{64,576},{128,640},{192,704},{256,0},{320,64},{384,128},{4... | collective-permute-start | bytes 319496 | tf_op jit(solution)/shard_map/ppermute | solution.py:150
  107.0 13.2 %collective-permute-start.9 = (bf16[416,128]{1,0:T(8,128)(2,1)S(1)}, bf16[416,128]{1,0:T(8,128)(2,1)S(1)}, u32[]{:S(2)}, u32[]{:S(2)}) collective-permute-start(bf16[416,128]{1,0:T(8,128)(2,1)S(1)} %shard_map.69.k0_ref), channel_id=1, source_target_pairs={{0,256},{64,320},{128,384},{192,448},{256,512},{320,576},{384,640}... | collective-permute-start | bytes 319496 | tf_op jit(solution)/shard_map/ppermute | solution.py:150
  113.4 11.4 %collective-permute-start.8 = (bf16[416,128]{1,0:T(8,128)(2,1)S(1)}, bf16[416,128]{1,0:T(8,128)(2,1)S(1)}, u32[]{:S(2)}, u32[]{:S(2)}) collective-permute-start(bf16[416,128]{1,0:T(8,128)(2,1)S(1)} %shard_map.69.k0_ref), channel_id=1, source_target_pairs={{0,512},{64,576},{128,640},{192,704},{256,0},{320,64},{384,128},{4... | collective-permute-start | bytes 319496 | tf_op jit(solution)/shard_map/ppermute | solution.py:150
  125.7 19.2 %all-to-all-start.3 = ((bf16[8,128,128]{2,1,0:T(8,128)(2,1)}), bf16[8,128,128]{2,1,0:T(8,128)(2,1)S(1)}, u32[]{:S(2)}, u32[]{:S(2)}) async-start(bf16[8,128,128]{2,1,0:T(8,128)(2,1)} %shard_map.71), calls=%async_computation.3 | async-start | bytes 524288 | tf_op jit(solution)/shard_map/all_to_all | solution.py:142
  129.1 22.8 %collective-permute-start.11 = (bf16[3,416,128]{2,1,0:T(8,128)(2,1)S(1)}, bf16[3,416,128]{2,1,0:T(8,128)(2,1)S(1)}, u32[]{:S(2)}, u32[]{:S(2)}) collective-permute-start(bf16[3,416,128]{2,1,0:T(8,128)(2,1)S(1)} %get-tuple-element.28.after_ref), channel_id=1, source_target_pairs={{0,704},{64,0},{128,64},{192,128},{256,192},{320,256},{384,320},{4... | collective-permute-start | bytes 958472 | tf_op jit(solution)/shard_map/ppermute | solution.py:150
  133.7 18.2 %collective-permute-start.10 = (bf16[3,416,128]{2,1,0:T(8,128)(2,1)S(1)}, bf16[3,416,128]{2,1,0:T(8,128)(2,1)S(1)}, u32[]{:S(2)}, u32[]{:S(2)}) collective-permute-start(bf16[3,416,128]{2,1,0:T(8,128)(2,1)S(1)} %get-tuple-element.28.after_ref), channel_id=1, source_target_pairs={{0,64},{64,128},{128,192},{192,256},{256,320},{320,384},{384,448},... | collective-permute-start | bytes 958472 | tf_op jit(solution)/shard_map/ppermute | solution.py:150
  135.7 15.8 %collective-permute-start.12 = (bf16[3,208,128]{2,1,0:T(8,128)(2,1)S(1)}, bf16[3,208,128]{2,1,0:T(8,128)(2,1)S(1)}, u32[]{:S(2)}, u32[]{:S(2)}) collective-permute-start(bf16[3,208,128]{2,1,0:T(8,128)(2,1)S(1)} %get-tuple-element.29), channel_id=1, source_target_pairs={{0,128},{64,192},{128,256},{192,320},{256,384},{320,448},{384,512}... | collective-permute-start | bytes 479240 | tf_op jit(solution)/shard_map/ppermute | solution.py:150
  143.0 9.0 %collective-permute-start.13 = (bf16[3,208,128]{2,1,0:T(8,128)(2,1)S(1)}, bf16[3,208,128]{2,1,0:T(8,128)(2,1)S(1)}, u32[]{:S(2)}, u32[]{:S(2)}) collective-permute-start(bf16[3,208,128]{2,1,0:T(8,128)(2,1)S(1)} %get-tuple-element.30), channel_id=1, source_target_pairs={{0,640},{64,704},{128,0},{192,64},{256,128},{320,192},{384,256},{4... | collective-permute-start | bytes 479240 | tf_op jit(solution)/shard_map/ppermute | solution.py:150
  145.0 9.2 %copy-start = (f32[128,128]{1,0:T(8,128)}, f32[128,128]{1,0:T(8,128)S(1)}, u32[]{:S(2)}) copy-start(f32[128,128]{1,0:T(8,128)S(1)} %convert_reduce_fusion.after_ref) | copy-start | bytes 196612

commit v3 on v1

v3 whole, which is shorter than its diff:
```python
import jax
import jax.numpy as jnp
from jax import lax
from jax.experimental import pallas as pl
from jax.experimental.pallas import tpu as pltpu
from jax.sharding import PartitionSpec as P

BS = 128
NY, NX, NC = 8, 4, 2
NZ = 12
HALF = NY * NX
Y_GROUPS = [[(y * NX + x) * NC + c for y in range(NY)] for x in range(NX) for c in range(NC)]
X_GROUPS = [[(y * NX + x) * NC + c for x in range(NX)] for y in range(NY) for c in range(NC)]
CORE_SWAP = [(i, i ^ 1) for i in range(HALF * NC)]
CHUNK = 416
Z_FAR = [[3 * i + r for i in range(4)] for r in range(3)]
F32, BF16 = jnp.float32, jnp.bfloat16


def gelu_parts(pre):
    inner = 0.7978845608 * (pre + 0.044715 * pre * pre * pre)
    tanh_val = jnp.tanh(inner)
    value = 0.5 * pre * (1.0 + tanh_val)
    slope = 0.5 * (1.0 + tanh_val) + 0.5 * pre * (1.0 - tanh_val * tanh_val) * 0.7978845608 * (
        1.0 + 3.0 * 0.044715 * pre * pre
    )
    return value, slope


def dot(a, b, dims):
    return lax.dot_general(a, b, (dims, ((), ())), preferred_element_type=F32)


def forward_kernel(idx_ref, col_ref, live_ref, rel_ref, own_ref, sib_ref, w_ref, g_ref,
                   act_ref, dpre_ref, keep_ref, up_ref, down_ref, x_ref, prod_ref, pre_ref, gw_ref):
    slots = w_ref.shape[0]
    x_ref[:HALF] = own_ref[...]
    x_ref[HALF:] = sib_ref[...]
    pre_ref[...] = jnp.zeros_like(pre_ref)
    for s in range(slots):
        prod_ref[s] = dot(x_ref[idx_ref[s]], w_ref[s], ((1,), (0,)))
    for s in range(slots):
        pre_ref[col_ref[s]] += prod_ref[s]
    for c in range(pre_ref.shape[0]):
        value, slope = gelu_parts(pre_ref[c])
        lanes = slice(c * BS, (c + 1) * BS)
        act_ref[:, lanes] = value
        dpre_ref[c] = (g_ref[:, lanes] * slope).astype(BF16)
    for s in range(slots):
        wgrad = dot(x_ref[idx_ref[s]], dpre_ref[col_ref[s]], ((0,), (0,)))
        wgrad = (wgrad * live_ref[s]).astype(BF16)
        done = 0
        while done < BS:
            chunk, at = divmod(s * BS + done, CHUNK)
            size = min(BS - done, CHUNK - at)
            gw_ref[rel_ref[chunk], at:at + size] = wgrad[done:done + size]
            done += size
    chunk, at = divmod(slots * BS, CHUNK)
    gw_ref[rel_ref[chunk], at:] = jnp.zeros((CHUNK - at, BS), BF16)
    for b in range(4):
        keep_ref[b] = gw_ref[3 * b]
        up_ref[b] = gw_ref[3 * b + 1]
        down_ref[b] = gw_ref[(3 * b + 11) % NZ]


def backward_kernel(idx_ref, col_ref, w_ref, dpre_ref, gx_own_ref, gx_sib_ref, prod_ref, gx_ref):
    slots = w_ref.shape[0]
    gx_ref[...] = jnp.zeros_like(gx_ref)
    for s in range(slots):
        prod_ref[s] = dot(dpre_ref[col_ref[s]], w_ref[s], ((1,), (1,)))
    for s in range(slots):
        gx_ref[idx_ref[s]] += prod_ref[s]
    gx_own_ref[...] = gx_ref[:HALF].astype(BF16)
    gx_sib_ref[...] = gx_ref[HALF:].astype(BF16)


def near_kernel(far_ref, after_ref, keep_ref, a_ref, b_ref, out_ref):
    for b in range(4):
        part = keep_ref[b].astype(F32) + a_ref[b].astype(F32) + b_ref[b].astype(F32)
        out_ref[far_ref[b]] = part.astype(BF16)


def far_kernel(after_ref, in_ref, out_ref):
    part = jnp.sum(in_ref[...].astype(F32), axis=0).astype(BF16)
    for b in range(4):
        out_ref[b] = part


def x_sum_kernel(in_ref, out_ref):
    out_ref[...] = jnp.sum(in_ref[...].astype(F32), axis=0).astype(BF16)


def whole_kernel(place_ref, after_ref, mid_ref, low_ref, high_ref, out_ref, gw_ref):
    for i, part in enumerate((low_ref, mid_ref, high_ref)):
        for b in range(4):
            gw_ref[3 * b + place_ref[i]] = part[b]
    rows = out_ref.shape[0]
    for j in range(NZ):
        size = min(CHUNK, rows - j * CHUNK)
        out_ref[j * CHUNK:j * CHUNK + size] = gw_ref[j, :size].astype(F32)


SMEM = pl.BlockSpec(memory_space=pltpu.SMEM)
VMEM = pl.BlockSpec(memory_space=pltpu.VMEM)
ORDER = pl.BlockSpec(memory_space=pl.ANY)


def call(kernel, specs, ins, outs, scratch=(), flops=0, moved=0):
    return pl.pallas_call(
        kernel,
        out_shape=outs,
        in_specs=specs,
        out_specs=jax.tree.map(lambda _: VMEM, outs),
        scratch_shapes=scratch,
        compiler_params=pltpu.CompilerParams(vmem_limit_bytes=40 << 20),
        cost_estimate=pl.CostEstimate(flops=flops, bytes_accessed=moved, transcendentals=0),
    )(*ins)


def array(shape, kind=BF16):
    return jax.ShapeDtypeStruct(shape, kind)


def forward(idx, col, live, rel, own, sib, wb, grad_act):
    slots = wb.shape[0]
    tokens, hidden = grad_act.shape
    cols = hidden // BS
    chunks = array((4, CHUNK, BS))
    return call(
        forward_kernel,
        [SMEM] * 4 + [VMEM] * 4,
        (idx, col, live, rel, own, sib, wb, grad_act),
        (array((tokens, hidden), F32), array((cols, tokens, BS)), chunks, chunks, chunks),
        [
            pltpu.VMEM((2 * HALF, tokens, BS), BF16),
            pltpu.VMEM((slots, tokens, BS), F32),
            pltpu.VMEM((cols, tokens, BS), F32),
            pltpu.VMEM((NZ, CHUNK, BS), BF16),
        ],
    )


def backward(idx, col, wb, dpre):
    slots = wb.shape[0]
    tokens = dpre.shape[1]
    half = array((HALF, tokens, BS))
    return call(
        backward_kernel,
        [SMEM] * 2 + [VMEM] * 2,
        (idx, col, wb, dpre),
        (half, half),
        [pltpu.VMEM((slots, tokens, BS), F32), pltpu.VMEM((2 * HALF, tokens, BS), F32)],
        flops=2 * slots * tokens * BS * BS,
        moved=8 << 20,
    )


def swap(x, axis, groups):
    return lax.all_to_all(x, axis, 0, 0, tiled=True, axis_index_groups=groups)


def total(x):
    return jnp.sum(x.astype(F32), axis=0)


def shift(x, by):
    return lax.ppermute(x, "dp", [(i, (i + by) % NZ) for i in range(NZ)])


def reduce_gradients(gx_own, gx_sib, keep, up, down, slots):
    tokens = gx_own.shape[1]
    z = lax.axis_index("dp")
    chunks = array((4, CHUNK, BS))
    from_low, from_high = shift(up, 1), shift(down, -1)
    gx_sib = lax.ppermute(gx_sib, "mp", CORE_SWAP)
    gx = (gx_own.astype(F32) + gx_sib.astype(F32)).astype(BF16)
    member = (jnp.arange(4, dtype=jnp.int32) + z // 3) % 4
    near = call(
        near_kernel, [SMEM, ORDER] + [VMEM] * 3, (member, gx, keep, from_low, from_high), chunks
    )

    far = swap(near, "dp", Z_FAR)
    gx = swap(gx.reshape(NX, NY, tokens, BS), "mp", X_GROUPS)
    mine = call(far_kernel, [ORDER, VMEM], (gx, far), chunks)

    mid = swap(mine, "dp", Z_FAR)
    gx = call(x_sum_kernel, [VMEM], (gx,), array((NY, tokens, BS)))
    grad_x = total(swap(gx, "mp", Y_GROUPS))

    low, high = shift(mid, 1), shift(mid, -1)
    place = (jnp.arange(3, dtype=jnp.int32) + z + 2) % 3
    grad_w = call(
        whole_kernel,
        [SMEM, ORDER] + [VMEM] * 3,
        (place, grad_x, mid, low, high),
        array((slots * BS, BS), F32),
        [pltpu.VMEM((NZ, CHUNK, BS), BF16)],
    )
    return grad_x, grad_w.reshape(slots, BS, BS)


def local(inputs, block_weights, block_list, grad_act):
    tokens = inputs.shape[0]
    slots = block_weights.shape[0]
    row_ids, col_ids = block_list[:, 0], block_list[:, 1]
    live = (row_ids >= 0).astype(F32)
    row = jnp.maximum(row_ids, 0)
    col = jnp.maximum(col_ids, 0)
    core = lax.axis_index("mp") % NC
    idx = ((row % NC) ^ core) * HALF + ((row // NC) % NX) * NY + row // (NC * NX)
    xb = inputs.astype(BF16)
    wb = (block_weights * live[:, None, None]).astype(BF16)

    by_y = swap(jnp.broadcast_to(xb[None], (NY, tokens, BS)), "mp", Y_GROUPS)
    by_xy = swap(jnp.broadcast_to(by_y[None], (NX, NY, tokens, BS)), "mp", X_GROUPS)
    own = by_xy.reshape(HALF, tokens, BS)
    sib = lax.ppermute(own, "mp", CORE_SWAP)

    rel = (jnp.arange(NZ, dtype=jnp.int32) + NZ - lax.axis_index("dp")) % NZ
    act, dpre, keep, up, down = forward(idx, col, live, rel, own, sib, wb, grad_act)
    gx_own, gx_sib = backward(idx, col, wb, dpre)
    grad_x, grad_w = reduce_gradients(gx_own, gx_sib, keep, up, down, slots)
    return act, grad_x, grad_w


def solution(mesh):
    in_specs = (P("dp", "mp"), P("mp", None, None), P("mp", None), P("dp", "mp"))
    out_specs = (P("dp", "mp"), P("dp", "mp"), P("mp", None, None))
    return jax.shard_map(local, mesh=mesh, in_specs=in_specs, out_specs=out_specs, check_vma=False)
```

time: 177 us -> 154 us (0.87)
  blocking collectives: 88.1 us -> 45.1 us
  starting transfers between devices: 18.5 us -> 47.2 us
  between operations: 14.1 us -> 0.82 us
  Pallas kernels: 3.73 us -> 9.18 us
  other arithmetic: 8.82 us -> 4.35 us
  waiting for transfers between devices: 40.3 us -> 44.6 us
    all_to_all x5 -> x2, blocking collectives: 88.1 us -> 45.1 us  [swap(): return lax.all_to_all(x, axis, 0, 0, tiled=True, axis_index_groups=groups)]
    all_gather x1 -> x0, waiting for transfers between devices: 25.5 us -> none  [local(): whole = lax.all_gather(mine, 'dp', axis=0, tiled=False)]
    ppermute x1 -> x5, starting transfers between devices: 1.92 us -> 25.6 us  [the longest x4 23.6 us: shift(): return lax.ppermute(x, 'dp', [(i, (i + by) % NZ) for i in range(NZ)])]
    all_to_all x1 -> x4, waiting for transfers between devices: 14.2 us -> 29.4 us  [swap(): return lax.all_to_all(x, axis, 0, 0, tiled=True, axis_index_groups=groups)]
    ppermute x1 -> x5, waiting for transfers between devices: 0.01 us -> 14.6 us  [the longest x4 12.1 us: shift(): return lax.ppermute(x, 'dp', [(i, (i + by) % NZ) for i in range(NZ)])]
    pallas_call x1 -> x6, Pallas kernels: 3.73 us -> 9.18 us  [call(): pl.pallas_call(kernel, out_shape=outs, in_specs=specs, out_specs=jax.tree...]
    all_to_all x1 -> x4, starting transfers between devices: 14.5 us -> 19.6 us  [swap(): return lax.all_to_all(x, axis, 0, 0, tiled=True, axis_index_groups=groups)]
    reduce_sum x4 -> x1, other arithmetic: 2.65 us -> 0.04 us  [total(): return jnp.sum(x.astype(F32), axis=0)]
  transfers between devices with their start and end apart: 4 -> 10, of which waited for: 3 -> 9; matrix products, arithmetic and copies ran while one was open for 3% -> 1% of each run, Pallas kernels for 0% -> 1%
where the time goes in v3:
time: 154 us; the launch traced here: 152 us
  starting transfers between devices  47.2 us (31%)
  blocking collectives  45.1 us (29%)
  waiting for transfers between devices  44.6 us (29%)
  Pallas kernels  9.18 us (6%)
  other arithmetic  4.35 us (3%)
    all_to_all x2, blocking collectives, swap(): return lax.all_to_all(x, axis, 0, 0, tiled=True, axis_index_groups=groups)  45.1 us
    all_to_all x4, waiting for transfers between devices, swap(): return lax.all_to_all(x, axis, 0, 0, tiled=True, axis_index_groups=groups)  29.4 us
    ppermute x4, starting transfers between devices, shift(): return lax.ppermute(x, 'dp', [(i, (i + by) % NZ) for i in range(NZ)])  23.6 us
    all_to_all x4, starting transfers between devices, swap(): return lax.all_to_all(x, axis, 0, 0, tiled=True, axis_index_groups=groups)  19.6 us
    ppermute x4, waiting for transfers between devices, shift(): return lax.ppermute(x, 'dp', [(i, (i + by) % NZ) for i in range(NZ)])  12.1 us
    pallas_call x6, Pallas kernels, call(): pl.pallas_call(kernel, out_shape=outs, in_specs=specs, out_specs=jax.tree...  9.18 us
  transfers between devices with their start and end apart: 10, of which 9 were waited for; matrix products, arithmetic and copies ran while one was open for 1% of the time, Pallas kernels for 1%

profile of v3, /device:TPU:6, one launch (start us, length us, event | category | flops | bytes accessed | tf_op | source)
XLA Modules:
  0.0 152.4 jit_solution(11962323206379606353)
XLA Ops:
  0.6 0.9 convert_element_type.25
  1.5 18.8 %all_to_all.30 = bf16[8,128,128]{2,1,0:T(8,128)(2,1)S(1)} all-to-all(bf16[8,128,128]{2,1,0:T(8,128)(2,1)S(1)} %broadcast_in_dim.4), channel_id=1, replica_groups={{0,8,16,24,32,40,48,56},{1,9,17,25,33,41,49,57},{2,10,18,26,34,42,50,58..., dimensions={0} | all-to-all | bytes 524288 | tf_op jit(solution)/shard_map/all_to_all | solution.py:159
  20.3 1.2 broadcast_in_dim.5
  21.5 7.2 %all-to-all-start.1 = ((bf16[4,8,128,128]{3,2,1,0:T(8,128)(2,1)}), bf16[4,8,128,128]{3,2,1,0:T(8,128)(2,1)S(1)}, u32[]{:S(2)}, u32[]{:S(2)}) async-start(bf16[4,8,128,128]{3,2,1,0:T(8,128)(2,1)} %broadcast_in_dim.5), calls=%async_computation.1 | async-start | bytes 2097152 | tf_op jit(solution)/shard_map/all_to_all | solution.py:159
  28.7 8.9 %all-to-all-done.1 = bf16[4,8,128,128]{3,2,1,0:T(8,128)(2,1)S(1)} async-done(((bf16[4,8,128,128]{3,2,1,0:T(8,128)(2,1)}), bf16[4,8,128,128]{3,2,1,0:T(8,128)(2,1)S(1)}, u32[]{:S(2)}, u32[]{:S(2)}) %all-to-all-start.1) | async-done | bytes 1048608 | tf_op jit(solution)/shard_map/all_to_all | solution.py:159
  37.7 1.9 %collective-permute-start = (bf16[32,128,128]{2,1,0:T(8,128)(2,1)S(1)}, bf16[32,128,128]{2,1,0:T(8,128)(2,1)S(1)}, u32[]{:S(2)}, u32[]{:S(2)}) collective-permute-start(bf16[32,128,128]{2,1,0:T(8,128)(2,1)S(1)} %bitcast.32), channel_id=1, source_target_pairs={{0,1},{1,0},{2,3},{3,2},{4,5},{5,4},{6,7},{7,6},{8,9},{9,8},{10,11... | collective-permute-start | bytes 3145736 | tf_op jit(solution)/shard_map/ppermute | solution.py:217
  39.7 2.0 %multiply_convert_fusion.w_ref = bf16[38,128,128]{2,1,0:T(8,128)(2,1)S(1)} fusion(f32[38,128,128]{2,1,0:T(8,128)} %param.5, f32[38]{0:T(128)S(1)} %fusion.7.live_ref), kind=kLoop, calls=%fused_computation | loop fusion | flops 1245184 | bytes 3735704 | tf_op jit(solution)/shard_map/convert_element_type | solution.py:212
  41.6 0.6 collective-permute-done.sib_ref
  42.2 2.8 %shard_map.67 = (f32[128,512]{1,0:T(8,128)}, bf16[4,128,128]{2,1,0:T(8,128)(2,1)S(1)}, bf16[4,416,128]{2,1,0:T(8,128)(2,1)S(1)}, bf16[4,416,128]{2,1,0:T(8,128)(2,1)}, bf16[4,416,128]{2,1,0:T(8,128)(2,1)S(1)}) custom-call(s32[38]{0:T(128)S(1)} %fusion.5.idx_ref, s32[38]{0:T(128)S(1)} %maximum_bitcast_fusion.col_ref, f32[38]{0:T(128)S(1)} %fusion.7.live_ref, ...), custom_call_target="tpu_custom_call" | custom-call | tf_op jit(solution)/shard_map/pallas_call | solution.py:109
  45.0 1.8 %shard_map.68 = (bf16[32,128,128]{2,1,0:T(8,128)(2,1)S(1)}, bf16[32,128,128]{2,1,0:T(8,128)(2,1)S(1)}) custom-call(s32[38]{0:T(128)S(1)} %fusion.5.idx_ref, s32[38]{0:T(128)S(1)} %maximum_bitcast_fusion.col_ref, bf16[38,128,128]{2,1,0:T(8,128)(2,1)S(1)} %multiply_convert_fusion.w_ref, bf16[4,128,128]{2,1,0:T(8,128)(2,1)S(1)} %get-tuple-element.11.dpre_ref), custom_call_target="tpu_custom_call" | custom-call | flops 159383552 | bytes 8388608 | tf_op jit(solution)/shard_map/pallas_call | solution.py:109
  46.8 2.0 %collective-permute-start.1 = (bf16[32,128,128]{2,1,0:T(8,128)(2,1)S(1)}, bf16[32,128,128]{2,1,0:T(8,128)(2,1)S(1)}, u32[]{:S(2)}, u32[]{:S(2)}) collective-permute-start(bf16[32,128,128]{2,1,0:T(8,128)(2,1)S(1)} %get-tuple-element.13), channel_id=1, source_target_pairs={{0,1},{1,0},{2,3},{3,2},{4,5},{5,4},{6,7},{7,6},{8,9},{9,8},{10,11... | collective-permute-start | bytes 3145736 | tf_op jit(solution)/shard_map/ppermute | solution.py:175
  48.9 2.5 %collective-permute-done.1 = bf16[32,128,128]{2,1,0:T(8,128)(2,1)S(1)} collective-permute-done((bf16[32,128,128]{2,1,0:T(8,128)(2,1)S(1)}, bf16[32,128,128]{2,1,0:T(8,128)(2,1)S(1)}, u32[]{:S(2)}, u32[]{:S(2)}) %collective-permute-start.1) | collective-permute-done | bytes 1048608 | tf_op jit(solution)/shard_map/ppermute | solution.py:175
  51.4 1.4 add_convert_fusion.after_ref
  52.8 5.6 %all-to-all-start.2 = ((bf16[4,8,128,128]{3,2,1,0:T(8,128)(2,1)}), bf16[4,8,128,128]{3,2,1,0:T(8,128)(2,1)S(1)}, u32[]{:S(2)}, u32[]{:S(2)}) async-start(bf16[4,8,128,128]{3,2,1,0:T(8,128)(2,1)} %bitcast.8), calls=%async_computation.2 | async-start | bytes 2097152 | tf_op jit(solution)/shard_map/all_to_all | solution.py:159
  58.4 4.3 %collective-permute-start.2 = (bf16[4,416,128]{2,1,0:T(8,128)(2,1)}, bf16[4,416,128]{2,1,0:T(8,128)(2,1)S(1)}, u32[]{:S(2)}, u32[]{:S(2)}) collective-permute-start(bf16[4,416,128]{2,1,0:T(8,128)(2,1)} %get-tuple-element.15), channel_id=1, source_target_pairs={{0,64},{64,128},{128,192},{192,256},{256,320},{320,384},{384,448},... | collective-permute-start | bytes 1277960 | tf_op jit(solution)/shard_map/ppermute | solution.py:167
  62.7 12.2 %collective-permute-start.3 = (bf16[4,416,128]{2,1,0:T(8,128)(2,1)S(1)}, bf16[4,416,128]{2,1,0:T(8,128)(2,1)S(1)}, u32[]{:S(2)}, u32[]{:S(2)}) collective-permute-start(bf16[4,416,128]{2,1,0:T(8,128)(2,1)S(1)} %get-tuple-element.16), channel_id=1, source_target_pairs={{0,704},{64,0},{128,64},{192,128},{256,192},{320,256},{384,320},{4... | collective-permute-start | bytes 1277960 | tf_op jit(solution)/shard_map/ppermute | solution.py:167
  74.9 8.1 %collective-permute-done.2.a_ref = bf16[4,416,128]{2,1,0:T(8,128)(2,1)S(1)} collective-permute-done((bf16[4,416,128]{2,1,0:T(8,128)(2,1)}, bf16[4,416,128]{2,1,0:T(8,128)(2,1)S(1)}, u32[]{:S(2)}, u32[]{:S(2)}) %collective-permute-start.2) | collective-permute-done | bytes 426016 | tf_op jit(solution)/shard_map/ppermute | solution.py:167
  83.0 1.0 collective-permute-done.3.b_ref
  84.0 0.7 shard_map.70
  84.7 26.3 %all_to_all.31.in_ref = bf16[4,416,128]{2,1,0:T(8,128)(2,1)S(1)} all-to-all(bf16[4,416,128]{2,1,0:T(8,128)(2,1)S(1)} %shard_map.70), channel_id=1, replica_groups={{0,192,384,576},{64,256,448,640},{128,320,512,704},{1,193,385,577},{65,..., dimensions={0} | all-to-all | bytes 851968 | tf_op jit(solution)/shard_map/all_to_all | solution.py:159
  111.0 0.8 shard_map.71
  111.8 3.5 %all-to-all-start.5 = ((bf16[4,416,128]{2,1,0:T(8,128)(2,1)}), bf16[4,416,128]{2,1,0:T(8,128)(2,1)S(1)}, u32[]{:S(2)}, u32[]{:S(2)}) async-start(bf16[4,416,128]{2,1,0:T(8,128)(2,1)} %shard_map.71), calls=%async_computation.5 | async-start | bytes 851968 | tf_op jit(solution)/shard_map/all_to_all | solution.py:159
  115.3 0.8 shard_map.69
  116.1 17.2 %all-to-all-done.5.mid_ref = bf16[4,416,128]{2,1,0:T(8,128)(2,1)S(1)} async-done(((bf16[4,416,128]{2,1,0:T(8,128)(2,1)}), bf16[4,416,128]{2,1,0:T(8,128)(2,1)S(1)}, u32[]{:S(2)}, u32[]{:S(2)}) %all-to-all-start.5) | async-done | bytes 426016 | tf_op jit(solution)/shard_map/all_to_all | solution.py:159
  133.3 3.4 %all-to-all-start.3 = ((bf16[8,128,128]{2,1,0:T(8,128)(2,1)}), bf16[8,128,128]{2,1,0:T(8,128)(2,1)S(1)}, u32[]{:S(2)}, u32[]{:S(2)}) async-start(bf16[8,128,128]{2,1,0:T(8,128)(2,1)} %shard_map.69), calls=%async_computation.3 | async-start | bytes 524288 | tf_op jit(solution)/shard_map/all_to_all | solution.py:159
  136.7 1.9 %collective-permute-start.4 = (bf16[4,416,128]{2,1,0:T(8,128)(2,1)S(1)}, bf16[4,416,128]{2,1,0:T(8,128)(2,1)S(1)}, u32[]{:S(2)}, u32[]{:S(2)}) collective-permute-start(bf16[4,416,128]{2,1,0:T(8,128)(2,1)S(1)} %all-to-all-done.5.mid_ref), channel_id=1, source_target_pairs={{0,64},{64,128},{128,192},{192,256},{256,320},{320,384},{384,448},... | collective-permute-start | bytes 1277960 | tf_op jit(solution)/shard_map/ppermute | solution.py:167
  138.6 5.1 %collective-permute-start.5 = (bf16[4,416,128]{2,1,0:T(8,128)(2,1)S(1)}, bf16[4,416,128]{2,1,0:T(8,128)(2,1)S(1)}, u32[]{:S(2)}, u32[]{:S(2)}) collective-permute-start(bf16[4,416,128]{2,1,0:T(8,128)(2,1)S(1)} %all-to-all-done.5.mid_ref), channel_id=1, source_target_pairs={{0,704},{64,0},{128,64},{192,128},{256,192},{320,256},{384,320},{4... | collective-permute-start | bytes 1277960 | tf_op jit(solution)/shard_map/ppermute | solution.py:167
  143.8 3.3 %all-to-all-done.3 = bf16[8,128,128]{2,1,0:T(8,128)(2,1)S(1)} async-done(((bf16[8,128,128]{2,1,0:T(8,128)(2,1)}), bf16[8,128,128]{2,1,0:T(8,128)(2,1)S(1)}, u32[]{:S(2)}, u32[]{:S(2)}) %all-to-all-start.3) | async-done | bytes 262176 | tf_op jit(solution)/shard_map/all_to_all | solution.py:159
  147.1 0.0 copy-start
  147.1 0.8 collective-permute-done.4.low_ref
  147.9 2.3 %collective-permute-done.5.high_ref = bf16[4,416,128]{2,1,0:T(8,128)(2,1)S(1)} collective-permute-done((bf16[4,416,128]{2,1,0:T(8,128)(2,1)S(1)}, bf16[4,416,128]{2,1,0:T(8,128)(2,1)S(1)}, u32[]{:S(2)}, u32[]{:S(2)}) %collective-permute-start.5) | collective-permute-done | bytes 426016 | tf_op jit(solution)/shard_map/ppermute | solution.py:167
  150.2 2.2 %shard_map.72 = f32[4864,128]{1,0:T(8,128)} custom-call(s32[3]{0:T(128)S(1)} %and_select_fusion.1.place_ref, f32[128,128]{1,0:T(8,128)S(1)} %convert_reduce_fusion.after_ref, bf16[4,416,128]{2,1,0:T(8,128)(2,1)S(1)} %all-to-all-done.5.mid_ref, bf16[4,416,128]{2,1,0:T(8,128)(2,1)S(1)} %collective-permute-done.4.low_ref, ...), custom_call_target="tpu_custom_call" | custom-call | tf_op jit(solution)/shard_map/pallas_call | solution.py:109
  (14 shorter events, 0.2 us)
Async XLA Ops:
  0.6 39.0 %copy-start.2 = (s32[38,2]{0,1:T(2,128)S(1)}, s32[38,2]{0,1:T(2,128)}, u32[]{:S(2)}) copy-start(s32[38,2]{0,1:T(2,128)} %param.6) | copy-start | bytes 916
  21.5 20.7 %copy-start.1 = (f32[128,512]{1,0:T(8,128)S(1)}, f32[128,512]{1,0:T(8,128)}, u32[]{:S(2)}) copy-start(f32[128,512]{1,0:T(8,128)} %g_ref.1) | copy-start | bytes 786436
  21.5 16.1 %all-to-all-start.1 = ((bf16[4,8,128,128]{3,2,1,0:T(8,128)(2,1)}), bf16[4,8,128,128]{3,2,1,0:T(8,128)(2,1)S(1)}, u32[]{:S(2)}, u32[]{:S(2)}) async-start(bf16[4,8,128,128]{3,2,1,0:T(8,128)(2,1)} %broadcast_in_dim.5), calls=%async_computation.1 | async-start | bytes 2097152 | tf_op jit(solution)/shard_map/all_to_all | solution.py:159
  37.7 4.5 %collective-permute-start = (bf16[32,128,128]{2,1,0:T(8,128)(2,1)S(1)}, bf16[32,128,128]{2,1,0:T(8,128)(2,1)S(1)}, u32[]{:S(2)}, u32[]{:S(2)}) collective-permute-start(bf16[32,128,128]{2,1,0:T(8,128)(2,1)S(1)} %bitcast.32), channel_id=1, source_target_pairs={{0,1},{1,0},{2,3},{3,2},{4,5},{5,4},{6,7},{7,6},{8,9},{9,8},{10,11... | collective-permute-start | bytes 3145736 | tf_op jit(solution)/shard_map/ppermute | solution.py:217
  46.8 4.6 %collective-permute-start.1 = (bf16[32,128,128]{2,1,0:T(8,128)(2,1)S(1)}, bf16[32,128,128]{2,1,0:T(8,128)(2,1)S(1)}, u32[]{:S(2)}, u32[]{:S(2)}) collective-permute-start(bf16[32,128,128]{2,1,0:T(8,128)(2,1)S(1)} %get-tuple-element.13), channel_id=1, source_target_pairs={{0,1},{1,0},{2,3},{3,2},{4,5},{5,4},{6,7},{7,6},{8,9},{9,8},{10,11... | collective-permute-start | bytes 3145736 | tf_op jit(solution)/shard_map/ppermute | solution.py:175
  52.8 31.9 %all-to-all-start.2 = ((bf16[4,8,128,128]{3,2,1,0:T(8,128)(2,1)}), bf16[4,8,128,128]{3,2,1,0:T(8,128)(2,1)S(1)}, u32[]{:S(2)}, u32[]{:S(2)}) async-start(bf16[4,8,128,128]{3,2,1,0:T(8,128)(2,1)} %bitcast.8), calls=%async_computation.2 | async-start | bytes 2097152 | tf_op jit(solution)/shard_map/all_to_all | solution.py:159
  58.4 24.6 %collective-permute-start.2 = (bf16[4,416,128]{2,1,0:T(8,128)(2,1)}, bf16[4,416,128]{2,1,0:T(8,128)(2,1)S(1)}, u32[]{:S(2)}, u32[]{:S(2)}) collective-permute-start(bf16[4,416,128]{2,1,0:T(8,128)(2,1)} %get-tuple-element.15), channel_id=1, source_target_pairs={{0,64},{64,128},{128,192},{192,256},{256,320},{320,384},{384,448},... | collective-permute-start | bytes 1277960 | tf_op jit(solution)/shard_map/ppermute | solution.py:167
  62.7 21.3 %collective-permute-start.3 = (bf16[4,416,128]{2,1,0:T(8,128)(2,1)S(1)}, bf16[4,416,128]{2,1,0:T(8,128)(2,1)S(1)}, u32[]{:S(2)}, u32[]{:S(2)}) collective-permute-start(bf16[4,416,128]{2,1,0:T(8,128)(2,1)S(1)} %get-tuple-element.16), channel_id=1, source_target_pairs={{0,704},{64,0},{128,64},{192,128},{256,192},{320,256},{384,320},{4... | collective-permute-start | bytes 1277960 | tf_op jit(solution)/shard_map/ppermute | solution.py:167
  111.8 21.5 %all-to-all-start.5 = ((bf16[4,416,128]{2,1,0:T(8,128)(2,1)}), bf16[4,416,128]{2,1,0:T(8,128)(2,1)S(1)}, u32[]{:S(2)}, u32[]{:S(2)}) async-start(bf16[4,416,128]{2,1,0:T(8,128)(2,1)} %shard_map.71), calls=%async_computation.5 | async-start | bytes 851968 | tf_op jit(solution)/shard_map/all_to_all | solution.py:159
  133.3 13.8 %all-to-all-start.3 = ((bf16[8,128,128]{2,1,0:T(8,128)(2,1)}), bf16[8,128,128]{2,1,0:T(8,128)(2,1)S(1)}, u32[]{:S(2)}, u32[]{:S(2)}) async-start(bf16[8,128,128]{2,1,0:T(8,128)(2,1)} %shard_map.69), calls=%async_computation.3 | async-start | bytes 524288 | tf_op jit(solution)/shard_map/all_to_all | solution.py:159
  136.7 11.2 %collective-permute-start.4 = (bf16[4,416,128]{2,1,0:T(8,128)(2,1)S(1)}, bf16[4,416,128]{2,1,0:T(8,128)(2,1)S(1)}, u32[]{:S(2)}, u32[]{:S(2)}) collective-permute-start(bf16[4,416,128]{2,1,0:T(8,128)(2,1)S(1)} %all-to-all-done.5.mid_ref), channel_id=1, source_target_pairs={{0,64},{64,128},{128,192},{192,256},{256,320},{320,384},{384,448},... | collective-permute-start | bytes 1277960 | tf_op jit(solution)/shard_map/ppermute | solution.py:167
  138.6 11.6 %collective-permute-start.5 = (bf16[4,416,128]{2,1,0:T(8,128)(2,1)S(1)}, bf16[4,416,128]{2,1,0:T(8,128)(2,1)S(1)}, u32[]{:S(2)}, u32[]{:S(2)}) collective-permute-start(bf16[4,416,128]{2,1,0:T(8,128)(2,1)S(1)} %all-to-all-done.5.mid_ref), channel_id=1, source_target_pairs={{0,704},{64,0},{128,64},{192,128},{256,192},{320,256},{384,320},{4... | collective-permute-start | bytes 1277960 | tf_op jit(solution)/shard_map/ppermute | solution.py:167
  147.1 5.3 %copy-start = (f32[128,128]{1,0:T(8,128)}, f32[128,128]{1,0:T(8,128)S(1)}, u32[]{:S(2)}) copy-start(f32[128,128]{1,0:T(8,128)S(1)} %convert_reduce_fusion.after_ref) | copy-start | bytes 196612

commit v4 on v2

v4 whole, which is shorter than its diff:
```python
import jax
import jax.numpy as jnp
from jax import lax
from jax.experimental import pallas as pl
from jax.experimental.pallas import tpu as pltpu
from jax.sharding import PartitionSpec as P

BS = 128
NY, NX, NC = 8, 4, 2
NZ = 12
HALF = NY * NX
Y_GROUPS = [[(y * NX + x) * NC + c for y in range(NY)] for x in range(NX) for c in range(NC)]
X_GROUPS = [[(y * NX + x) * NC + c for x in range(NX)] for y in range(NY) for c in range(NC)]
CORE_SWAP = [(i, i ^ 1) for i in range(HALF * NC)]
XC_GROUPS = [[y * NX * NC + k for k in range(NX * NC)] for y in range(NY)]
CHUNK = 416
SPLIT = 208
F32, BF16 = jnp.float32, jnp.bfloat16


def gelu_parts(pre):
    inner = 0.7978845608 * (pre + 0.044715 * pre * pre * pre)
    tanh_val = jnp.tanh(inner)
    value = 0.5 * pre * (1.0 + tanh_val)
    slope = 0.5 * (1.0 + tanh_val) + 0.5 * pre * (1.0 - tanh_val * tanh_val) * 0.7978845608 * (
        1.0 + 3.0 * 0.044715 * pre * pre
    )
    return value, slope


def dot(a, b, dims):
    return lax.dot_general(a, b, (dims, ((), ())), preferred_element_type=F32)


def block_kernel(idx_ref, out_idx_ref, col_ref, live_ref, rel_ref, own_ref, sib_ref, w_ref, g_ref,
                 act_ref, gx_out_ref, keep_ref, up1_ref, down1_ref, up2_ref, down2_ref,
                 x_ref, prod_ref, pre_ref, dpre_ref, gx_ref, gw_ref):
    slots = w_ref.shape[0]
    col_blocks = pre_ref.shape[0]
    x_ref[:HALF] = own_ref[...]
    x_ref[HALF:] = sib_ref[...]
    pre_ref[...] = jnp.zeros_like(pre_ref)
    for s in range(slots):
        prod_ref[s] = dot(x_ref[idx_ref[s]], w_ref[s], ((1,), (0,)))
    for s in range(slots):
        pre_ref[col_ref[s]] += prod_ref[s]
    for c in range(col_blocks):
        value, slope = gelu_parts(pre_ref[c])
        lanes = slice(c * BS, (c + 1) * BS)
        act_ref[:, lanes] = value
        dpre_ref[c] = (g_ref[:, lanes] * slope).astype(BF16)
    for s in range(slots):
        wgrad = dot(x_ref[idx_ref[s]], dpre_ref[col_ref[s]], ((0,), (0,)))
        wgrad = (wgrad * live_ref[s]).astype(BF16)
        done = 0
        while done < BS:
            chunk, at = divmod(s * BS + done, CHUNK)
            size = min(BS - done, CHUNK - at)
            gw_ref[rel_ref[chunk], at:at + size] = wgrad[done:done + size]
            done += size
    chunk, at = divmod(slots * BS, CHUNK)
    gw_ref[rel_ref[chunk], at:] = jnp.zeros((CHUNK - at, BS), BF16)
    for i in range(3):
        keep_ref[i] = gw_ref[4 * i]
        up1_ref[i] = gw_ref[4 * i + 1]
        down1_ref[i] = gw_ref[(4 * i + 11) % NZ]
        up2_ref[i] = gw_ref[4 * i + 2, :SPLIT]
        down2_ref[i] = gw_ref[(4 * i + 10) % NZ, SPLIT:]
    gx_ref[...] = jnp.zeros_like(gx_ref)
    for s in range(slots):
        prod_ref[s] = dot(dpre_ref[col_ref[s]], w_ref[s], ((1,), (1,)))
    for s in range(slots):
        gx_ref[out_idx_ref[s]] += prod_ref[s]
    gx_out_ref[...] = gx_ref[...].astype(BF16)


def near_kernel(keep_ref, a_ref, b_ref, c_ref, d_ref, stay_ref, up_ref, down_ref):
    for i, out in enumerate((stay_ref, up_ref, down_ref)):
        part = keep_ref[i].astype(F32) + a_ref[i].astype(F32) + b_ref[i].astype(F32)
        out[:SPLIT] = (part[:SPLIT] + c_ref[i].astype(F32)).astype(BF16)
        out[SPLIT:] = (part[SPLIT:] + d_ref[i].astype(F32)).astype(BF16)


def far_kernel(stay_ref, a_ref, b_ref, out_ref):
    out_ref[...] = (stay_ref[...].astype(F32) + a_ref[...].astype(F32) + b_ref[...].astype(F32)).astype(BF16)


def three_kernel(after_ref, k0_ref, k4_ref, k8_ref, all_ref, low_ref, high_ref):
    for i, part in enumerate((k0_ref, k4_ref, k8_ref)):
        all_ref[i] = part[...]
        low_ref[i] = part[:SPLIT]
        high_ref[i] = part[SPLIT:]


def x_sum_kernel(after_ref, in_ref, out_ref):
    out_ref[...] = jnp.sum(in_ref[...].astype(F32), axis=0).astype(BF16)


def whole_kernel(rel_ref, k0_ref, k4_ref, k8_ref, low1_ref, high1_ref, low2_ref, high2_ref, out_ref, gw_ref):
    gw_ref[0] = k0_ref[...]
    gw_ref[4] = k4_ref[...]
    gw_ref[8] = k8_ref[...]
    for i in range(3):
        gw_ref[(4 * i + 11) % NZ] = low1_ref[i]
        gw_ref[4 * i + 1] = high1_ref[i]
        gw_ref[(4 * i + 10) % NZ, :SPLIT] = low2_ref[i]
        gw_ref[4 * i + 2, SPLIT:] = high2_ref[i]
    rows = out_ref.shape[0]
    for j in range(NZ):
        size = min(CHUNK, rows - j * CHUNK)
        out_ref[j * CHUNK:j * CHUNK + size] = gw_ref[rel_ref[j], :size].astype(F32)


SMEM = pl.BlockSpec(memory_space=pltpu.SMEM)
VMEM = pl.BlockSpec(memory_space=pltpu.VMEM)
ORDER = pl.BlockSpec(memory_space=pl.ANY)


def call(kernel, specs, ins, outs, scratch=(), flops=0, moved=0):
    return pl.pallas_call(
        kernel,
        out_shape=outs,
        in_specs=specs,
        out_specs=jax.tree.map(lambda _: VMEM, outs),
        scratch_shapes=scratch,
        compiler_params=pltpu.CompilerParams(vmem_limit_bytes=40 << 20),
        cost_estimate=pl.CostEstimate(flops=flops, bytes_accessed=moved, transcendentals=0),
    )(*ins)


def array(shape, kind=BF16):
    return jax.ShapeDtypeStruct(shape, kind)


def run_blocks(idx, out_idx, col, live, rel, own, sib, wb, grad_act):
    slots = wb.shape[0]
    tokens, hidden = grad_act.shape
    cols = hidden // BS
    full, half = array((3, CHUNK, BS)), array((3, SPLIT, BS))
    return call(
        block_kernel,
        [SMEM] * 5 + [VMEM] * 4,
        (idx, out_idx, col, live, rel, own, sib, wb, grad_act),
        (array((tokens, hidden), F32), array((2 * HALF, tokens, BS)), full, full, full, half, half),
        [
            pltpu.VMEM((2 * HALF, tokens, BS), BF16),
            pltpu.VMEM((slots, tokens, BS), F32),
            pltpu.VMEM((cols, tokens, BS), F32),
            pltpu.VMEM((cols, tokens, BS), BF16),
            pltpu.VMEM((2 * HALF, tokens, BS), F32),
            pltpu.VMEM((NZ, CHUNK, BS), BF16),
        ],
    )


def swap(x, axis, groups):
    return lax.all_to_all(x, axis, 0, 0, tiled=True, axis_index_groups=groups)


def total(x):
    return jnp.sum(x.astype(F32), axis=0)


def shift(x, by):
    return lax.ppermute(x, "dp", [(i, (i + by) % NZ) for i in range(NZ)])


def reduce_gradients(gx, keep, up1, down1, up2, down2, rel, slots):
    tokens = gx.shape[1]
    one, full, half = array((CHUNK, BS)), array((3, CHUNK, BS)), array((3, SPLIT, BS))
    gx = swap(gx.reshape(NX * NC, NY, tokens, BS), "mp", XC_GROUPS)
    parts = shift(up1, 1), shift(down1, -1), shift(up2, 2), shift(down2, -2)
    stay, up, down = call(near_kernel, [VMEM] * 5, (keep, *parts), (one,) * 3)
    mine = call(far_kernel, [VMEM] * 3, (stay, shift(up, 4), shift(down, -4)), one)

    k8, k4 = shift(mine, 4), shift(mine, -4)
    gx = call(x_sum_kernel, [ORDER, VMEM], (mine, gx), array((NY, tokens, BS)))
    three, low, high = call(three_kernel, [ORDER] + [VMEM] * 3, (gx, mine, k4, k8), (full, half, half))
    grad_x = total(swap(gx, "mp", Y_GROUPS))

    low1, high1, low2, high2 = shift(three, 1), shift(three, -1), shift(low, 2), shift(high, -2)
    grad_w = call(
        whole_kernel,
        [SMEM] + [VMEM] * 7,
        (rel, mine, k4, k8, low1, high1, low2, high2),
        array((slots * BS, BS), F32),
        [pltpu.VMEM((NZ, CHUNK, BS), BF16)],
    )
    return grad_x, grad_w.reshape(slots, BS, BS)


def local(inputs, block_weights, block_list, grad_act):
    tokens = inputs.shape[0]
    slots = block_weights.shape[0]
    row_ids, col_ids = block_list[:, 0], block_list[:, 1]
    live = (row_ids >= 0).astype(F32)
    row = jnp.maximum(row_ids, 0)
    col = jnp.maximum(col_ids, 0)
    core = lax.axis_index("mp") % NC
    at_y, at_x, at_core = row // (NC * NX), (row // NC) % NX, row % NC
    idx = ((at_core ^ core) * NX + at_x) * NY + at_y
    out_idx = (at_x * NC + at_core) * NY + at_y
    xb = inputs.astype(BF16)
    wb = (block_weights * live[:, None, None]).astype(BF16)

    by_y = swap(jnp.broadcast_to(xb[None], (NY, tokens, BS)), "mp", Y_GROUPS)
    by_xy = swap(jnp.broadcast_to(by_y[None], (NX, NY, tokens, BS)), "mp", X_GROUPS)
    own = by_xy.reshape(HALF, tokens, BS)
    sib = lax.ppermute(own, "mp", CORE_SWAP)

    rel = (jnp.arange(NZ, dtype=jnp.int32) + NZ - lax.axis_index("dp")) % NZ
    act, gx, *parts = run_blocks(idx, out_idx, col, live, rel, own, sib, wb, grad_act)
    grad_x, grad_w = reduce_gradients(gx, *parts, rel, slots)
    return act, grad_x, grad_w


def solution(mesh):
    in_specs = (P("dp", "mp"), P("mp", None, None), P("mp", None), P("dp", "mp"))
    out_specs = (P("dp", "mp"), P("dp", "mp"), P("mp", None, None))
    return jax.shard_map(local, mesh=mesh, in_specs=in_specs, out_specs=out_specs, check_vma=False)
```

time: 157 us -> 154 us (0.981)
    ppermute x1 -> x0, waiting for transfers between devices: 2.5 us -> none  [reduce_gradients(): gx_sib = lax.ppermute(gx_sib, 'mp', CORE_SWAP)]
    ppermute x1 -> x0, starting transfers between devices: 2.04 us -> none  [reduce_gradients(): gx_sib = lax.ppermute(gx_sib, 'mp', CORE_SWAP)]
  transfers between devices with their start and end apart: 17 -> 16, of which waited for: 11 -> 9; matrix products, arithmetic and copies ran while one was open for 1% -> 1% of each run, Pallas kernels for 0% -> 2%
where the time goes in v4:
time: 154 us; the launch traced here: 152 us
  starting transfers between devices  79 us (51%)
  waiting for transfers between devices  40.6 us (26%)
  blocking collectives  18.8 us (12%)
  Pallas kernels  7.15 us (5%)
  other arithmetic  3.54 us (2%)
  local copies, waits for them, and re-layouts  2.57 us (2%)
    ppermute x12, starting transfers between devices, shift(): return lax.ppermute(x, 'dp', [(i, (i + by) % NZ) for i in range(NZ)])  60.8 us
    ppermute x12, waiting for transfers between devices, shift(): return lax.ppermute(x, 'dp', [(i, (i + by) % NZ) for i in range(NZ)])  31.1 us
    all_to_all x1, blocking collectives, swap(): return lax.all_to_all(x, axis, 0, 0, tiled=True, axis_index_groups=groups)  18.8 us
    all_to_all x3, starting transfers between devices, swap(): return lax.all_to_all(x, axis, 0, 0, tiled=True, axis_index_groups=groups)  16.2 us
    all_to_all x3, waiting for transfers between devices, swap(): return lax.all_to_all(x, axis, 0, 0, tiled=True, axis_index_groups=groups)  8.92 us
    pallas_call x6, Pallas kernels, call(): pl.pallas_call(kernel, out_shape=outs, in_specs=specs, out_specs=jax.tree...  7.15 us
  transfers between devices with their start and end apart: 16, of which 9 were waited for; matrix products, arithmetic and copies ran while one was open for 1% of the time, Pallas kernels for 2%

profile of v4, /device:TPU:6, one launch (start us, length us, event | category | flops | bytes accessed | tf_op | source)
XLA Modules:
  0.0 152.4 jit_solution(18372816423836547912)
XLA Ops:
  0.6 0.9 convert_element_type.16
  1.5 18.8 %all_to_all.20 = bf16[8,128,128]{2,1,0:T(8,128)(2,1)S(1)} all-to-all(bf16[8,128,128]{2,1,0:T(8,128)(2,1)S(1)} %broadcast_in_dim.4), channel_id=1, replica_groups={{0,8,16,24,32,40,48,56},{1,9,17,25,33,41,49,57},{2,10,18,26,34,42,50,58..., dimensions={0} | all-to-all | bytes 524288 | tf_op jit(solution)/shard_map/all_to_all | solution.py:157
  20.3 1.2 broadcast_in_dim.5
  21.5 7.2 %all-to-all-start.1 = ((bf16[4,8,128,128]{3,2,1,0:T(8,128)(2,1)}), bf16[4,8,128,128]{3,2,1,0:T(8,128)(2,1)S(1)}, u32[]{:S(2)}, u32[]{:S(2)}) async-start(bf16[4,8,128,128]{3,2,1,0:T(8,128)(2,1)} %broadcast_in_dim.5), calls=%async_computation.1 | async-start | bytes 2097152 | tf_op jit(solution)/shard_map/all_to_all | solution.py:157
  28.7 8.9 %all-to-all-done.1 = bf16[4,8,128,128]{3,2,1,0:T(8,128)(2,1)S(1)} async-done(((bf16[4,8,128,128]{3,2,1,0:T(8,128)(2,1)}), bf16[4,8,128,128]{3,2,1,0:T(8,128)(2,1)S(1)}, u32[]{:S(2)}, u32[]{:S(2)}) %all-to-all-start.1) | async-done | bytes 1048608 | tf_op jit(solution)/shard_map/all_to_all | solution.py:157
  37.7 1.9 %collective-permute-start = (bf16[32,128,128]{2,1,0:T(8,128)(2,1)S(1)}, bf16[32,128,128]{2,1,0:T(8,128)(2,1)S(1)}, u32[]{:S(2)}, u32[]{:S(2)}) collective-permute-start(bf16[32,128,128]{2,1,0:T(8,128)(2,1)S(1)} %bitcast.48), channel_id=1, source_target_pairs={{0,1},{1,0},{2,3},{3,2},{4,5},{5,4},{6,7},{7,6},{8,9},{9,8},{10,11... | collective-permute-start | bytes 3145736 | tf_op jit(solution)/shard_map/ppermute | solution.py:209
  39.7 2.0 %multiply_convert_fusion.w_ref = bf16[38,128,128]{2,1,0:T(8,128)(2,1)S(1)} fusion(f32[38,128,128]{2,1,0:T(8,128)} %param.5, f32[38]{0:T(128)S(1)} %fusion.2.live_ref), kind=kLoop, calls=%fused_computation | loop fusion | flops 1245184 | bytes 3735704 | tf_op jit(solution)/shard_map/convert_element_type | solution.py:204
  42.2 3.7 %shard_map.67 = (f32[128,512]{1,0:T(8,128)}, bf16[64,128,128]{2,1,0:T(8,128)(2,1)S(1)}, bf16[3,416,128]{2,1,0:T(8,128)(2,1)S(1)}, bf16[3,416,128]{2,1,0:T(8,128)...) custom-call(s32[38]{0:T(128)S(1)} %multiply_add_fusion.1.idx_ref, ...), custom_call_target="tpu_custom_call" | custom-call | tf_op jit(solution)/shard_map/pallas_call | solution.py:120
  45.9 1.3 copy-done
  47.2 5.6 %all-to-all-start.2 = ((bf16[8,8,128,128]{3,2,1,0:T(8,128)(2,1)}), bf16[8,8,128,128]{3,2,1,0:T(8,128)(2,1)S(1)}, u32[]{:S(2)}, u32[]{:S(2)}) async-start(bf16[8,8,128,128]{3,2,1,0:T(8,128)(2,1)} %bitcast.50), calls=%async_computation.2 | async-start | bytes 4194304 | tf_op jit(solution)/shard_map/all_to_all | solution.py:157
  52.8 4.3 %collective-permute-start.1 = (bf16[3,416,128]{2,1,0:T(8,128)(2,1)S(1)}, bf16[3,416,128]{2,1,0:T(8,128)(2,1)S(1)}, u32[]{:S(2)}, u32[]{:S(2)}) collective-permute-start(bf16[3,416,128]{2,1,0:T(8,128)(2,1)S(1)} %get-tuple-element.18), channel_id=1, source_target_pairs={{0,64},{64,128},{128,192},{192,256},{256,320},{320,384},{384,448},... | collective-permute-start | bytes 958472 | tf_op jit(solution)/shard_map/ppermute | solution.py:165
  57.1 12.2 %collective-permute-start.2 = (bf16[3,416,128]{2,1,0:T(8,128)(2,1)S(1)}, bf16[3,416,128]{2,1,0:T(8,128)(2,1)S(1)}, u32[]{:S(2)}, u32[]{:S(2)}) collective-permute-start(bf16[3,416,128]{2,1,0:T(8,128)(2,1)S(1)} %get-tuple-element.19), channel_id=1, source_target_pairs={{0,704},{64,0},{128,64},{192,128},{256,192},{320,256},{384,320},{4... | collective-permute-start | bytes 958472 | tf_op jit(solution)/shard_map/ppermute | solution.py:165
  69.3 1.9 %collective-permute-start.3 = (bf16[3,208,128]{2,1,0:T(8,128)(2,1)S(1)}, bf16[3,208,128]{2,1,0:T(8,128)(2,1)S(1)}, u32[]{:S(2)}, u32[]{:S(2)}) collective-permute-start(bf16[3,208,128]{2,1,0:T(8,128)(2,1)S(1)} %get-tuple-element.20), channel_id=1, source_target_pairs={{0,128},{64,192},{128,256},{192,320},{256,384},{320,448},{384,512}... | collective-permute-start | bytes 479240 | tf_op jit(solution)/shard_map/ppermute | solution.py:165
  71.2 6.0 %collective-permute-start.4 = (bf16[3,208,128]{2,1,0:T(8,128)(2,1)S(1)}, bf16[3,208,128]{2,1,0:T(8,128)(2,1)S(1)}, u32[]{:S(2)}, u32[]{:S(2)}) collective-permute-start(bf16[3,208,128]{2,1,0:T(8,128)(2,1)S(1)} %get-tuple-element.21), channel_id=1, source_target_pairs={{0,640},{64,704},{128,0},{192,64},{256,128},{320,192},{384,256},{4... | collective-permute-start | bytes 479240 | tf_op jit(solution)/shard_map/ppermute | solution.py:165
  77.3 4.3 %collective-permute-done.3.c_ref = bf16[3,208,128]{2,1,0:T(8,128)(2,1)S(1)} collective-permute-done((bf16[3,208,128]{2,1,0:T(8,128)(2,1)S(1)}, bf16[3,208,128]{2,1,0:T(8,128)(2,1)S(1)}, u32[]{:S(2)}, u32[]{:S(2)}) %collective-permute-start.3) | collective-permute-done | bytes 159776 | tf_op jit(solution)/shard_map/ppermute | solution.py:165
  81.6 2.1 %collective-permute-done.4.d_ref = bf16[3,208,128]{2,1,0:T(8,128)(2,1)S(1)} collective-permute-done((bf16[3,208,128]{2,1,0:T(8,128)(2,1)S(1)}, bf16[3,208,128]{2,1,0:T(8,128)(2,1)S(1)}, u32[]{:S(2)}, u32[]{:S(2)}) %collective-permute-start.4) | collective-permute-done | bytes 159776 | tf_op jit(solution)/shard_map/ppermute | solution.py:165
  83.9 5.1 %collective-permute-start.5 = (bf16[416,128]{1,0:T(8,128)(2,1)S(1)}, bf16[416,128]{1,0:T(8,128)(2,1)S(1)}, u32[]{:S(2)}, u32[]{:S(2)}) collective-permute-start(bf16[416,128]{1,0:T(8,128)(2,1)S(1)} %get-tuple-element.23), channel_id=1, source_target_pairs={{0,256},{64,320},{128,384},{192,448},{256,512},{320,576},{384,640}... | collective-permute-start | bytes 319496 | tf_op jit(solution)/shard_map/ppermute | solution.py:165
  89.0 4.7 %collective-permute-start.6 = (bf16[416,128]{1,0:T(8,128)(2,1)S(1)}, bf16[416,128]{1,0:T(8,128)(2,1)S(1)}, u32[]{:S(2)}, u32[]{:S(2)}) collective-permute-start(bf16[416,128]{1,0:T(8,128)(2,1)S(1)} %get-tuple-element.24), channel_id=1, source_target_pairs={{0,512},{64,576},{128,640},{192,704},{256,0},{320,64},{384,128},{4... | collective-permute-start | bytes 319496 | tf_op jit(solution)/shard_map/ppermute | solution.py:165
  93.6 4.2 %collective-permute-done.5.a_ref = bf16[416,128]{1,0:T(8,128)(2,1)S(1)} collective-permute-done((bf16[416,128]{1,0:T(8,128)(2,1)S(1)}, bf16[416,128]{1,0:T(8,128)(2,1)S(1)}, u32[]{:S(2)}, u32[]{:S(2)}) %collective-permute-start.5) | collective-permute-done | bytes 106528 | tf_op jit(solution)/shard_map/ppermute | solution.py:165
  97.8 3.9 %collective-permute-done.6.b_ref = bf16[416,128]{1,0:T(8,128)(2,1)S(1)} collective-permute-done((bf16[416,128]{1,0:T(8,128)(2,1)S(1)}, bf16[416,128]{1,0:T(8,128)(2,1)S(1)}, u32[]{:S(2)}, u32[]{:S(2)}) %collective-permute-start.6) | collective-permute-done | bytes 106528 | tf_op jit(solution)/shard_map/ppermute | solution.py:165
  101.8 1.0 shard_map.70.after_ref
  102.8 3.4 %all-to-all-start.3 = ((bf16[8,128,128]{2,1,0:T(8,128)(2,1)}), bf16[8,128,128]{2,1,0:T(8,128)(2,1)S(1)}, u32[]{:S(2)}, u32[]{:S(2)}) async-start(bf16[8,128,128]{2,1,0:T(8,128)(2,1)} %shard_map.70.after_ref), calls=%async_computation.3 | async-start | bytes 524288 | tf_op jit(solution)/shard_map/all_to_all | solution.py:157
  106.2 6.4 %collective-permute-start.8 = (bf16[416,128]{1,0:T(8,128)(2,1)S(1)}, bf16[416,128]{1,0:T(8,128)(2,1)S(1)}, u32[]{:S(2)}, u32[]{:S(2)}) collective-permute-start(bf16[416,128]{1,0:T(8,128)(2,1)S(1)} %shard_map.69.after_ref.k0_ref), channel_id=1, source_target_pairs={{0,256},{64,320},{128,384},{192,448},{256,512},{320,576},{384,640}... | collective-permute-start | bytes 319496 | tf_op jit(solution)/shard_map/ppermute | solution.py:165
  112.6 3.3 %collective-permute-start.7 = (bf16[416,128]{1,0:T(8,128)(2,1)S(1)}, bf16[416,128]{1,0:T(8,128)(2,1)S(1)}, u32[]{:S(2)}, u32[]{:S(2)}) collective-permute-start(bf16[416,128]{1,0:T(8,128)(2,1)S(1)} %shard_map.69.after_ref.k0_ref), channel_id=1, source_target_pairs={{0,512},{64,576},{128,640},{192,704},{256,0},{320,64},{384,128},{4... | collective-permute-start | bytes 319496 | tf_op jit(solution)/shard_map/ppermute | solution.py:165
  115.9 0.9 collective-permute-done.8.k8_ref
  116.9 7.0 %collective-permute-done.7.k4_ref = bf16[416,128]{1,0:T(8,128)(2,1)S(1)} collective-permute-done((bf16[416,128]{1,0:T(8,128)(2,1)S(1)}, bf16[416,128]{1,0:T(8,128)(2,1)S(1)}, u32[]{:S(2)}, u32[]{:S(2)}) %collective-permute-start.7) | collective-permute-done | bytes 106528 | tf_op jit(solution)/shard_map/ppermute | solution.py:165
  124.0 5.0 %collective-permute-start.10 = (bf16[3,416,128]{2,1,0:T(8,128)(2,1)S(1)}, bf16[3,416,128]{2,1,0:T(8,128)(2,1)S(1)}, u32[]{:S(2)}, u32[]{:S(2)}) collective-permute-start(bf16[3,416,128]{2,1,0:T(8,128)(2,1)S(1)} %get-tuple-element.26), channel_id=1, source_target_pairs={{0,704},{64,0},{128,64},{192,128},{256,192},{320,256},{384,320},{4... | collective-permute-start | bytes 958472 | tf_op jit(solution)/shard_map/ppermute | solution.py:165
  129.0 1.9 %collective-permute-start.9 = (bf16[3,416,128]{2,1,0:T(8,128)(2,1)S(1)}, bf16[3,416,128]{2,1,0:T(8,128)(2,1)S(1)}, u32[]{:S(2)}, u32[]{:S(2)}) collective-permute-start(bf16[3,416,128]{2,1,0:T(8,128)(2,1)S(1)} %get-tuple-element.26), channel_id=1, source_target_pairs={{0,64},{64,128},{128,192},{192,256},{256,320},{320,384},{384,448},... | collective-permute-start | bytes 958472 | tf_op jit(solution)/shard_map/ppermute | solution.py:165
  131.0 8.0 %collective-permute-start.11 = (bf16[3,208,128]{2,1,0:T(8,128)(2,1)S(1)}, bf16[3,208,128]{2,1,0:T(8,128)(2,1)S(1)}, u32[]{:S(2)}, u32[]{:S(2)}) collective-permute-start(bf16[3,208,128]{2,1,0:T(8,128)(2,1)S(1)} %get-tuple-element.27), channel_id=1, source_target_pairs={{0,128},{64,192},{128,256},{192,320},{256,384},{320,448},{384,512}... | collective-permute-start | bytes 479240 | tf_op jit(solution)/shard_map/ppermute | solution.py:165
  138.9 1.9 %collective-permute-start.12 = (bf16[3,208,128]{2,1,0:T(8,128)(2,1)S(1)}, bf16[3,208,128]{2,1,0:T(8,128)(2,1)S(1)}, u32[]{:S(2)}, u32[]{:S(2)}) collective-permute-start(bf16[3,208,128]{2,1,0:T(8,128)(2,1)S(1)} %get-tuple-element.28), channel_id=1, source_target_pairs={{0,640},{64,704},{128,0},{192,64},{256,128},{320,192},{384,256},{4... | collective-permute-start | bytes 479240 | tf_op jit(solution)/shard_map/ppermute | solution.py:165
  140.9 8.7 %collective-permute-done.11.low2_ref = bf16[3,208,128]{2,1,0:T(8,128)(2,1)S(1)} collective-permute-done((bf16[3,208,128]{2,1,0:T(8,128)(2,1)S(1)}, bf16[3,208,128]{2,1,0:T(8,128)(2,1)S(1)}, u32[]{:S(2)}, u32[]{:S(2)}) %collective-permute-start.11) | collective-permute-done | bytes 159776 | tf_op jit(solution)/shard_map/ppermute | solution.py:165
  149.5 2.2 %shard_map.72 = f32[4864,128]{1,0:T(8,128)} custom-call(s32[12]{0:T(128)S(1)} %and_select_fusion.rel_ref, bf16[416,128]{1,0:T(8,128)(2,1)S(1)} %shard_map.69.after_ref.k0_ref, bf16[416,128]{1,0:T(8,128)(2,1)S(1)} %collective-permute-done.7.k4_ref, bf16[416,128]{1,0:T(8,128)(2,1)S(1)} %collective-permute-done.8.k8_ref, ...), custom_call_target="tpu_custom_call" | custom-call | tf_op jit(solution)/shard_map/pallas_call | solution.py:120
  (23 shorter events, 1.7 us)
Async XLA Ops:
  0.6 28.1 %copy-start.2 = (s32[38,2]{0,1:T(2,128)S(1)}, s32[38,2]{0,1:T(2,128)}, u32[]{:S(2)}) copy-start(s32[38,2]{0,1:T(2,128)} %param.6) | copy-start | bytes 916
  21.5 20.7 %copy-start.1 = (f32[128,512]{1,0:T(8,128)S(1)}, f32[128,512]{1,0:T(8,128)}, u32[]{:S(2)}) copy-start(f32[128,512]{1,0:T(8,128)} %g_ref.1) | copy-start | bytes 786436
  21.5 16.1 %all-to-all-start.1 = ((bf16[4,8,128,128]{3,2,1,0:T(8,128)(2,1)}), bf16[4,8,128,128]{3,2,1,0:T(8,128)(2,1)S(1)}, u32[]{:S(2)}, u32[]{:S(2)}) async-start(bf16[4,8,128,128]{3,2,1,0:T(8,128)(2,1)} %broadcast_in_dim.5), calls=%async_computation.1 | async-start | bytes 2097152 | tf_op jit(solution)/shard_map/all_to_all | solution.py:157
  37.7 4.5 %collective-permute-start = (bf16[32,128,128]{2,1,0:T(8,128)(2,1)S(1)}, bf16[32,128,128]{2,1,0:T(8,128)(2,1)S(1)}, u32[]{:S(2)}, u32[]{:S(2)}) collective-permute-start(bf16[32,128,128]{2,1,0:T(8,128)(2,1)S(1)} %bitcast.48), channel_id=1, source_target_pairs={{0,1},{1,0},{2,3},{3,2},{4,5},{5,4},{6,7},{7,6},{8,9},{9,8},{10,11... | collective-permute-start | bytes 3145736 | tf_op jit(solution)/shard_map/ppermute | solution.py:209
  45.9 1.3 copy-start
  47.2 54.6 %all-to-all-start.2 = ((bf16[8,8,128,128]{3,2,1,0:T(8,128)(2,1)}), bf16[8,8,128,128]{3,2,1,0:T(8,128)(2,1)S(1)}, u32[]{:S(2)}, u32[]{:S(2)}) async-start(bf16[8,8,128,128]{3,2,1,0:T(8,128)(2,1)} %bitcast.50), calls=%async_computation.2 | async-start | bytes 4194304 | tf_op jit(solution)/shard_map/all_to_all | solution.py:157
  52.8 30.9 %collective-permute-start.1 = (bf16[3,416,128]{2,1,0:T(8,128)(2,1)S(1)}, bf16[3,416,128]{2,1,0:T(8,128)(2,1)S(1)}, u32[]{:S(2)}, u32[]{:S(2)}) collective-permute-start(bf16[3,416,128]{2,1,0:T(8,128)(2,1)S(1)} %get-tuple-element.18), channel_id=1, source_target_pairs={{0,64},{64,128},{128,192},{192,256},{256,320},{320,384},{384,448},... | collective-permute-start | bytes 958472 | tf_op jit(solution)/shard_map/ppermute | solution.py:165
  57.1 26.6 %collective-permute-start.2 = (bf16[3,416,128]{2,1,0:T(8,128)(2,1)S(1)}, bf16[3,416,128]{2,1,0:T(8,128)(2,1)S(1)}, u32[]{:S(2)}, u32[]{:S(2)}) collective-permute-start(bf16[3,416,128]{2,1,0:T(8,128)(2,1)S(1)} %get-tuple-element.19), channel_id=1, source_target_pairs={{0,704},{64,0},{128,64},{192,128},{256,192},{320,256},{384,320},{4... | collective-permute-start | bytes 958472 | tf_op jit(solution)/shard_map/ppermute | solution.py:165
  69.3 12.3 %collective-permute-start.3 = (bf16[3,208,128]{2,1,0:T(8,128)(2,1)S(1)}, bf16[3,208,128]{2,1,0:T(8,128)(2,1)S(1)}, u32[]{:S(2)}, u32[]{:S(2)}) collective-permute-start(bf16[3,208,128]{2,1,0:T(8,128)(2,1)S(1)} %get-tuple-element.20), channel_id=1, source_target_pairs={{0,128},{64,192},{128,256},{192,320},{256,384},{320,448},{384,512}... | collective-permute-start | bytes 479240 | tf_op jit(solution)/shard_map/ppermute | solution.py:165
  71.2 12.4 %collective-permute-start.4 = (bf16[3,208,128]{2,1,0:T(8,128)(2,1)S(1)}, bf16[3,208,128]{2,1,0:T(8,128)(2,1)S(1)}, u32[]{:S(2)}, u32[]{:S(2)}) collective-permute-start(bf16[3,208,128]{2,1,0:T(8,128)(2,1)S(1)} %get-tuple-element.21), channel_id=1, source_target_pairs={{0,640},{64,704},{128,0},{192,64},{256,128},{320,192},{384,256},{4... | collective-permute-start | bytes 479240 | tf_op jit(solution)/shard_map/ppermute | solution.py:165
  83.9 14.0 %collective-permute-start.5 = (bf16[416,128]{1,0:T(8,128)(2,1)S(1)}, bf16[416,128]{1,0:T(8,128)(2,1)S(1)}, u32[]{:S(2)}, u32[]{:S(2)}) collective-permute-start(bf16[416,128]{1,0:T(8,128)(2,1)S(1)} %get-tuple-element.23), channel_id=1, source_target_pairs={{0,256},{64,320},{128,384},{192,448},{256,512},{320,576},{384,640}... | collective-permute-start | bytes 319496 | tf_op jit(solution)/shard_map/ppermute | solution.py:165
  89.0 12.8 %collective-permute-start.6 = (bf16[416,128]{1,0:T(8,128)(2,1)S(1)}, bf16[416,128]{1,0:T(8,128)(2,1)S(1)}, u32[]{:S(2)}, u32[]{:S(2)}) collective-permute-start(bf16[416,128]{1,0:T(8,128)(2,1)S(1)} %get-tuple-element.24), channel_id=1, source_target_pairs={{0,512},{64,576},{128,640},{192,704},{256,0},{320,64},{384,128},{4... | collective-permute-start | bytes 319496 | tf_op jit(solution)/shard_map/ppermute | solution.py:165
  102.8 49.0 %all-to-all-start.3 = ((bf16[8,128,128]{2,1,0:T(8,128)(2,1)}), bf16[8,128,128]{2,1,0:T(8,128)(2,1)S(1)}, u32[]{:S(2)}, u32[]{:S(2)}) async-start(bf16[8,128,128]{2,1,0:T(8,128)(2,1)} %shard_map.70.after_ref), calls=%async_computation.3 | async-start | bytes 524288 | tf_op jit(solution)/shard_map/all_to_all | solution.py:157
  106.2 10.7 %collective-permute-start.8 = (bf16[416,128]{1,0:T(8,128)(2,1)S(1)}, bf16[416,128]{1,0:T(8,128)(2,1)S(1)}, u32[]{:S(2)}, u32[]{:S(2)}) collective-permute-start(bf16[416,128]{1,0:T(8,128)(2,1)S(1)} %shard_map.69.after_ref.k0_ref), channel_id=1, source_target_pairs={{0,256},{64,320},{128,384},{192,448},{256,512},{320,576},{384,640}... | collective-permute-start | bytes 319496 | tf_op jit(solution)/shard_map/ppermute | solution.py:165
  112.6 11.3 %collective-permute-start.7 = (bf16[416,128]{1,0:T(8,128)(2,1)S(1)}, bf16[416,128]{1,0:T(8,128)(2,1)S(1)}, u32[]{:S(2)}, u32[]{:S(2)}) collective-permute-start(bf16[416,128]{1,0:T(8,128)(2,1)S(1)} %shard_map.69.after_ref.k0_ref), channel_id=1, source_target_pairs={{0,512},{64,576},{128,640},{192,704},{256,0},{320,64},{384,128},{4... | collective-permute-start | bytes 319496 | tf_op jit(solution)/shard_map/ppermute | solution.py:165
  124.0 25.6 %collective-permute-start.10 = (bf16[3,416,128]{2,1,0:T(8,128)(2,1)S(1)}, bf16[3,416,128]{2,1,0:T(8,128)(2,1)S(1)}, u32[]{:S(2)}, u32[]{:S(2)}) collective-permute-start(bf16[3,416,128]{2,1,0:T(8,128)(2,1)S(1)} %get-tuple-element.26), channel_id=1, source_target_pairs={{0,704},{64,0},{128,64},{192,128},{256,192},{320,256},{384,320},{4... | collective-permute-start | bytes 958472 | tf_op jit(solution)/shard_map/ppermute | solution.py:165
  129.0 20.5 %collective-permute-start.9 = (bf16[3,416,128]{2,1,0:T(8,128)(2,1)S(1)}, bf16[3,416,128]{2,1,0:T(8,128)(2,1)S(1)}, u32[]{:S(2)}, u32[]{:S(2)}) collective-permute-start(bf16[3,416,128]{2,1,0:T(8,128)(2,1)S(1)} %get-tuple-element.26), channel_id=1, source_target_pairs={{0,64},{64,128},{128,192},{192,256},{256,320},{320,384},{384,448},... | collective-permute-start | bytes 958472 | tf_op jit(solution)/shard_map/ppermute | solution.py:165
  131.0 18.6 %collective-permute-start.11 = (bf16[3,208,128]{2,1,0:T(8,128)(2,1)S(1)}, bf16[3,208,128]{2,1,0:T(8,128)(2,1)S(1)}, u32[]{:S(2)}, u32[]{:S(2)}) collective-permute-start(bf16[3,208,128]{2,1,0:T(8,128)(2,1)S(1)} %get-tuple-element.27), channel_id=1, source_target_pairs={{0,128},{64,192},{128,256},{192,320},{256,384},{320,448},{384,512}... | collective-permute-start | bytes 479240 | tf_op jit(solution)/shard_map/ppermute | solution.py:165
  138.9 10.6 %collective-permute-start.12 = (bf16[3,208,128]{2,1,0:T(8,128)(2,1)S(1)}, bf16[3,208,128]{2,1,0:T(8,128)(2,1)S(1)}, u32[]{:S(2)}, u32[]{:S(2)}) collective-permute-start(bf16[3,208,128]{2,1,0:T(8,128)(2,1)S(1)} %get-tuple-element.28), channel_id=1, source_target_pairs={{0,640},{64,704},{128,0},{192,64},{256,128},{320,192},{384,256},{4... | collective-permute-start | bytes 479240 | tf_op jit(solution)/shard_map/ppermute | solution.py:165

commit v5 on v4

--- a/solution.py
+++ b/solution.py
@@ -81,34 +81,24 @@
         out[SPLIT:] = (part[SPLIT:] + d_ref[i].astype(F32)).astype(BF16)
 
 
-def far_kernel(stay_ref, a_ref, b_ref, out_ref):
-    out_ref[...] = (stay_ref[...].astype(F32) + a_ref[...].astype(F32) + b_ref[...].astype(F32)).astype(BF16)
-
-
-def three_kernel(after_ref, k0_ref, k4_ref, k8_ref, all_ref, low_ref, high_ref):
-    for i, part in enumerate((k0_ref, k4_ref, k8_ref)):
-        all_ref[i] = part[...]
-        low_ref[i] = part[:SPLIT]
-        high_ref[i] = part[SPLIT:]
-
-
-def x_sum_kernel(after_ref, in_ref, out_ref):
+def far_kernel(stay_ref, a_ref, b_ref, low_ref, high_ref):
+    part = (stay_ref[...].astype(F32) + a_ref[...].astype(F32) + b_ref[...].astype(F32)).astype(BF16)
+    low_ref[...] = part[:SPLIT]
+    high_ref[...] = part[SPLIT:]
+
+
+def x_sum_kernel(after_ref, in_ref, high_ref, out_ref, high_out_ref):
     out_ref[...] = jnp.sum(in_ref[...].astype(F32), axis=0).astype(BF16)
-
-
-def whole_kernel(rel_ref, k0_ref, k4_ref, k8_ref, low1_ref, high1_ref, low2_ref, high2_ref, out_ref, gw_ref):
-    gw_ref[0] = k0_ref[...]
-    gw_ref[4] = k4_ref[...]
-    gw_ref[8] = k8_ref[...]
-    for i in range(3):
-        gw_ref[(4 * i + 11) % NZ] = low1_ref[i]
-        gw_ref[4 * i + 1] = high1_ref[i]
-        gw_ref[(4 * i + 10) % NZ, :SPLIT] = low2_ref[i]
-        gw_ref[4 * i + 2, SPLIT:] = high2_ref[i]
+    high_out_ref[...] = high_ref[...]
+
+
+def whole_kernel(low_ref, high_ref, out_ref):
     rows = out_ref.shape[0]
     for j in range(NZ):
-        size = min(CHUNK, rows - j * CHUNK)
-        out_ref[j * CHUNK:j * CHUNK + size] = gw_ref[rel_ref[j], :size].astype(F32)
+        for half, part in enumerate((low_ref, high_ref)):
+            at = j * CHUNK + half * SPLIT
+            size = min(SPLIT, rows - at)
+            out_ref[at:at + size] = part[j, :size].astype(F32)
 
 
 SMEM = pl.BlockSpec(memory_space=pltpu.SMEM)
@@ -165,27 +155,22 @@
     return lax.ppermute(x, "dp", [(i, (i + by) % NZ) for i in range(NZ)])
 
 
-def reduce_gradients(gx, keep, up1, down1, up2, down2, rel, slots):
+def reduce_gradients(gx, keep, up1, down1, up2, down2, slots):
     tokens = gx.shape[1]
-    one, full, half = array((CHUNK, BS)), array((3, CHUNK, BS)), array((3, SPLIT, BS))
+    one = array((CHUNK, BS))
     gx = swap(gx.reshape(NX * NC, NY, tokens, BS), "mp", XC_GROUPS)
     parts = shift(up1, 1), shift(down1, -1), shift(up2, 2), shift(down2, -2)
     stay, up, down = call(near_kernel, [VMEM] * 5, (keep, *parts), (one,) * 3)
-    mine = call(far_kernel, [VMEM] * 3, (stay, shift(up, 4), shift(down, -4)), one)
-
-    k8, k4 = shift(mine, 4), shift(mine, -4)
-    gx = call(x_sum_kernel, [ORDER, VMEM], (mine, gx), array((NY, tokens, BS)))
-    three, low, high = call(three_kernel, [ORDER] + [VMEM] * 3, (gx, mine, k4, k8), (full, half, half))
+    piece = array((SPLIT, BS))
+    low, high = call(far_kernel, [VMEM] * 3, (stay, shift(up, 4), shift(down, -4)), (piece, piece))
+
+    low = lax.all_gather(low, "dp")
+    gx, high = call(
+        x_sum_kernel, [ORDER, VMEM, VMEM], (low, gx, high), (array((NY, tokens, BS)), piece)
+    )
     grad_x = total(swap(gx, "mp", Y_GROUPS))
-
-    low1, high1, low2, high2 = shift(three, 1), shift(three, -1), shift(low, 2), shift(high, -2)
-    grad_w = call(
-        whole_kernel,
-        [SMEM] + [VMEM] * 7,
-        (rel, mine, k4, k8, low1, high1, low2, high2),
-        array((slots * BS, BS), F32),
-        [pltpu.VMEM((NZ, CHUNK, BS), BF16)],
-    )
+    high = lax.all_gather(high, "dp")
+    grad_w = call(whole_kernel, [VMEM] * 2, (low, high), array((slots * BS, BS), F32))
     return grad_x, grad_w.reshape(slots, BS, BS)
 
 
@@ -210,7 +195,7 @@
 
     rel = (jnp.arange(NZ, dtype=jnp.int32) + NZ - lax.axis_index("dp")) % NZ
     act, gx, *parts = run_blocks(idx, out_idx, col, live, rel, own, sib, wb, grad_act)
-    grad_x, grad_w = reduce_gradients(gx, *parts, rel, slots)
+    grad_x, grad_w = reduce_gradients(gx, *parts, slots)
     return act, grad_x, grad_w
 
 

time: 154 us -> 161 us (1.045)
  blocking collectives: 18.8 us -> 70.8 us
  starting transfers between devices: 79 us -> 52.3 us
  waiting for transfers between devices: 40.6 us -> 24 us
    all_gather x0 -> x2, blocking collectives: none -> 52 us  [the longest x1 26.7 us: reduce_gradients(): low = lax.all_gather(low, 'dp')]
    ppermute x12 -> x6, starting transfers between devices: 60.8 us -> 34.2 us  [shift(): return lax.ppermute(x, 'dp', [(i, (i + by) % NZ) for i in range(NZ)])]
    ppermute x12 -> x6, waiting for transfers between devices: 31.1 us -> 14.5 us  [shift(): return lax.ppermute(x, 'dp', [(i, (i + by) % NZ) for i in range(NZ)])]
    pallas_call x6 -> x5, Pallas kernels: 7.15 us -> 6.42 us  [call(): pl.pallas_call(kernel, out_shape=outs, in_specs=specs, out_specs=jax.tree...]
  transfers between devices with their start and end apart: 16 -> 10, of which waited for: 9 -> 6; matrix products, arithmetic and copies ran while one was open for 1% -> 1% of each run, Pallas kernels for 2% -> 1%
where the time goes in v5:
time: 161 us; the launch traced here: 160 us
  blocking collectives  70.8 us (44%)
  starting transfers between devices  52.3 us (32%)
  waiting for transfers between devices  24 us (15%)
  Pallas kernels  6.42 us (4%)
  other arithmetic  3.54 us (2%)
  local copies, waits for them, and re-layouts  2.57 us (2%)
    ppermute x6, starting transfers between devices, shift(): return lax.ppermute(x, 'dp', [(i, (i + by) % NZ) for i in range(NZ)])  34.2 us
    all_gather x1, blocking collectives, reduce_gradients(): low = lax.all_gather(low, 'dp')  26.7 us
    all_gather x1, blocking collectives, reduce_gradients(): high = lax.all_gather(high, 'dp')  25.3 us
    all_to_all x1, blocking collectives, swap(): return lax.all_to_all(x, axis, 0, 0, tiled=True, axis_index_groups=groups)  18.8 us
    all_to_all x3, starting transfers between devices, swap(): return lax.all_to_all(x, axis, 0, 0, tiled=True, axis_index_groups=groups)  16.2 us
    ppermute x6, waiting for transfers between devices, shift(): return lax.ppermute(x, 'dp', [(i, (i + by) % NZ) for i in range(NZ)])  14.5 us
    all_to_all x3, waiting for transfers between devices, swap(): return lax.all_to_all(x, axis, 0, 0, tiled=True, axis_index_groups=groups)  8.92 us
    pallas_call x5, Pallas kernels, call(): pl.pallas_call(kernel, out_shape=outs, in_specs=specs, out_specs=jax.tree...  6.42 us
  transfers between devices with their start and end apart: 10, of which 6 were waited for; matrix products, arithmetic and copies ran while one was open for 1% of the time, Pallas kernels for 1%

profile of v5, /device:TPU:6, one launch (start us, length us, event | category | flops | bytes accessed | tf_op | source)
XLA Modules:
  0.0 160.4 jit_solution(4936700190875340228)
XLA Ops:
  0.6 0.9 convert_element_type.16
  1.5 18.8 %all_to_all.20 = bf16[8,128,128]{2,1,0:T(8,128)(2,1)S(1)} all-to-all(bf16[8,128,128]{2,1,0:T(8,128)(2,1)S(1)} %broadcast_in_dim.4), channel_id=1, replica_groups={{0,8,16,24,32,40,48,56},{1,9,17,25,33,41,49,57},{2,10,18,26,34,42,50,58..., dimensions={0} | all-to-all | bytes 524288 | tf_op jit(solution)/shard_map/all_to_all | solution.py:147
  20.3 1.2 broadcast_in_dim.5
  21.5 7.2 %all-to-all-start.1 = ((bf16[4,8,128,128]{3,2,1,0:T(8,128)(2,1)}), bf16[4,8,128,128]{3,2,1,0:T(8,128)(2,1)S(1)}, u32[]{:S(2)}, u32[]{:S(2)}) async-start(bf16[4,8,128,128]{3,2,1,0:T(8,128)(2,1)} %broadcast_in_dim.5), calls=%async_computation.1 | async-start | bytes 2097152 | tf_op jit(solution)/shard_map/all_to_all | solution.py:147
  28.7 8.9 %all-to-all-done.1 = bf16[4,8,128,128]{3,2,1,0:T(8,128)(2,1)S(1)} async-done(((bf16[4,8,128,128]{3,2,1,0:T(8,128)(2,1)}), bf16[4,8,128,128]{3,2,1,0:T(8,128)(2,1)S(1)}, u32[]{:S(2)}, u32[]{:S(2)}) %all-to-all-start.1) | async-done | bytes 1048608 | tf_op jit(solution)/shard_map/all_to_all | solution.py:147
  37.7 1.9 %collective-permute-start = (bf16[32,128,128]{2,1,0:T(8,128)(2,1)S(1)}, bf16[32,128,128]{2,1,0:T(8,128)(2,1)S(1)}, u32[]{:S(2)}, u32[]{:S(2)}) collective-permute-start(bf16[32,128,128]{2,1,0:T(8,128)(2,1)S(1)} %bitcast.52), channel_id=1, source_target_pairs={{0,1},{1,0},{2,3},{3,2},{4,5},{5,4},{6,7},{7,6},{8,9},{9,8},{10,11... | collective-permute-start | bytes 3145736 | tf_op jit(solution)/shard_map/ppermute | solution.py:194
  39.7 2.0 %multiply_convert_fusion.w_ref = bf16[38,128,128]{2,1,0:T(8,128)(2,1)S(1)} fusion(f32[38,128,128]{2,1,0:T(8,128)} %param.5, f32[38]{0:T(128)S(1)} %fusion.2.live_ref), kind=kLoop, calls=%fused_computation | loop fusion | flops 1245184 | bytes 3735704 | tf_op jit(solution)/shard_map/convert_element_type | solution.py:189
  41.6 0.6 collective-permute-done.sib_ref
  42.2 3.6 %shard_map.67 = (f32[128,512]{1,0:T(8,128)}, bf16[64,128,128]{2,1,0:T(8,128)(2,1)S(1)}, bf16[3,416,128]{2,1,0:T(8,128)(2,1)S(1)}, bf16[3,416,128]{2,1,0:T(8,128)...) custom-call(s32[38]{0:T(128)S(1)} %multiply_add_fusion.1.idx_ref, ...), custom_call_target="tpu_custom_call" | custom-call | tf_op jit(solution)/shard_map/pallas_call | solution.py:110
  45.8 1.3 copy-done
  47.2 5.6 %all-to-all-start.2 = ((bf16[8,8,128,128]{3,2,1,0:T(8,128)(2,1)}), bf16[8,8,128,128]{3,2,1,0:T(8,128)(2,1)S(1)}, u32[]{:S(2)}, u32[]{:S(2)}) async-start(bf16[8,8,128,128]{3,2,1,0:T(8,128)(2,1)} %bitcast.55), calls=%async_computation.2 | async-start | bytes 4194304 | tf_op jit(solution)/shard_map/all_to_all | solution.py:147
  52.8 4.3 %collective-permute-start.1 = (bf16[3,416,128]{2,1,0:T(8,128)(2,1)S(1)}, bf16[3,416,128]{2,1,0:T(8,128)(2,1)S(1)}, u32[]{:S(2)}, u32[]{:S(2)}) collective-permute-start(bf16[3,416,128]{2,1,0:T(8,128)(2,1)S(1)} %get-tuple-element.19), channel_id=1, source_target_pairs={{0,64},{64,128},{128,192},{192,256},{256,320},{320,384},{384,448},... | collective-permute-start | bytes 958472 | tf_op jit(solution)/shard_map/ppermute | solution.py:155
  57.0 12.2 %collective-permute-start.2 = (bf16[3,416,128]{2,1,0:T(8,128)(2,1)S(1)}, bf16[3,416,128]{2,1,0:T(8,128)(2,1)S(1)}, u32[]{:S(2)}, u32[]{:S(2)}) collective-permute-start(bf16[3,416,128]{2,1,0:T(8,128)(2,1)S(1)} %get-tuple-element.20), channel_id=1, source_target_pairs={{0,704},{64,0},{128,64},{192,128},{256,192},{320,256},{384,320},{4... | collective-permute-start | bytes 958472 | tf_op jit(solution)/shard_map/ppermute | solution.py:155
  69.3 1.9 %collective-permute-start.3 = (bf16[3,208,128]{2,1,0:T(8,128)(2,1)S(1)}, bf16[3,208,128]{2,1,0:T(8,128)(2,1)S(1)}, u32[]{:S(2)}, u32[]{:S(2)}) collective-permute-start(bf16[3,208,128]{2,1,0:T(8,128)(2,1)S(1)} %get-tuple-element.21), channel_id=1, source_target_pairs={{0,128},{64,192},{128,256},{192,320},{256,384},{320,448},{384,512}... | collective-permute-start | bytes 479240 | tf_op jit(solution)/shard_map/ppermute | solution.py:155
  71.2 6.0 %collective-permute-start.4 = (bf16[3,208,128]{2,1,0:T(8,128)(2,1)S(1)}, bf16[3,208,128]{2,1,0:T(8,128)(2,1)S(1)}, u32[]{:S(2)}, u32[]{:S(2)}) collective-permute-start(bf16[3,208,128]{2,1,0:T(8,128)(2,1)S(1)} %get-tuple-element.22), channel_id=1, source_target_pairs={{0,640},{64,704},{128,0},{192,64},{256,128},{320,192},{384,256},{4... | collective-permute-start | bytes 479240 | tf_op jit(solution)/shard_map/ppermute | solution.py:155
  77.2 4.3 %collective-permute-done.3.c_ref = bf16[3,208,128]{2,1,0:T(8,128)(2,1)S(1)} collective-permute-done((bf16[3,208,128]{2,1,0:T(8,128)(2,1)S(1)}, bf16[3,208,128]{2,1,0:T(8,128)(2,1)S(1)}, u32[]{:S(2)}, u32[]{:S(2)}) %collective-permute-start.3) | collective-permute-done | bytes 159776 | tf_op jit(solution)/shard_map/ppermute | solution.py:155
  81.5 2.1 %collective-permute-done.4.d_ref = bf16[3,208,128]{2,1,0:T(8,128)(2,1)S(1)} collective-permute-done((bf16[3,208,128]{2,1,0:T(8,128)(2,1)S(1)}, bf16[3,208,128]{2,1,0:T(8,128)(2,1)S(1)}, u32[]{:S(2)}, u32[]{:S(2)}) %collective-permute-start.4) | collective-permute-done | bytes 159776 | tf_op jit(solution)/shard_map/ppermute | solution.py:155
  83.7 0.0 collective-permute-done.1.a_ref
  83.7 0.0 collective-permute-done.2.b_ref
  83.7 0.2 shard_map.68
  83.8 5.1 %collective-permute-start.5 = (bf16[416,128]{1,0:T(8,128)(2,1)S(1)}, bf16[416,128]{1,0:T(8,128)(2,1)S(1)}, u32[]{:S(2)}, u32[]{:S(2)}) collective-permute-start(bf16[416,128]{1,0:T(8,128)(2,1)S(1)} %get-tuple-element.24), channel_id=1, source_target_pairs={{0,256},{64,320},{128,384},{192,448},{256,512},{320,576},{384,640}... | collective-permute-start | bytes 319496 | tf_op jit(solution)/shard_map/ppermute | solution.py:155
  88.9 4.7 %collective-permute-start.6 = (bf16[416,128]{1,0:T(8,128)(2,1)S(1)}, bf16[416,128]{1,0:T(8,128)(2,1)S(1)}, u32[]{:S(2)}, u32[]{:S(2)}) collective-permute-start(bf16[416,128]{1,0:T(8,128)(2,1)S(1)} %get-tuple-element.25), channel_id=1, source_target_pairs={{0,512},{64,576},{128,640},{192,704},{256,0},{320,64},{384,128},{4... | collective-permute-start | bytes 319496 | tf_op jit(solution)/shard_map/ppermute | solution.py:155
  93.6 4.2 %collective-permute-done.5.a_ref = bf16[416,128]{1,0:T(8,128)(2,1)S(1)} collective-permute-done((bf16[416,128]{1,0:T(8,128)(2,1)S(1)}, bf16[416,128]{1,0:T(8,128)(2,1)S(1)}, u32[]{:S(2)}, u32[]{:S(2)}) %collective-permute-start.5) | collective-permute-done | bytes 106528 | tf_op jit(solution)/shard_map/ppermute | solution.py:155
  97.8 3.9 %collective-permute-done.6.b_ref = bf16[416,128]{1,0:T(8,128)(2,1)S(1)} collective-permute-done((bf16[416,128]{1,0:T(8,128)(2,1)S(1)}, bf16[416,128]{1,0:T(8,128)(2,1)S(1)}, u32[]{:S(2)}, u32[]{:S(2)}) %collective-permute-start.6) | collective-permute-done | bytes 106528 | tf_op jit(solution)/shard_map/ppermute | solution.py:155
  101.7 26.7 %all-gather = bf16[2496,128]{1,0:T(8,128)(2,1)S(1)} all-gather(bf16[208,128]{1,0:T(8,128)(2,1)S(1)} %get-tuple-element.26), channel_id=2, replica_groups=mesh['dp'=12,'mp'=64] {'dp'}, dimensions={0}, use_global_device_ids=true | all-gather | bytes 692224 | tf_op jit(solution)/shard_map/all_gather | solution.py:167
  128.4 0.0 all-to-all-done.2.in_ref
  128.4 1.0 shard_map.70
  129.4 3.4 %all-to-all-start.3 = ((bf16[8,128,128]{2,1,0:T(8,128)(2,1)}), bf16[8,128,128]{2,1,0:T(8,128)(2,1)S(1)}, u32[]{:S(2)}, u32[]{:S(2)}) async-start(bf16[8,128,128]{2,1,0:T(8,128)(2,1)} %get-tuple-element.29), calls=%async_computation.3 | async-start | bytes 524288 | tf_op jit(solution)/shard_map/all_to_all | solution.py:147
  132.8 25.3 %all-gather.1 = bf16[2496,128]{1,0:T(8,128)(2,1)S(1)} all-gather(bf16[208,128]{1,0:T(8,128)(2,1)S(1)} %get-tuple-element.30), channel_id=3, replica_groups=mesh['dp'=12,'mp'=64] {'dp'}, dimensions={0}, use_global_device_ids=true | all-gather | bytes 692224 | tf_op jit(solution)/shard_map/all_gather | solution.py:172
  158.1 1.6 %shard_map.71 = f32[4864,128]{1,0:T(8,128)} custom-call(bf16[12,208,128]{2,1,0:T(8,128)(2,1)S(1)} %bitcast.51, bf16[12,208,128]{2,1,0:T(8,128)(2,1)S(1)} %bitcast.54), custom_call_target="tpu_custom_call" | custom-call | tf_op jit(solution)/shard_map/pallas_call | solution.py:110
  159.7 0.0 all-to-all-done.3
  159.7 0.7 convert_reduce_fusion
  (12 shorter events, 0.1 us)
Async XLA Ops:
  0.6 28.1 %copy-start.2 = (s32[38,2]{0,1:T(2,128)S(1)}, s32[38,2]{0,1:T(2,128)}, u32[]{:S(2)}) copy-start(s32[38,2]{0,1:T(2,128)} %param.6) | copy-start | bytes 916
  21.5 20.7 %copy-start.1 = (f32[128,512]{1,0:T(8,128)S(1)}, f32[128,512]{1,0:T(8,128)}, u32[]{:S(2)}) copy-start(f32[128,512]{1,0:T(8,128)} %g_ref.1) | copy-start | bytes 786436
  21.5 16.1 %all-to-all-start.1 = ((bf16[4,8,128,128]{3,2,1,0:T(8,128)(2,1)}), bf16[4,8,128,128]{3,2,1,0:T(8,128)(2,1)S(1)}, u32[]{:S(2)}, u32[]{:S(2)}) async-start(bf16[4,8,128,128]{3,2,1,0:T(8,128)(2,1)} %broadcast_in_dim.5), calls=%async_computation.1 | async-start | bytes 2097152 | tf_op jit(solution)/shard_map/all_to_all | solution.py:147
  37.7 4.5 %collective-permute-start = (bf16[32,128,128]{2,1,0:T(8,128)(2,1)S(1)}, bf16[32,128,128]{2,1,0:T(8,128)(2,1)S(1)}, u32[]{:S(2)}, u32[]{:S(2)}) collective-permute-start(bf16[32,128,128]{2,1,0:T(8,128)(2,1)S(1)} %bitcast.52), channel_id=1, source_target_pairs={{0,1},{1,0},{2,3},{3,2},{4,5},{5,4},{6,7},{7,6},{8,9},{9,8},{10,11... | collective-permute-start | bytes 3145736 | tf_op jit(solution)/shard_map/ppermute | solution.py:194
  45.8 1.3 copy-start
  47.2 81.3 %all-to-all-start.2 = ((bf16[8,8,128,128]{3,2,1,0:T(8,128)(2,1)}), bf16[8,8,128,128]{3,2,1,0:T(8,128)(2,1)S(1)}, u32[]{:S(2)}, u32[]{:S(2)}) async-start(bf16[8,8,128,128]{3,2,1,0:T(8,128)(2,1)} %bitcast.55), calls=%async_computation.2 | async-start | bytes 4194304 | tf_op jit(solution)/shard_map/all_to_all | solution.py:147
  52.8 30.9 %collective-permute-start.1 = (bf16[3,416,128]{2,1,0:T(8,128)(2,1)S(1)}, bf16[3,416,128]{2,1,0:T(8,128)(2,1)S(1)}, u32[]{:S(2)}, u32[]{:S(2)}) collective-permute-start(bf16[3,416,128]{2,1,0:T(8,128)(2,1)S(1)} %get-tuple-element.19), channel_id=1, source_target_pairs={{0,64},{64,128},{128,192},{192,256},{256,320},{320,384},{384,448},... | collective-permute-start | bytes 958472 | tf_op jit(solution)/shard_map/ppermute | solution.py:155
  57.0 26.6 %collective-permute-start.2 = (bf16[3,416,128]{2,1,0:T(8,128)(2,1)S(1)}, bf16[3,416,128]{2,1,0:T(8,128)(2,1)S(1)}, u32[]{:S(2)}, u32[]{:S(2)}) collective-permute-start(bf16[3,416,128]{2,1,0:T(8,128)(2,1)S(1)} %get-tuple-element.20), channel_id=1, source_target_pairs={{0,704},{64,0},{128,64},{192,128},{256,192},{320,256},{384,320},{4... | collective-permute-start | bytes 958472 | tf_op jit(solution)/shard_map/ppermute | solution.py:155
  69.3 12.3 %collective-permute-start.3 = (bf16[3,208,128]{2,1,0:T(8,128)(2,1)S(1)}, bf16[3,208,128]{2,1,0:T(8,128)(2,1)S(1)}, u32[]{:S(2)}, u32[]{:S(2)}) collective-permute-start(bf16[3,208,128]{2,1,0:T(8,128)(2,1)S(1)} %get-tuple-element.21), channel_id=1, source_target_pairs={{0,128},{64,192},{128,256},{192,320},{256,384},{320,448},{384,512}... | collective-permute-start | bytes 479240 | tf_op jit(solution)/shard_map/ppermute | solution.py:155
  71.2 12.4 %collective-permute-start.4 = (bf16[3,208,128]{2,1,0:T(8,128)(2,1)S(1)}, bf16[3,208,128]{2,1,0:T(8,128)(2,1)S(1)}, u32[]{:S(2)}, u32[]{:S(2)}) collective-permute-start(bf16[3,208,128]{2,1,0:T(8,128)(2,1)S(1)} %get-tuple-element.22), channel_id=1, source_target_pairs={{0,640},{64,704},{128,0},{192,64},{256,128},{320,192},{384,256},{4... | collective-permute-start | bytes 479240 | tf_op jit(solution)/shard_map/ppermute | solution.py:155
  83.8 14.0 %collective-permute-start.5 = (bf16[416,128]{1,0:T(8,128)(2,1)S(1)}, bf16[416,128]{1,0:T(8,128)(2,1)S(1)}, u32[]{:S(2)}, u32[]{:S(2)}) collective-permute-start(bf16[416,128]{1,0:T(8,128)(2,1)S(1)} %get-tuple-element.24), channel_id=1, source_target_pairs={{0,256},{64,320},{128,384},{192,448},{256,512},{320,576},{384,640}... | collective-permute-start | bytes 319496 | tf_op jit(solution)/shard_map/ppermute | solution.py:155
  88.9 12.8 %collective-permute-start.6 = (bf16[416,128]{1,0:T(8,128)(2,1)S(1)}, bf16[416,128]{1,0:T(8,128)(2,1)S(1)}, u32[]{:S(2)}, u32[]{:S(2)}) collective-permute-start(bf16[416,128]{1,0:T(8,128)(2,1)S(1)} %get-tuple-element.25), channel_id=1, source_target_pairs={{0,512},{64,576},{128,640},{192,704},{256,0},{320,64},{384,128},{4... | collective-permute-start | bytes 319496 | tf_op jit(solution)/shard_map/ppermute | solution.py:155
  129.4 30.3 %all-to-all-start.3 = ((bf16[8,128,128]{2,1,0:T(8,128)(2,1)}), bf16[8,128,128]{2,1,0:T(8,128)(2,1)S(1)}, u32[]{:S(2)}, u32[]{:S(2)}) async-start(bf16[8,128,128]{2,1,0:T(8,128)(2,1)} %get-tuple-element.29), calls=%async_computation.3 | async-start | bytes 524288 | tf_op jit(solution)/shard_map/all_to_all | solution.py:147

commit v6 on v4

--- a/solution.py
+++ b/solution.py
@@ -85,26 +85,20 @@
     out_ref[...] = (stay_ref[...].astype(F32) + a_ref[...].astype(F32) + b_ref[...].astype(F32)).astype(BF16)
 
 
-def three_kernel(after_ref, k0_ref, k4_ref, k8_ref, all_ref, low_ref, high_ref):
-    for i, part in enumerate((k0_ref, k4_ref, k8_ref)):
-        all_ref[i] = part[...]
-        low_ref[i] = part[:SPLIT]
-        high_ref[i] = part[SPLIT:]
+def four_kernel(after_ref, k0_ref, k3_ref, k6_ref, k9_ref, out_ref):
+    for i, part in enumerate((k0_ref, k3_ref, k6_ref, k9_ref)):
+        out_ref[i] = part[...]
 
 
 def x_sum_kernel(after_ref, in_ref, out_ref):
     out_ref[...] = jnp.sum(in_ref[...].astype(F32), axis=0).astype(BF16)
 
 
-def whole_kernel(rel_ref, k0_ref, k4_ref, k8_ref, low1_ref, high1_ref, low2_ref, high2_ref, out_ref, gw_ref):
-    gw_ref[0] = k0_ref[...]
-    gw_ref[4] = k4_ref[...]
-    gw_ref[8] = k8_ref[...]
-    for i in range(3):
-        gw_ref[(4 * i + 11) % NZ] = low1_ref[i]
-        gw_ref[4 * i + 1] = high1_ref[i]
-        gw_ref[(4 * i + 10) % NZ, :SPLIT] = low2_ref[i]
-        gw_ref[4 * i + 2, SPLIT:] = high2_ref[i]
+def whole_kernel(rel_ref, after_ref, mid_ref, low_ref, high_ref, out_ref, gw_ref):
+    for i in range(4):
+        gw_ref[3 * i] = mid_ref[i]
+        gw_ref[(3 * i + 11) % NZ] = low_ref[i]
+        gw_ref[3 * i + 1] = high_ref[i]
     rows = out_ref.shape[0]
     for j in range(NZ):
         size = min(CHUNK, rows - j * CHUNK)
@@ -167,22 +161,22 @@
 
 def reduce_gradients(gx, keep, up1, down1, up2, down2, rel, slots):
     tokens = gx.shape[1]
-    one, full, half = array((CHUNK, BS)), array((3, CHUNK, BS)), array((3, SPLIT, BS))
+    one = array((CHUNK, BS))
     gx = swap(gx.reshape(NX * NC, NY, tokens, BS), "mp", XC_GROUPS)
     parts = shift(up1, 1), shift(down1, -1), shift(up2, 2), shift(down2, -2)
     stay, up, down = call(near_kernel, [VMEM] * 5, (keep, *parts), (one,) * 3)
     mine = call(far_kernel, [VMEM] * 3, (stay, shift(up, 4), shift(down, -4)), one)
 
-    k8, k4 = shift(mine, 4), shift(mine, -4)
+    k9, k3, k6 = shift(mine, 3), shift(mine, -3), shift(mine, 6)
     gx = call(x_sum_kernel, [ORDER, VMEM], (mine, gx), array((NY, tokens, BS)))
-    three, low, high = call(three_kernel, [ORDER] + [VMEM] * 3, (gx, mine, k4, k8), (full, half, half))
+    mid = call(four_kernel, [ORDER] + [VMEM] * 4, (gx, mine, k3, k6, k9), array((4, CHUNK, BS)))
     grad_x = total(swap(gx, "mp", Y_GROUPS))
 
-    low1, high1, low2, high2 = shift(three, 1), shift(three, -1), shift(low, 2), shift(high, -2)
+    low, high = shift(mid, 1), shift(mid, -1)
     grad_w = call(
         whole_kernel,
-        [SMEM] + [VMEM] * 7,
-        (rel, mine, k4, k8, low1, high1, low2, high2),
+        [SMEM, ORDER] + [VMEM] * 3,
+        (rel, grad_x, mid, low, high),
         array((slots * BS, BS), F32),
         [pltpu.VMEM((NZ, CHUNK, BS), BF16)],
     )

time: 154 us -> 156 us (1.013)
  waiting for transfers between devices: 40.6 us -> 42.5 us
    ppermute x12 -> x11, waiting for transfers between devices: 31.1 us -> 33 us  [shift(): return lax.ppermute(x, 'dp', [(i, (i + by) % NZ) for i in range(NZ)])]
    ppermute x12 -> x11, starting transfers between devices: 60.8 us -> 61.6 us  [shift(): return lax.ppermute(x, 'dp', [(i, (i + by) % NZ) for i in range(NZ)])]
  transfers between devices with their start and end apart: 16 -> 15, of which waited for: 9 -> 10; matrix products, arithmetic and copies ran while one was open for 1% -> 1% of each run, Pallas kernels for 2% -> 0%
where the time goes in v6:
time: 156 us; the launch traced here: 154 us
  starting transfers between devices  79.7 us (51%)
  waiting for transfers between devices  42.5 us (27%)
  blocking collectives  18.8 us (12%)
  Pallas kernels  7.07 us (5%)
  other arithmetic  2.92 us (2%)
  local copies, waits for them, and re-layouts  2.58 us (2%)
    ppermute x11, starting transfers between devices, shift(): return lax.ppermute(x, 'dp', [(i, (i + by) % NZ) for i in range(NZ)])  61.6 us
    ppermute x11, waiting for transfers between devices, shift(): return lax.ppermute(x, 'dp', [(i, (i + by) % NZ) for i in range(NZ)])  33 us
    all_to_all x1, blocking collectives, swap(): return lax.all_to_all(x, axis, 0, 0, tiled=True, axis_index_groups=groups)  18.8 us
    all_to_all x3, starting transfers between devices, swap(): return lax.all_to_all(x, axis, 0, 0, tiled=True, axis_index_groups=groups)  16.2 us
    all_to_all x3, waiting for transfers between devices, swap(): return lax.all_to_all(x, axis, 0, 0, tiled=True, axis_index_groups=groups)  8.92 us
    pallas_call x6, Pallas kernels, call(): pl.pallas_call(kernel, out_shape=outs, in_specs=specs, out_specs=jax.tree...  7.07 us
  transfers between devices with their start and end apart: 15, of which 10 were waited for; matrix products, arithmetic and copies ran while one was open for 1% of the time, Pallas kernels for 0%

profile of v6, /device:TPU:6, one launch (start us, length us, event | category | flops | bytes accessed | tf_op | source)
XLA Modules:
  0.0 154.4 jit_solution(4436915038240187832)
XLA Ops:
  0.6 0.9 convert_element_type.16
  1.5 18.8 %all_to_all.20 = bf16[8,128,128]{2,1,0:T(8,128)(2,1)S(1)} all-to-all(bf16[8,128,128]{2,1,0:T(8,128)(2,1)S(1)} %broadcast_in_dim.4), channel_id=1, replica_groups={{0,8,16,24,32,40,48,56},{1,9,17,25,33,41,49,57},{2,10,18,26,34,42,50,58..., dimensions={0} | all-to-all | bytes 524288 | tf_op jit(solution)/shard_map/all_to_all | solution.py:151
  20.3 1.2 broadcast_in_dim.5
  21.5 7.2 %all-to-all-start.1 = ((bf16[4,8,128,128]{3,2,1,0:T(8,128)(2,1)}), bf16[4,8,128,128]{3,2,1,0:T(8,128)(2,1)S(1)}, u32[]{:S(2)}, u32[]{:S(2)}) async-start(bf16[4,8,128,128]{3,2,1,0:T(8,128)(2,1)} %broadcast_in_dim.5), calls=%async_computation.1 | async-start | bytes 2097152 | tf_op jit(solution)/shard_map/all_to_all | solution.py:151
  28.7 8.9 %all-to-all-done.1 = bf16[4,8,128,128]{3,2,1,0:T(8,128)(2,1)S(1)} async-done(((bf16[4,8,128,128]{3,2,1,0:T(8,128)(2,1)}), bf16[4,8,128,128]{3,2,1,0:T(8,128)(2,1)S(1)}, u32[]{:S(2)}, u32[]{:S(2)}) %all-to-all-start.1) | async-done | bytes 1048608 | tf_op jit(solution)/shard_map/all_to_all | solution.py:151
  37.7 1.9 %collective-permute-start = (bf16[32,128,128]{2,1,0:T(8,128)(2,1)S(1)}, bf16[32,128,128]{2,1,0:T(8,128)(2,1)S(1)}, u32[]{:S(2)}, u32[]{:S(2)}) collective-permute-start(bf16[32,128,128]{2,1,0:T(8,128)(2,1)S(1)} %bitcast.48), channel_id=1, source_target_pairs={{0,1},{1,0},{2,3},{3,2},{4,5},{5,4},{6,7},{7,6},{8,9},{9,8},{10,11... | collective-permute-start | bytes 3145736 | tf_op jit(solution)/shard_map/ppermute | solution.py:203
  39.7 2.0 %multiply_convert_fusion.w_ref = bf16[38,128,128]{2,1,0:T(8,128)(2,1)S(1)} fusion(f32[38,128,128]{2,1,0:T(8,128)} %param.5, f32[38]{0:T(128)S(1)} %fusion.2.live_ref), kind=kLoop, calls=%fused_computation | loop fusion | flops 1245184 | bytes 3735704 | tf_op jit(solution)/shard_map/convert_element_type | solution.py:198
  42.2 3.6 %shard_map.67 = (f32[128,512]{1,0:T(8,128)}, bf16[64,128,128]{2,1,0:T(8,128)(2,1)S(1)}, bf16[3,416,128]{2,1,0:T(8,128)(2,1)S(1)}, bf16[3,416,128]{2,1,0:T(8,128)...) custom-call(s32[38]{0:T(128)S(1)} %multiply_add_fusion.1.idx_ref, ...), custom_call_target="tpu_custom_call" | custom-call | tf_op jit(solution)/shard_map/pallas_call | solution.py:114
  45.8 1.3 copy-done
  47.2 5.6 %all-to-all-start.2 = ((bf16[8,8,128,128]{3,2,1,0:T(8,128)(2,1)}), bf16[8,8,128,128]{3,2,1,0:T(8,128)(2,1)S(1)}, u32[]{:S(2)}, u32[]{:S(2)}) async-start(bf16[8,8,128,128]{3,2,1,0:T(8,128)(2,1)} %bitcast.50), calls=%async_computation.2 | async-start | bytes 4194304 | tf_op jit(solution)/shard_map/all_to_all | solution.py:151
  52.8 4.3 %collective-permute-start.1 = (bf16[3,416,128]{2,1,0:T(8,128)(2,1)S(1)}, bf16[3,416,128]{2,1,0:T(8,128)(2,1)S(1)}, u32[]{:S(2)}, u32[]{:S(2)}) collective-permute-start(bf16[3,416,128]{2,1,0:T(8,128)(2,1)S(1)} %get-tuple-element.15), channel_id=1, source_target_pairs={{0,64},{64,128},{128,192},{192,256},{256,320},{320,384},{384,448},... | collective-permute-start | bytes 958472 | tf_op jit(solution)/shard_map/ppermute | solution.py:159
  57.0 12.2 %collective-permute-start.2 = (bf16[3,416,128]{2,1,0:T(8,128)(2,1)S(1)}, bf16[3,416,128]{2,1,0:T(8,128)(2,1)S(1)}, u32[]{:S(2)}, u32[]{:S(2)}) collective-permute-start(bf16[3,416,128]{2,1,0:T(8,128)(2,1)S(1)} %get-tuple-element.16), channel_id=1, source_target_pairs={{0,704},{64,0},{128,64},{192,128},{256,192},{320,256},{384,320},{4... | collective-permute-start | bytes 958472 | tf_op jit(solution)/shard_map/ppermute | solution.py:159
  69.3 1.9 %collective-permute-start.3 = (bf16[3,208,128]{2,1,0:T(8,128)(2,1)S(1)}, bf16[3,208,128]{2,1,0:T(8,128)(2,1)S(1)}, u32[]{:S(2)}, u32[]{:S(2)}) collective-permute-start(bf16[3,208,128]{2,1,0:T(8,128)(2,1)S(1)} %get-tuple-element.17), channel_id=1, source_target_pairs={{0,128},{64,192},{128,256},{192,320},{256,384},{320,448},{384,512}... | collective-permute-start | bytes 479240 | tf_op jit(solution)/shard_map/ppermute | solution.py:159
  71.2 6.0 %collective-permute-start.4 = (bf16[3,208,128]{2,1,0:T(8,128)(2,1)S(1)}, bf16[3,208,128]{2,1,0:T(8,128)(2,1)S(1)}, u32[]{:S(2)}, u32[]{:S(2)}) collective-permute-start(bf16[3,208,128]{2,1,0:T(8,128)(2,1)S(1)} %get-tuple-element.18), channel_id=1, source_target_pairs={{0,640},{64,704},{128,0},{192,64},{256,128},{320,192},{384,256},{4... | collective-permute-start | bytes 479240 | tf_op jit(solution)/shard_map/ppermute | solution.py:159
  77.3 4.3 %collective-permute-done.3.c_ref = bf16[3,208,128]{2,1,0:T(8,128)(2,1)S(1)} collective-permute-done((bf16[3,208,128]{2,1,0:T(8,128)(2,1)S(1)}, bf16[3,208,128]{2,1,0:T(8,128)(2,1)S(1)}, u32[]{:S(2)}, u32[]{:S(2)}) %collective-permute-start.3) | collective-permute-done | bytes 159776 | tf_op jit(solution)/shard_map/ppermute | solution.py:159
  81.5 2.2 %collective-permute-done.4.d_ref = bf16[3,208,128]{2,1,0:T(8,128)(2,1)S(1)} collective-permute-done((bf16[3,208,128]{2,1,0:T(8,128)(2,1)S(1)}, bf16[3,208,128]{2,1,0:T(8,128)(2,1)S(1)}, u32[]{:S(2)}, u32[]{:S(2)}) %collective-permute-start.4) | collective-permute-done | bytes 159776 | tf_op jit(solution)/shard_map/ppermute | solution.py:159
  83.8 5.1 %collective-permute-start.5 = (bf16[416,128]{1,0:T(8,128)(2,1)S(1)}, bf16[416,128]{1,0:T(8,128)(2,1)S(1)}, u32[]{:S(2)}, u32[]{:S(2)}) collective-permute-start(bf16[416,128]{1,0:T(8,128)(2,1)S(1)} %get-tuple-element.20), channel_id=1, source_target_pairs={{0,256},{64,320},{128,384},{192,448},{256,512},{320,576},{384,640}... | collective-permute-start | bytes 319496 | tf_op jit(solution)/shard_map/ppermute | solution.py:159
  88.9 4.7 %collective-permute-start.6 = (bf16[416,128]{1,0:T(8,128)(2,1)S(1)}, bf16[416,128]{1,0:T(8,128)(2,1)S(1)}, u32[]{:S(2)}, u32[]{:S(2)}) collective-permute-start(bf16[416,128]{1,0:T(8,128)(2,1)S(1)} %get-tuple-element.21), channel_id=1, source_target_pairs={{0,512},{64,576},{128,640},{192,704},{256,0},{320,64},{384,128},{4... | collective-permute-start | bytes 319496 | tf_op jit(solution)/shard_map/ppermute | solution.py:159
  93.6 4.2 %collective-permute-done.5.a_ref = bf16[416,128]{1,0:T(8,128)(2,1)S(1)} collective-permute-done((bf16[416,128]{1,0:T(8,128)(2,1)S(1)}, bf16[416,128]{1,0:T(8,128)(2,1)S(1)}, u32[]{:S(2)}, u32[]{:S(2)}) %collective-permute-start.5) | collective-permute-done | bytes 106528 | tf_op jit(solution)/shard_map/ppermute | solution.py:159
  97.8 3.9 %collective-permute-done.6.b_ref = bf16[416,128]{1,0:T(8,128)(2,1)S(1)} collective-permute-done((bf16[416,128]{1,0:T(8,128)(2,1)S(1)}, bf16[416,128]{1,0:T(8,128)(2,1)S(1)}, u32[]{:S(2)}, u32[]{:S(2)}) %collective-permute-start.6) | collective-permute-done | bytes 106528 | tf_op jit(solution)/shard_map/ppermute | solution.py:159
  101.8 1.0 shard_map.70.after_ref
  102.7 3.4 %all-to-all-start.3 = ((bf16[8,128,128]{2,1,0:T(8,128)(2,1)}), bf16[8,128,128]{2,1,0:T(8,128)(2,1)S(1)}, u32[]{:S(2)}, u32[]{:S(2)}) async-start(bf16[8,128,128]{2,1,0:T(8,128)(2,1)} %shard_map.70.after_ref), calls=%async_computation.3 | async-start | bytes 524288 | tf_op jit(solution)/shard_map/all_to_all | solution.py:151
  106.2 4.1 %collective-permute-start.9 = (bf16[416,128]{1,0:T(8,128)(2,1)S(1)}, bf16[416,128]{1,0:T(8,128)(2,1)S(1)}, u32[]{:S(2)}, u32[]{:S(2)}) collective-permute-start(bf16[416,128]{1,0:T(8,128)(2,1)S(1)} %shard_map.69.after_ref.k0_ref), channel_id=1, source_target_pairs={{0,192},{64,256},{128,320},{192,384},{256,448},{320,512},{384,576}... | collective-permute-start | bytes 319496 | tf_op jit(solution)/shard_map/ppermute | solution.py:159
  110.2 9.5 %collective-permute-start.8 = (bf16[416,128]{1,0:T(8,128)(2,1)S(1)}, bf16[416,128]{1,0:T(8,128)(2,1)S(1)}, u32[]{:S(2)}, u32[]{:S(2)}) collective-permute-start(bf16[416,128]{1,0:T(8,128)(2,1)S(1)} %shard_map.69.after_ref.k0_ref), channel_id=1, source_target_pairs={{0,384},{64,448},{128,512},{192,576},{256,640},{320,704},{384,0},{... | collective-permute-start | bytes 319496 | tf_op jit(solution)/shard_map/ppermute | solution.py:159
  119.8 5.7 %collective-permute-start.7 = (bf16[416,128]{1,0:T(8,128)(2,1)S(1)}, bf16[416,128]{1,0:T(8,128)(2,1)S(1)}, u32[]{:S(2)}, u32[]{:S(2)}) collective-permute-start(bf16[416,128]{1,0:T(8,128)(2,1)S(1)} %shard_map.69.after_ref.k0_ref), channel_id=1, source_target_pairs={{0,576},{64,640},{128,704},{192,0},{256,64},{320,128},{384,192},{4... | collective-permute-start | bytes 319496 | tf_op jit(solution)/shard_map/ppermute | solution.py:159
  125.5 5.0 %collective-permute-done.8.k6_ref = bf16[416,128]{1,0:T(8,128)(2,1)S(1)} collective-permute-done((bf16[416,128]{1,0:T(8,128)(2,1)S(1)}, bf16[416,128]{1,0:T(8,128)(2,1)S(1)}, u32[]{:S(2)}, u32[]{:S(2)}) %collective-permute-start.8) | collective-permute-done | bytes 106528 | tf_op jit(solution)/shard_map/ppermute | solution.py:159
  130.4 2.1 %collective-permute-done.7.k3_ref = bf16[416,128]{1,0:T(8,128)(2,1)S(1)} collective-permute-done((bf16[416,128]{1,0:T(8,128)(2,1)S(1)}, bf16[416,128]{1,0:T(8,128)(2,1)S(1)}, u32[]{:S(2)}, u32[]{:S(2)}) %collective-permute-start.7) | collective-permute-done | bytes 106528 | tf_op jit(solution)/shard_map/ppermute | solution.py:159
  132.6 6.2 %collective-permute-start.11 = (bf16[4,416,128]{2,1,0:T(8,128)(2,1)S(1)}, bf16[4,416,128]{2,1,0:T(8,128)(2,1)S(1)}, u32[]{:S(2)}, u32[]{:S(2)}) collective-permute-start(bf16[4,416,128]{2,1,0:T(8,128)(2,1)S(1)} %shard_map.71.mid_ref), channel_id=1, source_target_pairs={{0,704},{64,0},{128,64},{192,128},{256,192},{320,256},{384,320},{4... | collective-permute-start | bytes 1277960 | tf_op jit(solution)/shard_map/ppermute | solution.py:159
  138.8 1.9 %collective-permute-start.10 = (bf16[4,416,128]{2,1,0:T(8,128)(2,1)S(1)}, bf16[4,416,128]{2,1,0:T(8,128)(2,1)S(1)}, u32[]{:S(2)}, u32[]{:S(2)}) collective-permute-start(bf16[4,416,128]{2,1,0:T(8,128)(2,1)S(1)} %shard_map.71.mid_ref), channel_id=1, source_target_pairs={{0,64},{64,128},{128,192},{192,256},{256,320},{320,384},{384,448},... | collective-permute-start | bytes 1277960 | tf_op jit(solution)/shard_map/ppermute | solution.py:159
  140.8 6.0 %collective-permute-done.11.high_ref = bf16[4,416,128]{2,1,0:T(8,128)(2,1)S(1)} collective-permute-done((bf16[4,416,128]{2,1,0:T(8,128)(2,1)S(1)}, bf16[4,416,128]{2,1,0:T(8,128)(2,1)S(1)}, u32[]{:S(2)}, u32[]{:S(2)}) %collective-permute-start.11) | collective-permute-done | bytes 426016 | tf_op jit(solution)/shard_map/ppermute | solution.py:159
  146.8 5.3 %collective-permute-done.10.low_ref = bf16[4,416,128]{2,1,0:T(8,128)(2,1)S(1)} collective-permute-done((bf16[4,416,128]{2,1,0:T(8,128)(2,1)S(1)}, bf16[4,416,128]{2,1,0:T(8,128)(2,1)S(1)}, u32[]{:S(2)}, u32[]{:S(2)}) %collective-permute-start.10) | collective-permute-done | bytes 426016 | tf_op jit(solution)/shard_map/ppermute | solution.py:159
  152.1 2.2 %shard_map.72 = f32[4864,128]{1,0:T(8,128)} custom-call(s32[12]{0:T(128)S(1)} %and_select_fusion.rel_ref, f32[128,128]{1,0:T(8,128)S(1)} %convert_reduce_fusion.after_ref, bf16[4,416,128]{2,1,0:T(8,128)(2,1)S(1)} %shard_map.71.mid_ref, bf16[4,416,128]{2,1,0:T(8,128)(2,1)S(1)} %collective-permute-done.10.low_ref, ...), custom_call_target="tpu_custom_call" | custom-call | tf_op jit(solution)/shard_map/pallas_call | solution.py:114
  (23 shorter events, 1.0 us)
Async XLA Ops:
  0.6 28.1 %copy-start.3 = (s32[38,2]{0,1:T(2,128)S(1)}, s32[38,2]{0,1:T(2,128)}, u32[]{:S(2)}) copy-start(s32[38,2]{0,1:T(2,128)} %param.6) | copy-start | bytes 916
  21.5 20.7 %copy-start.2 = (f32[128,512]{1,0:T(8,128)S(1)}, f32[128,512]{1,0:T(8,128)}, u32[]{:S(2)}) copy-start(f32[128,512]{1,0:T(8,128)} %g_ref.1) | copy-start | bytes 786436
  21.5 16.1 %all-to-all-start.1 = ((bf16[4,8,128,128]{3,2,1,0:T(8,128)(2,1)}), bf16[4,8,128,128]{3,2,1,0:T(8,128)(2,1)S(1)}, u32[]{:S(2)}, u32[]{:S(2)}) async-start(bf16[4,8,128,128]{3,2,1,0:T(8,128)(2,1)} %broadcast_in_dim.5), calls=%async_computation.1 | async-start | bytes 2097152 | tf_op jit(solution)/shard_map/all_to_all | solution.py:151
  37.7 4.5 %collective-permute-start = (bf16[32,128,128]{2,1,0:T(8,128)(2,1)S(1)}, bf16[32,128,128]{2,1,0:T(8,128)(2,1)S(1)}, u32[]{:S(2)}, u32[]{:S(2)}) collective-permute-start(bf16[32,128,128]{2,1,0:T(8,128)(2,1)S(1)} %bitcast.48), channel_id=1, source_target_pairs={{0,1},{1,0},{2,3},{3,2},{4,5},{5,4},{6,7},{7,6},{8,9},{9,8},{10,11... | collective-permute-start | bytes 3145736 | tf_op jit(solution)/shard_map/ppermute | solution.py:203
  45.8 1.3 copy-start
  47.2 54.6 %all-to-all-start.2 = ((bf16[8,8,128,128]{3,2,1,0:T(8,128)(2,1)}), bf16[8,8,128,128]{3,2,1,0:T(8,128)(2,1)S(1)}, u32[]{:S(2)}, u32[]{:S(2)}) async-start(bf16[8,8,128,128]{3,2,1,0:T(8,128)(2,1)} %bitcast.50), calls=%async_computation.2 | async-start | bytes 4194304 | tf_op jit(solution)/shard_map/all_to_all | solution.py:151
  52.8 30.9 %collective-permute-start.1 = (bf16[3,416,128]{2,1,0:T(8,128)(2,1)S(1)}, bf16[3,416,128]{2,1,0:T(8,128)(2,1)S(1)}, u32[]{:S(2)}, u32[]{:S(2)}) collective-permute-start(bf16[3,416,128]{2,1,0:T(8,128)(2,1)S(1)} %get-tuple-element.15), channel_id=1, source_target_pairs={{0,64},{64,128},{128,192},{192,256},{256,320},{320,384},{384,448},... | collective-permute-start | bytes 958472 | tf_op jit(solution)/shard_map/ppermute | solution.py:159
  57.0 26.6 %collective-permute-start.2 = (bf16[3,416,128]{2,1,0:T(8,128)(2,1)S(1)}, bf16[3,416,128]{2,1,0:T(8,128)(2,1)S(1)}, u32[]{:S(2)}, u32[]{:S(2)}) collective-permute-start(bf16[3,416,128]{2,1,0:T(8,128)(2,1)S(1)} %get-tuple-element.16), channel_id=1, source_target_pairs={{0,704},{64,0},{128,64},{192,128},{256,192},{320,256},{384,320},{4... | collective-permute-start | bytes 958472 | tf_op jit(solution)/shard_map/ppermute | solution.py:159
  69.3 12.2 %collective-permute-start.3 = (bf16[3,208,128]{2,1,0:T(8,128)(2,1)S(1)}, bf16[3,208,128]{2,1,0:T(8,128)(2,1)S(1)}, u32[]{:S(2)}, u32[]{:S(2)}) collective-permute-start(bf16[3,208,128]{2,1,0:T(8,128)(2,1)S(1)} %get-tuple-element.17), channel_id=1, source_target_pairs={{0,128},{64,192},{128,256},{192,320},{256,384},{320,448},{384,512}... | collective-permute-start | bytes 479240 | tf_op jit(solution)/shard_map/ppermute | solution.py:159
  71.2 12.4 %collective-permute-start.4 = (bf16[3,208,128]{2,1,0:T(8,128)(2,1)S(1)}, bf16[3,208,128]{2,1,0:T(8,128)(2,1)S(1)}, u32[]{:S(2)}, u32[]{:S(2)}) collective-permute-start(bf16[3,208,128]{2,1,0:T(8,128)(2,1)S(1)} %get-tuple-element.18), channel_id=1, source_target_pairs={{0,640},{64,704},{128,0},{192,64},{256,128},{320,192},{384,256},{4... | collective-permute-start | bytes 479240 | tf_op jit(solution)/shard_map/ppermute | solution.py:159
  83.8 14.0 %collective-permute-start.5 = (bf16[416,128]{1,0:T(8,128)(2,1)S(1)}, bf16[416,128]{1,0:T(8,128)(2,1)S(1)}, u32[]{:S(2)}, u32[]{:S(2)}) collective-permute-start(bf16[416,128]{1,0:T(8,128)(2,1)S(1)} %get-tuple-element.20), channel_id=1, source_target_pairs={{0,256},{64,320},{128,384},{192,448},{256,512},{320,576},{384,640}... | collective-permute-start | bytes 319496 | tf_op jit(solution)/shard_map/ppermute | solution.py:159
  88.9 12.8 %collective-permute-start.6 = (bf16[416,128]{1,0:T(8,128)(2,1)S(1)}, bf16[416,128]{1,0:T(8,128)(2,1)S(1)}, u32[]{:S(2)}, u32[]{:S(2)}) collective-permute-start(bf16[416,128]{1,0:T(8,128)(2,1)S(1)} %get-tuple-element.21), channel_id=1, source_target_pairs={{0,512},{64,576},{128,640},{192,704},{256,0},{320,64},{384,128},{4... | collective-permute-start | bytes 319496 | tf_op jit(solution)/shard_map/ppermute | solution.py:159
  102.7 38.0 %all-to-all-start.3 = ((bf16[8,128,128]{2,1,0:T(8,128)(2,1)}), bf16[8,128,128]{2,1,0:T(8,128)(2,1)S(1)}, u32[]{:S(2)}, u32[]{:S(2)}) async-start(bf16[8,128,128]{2,1,0:T(8,128)(2,1)} %shard_map.70.after_ref), calls=%async_computation.3 | async-start | bytes 524288 | tf_op jit(solution)/shard_map/all_to_all | solution.py:151
  106.2 19.3 %collective-permute-start.9 = (bf16[416,128]{1,0:T(8,128)(2,1)S(1)}, bf16[416,128]{1,0:T(8,128)(2,1)S(1)}, u32[]{:S(2)}, u32[]{:S(2)}) collective-permute-start(bf16[416,128]{1,0:T(8,128)(2,1)S(1)} %shard_map.69.after_ref.k0_ref), channel_id=1, source_target_pairs={{0,192},{64,256},{128,320},{192,384},{256,448},{320,512},{384,576}... | collective-permute-start | bytes 319496 | tf_op jit(solution)/shard_map/ppermute | solution.py:159
  110.2 20.2 %collective-permute-start.8 = (bf16[416,128]{1,0:T(8,128)(2,1)S(1)}, bf16[416,128]{1,0:T(8,128)(2,1)S(1)}, u32[]{:S(2)}, u32[]{:S(2)}) collective-permute-start(bf16[416,128]{1,0:T(8,128)(2,1)S(1)} %shard_map.69.after_ref.k0_ref), channel_id=1, source_target_pairs={{0,384},{64,448},{128,512},{192,576},{256,640},{320,704},{384,0},{... | collective-permute-start | bytes 319496 | tf_op jit(solution)/shard_map/ppermute | solution.py:159
  119.8 12.8 %collective-permute-start.7 = (bf16[416,128]{1,0:T(8,128)(2,1)S(1)}, bf16[416,128]{1,0:T(8,128)(2,1)S(1)}, u32[]{:S(2)}, u32[]{:S(2)}) collective-permute-start(bf16[416,128]{1,0:T(8,128)(2,1)S(1)} %shard_map.69.after_ref.k0_ref), channel_id=1, source_target_pairs={{0,576},{64,640},{128,704},{192,0},{256,64},{320,128},{384,192},{4... | collective-permute-start | bytes 319496 | tf_op jit(solution)/shard_map/ppermute | solution.py:159
  132.6 14.2 %collective-permute-start.11 = (bf16[4,416,128]{2,1,0:T(8,128)(2,1)S(1)}, bf16[4,416,128]{2,1,0:T(8,128)(2,1)S(1)}, u32[]{:S(2)}, u32[]{:S(2)}) collective-permute-start(bf16[4,416,128]{2,1,0:T(8,128)(2,1)S(1)} %shard_map.71.mid_ref), channel_id=1, source_target_pairs={{0,704},{64,0},{128,64},{192,128},{256,192},{320,256},{384,320},{4... | collective-permute-start | bytes 1277960 | tf_op jit(solution)/shard_map/ppermute | solution.py:159
  138.8 13.4 %collective-permute-start.10 = (bf16[4,416,128]{2,1,0:T(8,128)(2,1)S(1)}, bf16[4,416,128]{2,1,0:T(8,128)(2,1)S(1)}, u32[]{:S(2)}, u32[]{:S(2)}) collective-permute-start(bf16[4,416,128]{2,1,0:T(8,128)(2,1)S(1)} %shard_map.71.mid_ref), channel_id=1, source_target_pairs={{0,64},{64,128},{128,192},{192,256},{256,320},{320,384},{384,448},... | collective-permute-start | bytes 1277960 | tf_op jit(solution)/shard_map/ppermute | solution.py:159
  140.8 13.6 %copy-start.1 = (f32[128,128]{1,0:T(8,128)}, f32[128,128]{1,0:T(8,128)S(1)}, u32[]{:S(2)}) copy-start(f32[128,128]{1,0:T(8,128)S(1)} %convert_reduce_fusion.after_ref) | copy-start | bytes 196612

commit v7 on v4

--- a/solution.py
+++ b/solution.py
@@ -12,7 +12,6 @@
 Y_GROUPS = [[(y * NX + x) * NC + c for y in range(NY)] for x in range(NX) for c in range(NC)]
 X_GROUPS = [[(y * NX + x) * NC + c for x in range(NX)] for y in range(NY) for c in range(NC)]
 CORE_SWAP = [(i, i ^ 1) for i in range(HALF * NC)]
-XC_GROUPS = [[y * NX * NC + k for k in range(NX * NC)] for y in range(NY)]
 CHUNK = 416
 SPLIT = 208
 F32, BF16 = jnp.float32, jnp.bfloat16
@@ -85,18 +84,18 @@
     out_ref[...] = (stay_ref[...].astype(F32) + a_ref[...].astype(F32) + b_ref[...].astype(F32)).astype(BF16)
 
 
-def three_kernel(after_ref, k0_ref, k4_ref, k8_ref, all_ref, low_ref, high_ref):
+def three_kernel(k0_ref, k4_ref, k8_ref, all_ref, low_ref, high_ref):
     for i, part in enumerate((k0_ref, k4_ref, k8_ref)):
         all_ref[i] = part[...]
         low_ref[i] = part[:SPLIT]
         high_ref[i] = part[SPLIT:]
 
 
-def x_sum_kernel(after_ref, in_ref, out_ref):
-    out_ref[...] = jnp.sum(in_ref[...].astype(F32), axis=0).astype(BF16)
-
-
-def whole_kernel(rel_ref, k0_ref, k4_ref, k8_ref, low1_ref, high1_ref, low2_ref, high2_ref, out_ref, gw_ref):
+def sum_kernel(after_ref, in_ref, out_ref):
+    out_ref[...] = jnp.sum(in_ref[...].astype(F32), axis=0)
+
+
+def whole_kernel(rel_ref, after_ref, k0_ref, k4_ref, k8_ref, low1_ref, high1_ref, low2_ref, high2_ref, out_ref, gw_ref):
     gw_ref[0] = k0_ref[...]
     gw_ref[4] = k4_ref[...]
     gw_ref[8] = k8_ref[...]
@@ -157,10 +156,6 @@
     return lax.all_to_all(x, axis, 0, 0, tiled=True, axis_index_groups=groups)
 
 
-def total(x):
-    return jnp.sum(x.astype(F32), axis=0)
-
-
 def shift(x, by):
     return lax.ppermute(x, "dp", [(i, (i + by) % NZ) for i in range(NZ)])
 
@@ -168,21 +163,20 @@
 def reduce_gradients(gx, keep, up1, down1, up2, down2, rel, slots):
     tokens = gx.shape[1]
     one, full, half = array((CHUNK, BS)), array((3, CHUNK, BS)), array((3, SPLIT, BS))
-    gx = swap(gx.reshape(NX * NC, NY, tokens, BS), "mp", XC_GROUPS)
+    gx = swap(gx, "mp", None)
     parts = shift(up1, 1), shift(down1, -1), shift(up2, 2), shift(down2, -2)
     stay, up, down = call(near_kernel, [VMEM] * 5, (keep, *parts), (one,) * 3)
     mine = call(far_kernel, [VMEM] * 3, (stay, shift(up, 4), shift(down, -4)), one)
 
     k8, k4 = shift(mine, 4), shift(mine, -4)
-    gx = call(x_sum_kernel, [ORDER, VMEM], (mine, gx), array((NY, tokens, BS)))
-    three, low, high = call(three_kernel, [ORDER] + [VMEM] * 3, (gx, mine, k4, k8), (full, half, half))
-    grad_x = total(swap(gx, "mp", Y_GROUPS))
+    three, low, high = call(three_kernel, [VMEM] * 3, (mine, k4, k8), (full, half, half))
+    grad_x = call(sum_kernel, [ORDER, VMEM], (three, gx), array((tokens, BS), F32))
 
     low1, high1, low2, high2 = shift(three, 1), shift(three, -1), shift(low, 2), shift(high, -2)
     grad_w = call(
         whole_kernel,
-        [SMEM] + [VMEM] * 7,
-        (rel, mine, k4, k8, low1, high1, low2, high2),
+        [SMEM, ORDER] + [VMEM] * 7,
+        (rel, grad_x, mine, k4, k8, low1, high1, low2, high2),
         array((slots * BS, BS), F32),
         [pltpu.VMEM((NZ, CHUNK, BS), BF16)],
     )
@@ -199,7 +193,6 @@
     core = lax.axis_index("mp") % NC
     at_y, at_x, at_core = row // (NC * NX), (row // NC) % NX, row % NC
     idx = ((at_core ^ core) * NX + at_x) * NY + at_y
-    out_idx = (at_x * NC + at_core) * NY + at_y
     xb = inputs.astype(BF16)
     wb = (block_weights * live[:, None, None]).astype(BF16)
 
@@ -209,7 +202,7 @@
     sib = lax.ppermute(own, "mp", CORE_SWAP)
 
     rel = (jnp.arange(NZ, dtype=jnp.int32) + NZ - lax.axis_index("dp")) % NZ
-    act, gx, *parts = run_blocks(idx, out_idx, col, live, rel, own, sib, wb, grad_act)
+    act, gx, *parts = run_blocks(idx, row, col, live, rel, own, sib, wb, grad_act)
     grad_x, grad_w = reduce_gradients(gx, *parts, rel, slots)
     return act, grad_x, grad_w
 

time: 154 us -> 152 us (0.987)
  starting transfers between devices: 79 us -> 76.2 us
    all_to_all x3 -> x2, starting transfers between devices: 16.2 us -> 13.5 us  [swap(): return lax.all_to_all(x, axis, 0, 0, tiled=True, axis_index_groups=groups)]
    all_to_all x3 -> x2, waiting for transfers between devices: 8.92 us -> 8.93 us  [swap(): return lax.all_to_all(x, axis, 0, 0, tiled=True, axis_index_groups=groups)]
  transfers between devices with their start and end apart: 16 -> 15, of which waited for: 9 -> 10; matrix products, arithmetic and copies ran while one was open for 1% -> 1% of each run, Pallas kernels for 2% -> 1%
where the time goes in v7:
time: 152 us; the launch traced here: 151 us
  starting transfers between devices  76.2 us (50%)
  waiting for transfers between devices  40.4 us (27%)
  blocking collectives  18.8 us (12%)
  Pallas kernels  8.25 us (5%)
  local copies, waits for them, and re-layouts  3.41 us (2%)
  other arithmetic  2.86 us (2%)
    ppermute x12, starting transfers between devices, shift(): return lax.ppermute(x, 'dp', [(i, (i + by) % NZ) for i in range(NZ)])  60.8 us
    ppermute x12, waiting for transfers between devices, shift(): return lax.ppermute(x, 'dp', [(i, (i + by) % NZ) for i in range(NZ)])  30.9 us
    all_to_all x1, blocking collectives, swap(): return lax.all_to_all(x, axis, 0, 0, tiled=True, axis_index_groups=groups)  18.8 us
    all_to_all x2, starting transfers between devices, swap(): return lax.all_to_all(x, axis, 0, 0, tiled=True, axis_index_groups=groups)  13.5 us
    all_to_all x2, waiting for transfers between devices, swap(): return lax.all_to_all(x, axis, 0, 0, tiled=True, axis_index_groups=groups)  8.93 us
    pallas_call x6, Pallas kernels, call(): pl.pallas_call(kernel, out_shape=outs, in_specs=specs, out_specs=jax.tree...  8.25 us
  transfers between devices with their start and end apart: 15, of which 10 were waited for; matrix products, arithmetic and copies ran while one was open for 1% of the time, Pallas kernels for 1%

profile of v7, /device:TPU:6, one launch (start us, length us, event | category | flops | bytes accessed | tf_op | source)
XLA Modules:
  0.0 150.7 jit_solution(1578876563026474810)
XLA Ops:
  0.6 0.9 convert_element_type.13
  1.5 18.8 %all_to_all.15 = bf16[8,128,128]{2,1,0:T(8,128)(2,1)S(1)} all-to-all(bf16[8,128,128]{2,1,0:T(8,128)(2,1)S(1)} %broadcast_in_dim.4), channel_id=1, replica_groups={{0,8,16,24,32,40,48,56},{1,9,17,25,33,41,49,57},{2,10,18,26,34,42,50,58..., dimensions={0} | all-to-all | bytes 524288 | tf_op jit(solution)/shard_map/all_to_all | solution.py:156
  20.3 1.2 broadcast_in_dim.5
  21.5 7.2 %all-to-all-start.1 = ((bf16[4,8,128,128]{3,2,1,0:T(8,128)(2,1)}), bf16[4,8,128,128]{3,2,1,0:T(8,128)(2,1)S(1)}, u32[]{:S(2)}, u32[]{:S(2)}) async-start(bf16[4,8,128,128]{3,2,1,0:T(8,128)(2,1)} %broadcast_in_dim.5), calls=%async_computation.1 | async-start | bytes 2097152 | tf_op jit(solution)/shard_map/all_to_all | solution.py:156
  28.7 8.9 %all-to-all-done.1 = bf16[4,8,128,128]{3,2,1,0:T(8,128)(2,1)S(1)} async-done(((bf16[4,8,128,128]{3,2,1,0:T(8,128)(2,1)}), bf16[4,8,128,128]{3,2,1,0:T(8,128)(2,1)S(1)}, u32[]{:S(2)}, u32[]{:S(2)}) %all-to-all-start.1) | async-done | bytes 1048608 | tf_op jit(solution)/shard_map/all_to_all | solution.py:156
  37.7 1.9 %collective-permute-start = (bf16[32,128,128]{2,1,0:T(8,128)(2,1)S(1)}, bf16[32,128,128]{2,1,0:T(8,128)(2,1)S(1)}, u32[]{:S(2)}, u32[]{:S(2)}) collective-permute-start(bf16[32,128,128]{2,1,0:T(8,128)(2,1)S(1)} %bitcast.10), channel_id=1, source_target_pairs={{0,1},{1,0},{2,3},{3,2},{4,5},{5,4},{6,7},{7,6},{8,9},{9,8},{10,11... | collective-permute-start | bytes 3145736 | tf_op jit(solution)/shard_map/ppermute | solution.py:202
  39.7 2.0 %multiply_convert_fusion.w_ref = bf16[38,128,128]{2,1,0:T(8,128)(2,1)S(1)} fusion(f32[38,128,128]{2,1,0:T(8,128)} %param.5, f32[38]{0:T(128)S(1)} %fusion.3.live_ref), kind=kLoop, calls=%fused_computation | loop fusion | flops 1245184 | bytes 3735704 | tf_op jit(solution)/shard_map/convert_element_type | solution.py:197
  42.2 3.7 %shard_map.67 = (f32[128,512]{1,0:T(8,128)}, bf16[64,128,128]{2,1,0:T(8,128)(2,1)S(1)}, bf16[3,416,128]{2,1,0:T(8,128)(2,1)S(1)}, bf16[3,416,128]{2,1,0:T(8,128)...) custom-call(s32[38]{0:T(128)S(1)} %fusion.5.idx_ref, ...), custom_call_target="tpu_custom_call" | custom-call | tf_op jit(solution)/shard_map/pallas_call | solution.py:119
  45.9 1.3 copy-done
  47.2 6.3 %all-to-all-start.2 = ((bf16[64,128,128]{2,1,0:T(8,128)(2,1)}), bf16[64,128,128]{2,1,0:T(8,128)(2,1)S(1)}, u32[]{:S(2)}, u32[]{:S(2)}) async-start(bf16[64,128,128]{2,1,0:T(8,128)(2,1)} %copy-done), calls=%async_computation.2 | async-start | bytes 4194304 | tf_op jit(solution)/shard_map/all_to_all | solution.py:156
  53.5 4.3 %collective-permute-start.1 = (bf16[3,416,128]{2,1,0:T(8,128)(2,1)S(1)}, bf16[3,416,128]{2,1,0:T(8,128)(2,1)S(1)}, u32[]{:S(2)}, u32[]{:S(2)}) collective-permute-start(bf16[3,416,128]{2,1,0:T(8,128)(2,1)S(1)} %get-tuple-element.18), channel_id=1, source_target_pairs={{0,64},{64,128},{128,192},{192,256},{256,320},{320,384},{384,448},... | collective-permute-start | bytes 958472 | tf_op jit(solution)/shard_map/ppermute | solution.py:160
  57.8 12.2 %collective-permute-start.2 = (bf16[3,416,128]{2,1,0:T(8,128)(2,1)S(1)}, bf16[3,416,128]{2,1,0:T(8,128)(2,1)S(1)}, u32[]{:S(2)}, u32[]{:S(2)}) collective-permute-start(bf16[3,416,128]{2,1,0:T(8,128)(2,1)S(1)} %get-tuple-element.19), channel_id=1, source_target_pairs={{0,704},{64,0},{128,64},{192,128},{256,192},{320,256},{384,320},{4... | collective-permute-start | bytes 958472 | tf_op jit(solution)/shard_map/ppermute | solution.py:160
  70.0 1.9 %collective-permute-start.3 = (bf16[3,208,128]{2,1,0:T(8,128)(2,1)S(1)}, bf16[3,208,128]{2,1,0:T(8,128)(2,1)S(1)}, u32[]{:S(2)}, u32[]{:S(2)}) collective-permute-start(bf16[3,208,128]{2,1,0:T(8,128)(2,1)S(1)} %get-tuple-element.20), channel_id=1, source_target_pairs={{0,128},{64,192},{128,256},{192,320},{256,384},{320,448},{384,512}... | collective-permute-start | bytes 479240 | tf_op jit(solution)/shard_map/ppermute | solution.py:160
  71.9 6.0 %collective-permute-start.4 = (bf16[3,208,128]{2,1,0:T(8,128)(2,1)S(1)}, bf16[3,208,128]{2,1,0:T(8,128)(2,1)S(1)}, u32[]{:S(2)}, u32[]{:S(2)}) collective-permute-start(bf16[3,208,128]{2,1,0:T(8,128)(2,1)S(1)} %get-tuple-element.21), channel_id=1, source_target_pairs={{0,640},{64,704},{128,0},{192,64},{256,128},{320,192},{384,256},{4... | collective-permute-start | bytes 479240 | tf_op jit(solution)/shard_map/ppermute | solution.py:160
  78.0 4.3 %collective-permute-done.3.c_ref = bf16[3,208,128]{2,1,0:T(8,128)(2,1)S(1)} collective-permute-done((bf16[3,208,128]{2,1,0:T(8,128)(2,1)S(1)}, bf16[3,208,128]{2,1,0:T(8,128)(2,1)S(1)}, u32[]{:S(2)}, u32[]{:S(2)}) %collective-permute-start.3) | collective-permute-done | bytes 159776 | tf_op jit(solution)/shard_map/ppermute | solution.py:160
  82.2 2.1 %collective-permute-done.4.d_ref = bf16[3,208,128]{2,1,0:T(8,128)(2,1)S(1)} collective-permute-done((bf16[3,208,128]{2,1,0:T(8,128)(2,1)S(1)}, bf16[3,208,128]{2,1,0:T(8,128)(2,1)S(1)}, u32[]{:S(2)}, u32[]{:S(2)}) %collective-permute-start.4) | collective-permute-done | bytes 159776 | tf_op jit(solution)/shard_map/ppermute | solution.py:160
  84.5 5.1 %collective-permute-start.5 = (bf16[416,128]{1,0:T(8,128)(2,1)S(1)}, bf16[416,128]{1,0:T(8,128)(2,1)S(1)}, u32[]{:S(2)}, u32[]{:S(2)}) collective-permute-start(bf16[416,128]{1,0:T(8,128)(2,1)S(1)} %get-tuple-element.23), channel_id=1, source_target_pairs={{0,256},{64,320},{128,384},{192,448},{256,512},{320,576},{384,640}... | collective-permute-start | bytes 319496 | tf_op jit(solution)/shard_map/ppermute | solution.py:160
  89.6 4.7 %collective-permute-start.6 = (bf16[416,128]{1,0:T(8,128)(2,1)S(1)}, bf16[416,128]{1,0:T(8,128)(2,1)S(1)}, u32[]{:S(2)}, u32[]{:S(2)}) collective-permute-start(bf16[416,128]{1,0:T(8,128)(2,1)S(1)} %get-tuple-element.24), channel_id=1, source_target_pairs={{0,512},{64,576},{128,640},{192,704},{256,0},{320,64},{384,128},{4... | collective-permute-start | bytes 319496 | tf_op jit(solution)/shard_map/ppermute | solution.py:160
  94.3 4.2 %collective-permute-done.5.a_ref = bf16[416,128]{1,0:T(8,128)(2,1)S(1)} collective-permute-done((bf16[416,128]{1,0:T(8,128)(2,1)S(1)}, bf16[416,128]{1,0:T(8,128)(2,1)S(1)}, u32[]{:S(2)}, u32[]{:S(2)}) %collective-permute-start.5) | collective-permute-done | bytes 106528 | tf_op jit(solution)/shard_map/ppermute | solution.py:160
  98.5 3.9 %collective-permute-done.6.b_ref = bf16[416,128]{1,0:T(8,128)(2,1)S(1)} collective-permute-done((bf16[416,128]{1,0:T(8,128)(2,1)S(1)}, bf16[416,128]{1,0:T(8,128)(2,1)S(1)}, u32[]{:S(2)}, u32[]{:S(2)}) %collective-permute-start.6) | collective-permute-done | bytes 106528 | tf_op jit(solution)/shard_map/ppermute | solution.py:160
  102.5 6.4 %collective-permute-start.8 = (bf16[416,128]{1,0:T(8,128)(2,1)S(1)}, bf16[416,128]{1,0:T(8,128)(2,1)S(1)}, u32[]{:S(2)}, u32[]{:S(2)}) collective-permute-start(bf16[416,128]{1,0:T(8,128)(2,1)S(1)} %shard_map.69.k0_ref), channel_id=1, source_target_pairs={{0,256},{64,320},{128,384},{192,448},{256,512},{320,576},{384,640}... | collective-permute-start | bytes 319496 | tf_op jit(solution)/shard_map/ppermute | solution.py:160
  108.9 3.3 %collective-permute-start.7 = (bf16[416,128]{1,0:T(8,128)(2,1)S(1)}, bf16[416,128]{1,0:T(8,128)(2,1)S(1)}, u32[]{:S(2)}, u32[]{:S(2)}) collective-permute-start(bf16[416,128]{1,0:T(8,128)(2,1)S(1)} %shard_map.69.k0_ref), channel_id=1, source_target_pairs={{0,512},{64,576},{128,640},{192,704},{256,0},{320,64},{384,128},{4... | collective-permute-start | bytes 319496 | tf_op jit(solution)/shard_map/ppermute | solution.py:160
  112.2 0.9 collective-permute-done.8.k8_ref
  113.2 7.0 %collective-permute-done.7.k4_ref = bf16[416,128]{1,0:T(8,128)(2,1)S(1)} collective-permute-done((bf16[416,128]{1,0:T(8,128)(2,1)S(1)}, bf16[416,128]{1,0:T(8,128)(2,1)S(1)}, u32[]{:S(2)}, u32[]{:S(2)}) %collective-permute-start.7) | collective-permute-done | bytes 106528 | tf_op jit(solution)/shard_map/ppermute | solution.py:160
  121.0 5.0 %collective-permute-start.10 = (bf16[3,416,128]{2,1,0:T(8,128)(2,1)S(1)}, bf16[3,416,128]{2,1,0:T(8,128)(2,1)S(1)}, u32[]{:S(2)}, u32[]{:S(2)}) collective-permute-start(bf16[3,416,128]{2,1,0:T(8,128)(2,1)S(1)} %get-tuple-element.25.after_ref), channel_id=1, source_target_pairs={{0,704},{64,0},{128,64},{192,128},{256,192},{320,256},{384,320},{4... | collective-permute-start | bytes 958472 | tf_op jit(solution)/shard_map/ppermute | solution.py:160
  126.0 1.9 %collective-permute-start.9 = (bf16[3,416,128]{2,1,0:T(8,128)(2,1)S(1)}, bf16[3,416,128]{2,1,0:T(8,128)(2,1)S(1)}, u32[]{:S(2)}, u32[]{:S(2)}) collective-permute-start(bf16[3,416,128]{2,1,0:T(8,128)(2,1)S(1)} %get-tuple-element.25.after_ref), channel_id=1, source_target_pairs={{0,64},{64,128},{128,192},{192,256},{256,320},{320,384},{384,448},... | collective-permute-start | bytes 958472 | tf_op jit(solution)/shard_map/ppermute | solution.py:160
  128.0 8.0 %collective-permute-start.11 = (bf16[3,208,128]{2,1,0:T(8,128)(2,1)}, bf16[3,208,128]{2,1,0:T(8,128)(2,1)S(1)}, u32[]{:S(2)}, u32[]{:S(2)}) collective-permute-start(bf16[3,208,128]{2,1,0:T(8,128)(2,1)} %get-tuple-element.27), channel_id=1, source_target_pairs={{0,128},{64,192},{128,256},{192,320},{256,384},{320,448},{384,512}... | collective-permute-start | bytes 479240 | tf_op jit(solution)/shard_map/ppermute | solution.py:160
  135.9 1.9 %collective-permute-start.12 = (bf16[3,208,128]{2,1,0:T(8,128)(2,1)}, bf16[3,208,128]{2,1,0:T(8,128)(2,1)}, u32[]{:S(2)}, u32[]{:S(2)}) collective-permute-start(bf16[3,208,128]{2,1,0:T(8,128)(2,1)} %get-tuple-element.28), channel_id=1, source_target_pairs={{0,640},{64,704},{128,0},{192,64},{256,128},{320,192},{384,256},{4... | collective-permute-start | bytes 479240 | tf_op jit(solution)/shard_map/ppermute | solution.py:160
  137.9 0.9 shard_map.71.after_ref
  138.8 7.6 %collective-permute-done.11.low2_ref = bf16[3,208,128]{2,1,0:T(8,128)(2,1)S(1)} collective-permute-done((bf16[3,208,128]{2,1,0:T(8,128)(2,1)}, bf16[3,208,128]{2,1,0:T(8,128)(2,1)S(1)}, u32[]{:S(2)}, u32[]{:S(2)}) %collective-permute-start.11) | collective-permute-done | bytes 159776 | tf_op jit(solution)/shard_map/ppermute | solution.py:160
  147.3 0.8 copy-done.1
  148.1 2.6 %shard_map.72 = f32[4864,128]{1,0:T(8,128)} custom-call(s32[12]{0:T(128)S(1)} %and_select_fusion.rel_ref, f32[128,128]{1,0:T(8,128)S(1)} %copy-done.1, bf16[416,128]{1,0:T(8,128)(2,1)S(1)} %shard_map.69.k0_ref, bf16[416,128]{1,0:T(8,128)(2,1)S(1)} %collective-permute-done.7.k4_ref, bf16[416,128]{1,0:T(8,128)(2,1)S(1)} %collective-permute-done.8.k8_ref, ...), custom_call_target="tpu_custom_call" | custom-call | tf_op jit(solution)/shard_map/pallas_call | solution.py:119
  (21 shorter events, 2.5 us)
Async XLA Ops:
  0.6 39.0 %copy-start.3 = (s32[38,2]{0,1:T(2,128)S(1)}, s32[38,2]{0,1:T(2,128)}, u32[]{:S(2)}) copy-start(s32[38,2]{0,1:T(2,128)} %param.6) | copy-start | bytes 916
  21.5 20.7 %copy-start.2 = (f32[128,512]{1,0:T(8,128)S(1)}, f32[128,512]{1,0:T(8,128)}, u32[]{:S(2)}) copy-start(f32[128,512]{1,0:T(8,128)} %g_ref.1) | copy-start | bytes 786436
  21.5 16.1 %all-to-all-start.1 = ((bf16[4,8,128,128]{3,2,1,0:T(8,128)(2,1)}), bf16[4,8,128,128]{3,2,1,0:T(8,128)(2,1)S(1)}, u32[]{:S(2)}, u32[]{:S(2)}) async-start(bf16[4,8,128,128]{3,2,1,0:T(8,128)(2,1)} %broadcast_in_dim.5), calls=%async_computation.1 | async-start | bytes 2097152 | tf_op jit(solution)/shard_map/all_to_all | solution.py:156
  37.7 4.5 %collective-permute-start = (bf16[32,128,128]{2,1,0:T(8,128)(2,1)S(1)}, bf16[32,128,128]{2,1,0:T(8,128)(2,1)S(1)}, u32[]{:S(2)}, u32[]{:S(2)}) collective-permute-start(bf16[32,128,128]{2,1,0:T(8,128)(2,1)S(1)} %bitcast.10), channel_id=1, source_target_pairs={{0,1},{1,0},{2,3},{3,2},{4,5},{5,4},{6,7},{7,6},{8,9},{9,8},{10,11... | collective-permute-start | bytes 3145736 | tf_op jit(solution)/shard_map/ppermute | solution.py:202
  45.9 1.3 copy-start
  47.2 90.7 %all-to-all-start.2 = ((bf16[64,128,128]{2,1,0:T(8,128)(2,1)}), bf16[64,128,128]{2,1,0:T(8,128)(2,1)S(1)}, u32[]{:S(2)}, u32[]{:S(2)}) async-start(bf16[64,128,128]{2,1,0:T(8,128)(2,1)} %copy-done), calls=%async_computation.2 | async-start | bytes 4194304 | tf_op jit(solution)/shard_map/all_to_all | solution.py:156
  53.5 30.9 %collective-permute-start.1 = (bf16[3,416,128]{2,1,0:T(8,128)(2,1)S(1)}, bf16[3,416,128]{2,1,0:T(8,128)(2,1)S(1)}, u32[]{:S(2)}, u32[]{:S(2)}) collective-permute-start(bf16[3,416,128]{2,1,0:T(8,128)(2,1)S(1)} %get-tuple-element.18), channel_id=1, source_target_pairs={{0,64},{64,128},{128,192},{192,256},{256,320},{320,384},{384,448},... | collective-permute-start | bytes 958472 | tf_op jit(solution)/shard_map/ppermute | solution.py:160
  57.8 26.6 %collective-permute-start.2 = (bf16[3,416,128]{2,1,0:T(8,128)(2,1)S(1)}, bf16[3,416,128]{2,1,0:T(8,128)(2,1)S(1)}, u32[]{:S(2)}, u32[]{:S(2)}) collective-permute-start(bf16[3,416,128]{2,1,0:T(8,128)(2,1)S(1)} %get-tuple-element.19), channel_id=1, source_target_pairs={{0,704},{64,0},{128,64},{192,128},{256,192},{320,256},{384,320},{4... | collective-permute-start | bytes 958472 | tf_op jit(solution)/shard_map/ppermute | solution.py:160
  70.0 12.2 %collective-permute-start.3 = (bf16[3,208,128]{2,1,0:T(8,128)(2,1)S(1)}, bf16[3,208,128]{2,1,0:T(8,128)(2,1)S(1)}, u32[]{:S(2)}, u32[]{:S(2)}) collective-permute-start(bf16[3,208,128]{2,1,0:T(8,128)(2,1)S(1)} %get-tuple-element.20), channel_id=1, source_target_pairs={{0,128},{64,192},{128,256},{192,320},{256,384},{320,448},{384,512}... | collective-permute-start | bytes 479240 | tf_op jit(solution)/shard_map/ppermute | solution.py:160
  71.9 12.4 %collective-permute-start.4 = (bf16[3,208,128]{2,1,0:T(8,128)(2,1)S(1)}, bf16[3,208,128]{2,1,0:T(8,128)(2,1)S(1)}, u32[]{:S(2)}, u32[]{:S(2)}) collective-permute-start(bf16[3,208,128]{2,1,0:T(8,128)(2,1)S(1)} %get-tuple-element.21), channel_id=1, source_target_pairs={{0,640},{64,704},{128,0},{192,64},{256,128},{320,192},{384,256},{4... | collective-permute-start | bytes 479240 | tf_op jit(solution)/shard_map/ppermute | solution.py:160
  84.5 14.0 %collective-permute-start.5 = (bf16[416,128]{1,0:T(8,128)(2,1)S(1)}, bf16[416,128]{1,0:T(8,128)(2,1)S(1)}, u32[]{:S(2)}, u32[]{:S(2)}) collective-permute-start(bf16[416,128]{1,0:T(8,128)(2,1)S(1)} %get-tuple-element.23), channel_id=1, source_target_pairs={{0,256},{64,320},{128,384},{192,448},{256,512},{320,576},{384,640}... | collective-permute-start | bytes 319496 | tf_op jit(solution)/shard_map/ppermute | solution.py:160
  89.6 12.8 %collective-permute-start.6 = (bf16[416,128]{1,0:T(8,128)(2,1)S(1)}, bf16[416,128]{1,0:T(8,128)(2,1)S(1)}, u32[]{:S(2)}, u32[]{:S(2)}) collective-permute-start(bf16[416,128]{1,0:T(8,128)(2,1)S(1)} %get-tuple-element.24), channel_id=1, source_target_pairs={{0,512},{64,576},{128,640},{192,704},{256,0},{320,64},{384,128},{4... | collective-permute-start | bytes 319496 | tf_op jit(solution)/shard_map/ppermute | solution.py:160
  102.5 10.7 %collective-permute-start.8 = (bf16[416,128]{1,0:T(8,128)(2,1)S(1)}, bf16[416,128]{1,0:T(8,128)(2,1)S(1)}, u32[]{:S(2)}, u32[]{:S(2)}) collective-permute-start(bf16[416,128]{1,0:T(8,128)(2,1)S(1)} %shard_map.69.k0_ref), channel_id=1, source_target_pairs={{0,256},{64,320},{128,384},{192,448},{256,512},{320,576},{384,640}... | collective-permute-start | bytes 319496 | tf_op jit(solution)/shard_map/ppermute | solution.py:160
  108.9 11.3 %collective-permute-start.7 = (bf16[416,128]{1,0:T(8,128)(2,1)S(1)}, bf16[416,128]{1,0:T(8,128)(2,1)S(1)}, u32[]{:S(2)}, u32[]{:S(2)}) collective-permute-start(bf16[416,128]{1,0:T(8,128)(2,1)S(1)} %shard_map.69.k0_ref), channel_id=1, source_target_pairs={{0,512},{64,576},{128,640},{192,704},{256,0},{320,64},{384,128},{4... | collective-permute-start | bytes 319496 | tf_op jit(solution)/shard_map/ppermute | solution.py:160
  121.0 26.2 %collective-permute-start.10 = (bf16[3,416,128]{2,1,0:T(8,128)(2,1)S(1)}, bf16[3,416,128]{2,1,0:T(8,128)(2,1)S(1)}, u32[]{:S(2)}, u32[]{:S(2)}) collective-permute-start(bf16[3,416,128]{2,1,0:T(8,128)(2,1)S(1)} %get-tuple-element.25.after_ref), channel_id=1, source_target_pairs={{0,704},{64,0},{128,64},{192,128},{256,192},{320,256},{384,320},{4... | collective-permute-start | bytes 958472 | tf_op jit(solution)/shard_map/ppermute | solution.py:160
  126.0 21.2 %collective-permute-start.9 = (bf16[3,416,128]{2,1,0:T(8,128)(2,1)S(1)}, bf16[3,416,128]{2,1,0:T(8,128)(2,1)S(1)}, u32[]{:S(2)}, u32[]{:S(2)}) collective-permute-start(bf16[3,416,128]{2,1,0:T(8,128)(2,1)S(1)} %get-tuple-element.25.after_ref), channel_id=1, source_target_pairs={{0,64},{64,128},{128,192},{192,256},{256,320},{320,384},{384,448},... | collective-permute-start | bytes 958472 | tf_op jit(solution)/shard_map/ppermute | solution.py:160
  128.0 18.5 %collective-permute-start.11 = (bf16[3,208,128]{2,1,0:T(8,128)(2,1)}, bf16[3,208,128]{2,1,0:T(8,128)(2,1)S(1)}, u32[]{:S(2)}, u32[]{:S(2)}) collective-permute-start(bf16[3,208,128]{2,1,0:T(8,128)(2,1)} %get-tuple-element.27), channel_id=1, source_target_pairs={{0,128},{64,192},{128,256},{192,320},{256,384},{320,448},{384,512}... | collective-permute-start | bytes 479240 | tf_op jit(solution)/shard_map/ppermute | solution.py:160
  135.9 11.3 %collective-permute-start.12 = (bf16[3,208,128]{2,1,0:T(8,128)(2,1)}, bf16[3,208,128]{2,1,0:T(8,128)(2,1)}, u32[]{:S(2)}, u32[]{:S(2)}) collective-permute-start(bf16[3,208,128]{2,1,0:T(8,128)(2,1)} %get-tuple-element.28), channel_id=1, source_target_pairs={{0,640},{64,704},{128,0},{192,64},{256,128},{320,192},{384,256},{4... | collective-permute-start | bytes 479240 | tf_op jit(solution)/shard_map/ppermute | solution.py:160
  147.3 0.8 copy-start.1

commit v8 on v7

--- a/solution.py
+++ b/solution.py
@@ -13,7 +13,7 @@
 X_GROUPS = [[(y * NX + x) * NC + c for x in range(NX)] for y in range(NY) for c in range(NC)]
 CORE_SWAP = [(i, i ^ 1) for i in range(HALF * NC)]
 CHUNK = 416
-SPLIT = 208
+Z_FAR = [[3 * i + r for i in range(4)] for r in range(3)]
 F32, BF16 = jnp.float32, jnp.bfloat16
 
 
@@ -32,7 +32,7 @@
 
 
 def block_kernel(idx_ref, out_idx_ref, col_ref, live_ref, rel_ref, own_ref, sib_ref, w_ref, g_ref,
-                 act_ref, gx_out_ref, keep_ref, up1_ref, down1_ref, up2_ref, down2_ref,
+                 act_ref, gx_out_ref, keep_ref, up1_ref, down1_ref, up2_ref,
                  x_ref, prod_ref, pre_ref, dpre_ref, gx_ref, gw_ref):
     slots = w_ref.shape[0]
     col_blocks = pre_ref.shape[0]
@@ -63,8 +63,7 @@
         keep_ref[i] = gw_ref[4 * i]
         up1_ref[i] = gw_ref[4 * i + 1]
         down1_ref[i] = gw_ref[(4 * i + 11) % NZ]
-        up2_ref[i] = gw_ref[4 * i + 2, :SPLIT]
-        down2_ref[i] = gw_ref[(4 * i + 10) % NZ, SPLIT:]
+        up2_ref[i] = gw_ref[4 * i + 2]
     gx_ref[...] = jnp.zeros_like(gx_ref)
     for s in range(slots):
         prod_ref[s] = dot(dpre_ref[col_ref[s]], w_ref[s], ((1,), (1,)))
@@ -73,41 +72,28 @@
     gx_out_ref[...] = gx_ref[...].astype(BF16)
 
 
-def near_kernel(keep_ref, a_ref, b_ref, c_ref, d_ref, stay_ref, up_ref, down_ref):
+def near_kernel(keep_ref, a_ref, b_ref, c_ref, stay_ref, up_ref, down_ref):
     for i, out in enumerate((stay_ref, up_ref, down_ref)):
         part = keep_ref[i].astype(F32) + a_ref[i].astype(F32) + b_ref[i].astype(F32)
-        out[:SPLIT] = (part[:SPLIT] + c_ref[i].astype(F32)).astype(BF16)
-        out[SPLIT:] = (part[SPLIT:] + d_ref[i].astype(F32)).astype(BF16)
+        out[...] = (part + c_ref[i].astype(F32)).astype(BF16)
 
 
 def far_kernel(stay_ref, a_ref, b_ref, out_ref):
     out_ref[...] = (stay_ref[...].astype(F32) + a_ref[...].astype(F32) + b_ref[...].astype(F32)).astype(BF16)
 
 
-def three_kernel(k0_ref, k4_ref, k8_ref, all_ref, low_ref, high_ref):
-    for i, part in enumerate((k0_ref, k4_ref, k8_ref)):
-        all_ref[i] = part[...]
-        low_ref[i] = part[:SPLIT]
-        high_ref[i] = part[SPLIT:]
-
-
 def sum_kernel(after_ref, in_ref, out_ref):
     out_ref[...] = jnp.sum(in_ref[...].astype(F32), axis=0)
 
 
-def whole_kernel(rel_ref, after_ref, k0_ref, k4_ref, k8_ref, low1_ref, high1_ref, low2_ref, high2_ref, out_ref, gw_ref):
-    gw_ref[0] = k0_ref[...]
-    gw_ref[4] = k4_ref[...]
-    gw_ref[8] = k8_ref[...]
-    for i in range(3):
-        gw_ref[(4 * i + 11) % NZ] = low1_ref[i]
-        gw_ref[4 * i + 1] = high1_ref[i]
-        gw_ref[(4 * i + 10) % NZ, :SPLIT] = low2_ref[i]
-        gw_ref[4 * i + 2, SPLIT:] = high2_ref[i]
+def whole_kernel(place_ref, after_ref, low_ref, mid_ref, high_ref, out_ref, gw_ref):
+    for i, part in enumerate((low_ref, mid_ref, high_ref)):
+        for b in range(4):
+            gw_ref[3 * b + place_ref[i]] = part[b]
     rows = out_ref.shape[0]
     for j in range(NZ):
         size = min(CHUNK, rows - j * CHUNK)
-        out_ref[j * CHUNK:j * CHUNK + size] = gw_ref[rel_ref[j], :size].astype(F32)
+        out_ref[j * CHUNK:j * CHUNK + size] = gw_ref[j, :size].astype(F32)
 
 
 SMEM = pl.BlockSpec(memory_space=pltpu.SMEM)
@@ -135,12 +121,12 @@
     slots = wb.shape[0]
     tokens, hidden = grad_act.shape
     cols = hidden // BS
-    full, half = array((3, CHUNK, BS)), array((3, SPLIT, BS))
+    full = array((3, CHUNK, BS))
     return call(
         block_kernel,
         [SMEM] * 5 + [VMEM] * 4,
         (idx, out_idx, col, live, rel, own, sib, wb, grad_act),
-        (array((tokens, hidden), F32), array((2 * HALF, tokens, BS)), full, full, full, half, half),
+        (array((tokens, hidden), F32), array((2 * HALF, tokens, BS)), full, full, full, full),
         [
             pltpu.VMEM((2 * HALF, tokens, BS), BF16),
             pltpu.VMEM((slots, tokens, BS), F32),
@@ -160,23 +146,22 @@
     return lax.ppermute(x, "dp", [(i, (i + by) % NZ) for i in range(NZ)])
 
 
-def reduce_gradients(gx, keep, up1, down1, up2, down2, rel, slots):
+def reduce_gradients(gx, keep, up1, down1, up2, slots):
     tokens = gx.shape[1]
-    one, full, half = array((CHUNK, BS)), array((3, CHUNK, BS)), array((3, SPLIT, BS))
+    one = array((CHUNK, BS))
     gx = swap(gx, "mp", None)
-    parts = shift(up1, 1), shift(down1, -1), shift(up2, 2), shift(down2, -2)
-    stay, up, down = call(near_kernel, [VMEM] * 5, (keep, *parts), (one,) * 3)
+    parts = shift(up1, 1), shift(down1, -1), shift(up2, 2)
+    stay, up, down = call(near_kernel, [VMEM] * 4, (keep, *parts), (one,) * 3)
     mine = call(far_kernel, [VMEM] * 3, (stay, shift(up, 4), shift(down, -4)), one)
 
-    k8, k4 = shift(mine, 4), shift(mine, -4)
-    three, low, high = call(three_kernel, [VMEM] * 3, (mine, k4, k8), (full, half, half))
-    grad_x = call(sum_kernel, [ORDER, VMEM], (three, gx), array((tokens, BS), F32))
-
-    low1, high1, low2, high2 = shift(three, 1), shift(three, -1), shift(low, 2), shift(high, -2)
+    mid = lax.all_gather(mine, "dp", axis_index_groups=Z_FAR)
+    grad_x = call(sum_kernel, [ORDER, VMEM], (mid, gx), array((tokens, BS), F32))
+    low, high = shift(mid, 1), shift(mid, -1)
+    place = (jnp.arange(3, dtype=jnp.int32) + lax.axis_index("dp") + 2) % 3
     grad_w = call(
         whole_kernel,
-        [SMEM, ORDER] + [VMEM] * 7,
-        (rel, grad_x, mine, k4, k8, low1, high1, low2, high2),
+        [SMEM, ORDER] + [VMEM] * 3,
+        (place, grad_x, low, mid, high),
         array((slots * BS, BS), F32),
         [pltpu.VMEM((NZ, CHUNK, BS), BF16)],
     )
@@ -203,7 +188,7 @@
 
     rel = (jnp.arange(NZ, dtype=jnp.int32) + NZ - lax.axis_index("dp")) % NZ
     act, gx, *parts = run_blocks(idx, row, col, live, rel, own, sib, wb, grad_act)
-    grad_x, grad_w = reduce_gradients(gx, *parts, rel, slots)
+    grad_x, grad_w = reduce_gradients(gx, *parts, slots)
     return act, grad_x, grad_w
 
 

time: 152 us -> 146 us (0.961)
  starting transfers between devices: 76.2 us -> 49.4 us
  blocking collectives: 18.8 us -> 38.3 us
  waiting for transfers between devices: 40.4 us -> 43.5 us
    ppermute x12 -> x7, starting transfers between devices: 60.8 us -> 34 us  [shift(): return lax.ppermute(x, 'dp', [(i, (i + by) % NZ) for i in range(NZ)])]
    all_gather x0 -> x1, blocking collectives: none -> 19.5 us  [reduce_gradients(): mid = lax.all_gather(mine, 'dp', axis_index_groups=Z_FAR)]
    ppermute x12 -> x7, waiting for transfers between devices: 30.9 us -> 34 us  [shift(): return lax.ppermute(x, 'dp', [(i, (i + by) % NZ) for i in range(NZ)])]
    pallas_call x6 -> x5, Pallas kernels: 8.25 us -> 7.01 us  [call(): pl.pallas_call(kernel, out_shape=outs, in_specs=specs, out_specs=jax.tree...]
  transfers between devices with their start and end apart: 15 -> 10, of which waited for: 10 -> 9; matrix products, arithmetic and copies ran while one was open for 1% -> 1% of each run, Pallas kernels for 1% -> 1%
where the time goes in v8:
time: 146 us; the launch traced here: 145 us
  starting transfers between devices  49.4 us (34%)
  waiting for transfers between devices  43.5 us (30%)
  blocking collectives  38.3 us (26%)
  Pallas kernels  7.01 us (5%)
  local copies, waits for them, and re-layouts  3.41 us (2%)
  other arithmetic  2.88 us (2%)
    ppermute x7, starting transfers between devices, shift(): return lax.ppermute(x, 'dp', [(i, (i + by) % NZ) for i in range(NZ)])  34 us
    ppermute x7, waiting for transfers between devices, shift(): return lax.ppermute(x, 'dp', [(i, (i + by) % NZ) for i in range(NZ)])  34 us
    all_gather x1, blocking collectives, reduce_gradients(): mid = lax.all_gather(mine, 'dp', axis_index_groups=Z_FAR)  19.5 us
    all_to_all x1, blocking collectives, swap(): return lax.all_to_all(x, axis, 0, 0, tiled=True, axis_index_groups=groups)  18.8 us
    all_to_all x2, starting transfers between devices, swap(): return lax.all_to_all(x, axis, 0, 0, tiled=True, axis_index_groups=groups)  13.5 us
    all_to_all x2, waiting for transfers between devices, swap(): return lax.all_to_all(x, axis, 0, 0, tiled=True, axis_index_groups=groups)  8.93 us
    pallas_call x5, Pallas kernels, call(): pl.pallas_call(kernel, out_shape=outs, in_specs=specs, out_specs=jax.tree...  7.01 us
  transfers between devices with their start and end apart: 10, of which 9 were waited for; matrix products, arithmetic and copies ran while one was open for 1% of the time, Pallas kernels for 1%

profile of v8, /device:TPU:6, one launch (start us, length us, event | category | flops | bytes accessed | tf_op | source)
XLA Modules:
  0.0 145.3 jit_solution(5820284507466260515)
XLA Ops:
  0.6 0.0 copy-start.3
  0.6 0.9 convert_element_type.13
  1.5 18.8 %all_to_all.15 = bf16[8,128,128]{2,1,0:T(8,128)(2,1)S(1)} all-to-all(bf16[8,128,128]{2,1,0:T(8,128)(2,1)S(1)} %broadcast_in_dim.4), channel_id=1, replica_groups={{0,8,16,24,32,40,48,56},{1,9,17,25,33,41,49,57},{2,10,18,26,34,42,50,58..., dimensions={0} | all-to-all | bytes 524288 | tf_op jit(solution)/shard_map/all_to_all | solution.py:142
  20.3 1.2 broadcast_in_dim.5
  21.5 7.2 %all-to-all-start.1 = ((bf16[4,8,128,128]{3,2,1,0:T(8,128)(2,1)}), bf16[4,8,128,128]{3,2,1,0:T(8,128)(2,1)S(1)}, u32[]{:S(2)}, u32[]{:S(2)}) async-start(bf16[4,8,128,128]{3,2,1,0:T(8,128)(2,1)} %broadcast_in_dim.5), calls=%async_computation.1 | async-start | bytes 2097152 | tf_op jit(solution)/shard_map/all_to_all | solution.py:142
  28.7 8.9 %all-to-all-done.1 = bf16[4,8,128,128]{3,2,1,0:T(8,128)(2,1)S(1)} async-done(((bf16[4,8,128,128]{3,2,1,0:T(8,128)(2,1)}), bf16[4,8,128,128]{3,2,1,0:T(8,128)(2,1)S(1)}, u32[]{:S(2)}, u32[]{:S(2)}) %all-to-all-start.1) | async-done | bytes 1048608 | tf_op jit(solution)/shard_map/all_to_all | solution.py:142
  37.7 1.9 %collective-permute-start = (bf16[32,128,128]{2,1,0:T(8,128)(2,1)S(1)}, bf16[32,128,128]{2,1,0:T(8,128)(2,1)S(1)}, u32[]{:S(2)}, u32[]{:S(2)}) collective-permute-start(bf16[32,128,128]{2,1,0:T(8,128)(2,1)S(1)} %bitcast.11), channel_id=1, source_target_pairs={{0,1},{1,0},{2,3},{3,2},{4,5},{5,4},{6,7},{7,6},{8,9},{9,8},{10,11... | collective-permute-start | bytes 3145736 | tf_op jit(solution)/shard_map/ppermute | solution.py:187
  39.7 2.0 %multiply_convert_fusion.w_ref = bf16[38,128,128]{2,1,0:T(8,128)(2,1)S(1)} fusion(f32[38,128,128]{2,1,0:T(8,128)} %param.5, f32[38]{0:T(128)S(1)} %fusion.3.live_ref), kind=kLoop, calls=%fused_computation | loop fusion | flops 1245184 | bytes 3735704 | tf_op jit(solution)/shard_map/convert_element_type | solution.py:182
  41.6 0.6 collective-permute-done.sib_ref
  42.2 3.6 %shard_map.67 = (f32[128,512]{1,0:T(8,128)}, bf16[64,128,128]{2,1,0:T(8,128)(2,1)S(1)}, bf16[3,416,128]{2,1,0:T(8,128)(2,1)S(1)}, bf16[3,416,128]{2,1,0:T(8,128)...) custom-call(s32[38]{0:T(128)S(1)} %fusion.5.idx_ref, s32[38]{0:T(128)S(1)} %get-tuple-element.22.out_idx_ref, ...), custom_call_target="tpu_custom_call" | custom-call | tf_op jit(solution)/shard_map/pallas_call | solution.py:105
  45.8 1.3 copy-done
  47.2 6.3 %all-to-all-start.2 = ((bf16[64,128,128]{2,1,0:T(8,128)(2,1)}), bf16[64,128,128]{2,1,0:T(8,128)(2,1)S(1)}, u32[]{:S(2)}, u32[]{:S(2)}) async-start(bf16[64,128,128]{2,1,0:T(8,128)(2,1)} %copy-done), calls=%async_computation.2 | async-start | bytes 4194304 | tf_op jit(solution)/shard_map/all_to_all | solution.py:142
  53.4 4.3 %collective-permute-start.1 = (bf16[3,416,128]{2,1,0:T(8,128)(2,1)S(1)}, bf16[3,416,128]{2,1,0:T(8,128)(2,1)S(1)}, u32[]{:S(2)}, u32[]{:S(2)}) collective-permute-start(bf16[3,416,128]{2,1,0:T(8,128)(2,1)S(1)} %get-tuple-element.14), channel_id=1, source_target_pairs={{0,64},{64,128},{128,192},{192,256},{256,320},{320,384},{384,448},... | collective-permute-start | bytes 958472 | tf_op jit(solution)/shard_map/ppermute | solution.py:146
  57.7 12.2 %collective-permute-start.2 = (bf16[3,416,128]{2,1,0:T(8,128)(2,1)S(1)}, bf16[3,416,128]{2,1,0:T(8,128)(2,1)S(1)}, u32[]{:S(2)}, u32[]{:S(2)}) collective-permute-start(bf16[3,416,128]{2,1,0:T(8,128)(2,1)S(1)} %get-tuple-element.15), channel_id=1, source_target_pairs={{0,704},{64,0},{128,64},{192,128},{256,192},{320,256},{384,320},{4... | collective-permute-start | bytes 958472 | tf_op jit(solution)/shard_map/ppermute | solution.py:146
  70.0 1.9 %collective-permute-start.3 = (bf16[3,416,128]{2,1,0:T(8,128)(2,1)S(1)}, bf16[3,416,128]{2,1,0:T(8,128)(2,1)S(1)}, u32[]{:S(2)}, u32[]{:S(2)}) collective-permute-start(bf16[3,416,128]{2,1,0:T(8,128)(2,1)S(1)} %get-tuple-element.16), channel_id=1, source_target_pairs={{0,128},{64,192},{128,256},{192,320},{256,384},{320,448},{384,512}... | collective-permute-start | bytes 958472 | tf_op jit(solution)/shard_map/ppermute | solution.py:146
  71.9 4.4 %collective-permute-done.1.a_ref = bf16[3,416,128]{2,1,0:T(8,128)(2,1)S(1)} collective-permute-done((bf16[3,416,128]{2,1,0:T(8,128)(2,1)S(1)}, bf16[3,416,128]{2,1,0:T(8,128)(2,1)S(1)}, u32[]{:S(2)}, u32[]{:S(2)}) %collective-permute-start.1) | collective-permute-done | bytes 319520 | tf_op jit(solution)/shard_map/ppermute | solution.py:146
  76.3 0.7 collective-permute-done.2.b_ref
  77.0 11.9 %collective-permute-done.3.c_ref = bf16[3,416,128]{2,1,0:T(8,128)(2,1)S(1)} collective-permute-done((bf16[3,416,128]{2,1,0:T(8,128)(2,1)S(1)}, bf16[3,416,128]{2,1,0:T(8,128)(2,1)S(1)}, u32[]{:S(2)}, u32[]{:S(2)}) %collective-permute-start.3) | collective-permute-done | bytes 319520 | tf_op jit(solution)/shard_map/ppermute | solution.py:146
  88.9 0.2 shard_map.68
  89.1 1.9 %collective-permute-start.4 = (bf16[416,128]{1,0:T(8,128)(2,1)S(1)}, bf16[416,128]{1,0:T(8,128)(2,1)S(1)}, u32[]{:S(2)}, u32[]{:S(2)}) collective-permute-start(bf16[416,128]{1,0:T(8,128)(2,1)S(1)} %get-tuple-element.18), channel_id=1, source_target_pairs={{0,256},{64,320},{128,384},{192,448},{256,512},{320,576},{384,640}... | collective-permute-start | bytes 319496 | tf_op jit(solution)/shard_map/ppermute | solution.py:146
  91.0 7.8 %collective-permute-start.5 = (bf16[416,128]{1,0:T(8,128)(2,1)S(1)}, bf16[416,128]{1,0:T(8,128)(2,1)S(1)}, u32[]{:S(2)}, u32[]{:S(2)}) collective-permute-start(bf16[416,128]{1,0:T(8,128)(2,1)S(1)} %get-tuple-element.19), channel_id=1, source_target_pairs={{0,512},{64,576},{128,640},{192,704},{256,0},{320,64},{384,128},{4... | collective-permute-start | bytes 319496 | tf_op jit(solution)/shard_map/ppermute | solution.py:146
  98.8 5.4 %collective-permute-done.4.a_ref = bf16[416,128]{1,0:T(8,128)(2,1)S(1)} collective-permute-done((bf16[416,128]{1,0:T(8,128)(2,1)S(1)}, bf16[416,128]{1,0:T(8,128)(2,1)S(1)}, u32[]{:S(2)}, u32[]{:S(2)}) %collective-permute-start.4) | collective-permute-done | bytes 106528 | tf_op jit(solution)/shard_map/ppermute | solution.py:146
  104.2 5.0 %collective-permute-done.5.b_ref = bf16[416,128]{1,0:T(8,128)(2,1)S(1)} collective-permute-done((bf16[416,128]{1,0:T(8,128)(2,1)S(1)}, bf16[416,128]{1,0:T(8,128)(2,1)S(1)}, u32[]{:S(2)}, u32[]{:S(2)}) %collective-permute-start.5) | collective-permute-done | bytes 106528 | tf_op jit(solution)/shard_map/ppermute | solution.py:146
  109.3 19.5 %all-gather = bf16[1664,128]{1,0:T(8,128)(2,1)S(1)} all-gather(bf16[416,128]{1,0:T(8,128)(2,1)S(1)} %shard_map.69), channel_id=2, replica_groups={{0,192,384,576},{64,256,448,640},{128,320,512,704},{1,193,385,577},{65,..., dimensions={0}, use_global_device_ids=true | all-gather | bytes 532480 | tf_op jit(solution)/shard_map/all_gather | solution.py:157
  128.8 1.9 %collective-permute-start.7 = (bf16[4,416,128]{2,1,0:T(8,128)(2,1)S(1)}, bf16[4,416,128]{2,1,0:T(8,128)(2,1)S(1)}, u32[]{:S(2)}, u32[]{:S(2)}) collective-permute-start(bf16[4,416,128]{2,1,0:T(8,128)(2,1)S(1)} %bitcast.13), channel_id=1, source_target_pairs={{0,704},{64,0},{128,64},{192,128},{256,192},{320,256},{384,320},{4... | collective-permute-start | bytes 1277960 | tf_op jit(solution)/shard_map/ppermute | solution.py:146
  130.7 3.9 %collective-permute-start.6 = (bf16[4,416,128]{2,1,0:T(8,128)(2,1)S(1)}, bf16[4,416,128]{2,1,0:T(8,128)(2,1)S(1)}, u32[]{:S(2)}, u32[]{:S(2)}) collective-permute-start(bf16[4,416,128]{2,1,0:T(8,128)(2,1)S(1)} %bitcast.14), channel_id=1, source_target_pairs={{0,64},{64,128},{128,192},{192,256},{256,320},{320,384},{384,448},... | collective-permute-start | bytes 1277960 | tf_op jit(solution)/shard_map/ppermute | solution.py:146
  134.6 0.0 all-to-all-done.2.in_ref
  134.7 0.9 shard_map.70.after_ref
  135.6 3.2 %collective-permute-done.7.high_ref = bf16[4,416,128]{2,1,0:T(8,128)(2,1)S(1)} collective-permute-done((bf16[4,416,128]{2,1,0:T(8,128)(2,1)S(1)}, bf16[4,416,128]{2,1,0:T(8,128)(2,1)S(1)}, u32[]{:S(2)}, u32[]{:S(2)}) %collective-permute-start.7) | collective-permute-done | bytes 426016 | tf_op jit(solution)/shard_map/ppermute | solution.py:146
  138.8 3.4 %collective-permute-done.6.low_ref = bf16[4,416,128]{2,1,0:T(8,128)(2,1)S(1)} collective-permute-done((bf16[4,416,128]{2,1,0:T(8,128)(2,1)S(1)}, bf16[4,416,128]{2,1,0:T(8,128)(2,1)S(1)}, u32[]{:S(2)}, u32[]{:S(2)}) %collective-permute-start.6) | collective-permute-done | bytes 426016 | tf_op jit(solution)/shard_map/ppermute | solution.py:146
  142.2 0.8 copy-done.1
  143.0 2.2 %shard_map.71 = f32[4864,128]{1,0:T(8,128)} custom-call(s32[3]{0:T(128)S(1)} %and_select_fusion.place_ref, f32[128,128]{1,0:T(8,128)S(1)} %copy-done.1, bf16[4,416,128]{2,1,0:T(8,128)(2,1)S(1)} %collective-permute-done.6.low_ref, bf16[4,416,128]{2,1,0:T(8,128)(2,1)S(1)} %bitcast.16, bf16[4,416,128]{2,1,0:T(8,128)(2,1)S(1)} %collective-permute-done.7.high_ref), custom_call_target="tpu_custom_call" | custom-call | tf_op jit(solution)/shard_map/pallas_call | solution.py:105
  (12 shorter events, 0.1 us)
Async XLA Ops:
  0.6 39.0 %copy-start.3 = (s32[38,2]{0,1:T(2,128)S(1)}, s32[38,2]{0,1:T(2,128)}, u32[]{:S(2)}) copy-start(s32[38,2]{0,1:T(2,128)} %param.6) | copy-start | bytes 916
  21.5 20.7 %copy-start.2 = (f32[128,512]{1,0:T(8,128)S(1)}, f32[128,512]{1,0:T(8,128)}, u32[]{:S(2)}) copy-start(f32[128,512]{1,0:T(8,128)} %g_ref.1) | copy-start | bytes 786436
  21.5 16.1 %all-to-all-start.1 = ((bf16[4,8,128,128]{3,2,1,0:T(8,128)(2,1)}), bf16[4,8,128,128]{3,2,1,0:T(8,128)(2,1)S(1)}, u32[]{:S(2)}, u32[]{:S(2)}) async-start(bf16[4,8,128,128]{3,2,1,0:T(8,128)(2,1)} %broadcast_in_dim.5), calls=%async_computation.1 | async-start | bytes 2097152 | tf_op jit(solution)/shard_map/all_to_all | solution.py:142
  37.7 4.5 %collective-permute-start = (bf16[32,128,128]{2,1,0:T(8,128)(2,1)S(1)}, bf16[32,128,128]{2,1,0:T(8,128)(2,1)S(1)}, u32[]{:S(2)}, u32[]{:S(2)}) collective-permute-start(bf16[32,128,128]{2,1,0:T(8,128)(2,1)S(1)} %bitcast.11), channel_id=1, source_target_pairs={{0,1},{1,0},{2,3},{3,2},{4,5},{5,4},{6,7},{7,6},{8,9},{9,8},{10,11... | collective-permute-start | bytes 3145736 | tf_op jit(solution)/shard_map/ppermute | solution.py:187
  45.8 1.3 copy-start
  47.2 87.5 %all-to-all-start.2 = ((bf16[64,128,128]{2,1,0:T(8,128)(2,1)}), bf16[64,128,128]{2,1,0:T(8,128)(2,1)S(1)}, u32[]{:S(2)}, u32[]{:S(2)}) async-start(bf16[64,128,128]{2,1,0:T(8,128)(2,1)} %copy-done), calls=%async_computation.2 | async-start | bytes 4194304 | tf_op jit(solution)/shard_map/all_to_all | solution.py:142
  53.4 22.9 %collective-permute-start.1 = (bf16[3,416,128]{2,1,0:T(8,128)(2,1)S(1)}, bf16[3,416,128]{2,1,0:T(8,128)(2,1)S(1)}, u32[]{:S(2)}, u32[]{:S(2)}) collective-permute-start(bf16[3,416,128]{2,1,0:T(8,128)(2,1)S(1)} %get-tuple-element.14), channel_id=1, source_target_pairs={{0,64},{64,128},{128,192},{192,256},{256,320},{320,384},{384,448},... | collective-permute-start | bytes 958472 | tf_op jit(solution)/shard_map/ppermute | solution.py:146
  57.7 19.3 %collective-permute-start.2 = (bf16[3,416,128]{2,1,0:T(8,128)(2,1)S(1)}, bf16[3,416,128]{2,1,0:T(8,128)(2,1)S(1)}, u32[]{:S(2)}, u32[]{:S(2)}) collective-permute-start(bf16[3,416,128]{2,1,0:T(8,128)(2,1)S(1)} %get-tuple-element.15), channel_id=1, source_target_pairs={{0,704},{64,0},{128,64},{192,128},{256,192},{320,256},{384,320},{4... | collective-permute-start | bytes 958472 | tf_op jit(solution)/shard_map/ppermute | solution.py:146
  70.0 18.9 %collective-permute-start.3 = (bf16[3,416,128]{2,1,0:T(8,128)(2,1)S(1)}, bf16[3,416,128]{2,1,0:T(8,128)(2,1)S(1)}, u32[]{:S(2)}, u32[]{:S(2)}) collective-permute-start(bf16[3,416,128]{2,1,0:T(8,128)(2,1)S(1)} %get-tuple-element.16), channel_id=1, source_target_pairs={{0,128},{64,192},{128,256},{192,320},{256,384},{320,448},{384,512}... | collective-permute-start | bytes 958472 | tf_op jit(solution)/shard_map/ppermute | solution.py:146
  89.1 15.1 %collective-permute-start.4 = (bf16[416,128]{1,0:T(8,128)(2,1)S(1)}, bf16[416,128]{1,0:T(8,128)(2,1)S(1)}, u32[]{:S(2)}, u32[]{:S(2)}) collective-permute-start(bf16[416,128]{1,0:T(8,128)(2,1)S(1)} %get-tuple-element.18), channel_id=1, source_target_pairs={{0,256},{64,320},{128,384},{192,448},{256,512},{320,576},{384,640}... | collective-permute-start | bytes 319496 | tf_op jit(solution)/shard_map/ppermute | solution.py:146
  91.0 18.2 %collective-permute-start.5 = (bf16[416,128]{1,0:T(8,128)(2,1)S(1)}, bf16[416,128]{1,0:T(8,128)(2,1)S(1)}, u32[]{:S(2)}, u32[]{:S(2)}) collective-permute-start(bf16[416,128]{1,0:T(8,128)(2,1)S(1)} %get-tuple-element.19), channel_id=1, source_target_pairs={{0,512},{64,576},{128,640},{192,704},{256,0},{320,64},{384,128},{4... | collective-permute-start | bytes 319496 | tf_op jit(solution)/shard_map/ppermute | solution.py:146
  128.8 10.0 %collective-permute-start.7 = (bf16[4,416,128]{2,1,0:T(8,128)(2,1)S(1)}, bf16[4,416,128]{2,1,0:T(8,128)(2,1)S(1)}, u32[]{:S(2)}, u32[]{:S(2)}) collective-permute-start(bf16[4,416,128]{2,1,0:T(8,128)(2,1)S(1)} %bitcast.13), channel_id=1, source_target_pairs={{0,704},{64,0},{128,64},{192,128},{256,192},{320,256},{384,320},{4... | collective-permute-start | bytes 1277960 | tf_op jit(solution)/shard_map/ppermute | solution.py:146
  130.7 11.5 %collective-permute-start.6 = (bf16[4,416,128]{2,1,0:T(8,128)(2,1)S(1)}, bf16[4,416,128]{2,1,0:T(8,128)(2,1)S(1)}, u32[]{:S(2)}, u32[]{:S(2)}) collective-permute-start(bf16[4,416,128]{2,1,0:T(8,128)(2,1)S(1)} %bitcast.14), channel_id=1, source_target_pairs={{0,64},{64,128},{128,192},{192,256},{256,320},{320,384},{384,448},... | collective-permute-start | bytes 1277960 | tf_op jit(solution)/shard_map/ppermute | solution.py:146
  142.2 0.8 copy-start.1

commit v9 on v8

--- a/solution.py
+++ b/solution.py
@@ -13,6 +13,7 @@
 X_GROUPS = [[(y * NX + x) * NC + c for x in range(NX)] for y in range(NY) for c in range(NC)]
 CORE_SWAP = [(i, i ^ 1) for i in range(HALF * NC)]
 CHUNK = 416
+SPLIT = 208
 Z_FAR = [[3 * i + r for i in range(4)] for r in range(3)]
 F32, BF16 = jnp.float32, jnp.bfloat16
 
@@ -32,8 +33,8 @@
 
 
 def block_kernel(idx_ref, out_idx_ref, col_ref, live_ref, rel_ref, own_ref, sib_ref, w_ref, g_ref,
-                 act_ref, gx_out_ref, keep_ref, up1_ref, down1_ref, up2_ref,
-                 x_ref, prod_ref, pre_ref, dpre_ref, gx_ref, gw_ref):
+                 act_ref, gx_out_ref, keep_ref, up1_ref, down1_ref, up2_ref, down2_ref,
+                 x_ref, prod_ref, pre_ref, dpre_ref, gx_ref, gw_ref, x_out_ref, sem):
     slots = w_ref.shape[0]
     col_blocks = pre_ref.shape[0]
     x_ref[:HALF] = own_ref[...]
@@ -48,6 +49,14 @@
         lanes = slice(c * BS, (c + 1) * BS)
         act_ref[:, lanes] = value
         dpre_ref[c] = (g_ref[:, lanes] * slope).astype(BF16)
+    gx_ref[...] = jnp.zeros_like(gx_ref)
+    for s in range(slots):
+        prod_ref[s] = dot(dpre_ref[col_ref[s]], w_ref[s], ((1,), (1,)))
+    for s in range(slots):
+        gx_ref[out_idx_ref[s]] += prod_ref[s]
+    x_out_ref[...] = gx_ref[...].astype(BF16)
+    copy = pltpu.make_async_copy(x_out_ref, gx_out_ref, sem)
+    copy.start()
     for s in range(slots):
         wgrad = dot(x_ref[idx_ref[s]], dpre_ref[col_ref[s]], ((0,), (0,)))
         wgrad = (wgrad * live_ref[s]).astype(BF16)
@@ -63,19 +72,16 @@
         keep_ref[i] = gw_ref[4 * i]
         up1_ref[i] = gw_ref[4 * i + 1]
         down1_ref[i] = gw_ref[(4 * i + 11) % NZ]
-        up2_ref[i] = gw_ref[4 * i + 2]
-    gx_ref[...] = jnp.zeros_like(gx_ref)
-    for s in range(slots):
-        prod_ref[s] = dot(dpre_ref[col_ref[s]], w_ref[s], ((1,), (1,)))
-    for s in range(slots):
-        gx_ref[out_idx_ref[s]] += prod_ref[s]
-    gx_out_ref[...] = gx_ref[...].astype(BF16)
-
-
-def near_kernel(keep_ref, a_ref, b_ref, c_ref, stay_ref, up_ref, down_ref):
+        up2_ref[i] = gw_ref[4 * i + 2, :SPLIT]
+        down2_ref[i] = gw_ref[(4 * i + 10) % NZ, SPLIT:]
+    copy.wait()
+
+
+def near_kernel(keep_ref, a_ref, b_ref, c_ref, d_ref, stay_ref, up_ref, down_ref):
     for i, out in enumerate((stay_ref, up_ref, down_ref)):
         part = keep_ref[i].astype(F32) + a_ref[i].astype(F32) + b_ref[i].astype(F32)
-        out[...] = (part + c_ref[i].astype(F32)).astype(BF16)
+        out[:SPLIT] = (part[:SPLIT] + c_ref[i].astype(F32)).astype(BF16)
+        out[SPLIT:] = (part[SPLIT:] + d_ref[i].astype(F32)).astype(BF16)
 
 
 def far_kernel(stay_ref, a_ref, b_ref, out_ref):
@@ -101,15 +107,14 @@
 ORDER = pl.BlockSpec(memory_space=pl.ANY)
 
 
-def call(kernel, specs, ins, outs, scratch=(), flops=0, moved=0):
+def call(kernel, specs, ins, outs, scratch=(), out_specs=None):
     return pl.pallas_call(
         kernel,
         out_shape=outs,
         in_specs=specs,
-        out_specs=jax.tree.map(lambda _: VMEM, outs),
+        out_specs=out_specs or jax.tree.map(lambda _: VMEM, outs),
         scratch_shapes=scratch,
         compiler_params=pltpu.CompilerParams(vmem_limit_bytes=40 << 20),
-        cost_estimate=pl.CostEstimate(flops=flops, bytes_accessed=moved, transcendentals=0),
     )(*ins)
 
 
@@ -121,12 +126,12 @@
     slots = wb.shape[0]
     tokens, hidden = grad_act.shape
     cols = hidden // BS
-    full = array((3, CHUNK, BS))
+    full, half = array((3, CHUNK, BS)), array((3, SPLIT, BS))
     return call(
         block_kernel,
         [SMEM] * 5 + [VMEM] * 4,
         (idx, out_idx, col, live, rel, own, sib, wb, grad_act),
-        (array((tokens, hidden), F32), array((2 * HALF, tokens, BS)), full, full, full, full),
+        (array((tokens, hidden), F32), pltpu.HBM((2 * HALF, tokens, BS), BF16), full, full, full, half, half),
         [
             pltpu.VMEM((2 * HALF, tokens, BS), BF16),
             pltpu.VMEM((slots, tokens, BS), F32),
@@ -134,7 +139,10 @@
             pltpu.VMEM((cols, tokens, BS), BF16),
             pltpu.VMEM((2 * HALF, tokens, BS), F32),
             pltpu.VMEM((NZ, CHUNK, BS), BF16),
+            pltpu.VMEM((2 * HALF, tokens, BS), BF16),
+            pltpu.SemaphoreType.DMA,
         ],
+        (VMEM, pl.BlockSpec(memory_space=pltpu.HBM)) + (VMEM,) * 5,
     )
 
 
@@ -146,12 +154,12 @@
     return lax.ppermute(x, "dp", [(i, (i + by) % NZ) for i in range(NZ)])
 
 
-def reduce_gradients(gx, keep, up1, down1, up2, slots):
+def reduce_gradients(gx, keep, up1, down1, up2, down2, slots):
     tokens = gx.shape[1]
     one = array((CHUNK, BS))
     gx = swap(gx, "mp", None)
-    parts = shift(up1, 1), shift(down1, -1), shift(up2, 2)
-    stay, up, down = call(near_kernel, [VMEM] * 4, (keep, *parts), (one,) * 3)
+    parts = shift(up1, 1), shift(down1, -1), shift(up2, 2), shift(down2, -2)
+    stay, up, down = call(near_kernel, [VMEM] * 5, (keep, *parts), (one,) * 3)
     mine = call(far_kernel, [VMEM] * 3, (stay, shift(up, 4), shift(down, -4)), one)
 
     mid = lax.all_gather(mine, "dp", axis_index_groups=Z_FAR)

time: 146 us -> 145 us (level)
  waiting for transfers between devices: 43.5 us -> 31.3 us
  starting transfers between devices: 49.4 us -> 55.5 us
  blocking collectives: 38.3 us -> 43.2 us
  Pallas kernels: 7.01 us -> 8.71 us
    ppermute x7 -> x8, waiting for transfers between devices: 34 us -> 21.9 us  [shift(): return lax.ppermute(x, 'dp', [(i, (i + by) % NZ) for i in range(NZ)])]
    ppermute x7 -> x8, starting transfers between devices: 34 us -> 40.1 us  [shift(): return lax.ppermute(x, 'dp', [(i, (i + by) % NZ) for i in range(NZ)])]
    all_gather x1, blocking collectives: 19.5 us -> 24.5 us  [reduce_gradients(): mid = lax.all_gather(mine, 'dp', axis_index_groups=Z_FAR)]
    pallas_call x5, Pallas kernels: 7.01 us -> 8.71 us  [call(): pl.pallas_call(kernel, out_shape=outs, in_specs=specs, out_specs=out_spec...]
  transfers between devices with their start and end apart: 10 -> 11, of which waited for: 9 -> 8; matrix products, arithmetic and copies ran while one was open for 1% -> 1% of each run, Pallas kernels for 1% -> 1%
where the time goes in v9:
time: 145 us
  starting transfers between devices  55.5 us (38%)
  blocking collectives  43.2 us (30%)
  waiting for transfers between devices  31.3 us (22%)
  Pallas kernels  8.71 us (6%)
  other arithmetic  2.88 us (2%)
  local copies, waits for them, and re-layouts  2.1 us (1%)
    ppermute x8, starting transfers between devices, shift(): return lax.ppermute(x, 'dp', [(i, (i + by) % NZ) for i in range(NZ)])  40.1 us
    all_gather x1, blocking collectives, reduce_gradients(): mid = lax.all_gather(mine, 'dp', axis_index_groups=Z_FAR)  24.5 us
    ppermute x8, waiting for transfers between devices, shift(): return lax.ppermute(x, 'dp', [(i, (i + by) % NZ) for i in range(NZ)])  21.9 us
    all_to_all x1, blocking collectives, swap(): return lax.all_to_all(x, axis, 0, 0, tiled=True, axis_index_groups=groups)  18.8 us
    all_to_all x2, starting transfers between devices, swap(): return lax.all_to_all(x, axis, 0, 0, tiled=True, axis_index_groups=groups)  13.5 us
    all_to_all x2, waiting for transfers between devices, swap(): return lax.all_to_all(x, axis, 0, 0, tiled=True, axis_index_groups=groups)  8.93 us
    pallas_call x5, Pallas kernels, call(): pl.pallas_call(kernel, out_shape=outs, in_specs=specs, out_specs=out_spec...  8.71 us
  transfers between devices with their start and end apart: 11, of which 8 were waited for; matrix products, arithmetic and copies ran while one was open for 1% of the time, Pallas kernels for 1%

profile of v9, /device:TPU:6, one launch (start us, length us, event | category | flops | bytes accessed | tf_op | source)
XLA Modules:
  0.0 144.5 jit_solution(8348609663643470086)
XLA Ops:
  0.6 0.9 convert_element_type.13
  1.5 18.8 %all_to_all.15 = bf16[8,128,128]{2,1,0:T(8,128)(2,1)S(1)} all-to-all(bf16[8,128,128]{2,1,0:T(8,128)(2,1)S(1)} %broadcast_in_dim.4), channel_id=1, replica_groups={{0,8,16,24,32,40,48,56},{1,9,17,25,33,41,49,57},{2,10,18,26,34,42,50,58..., dimensions={0} | all-to-all | bytes 524288 | tf_op jit(solution)/shard_map/all_to_all | solution.py:150
  20.3 1.2 broadcast_in_dim.5
  21.5 7.2 %all-to-all-start.1 = ((bf16[4,8,128,128]{3,2,1,0:T(8,128)(2,1)}), bf16[4,8,128,128]{3,2,1,0:T(8,128)(2,1)S(1)}, u32[]{:S(2)}, u32[]{:S(2)}) async-start(bf16[4,8,128,128]{3,2,1,0:T(8,128)(2,1)} %broadcast_in_dim.5), calls=%async_computation.1 | async-start | bytes 2097152 | tf_op jit(solution)/shard_map/all_to_all | solution.py:150
  28.7 8.9 %all-to-all-done.1 = bf16[4,8,128,128]{3,2,1,0:T(8,128)(2,1)S(1)} async-done(((bf16[4,8,128,128]{3,2,1,0:T(8,128)(2,1)}), bf16[4,8,128,128]{3,2,1,0:T(8,128)(2,1)S(1)}, u32[]{:S(2)}, u32[]{:S(2)}) %all-to-all-start.1) | async-done | bytes 1048608 | tf_op jit(solution)/shard_map/all_to_all | solution.py:150
  37.7 1.9 %collective-permute-start = (bf16[32,128,128]{2,1,0:T(8,128)(2,1)S(1)}, bf16[32,128,128]{2,1,0:T(8,128)(2,1)S(1)}, u32[]{:S(2)}, u32[]{:S(2)}) collective-permute-start(bf16[32,128,128]{2,1,0:T(8,128)(2,1)S(1)} %bitcast.11), channel_id=1, source_target_pairs={{0,1},{1,0},{2,3},{3,2},{4,5},{5,4},{6,7},{7,6},{8,9},{9,8},{10,11... | collective-permute-start | bytes 3145736 | tf_op jit(solution)/shard_map/ppermute | solution.py:195
  39.7 2.0 %multiply_convert_fusion.w_ref = bf16[38,128,128]{2,1,0:T(8,128)(2,1)S(1)} fusion(f32[38,128,128]{2,1,0:T(8,128)} %param.5, f32[38]{0:T(128)S(1)} %fusion.3.live_ref), kind=kLoop, calls=%fused_computation | loop fusion | flops 1245184 | bytes 3735704 | tf_op jit(solution)/shard_map/convert_element_type | solution.py:190
  41.6 0.6 collective-permute-done.sib_ref
  42.2 5.3 %shard_map.67 = (f32[128,512]{1,0:T(8,128)}, bf16[64,128,128]{2,1,0:T(8,128)(2,1)}, bf16[3,416,128]{2,1,0:T(8,128)(2,1)S(1)}, bf16[3,416,128]{2,1,0:T(8,128)(2,1...) custom-call(s32[38]{0:T(128)S(1)} %fusion.5.idx_ref, ...), custom_call_target="tpu_custom_call" | custom-call | tf_op jit(solution)/shard_map/pallas_call | solution.py:111
  47.5 6.3 %all-to-all-start.2 = ((bf16[64,128,128]{2,1,0:T(8,128)(2,1)}), bf16[64,128,128]{2,1,0:T(8,128)(2,1)S(1)}, u32[]{:S(2)}, u32[]{:S(2)}) async-start(bf16[64,128,128]{2,1,0:T(8,128)(2,1)} %get-tuple-element.22), calls=%async_computation.2 | async-start | bytes 4194304 | tf_op jit(solution)/shard_map/all_to_all | solution.py:150
  53.8 4.3 %collective-permute-start.1 = (bf16[3,416,128]{2,1,0:T(8,128)(2,1)S(1)}, bf16[3,416,128]{2,1,0:T(8,128)(2,1)S(1)}, u32[]{:S(2)}, u32[]{:S(2)}) collective-permute-start(bf16[3,416,128]{2,1,0:T(8,128)(2,1)S(1)} %get-tuple-element.15), channel_id=1, source_target_pairs={{0,64},{64,128},{128,192},{192,256},{256,320},{320,384},{384,448},... | collective-permute-start | bytes 958472 | tf_op jit(solution)/shard_map/ppermute | solution.py:154
  58.1 12.2 %collective-permute-start.2 = (bf16[3,416,128]{2,1,0:T(8,128)(2,1)S(1)}, bf16[3,416,128]{2,1,0:T(8,128)(2,1)S(1)}, u32[]{:S(2)}, u32[]{:S(2)}) collective-permute-start(bf16[3,416,128]{2,1,0:T(8,128)(2,1)S(1)} %get-tuple-element.16), channel_id=1, source_target_pairs={{0,704},{64,0},{128,64},{192,128},{256,192},{320,256},{384,320},{4... | collective-permute-start | bytes 958472 | tf_op jit(solution)/shard_map/ppermute | solution.py:154
  70.3 1.9 %collective-permute-start.3 = (bf16[3,208,128]{2,1,0:T(8,128)(2,1)S(1)}, bf16[3,208,128]{2,1,0:T(8,128)(2,1)S(1)}, u32[]{:S(2)}, u32[]{:S(2)}) collective-permute-start(bf16[3,208,128]{2,1,0:T(8,128)(2,1)S(1)} %get-tuple-element.17), channel_id=1, source_target_pairs={{0,128},{64,192},{128,256},{192,320},{256,384},{320,448},{384,512}... | collective-permute-start | bytes 479240 | tf_op jit(solution)/shard_map/ppermute | solution.py:154
  72.3 6.0 %collective-permute-start.4 = (bf16[3,208,128]{2,1,0:T(8,128)(2,1)S(1)}, bf16[3,208,128]{2,1,0:T(8,128)(2,1)S(1)}, u32[]{:S(2)}, u32[]{:S(2)}) collective-permute-start(bf16[3,208,128]{2,1,0:T(8,128)(2,1)S(1)} %get-tuple-element.18), channel_id=1, source_target_pairs={{0,640},{64,704},{128,0},{192,64},{256,128},{320,192},{384,256},{4... | collective-permute-start | bytes 479240 | tf_op jit(solution)/shard_map/ppermute | solution.py:154
  78.3 4.2 %collective-permute-done.3.c_ref = bf16[3,208,128]{2,1,0:T(8,128)(2,1)S(1)} collective-permute-done((bf16[3,208,128]{2,1,0:T(8,128)(2,1)S(1)}, bf16[3,208,128]{2,1,0:T(8,128)(2,1)S(1)}, u32[]{:S(2)}, u32[]{:S(2)}) %collective-permute-start.3) | collective-permute-done | bytes 159776 | tf_op jit(solution)/shard_map/ppermute | solution.py:154
  82.6 2.2 %collective-permute-done.4.d_ref = bf16[3,208,128]{2,1,0:T(8,128)(2,1)S(1)} collective-permute-done((bf16[3,208,128]{2,1,0:T(8,128)(2,1)S(1)}, bf16[3,208,128]{2,1,0:T(8,128)(2,1)S(1)}, u32[]{:S(2)}, u32[]{:S(2)}) %collective-permute-start.4) | collective-permute-done | bytes 159776 | tf_op jit(solution)/shard_map/ppermute | solution.py:154
  84.7 0.0 collective-permute-done.1.a_ref
  84.7 0.0 collective-permute-done.2.b_ref
  84.7 0.2 shard_map.68
  84.9 5.1 %collective-permute-start.5 = (bf16[416,128]{1,0:T(8,128)(2,1)S(1)}, bf16[416,128]{1,0:T(8,128)(2,1)S(1)}, u32[]{:S(2)}, u32[]{:S(2)}) collective-permute-start(bf16[416,128]{1,0:T(8,128)(2,1)S(1)} %get-tuple-element.20), channel_id=1, source_target_pairs={{0,256},{64,320},{128,384},{192,448},{256,512},{320,576},{384,640}... | collective-permute-start | bytes 319496 | tf_op jit(solution)/shard_map/ppermute | solution.py:154
  90.0 4.7 %collective-permute-start.6 = (bf16[416,128]{1,0:T(8,128)(2,1)S(1)}, bf16[416,128]{1,0:T(8,128)(2,1)S(1)}, u32[]{:S(2)}, u32[]{:S(2)}) collective-permute-start(bf16[416,128]{1,0:T(8,128)(2,1)S(1)} %get-tuple-element.21), channel_id=1, source_target_pairs={{0,512},{64,576},{128,640},{192,704},{256,0},{320,64},{384,128},{4... | collective-permute-start | bytes 319496 | tf_op jit(solution)/shard_map/ppermute | solution.py:154
  94.7 4.2 %collective-permute-done.5.a_ref = bf16[416,128]{1,0:T(8,128)(2,1)S(1)} collective-permute-done((bf16[416,128]{1,0:T(8,128)(2,1)S(1)}, bf16[416,128]{1,0:T(8,128)(2,1)S(1)}, u32[]{:S(2)}, u32[]{:S(2)}) %collective-permute-start.5) | collective-permute-done | bytes 106528 | tf_op jit(solution)/shard_map/ppermute | solution.py:154
  98.9 3.9 %collective-permute-done.6.b_ref = bf16[416,128]{1,0:T(8,128)(2,1)S(1)} collective-permute-done((bf16[416,128]{1,0:T(8,128)(2,1)S(1)}, bf16[416,128]{1,0:T(8,128)(2,1)S(1)}, u32[]{:S(2)}, u32[]{:S(2)}) %collective-permute-start.6) | collective-permute-done | bytes 106528 | tf_op jit(solution)/shard_map/ppermute | solution.py:154
  102.8 24.5 %all-gather = bf16[1664,128]{1,0:T(8,128)(2,1)S(1)} all-gather(bf16[416,128]{1,0:T(8,128)(2,1)S(1)} %shard_map.69), channel_id=2, replica_groups={{0,192,384,576},{64,256,448,640},{128,320,512,704},{1,193,385,577},{65,..., dimensions={0}, use_global_device_ids=true | all-gather | bytes 532480 | tf_op jit(solution)/shard_map/all_gather | solution.py:165
  127.3 1.9 %collective-permute-start.8 = (bf16[4,416,128]{2,1,0:T(8,128)(2,1)S(1)}, bf16[4,416,128]{2,1,0:T(8,128)(2,1)S(1)}, u32[]{:S(2)}, u32[]{:S(2)}) collective-permute-start(bf16[4,416,128]{2,1,0:T(8,128)(2,1)S(1)} %bitcast.13), channel_id=1, source_target_pairs={{0,704},{64,0},{128,64},{192,128},{256,192},{320,256},{384,320},{4... | collective-permute-start | bytes 1277960 | tf_op jit(solution)/shard_map/ppermute | solution.py:154
  129.2 3.9 %collective-permute-start.7 = (bf16[4,416,128]{2,1,0:T(8,128)(2,1)S(1)}, bf16[4,416,128]{2,1,0:T(8,128)(2,1)S(1)}, u32[]{:S(2)}, u32[]{:S(2)}) collective-permute-start(bf16[4,416,128]{2,1,0:T(8,128)(2,1)S(1)} %bitcast.14), channel_id=1, source_target_pairs={{0,64},{64,128},{128,192},{192,256},{256,320},{320,384},{384,448},... | collective-permute-start | bytes 1277960 | tf_op jit(solution)/shard_map/ppermute | solution.py:154
  133.1 0.0 all-to-all-done.2.in_ref
  133.1 0.9 shard_map.70.after_ref
  134.1 4.2 %collective-permute-done.8.high_ref = bf16[4,416,128]{2,1,0:T(8,128)(2,1)S(1)} collective-permute-done((bf16[4,416,128]{2,1,0:T(8,128)(2,1)S(1)}, bf16[4,416,128]{2,1,0:T(8,128)(2,1)S(1)}, u32[]{:S(2)}, u32[]{:S(2)}) %collective-permute-start.8) | collective-permute-done | bytes 426016 | tf_op jit(solution)/shard_map/ppermute | solution.py:154
  138.3 3.1 %collective-permute-done.7.low_ref = bf16[4,416,128]{2,1,0:T(8,128)(2,1)S(1)} collective-permute-done((bf16[4,416,128]{2,1,0:T(8,128)(2,1)S(1)}, bf16[4,416,128]{2,1,0:T(8,128)(2,1)S(1)}, u32[]{:S(2)}, u32[]{:S(2)}) %collective-permute-start.7) | collective-permute-done | bytes 426016 | tf_op jit(solution)/shard_map/ppermute | solution.py:154
  141.4 0.8 copy-done
  142.3 2.2 %shard_map.71 = f32[4864,128]{1,0:T(8,128)} custom-call(s32[3]{0:T(128)S(1)} %and_select_fusion.place_ref, f32[128,128]{1,0:T(8,128)S(1)} %copy-done, bf16[4,416,128]{2,1,0:T(8,128)(2,1)S(1)} %collective-permute-done.7.low_ref, bf16[4,416,128]{2,1,0:T(8,128)(2,1)S(1)} %bitcast.16, bf16[4,416,128]{2,1,0:T(8,128)(2,1)S(1)} %collective-permute-done.8.high_ref), custom_call_target="tpu_custom_call" | custom-call | tf_op jit(solution)/shard_map/pallas_call | solution.py:111
  (12 shorter events, 0.1 us)
Async XLA Ops:
  0.6 39.0 %copy-start.2 = (s32[38,2]{0,1:T(2,128)S(1)}, s32[38,2]{0,1:T(2,128)}, u32[]{:S(2)}) copy-start(s32[38,2]{0,1:T(2,128)} %param.6) | copy-start | bytes 916
  21.5 20.7 %copy-start.1 = (f32[128,512]{1,0:T(8,128)S(1)}, f32[128,512]{1,0:T(8,128)}, u32[]{:S(2)}) copy-start(f32[128,512]{1,0:T(8,128)} %g_ref.1) | copy-start | bytes 786436
  21.5 16.1 %all-to-all-start.1 = ((bf16[4,8,128,128]{3,2,1,0:T(8,128)(2,1)}), bf16[4,8,128,128]{3,2,1,0:T(8,128)(2,1)S(1)}, u32[]{:S(2)}, u32[]{:S(2)}) async-start(bf16[4,8,128,128]{3,2,1,0:T(8,128)(2,1)} %broadcast_in_dim.5), calls=%async_computation.1 | async-start | bytes 2097152 | tf_op jit(solution)/shard_map/all_to_all | solution.py:150
  37.7 4.5 %collective-permute-start = (bf16[32,128,128]{2,1,0:T(8,128)(2,1)S(1)}, bf16[32,128,128]{2,1,0:T(8,128)(2,1)S(1)}, u32[]{:S(2)}, u32[]{:S(2)}) collective-permute-start(bf16[32,128,128]{2,1,0:T(8,128)(2,1)S(1)} %bitcast.11), channel_id=1, source_target_pairs={{0,1},{1,0},{2,3},{3,2},{4,5},{5,4},{6,7},{7,6},{8,9},{9,8},{10,11... | collective-permute-start | bytes 3145736 | tf_op jit(solution)/shard_map/ppermute | solution.py:195
  47.5 85.6 %all-to-all-start.2 = ((bf16[64,128,128]{2,1,0:T(8,128)(2,1)}), bf16[64,128,128]{2,1,0:T(8,128)(2,1)S(1)}, u32[]{:S(2)}, u32[]{:S(2)}) async-start(bf16[64,128,128]{2,1,0:T(8,128)(2,1)} %get-tuple-element.22), calls=%async_computation.2 | async-start | bytes 4194304 | tf_op jit(solution)/shard_map/all_to_all | solution.py:150
  53.8 30.9 %collective-permute-start.1 = (bf16[3,416,128]{2,1,0:T(8,128)(2,1)S(1)}, bf16[3,416,128]{2,1,0:T(8,128)(2,1)S(1)}, u32[]{:S(2)}, u32[]{:S(2)}) collective-permute-start(bf16[3,416,128]{2,1,0:T(8,128)(2,1)S(1)} %get-tuple-element.15), channel_id=1, source_target_pairs={{0,64},{64,128},{128,192},{192,256},{256,320},{320,384},{384,448},... | collective-permute-start | bytes 958472 | tf_op jit(solution)/shard_map/ppermute | solution.py:154
  58.1 26.6 %collective-permute-start.2 = (bf16[3,416,128]{2,1,0:T(8,128)(2,1)S(1)}, bf16[3,416,128]{2,1,0:T(8,128)(2,1)S(1)}, u32[]{:S(2)}, u32[]{:S(2)}) collective-permute-start(bf16[3,416,128]{2,1,0:T(8,128)(2,1)S(1)} %get-tuple-element.16), channel_id=1, source_target_pairs={{0,704},{64,0},{128,64},{192,128},{256,192},{320,256},{384,320},{4... | collective-permute-start | bytes 958472 | tf_op jit(solution)/shard_map/ppermute | solution.py:154
  70.3 12.2 %collective-permute-start.3 = (bf16[3,208,128]{2,1,0:T(8,128)(2,1)S(1)}, bf16[3,208,128]{2,1,0:T(8,128)(2,1)S(1)}, u32[]{:S(2)}, u32[]{:S(2)}) collective-permute-start(bf16[3,208,128]{2,1,0:T(8,128)(2,1)S(1)} %get-tuple-element.17), channel_id=1, source_target_pairs={{0,128},{64,192},{128,256},{192,320},{256,384},{320,448},{384,512}... | collective-permute-start | bytes 479240 | tf_op jit(solution)/shard_map/ppermute | solution.py:154
  72.3 12.5 %collective-permute-start.4 = (bf16[3,208,128]{2,1,0:T(8,128)(2,1)S(1)}, bf16[3,208,128]{2,1,0:T(8,128)(2,1)S(1)}, u32[]{:S(2)}, u32[]{:S(2)}) collective-permute-start(bf16[3,208,128]{2,1,0:T(8,128)(2,1)S(1)} %get-tuple-element.18), channel_id=1, source_target_pairs={{0,640},{64,704},{128,0},{192,64},{256,128},{320,192},{384,256},{4... | collective-permute-start | bytes 479240 | tf_op jit(solution)/shard_map/ppermute | solution.py:154
  84.9 13.9 %collective-permute-start.5 = (bf16[416,128]{1,0:T(8,128)(2,1)S(1)}, bf16[416,128]{1,0:T(8,128)(2,1)S(1)}, u32[]{:S(2)}, u32[]{:S(2)}) collective-permute-start(bf16[416,128]{1,0:T(8,128)(2,1)S(1)} %get-tuple-element.20), channel_id=1, source_target_pairs={{0,256},{64,320},{128,384},{192,448},{256,512},{320,576},{384,640}... | collective-permute-start | bytes 319496 | tf_op jit(solution)/shard_map/ppermute | solution.py:154
  90.0 12.8 %collective-permute-start.6 = (bf16[416,128]{1,0:T(8,128)(2,1)S(1)}, bf16[416,128]{1,0:T(8,128)(2,1)S(1)}, u32[]{:S(2)}, u32[]{:S(2)}) collective-permute-start(bf16[416,128]{1,0:T(8,128)(2,1)S(1)} %get-tuple-element.21), channel_id=1, source_target_pairs={{0,512},{64,576},{128,640},{192,704},{256,0},{320,64},{384,128},{4... | collective-permute-start | bytes 319496 | tf_op jit(solution)/shard_map/ppermute | solution.py:154
  127.3 11.0 %collective-permute-start.8 = (bf16[4,416,128]{2,1,0:T(8,128)(2,1)S(1)}, bf16[4,416,128]{2,1,0:T(8,128)(2,1)S(1)}, u32[]{:S(2)}, u32[]{:S(2)}) collective-permute-start(bf16[4,416,128]{2,1,0:T(8,128)(2,1)S(1)} %bitcast.13), channel_id=1, source_target_pairs={{0,704},{64,0},{128,64},{192,128},{256,192},{320,256},{384,320},{4... | collective-permute-start | bytes 1277960 | tf_op jit(solution)/shard_map/ppermute | solution.py:154
  129.2 12.2 %collective-permute-start.7 = (bf16[4,416,128]{2,1,0:T(8,128)(2,1)S(1)}, bf16[4,416,128]{2,1,0:T(8,128)(2,1)S(1)}, u32[]{:S(2)}, u32[]{:S(2)}) collective-permute-start(bf16[4,416,128]{2,1,0:T(8,128)(2,1)S(1)} %bitcast.14), channel_id=1, source_target_pairs={{0,64},{64,128},{128,192},{192,256},{256,320},{320,384},{384,448},... | collective-permute-start | bytes 1277960 | tf_op jit(solution)/shard_map/ppermute | solution.py:154
  141.4 0.8 copy-start

commit v10 on v9

--- a/solution.py
+++ b/solution.py
@@ -14,6 +14,7 @@
 CORE_SWAP = [(i, i ^ 1) for i in range(HALF * NC)]
 CHUNK = 416
 SPLIT = 208
+PIECES = 4
 Z_FAR = [[3 * i + r for i in range(4)] for r in range(3)]
 F32, BF16 = jnp.float32, jnp.bfloat16
 
@@ -34,7 +35,7 @@
 
 def block_kernel(idx_ref, out_idx_ref, col_ref, live_ref, rel_ref, own_ref, sib_ref, w_ref, g_ref,
                  act_ref, gx_out_ref, keep_ref, up1_ref, down1_ref, up2_ref, down2_ref,
-                 x_ref, prod_ref, pre_ref, dpre_ref, gx_ref, gw_ref, x_out_ref, sem):
+                 x_ref, prod_ref, pre_ref, dpre_ref, gx_ref, gw_ref, x_out_ref, sems):
     slots = w_ref.shape[0]
     col_blocks = pre_ref.shape[0]
     x_ref[:HALF] = own_ref[...]
@@ -49,14 +50,6 @@
         lanes = slice(c * BS, (c + 1) * BS)
         act_ref[:, lanes] = value
         dpre_ref[c] = (g_ref[:, lanes] * slope).astype(BF16)
-    gx_ref[...] = jnp.zeros_like(gx_ref)
-    for s in range(slots):
-        prod_ref[s] = dot(dpre_ref[col_ref[s]], w_ref[s], ((1,), (1,)))
-    for s in range(slots):
-        gx_ref[out_idx_ref[s]] += prod_ref[s]
-    x_out_ref[...] = gx_ref[...].astype(BF16)
-    copy = pltpu.make_async_copy(x_out_ref, gx_out_ref, sem)
-    copy.start()
     for s in range(slots):
         wgrad = dot(x_ref[idx_ref[s]], dpre_ref[col_ref[s]], ((0,), (0,)))
         wgrad = (wgrad * live_ref[s]).astype(BF16)
@@ -74,7 +67,20 @@
         down1_ref[i] = gw_ref[(4 * i + 11) % NZ]
         up2_ref[i] = gw_ref[4 * i + 2, :SPLIT]
         down2_ref[i] = gw_ref[(4 * i + 10) % NZ, SPLIT:]
-    copy.wait()
+    gx_ref[...] = jnp.zeros_like(gx_ref)
+    for s in range(slots):
+        prod_ref[s] = dot(dpre_ref[col_ref[s]], w_ref[s], ((1,), (1,)))
+    for s in range(slots):
+        gx_ref[out_idx_ref[s]] += prod_ref[s]
+    copies = []
+    size = gx_ref.shape[0] // PIECES
+    for p in range(PIECES):
+        part = pl.ds(p * size, size)
+        x_out_ref[part] = gx_ref[part].astype(BF16)
+        copies.append(pltpu.make_async_copy(x_out_ref.at[part], gx_out_ref.at[part], sems.at[p]))
+        copies[-1].start()
+    for copy in copies:
+        copy.wait()
 
 
 def near_kernel(keep_ref, a_ref, b_ref, c_ref, d_ref, stay_ref, up_ref, down_ref):
@@ -92,18 +98,44 @@
     out_ref[...] = jnp.sum(in_ref[...].astype(F32), axis=0)
 
 
-def whole_kernel(place_ref, after_ref, low_ref, mid_ref, high_ref, out_ref, gw_ref):
+def whole_kernel(place_ref, after_ref, low_ref, mid_ref, high_ref, out_ref, gw_ref, wide_ref, sems):
     for i, part in enumerate((low_ref, mid_ref, high_ref)):
         for b in range(4):
             gw_ref[3 * b + place_ref[i]] = part[b]
     rows = out_ref.shape[0]
+    copies = []
     for j in range(NZ):
         size = min(CHUNK, rows - j * CHUNK)
-        out_ref[j * CHUNK:j * CHUNK + size] = gw_ref[j, :size].astype(F32)
+        wide_ref[j, :size] = gw_ref[j, :size].astype(F32)
+        copies.append(
+            pltpu.make_async_copy(
+                wide_ref.at[j, pl.ds(0, size)], out_ref.at[pl.ds(j * CHUNK, size)], sems.at[j]
+            )
+        )
+        copies[-1].start()
+    for copy in copies:
+        copy.wait()
+
+
+def first_spread_kernel(in_ref, out_ref):
+    value = in_ref[...].astype(BF16)
+    for i in range(out_ref.shape[0]):
+        out_ref[i] = value
+
+
+def second_spread_kernel(in_ref, out_ref, sems):
+    copies = [
+        pltpu.make_async_copy(in_ref, out_ref.at[i], sems.at[i]) for i in range(out_ref.shape[0])
+    ]
+    for copy in copies:
+        copy.start()
+    for copy in copies:
+        copy.wait()
 
 
 SMEM = pl.BlockSpec(memory_space=pltpu.SMEM)
 VMEM = pl.BlockSpec(memory_space=pltpu.VMEM)
+HBM = pl.BlockSpec(memory_space=pltpu.HBM)
 ORDER = pl.BlockSpec(memory_space=pl.ANY)
 
 
@@ -140,9 +172,9 @@
             pltpu.VMEM((2 * HALF, tokens, BS), F32),
             pltpu.VMEM((NZ, CHUNK, BS), BF16),
             pltpu.VMEM((2 * HALF, tokens, BS), BF16),
-            pltpu.SemaphoreType.DMA,
+            pltpu.SemaphoreType.DMA((PIECES,)),
         ],
-        (VMEM, pl.BlockSpec(memory_space=pltpu.HBM)) + (VMEM,) * 5,
+        (VMEM, HBM) + (VMEM,) * 5,
     )
 
 
@@ -170,8 +202,13 @@
         whole_kernel,
         [SMEM, ORDER] + [VMEM] * 3,
         (place, grad_x, low, mid, high),
-        array((slots * BS, BS), F32),
-        [pltpu.VMEM((NZ, CHUNK, BS), BF16)],
+        pltpu.HBM((slots * BS, BS), F32),
+        [
+            pltpu.VMEM((NZ, CHUNK, BS), BF16),
+            pltpu.VMEM((NZ, CHUNK, BS), F32),
+            pltpu.SemaphoreType.DMA((NZ,)),
+        ],
+        HBM,
     )
     return grad_x, grad_w.reshape(slots, BS, BS)
 
@@ -186,11 +223,19 @@
     core = lax.axis_index("mp") % NC
     at_y, at_x, at_core = row // (NC * NX), (row // NC) % NX, row % NC
     idx = ((at_core ^ core) * NX + at_x) * NY + at_y
-    xb = inputs.astype(BF16)
     wb = (block_weights * live[:, None, None]).astype(BF16)
 
-    by_y = swap(jnp.broadcast_to(xb[None], (NY, tokens, BS)), "mp", Y_GROUPS)
-    by_xy = swap(jnp.broadcast_to(by_y[None], (NX, NY, tokens, BS)), "mp", X_GROUPS)
+    by_y = call(first_spread_kernel, [VMEM], (inputs,), array((NY, tokens, BS)))
+    by_y = swap(by_y, "mp", Y_GROUPS)
+    by_xy = call(
+        second_spread_kernel,
+        [VMEM],
+        (by_y,),
+        pltpu.HBM((NX, NY, tokens, BS), BF16),
+        [pltpu.SemaphoreType.DMA((NX,))],
+        HBM,
+    )
+    by_xy = swap(by_xy, "mp", X_GROUPS)
     own = by_xy.reshape(HALF, tokens, BS)
     sib = lax.ppermute(own, "mp", CORE_SWAP)
 

time: 145 us -> 145 us (level)
    pallas_call x5 -> x7, Pallas kernels: 8.71 us -> 9.53 us  [call(): pl.pallas_call(kernel, out_shape=outs, in_specs=specs, out_specs=out_spec...]
where the time goes in v10:
time: 145 us; the launch traced here: 144 us
  starting transfers between devices  55.5 us (38%)
  blocking collectives  43.3 us (30%)
  waiting for transfers between devices  31.3 us (22%)
  Pallas kernels  9.53 us (7%)
  other arithmetic  2.03 us (1%)
  local copies, waits for them, and re-layouts  1.68 us (1%)
    ppermute x8, starting transfers between devices, shift(): return lax.ppermute(x, 'dp', [(i, (i + by) % NZ) for i in range(NZ)])  40 us
    all_gather x1, blocking collectives, reduce_gradients(): mid = lax.all_gather(mine, 'dp', axis_index_groups=Z_FAR)  24.5 us
    ppermute x8, waiting for transfers between devices, shift(): return lax.ppermute(x, 'dp', [(i, (i + by) % NZ) for i in range(NZ)])  21.9 us
    all_to_all x1, blocking collectives, swap(): return lax.all_to_all(x, axis, 0, 0, tiled=True, axis_index_groups=groups)  18.8 us
    all_to_all x2, starting transfers between devices, swap(): return lax.all_to_all(x, axis, 0, 0, tiled=True, axis_index_groups=groups)  13.5 us
    pallas_call x7, Pallas kernels, call(): pl.pallas_call(kernel, out_shape=outs, in_specs=specs, out_specs=out_spec...  9.53 us
    all_to_all x2, waiting for transfers between devices, swap(): return lax.all_to_all(x, axis, 0, 0, tiled=True, axis_index_groups=groups)  8.93 us
  transfers between devices with their start and end apart: 11, of which 8 were waited for; matrix products, arithmetic and copies ran while one was open for 1% of the time, Pallas kernels for 1%

profile of v10, /device:TPU:6, one launch (start us, length us, event | category | flops | bytes accessed | tf_op | source)
XLA Modules:
  0.0 144.1 jit_solution(12566095298395679932)
XLA Ops:
  0.6 0.8 copy-done.2
  1.5 18.8 %all_to_all.15.in_ref = bf16[8,128,128]{2,1,0:T(8,128)(2,1)S(1)} all-to-all(bf16[8,128,128]{2,1,0:T(8,128)(2,1)S(1)} %shard_map.67), channel_id=1, replica_groups={{0,8,16,24,32,40,48,56},{1,9,17,25,33,41,49,57},{2,10,18,26,34,42,50,58..., dimensions={0} | all-to-all | bytes 524288 | tf_op jit(solution)/shard_map/all_to_all | solution.py:182
  20.3 1.0 shard_map.68
  21.3 0.0 copy-start.1
  21.3 7.2 %all-to-all-start.1 = ((bf16[4,8,128,128]{3,2,1,0:T(8,128)(2,1)}), bf16[4,8,128,128]{3,2,1,0:T(8,128)(2,1)S(1)}, u32[]{:S(2)}, u32[]{:S(2)}) async-start(bf16[4,8,128,128]{3,2,1,0:T(8,128)(2,1)} %shard_map.68), calls=%async_computation.1 | async-start | bytes 2097152 | tf_op jit(solution)/shard_map/all_to_all | solution.py:182
  28.5 8.9 %all-to-all-done.1 = bf16[4,8,128,128]{3,2,1,0:T(8,128)(2,1)S(1)} async-done(((bf16[4,8,128,128]{3,2,1,0:T(8,128)(2,1)}), bf16[4,8,128,128]{3,2,1,0:T(8,128)(2,1)S(1)}, u32[]{:S(2)}, u32[]{:S(2)}) %all-to-all-start.1) | async-done | bytes 1048608 | tf_op jit(solution)/shard_map/all_to_all | solution.py:182
  37.4 1.9 %collective-permute-start = (bf16[32,128,128]{2,1,0:T(8,128)(2,1)S(1)}, bf16[32,128,128]{2,1,0:T(8,128)(2,1)S(1)}, u32[]{:S(2)}, u32[]{:S(2)}) collective-permute-start(bf16[32,128,128]{2,1,0:T(8,128)(2,1)S(1)} %bitcast.11), channel_id=1, source_target_pairs={{0,1},{1,0},{2,3},{3,2},{4,5},{5,4},{6,7},{7,6},{8,9},{9,8},{10,11... | collective-permute-start | bytes 3145736 | tf_op jit(solution)/shard_map/ppermute | solution.py:240
  39.4 2.0 %multiply_convert_fusion.w_ref = bf16[38,128,128]{2,1,0:T(8,128)(2,1)S(1)} fusion(f32[38,128,128]{2,1,0:T(8,128)} %param.5, f32[38]{0:T(128)S(1)} %fusion.3.live_ref), kind=kLoop, calls=%fused_computation | loop fusion | flops 1245184 | bytes 3735704 | tf_op jit(solution)/shard_map/convert_element_type | solution.py:226
  41.4 0.6 collective-permute-done.sib_ref
  42.0 5.2 %shard_map.69 = (f32[128,512]{1,0:T(8,128)}, bf16[64,128,128]{2,1,0:T(8,128)(2,1)}, bf16[3,416,128]{2,1,0:T(8,128)(2,1)S(1)}, bf16[3,416,128]{2,1,0:T(8,128)(2,1...) custom-call(s32[38]{0:T(128)S(1)} %fusion.5.idx_ref, ...), custom_call_target="tpu_custom_call" | custom-call | tf_op jit(solution)/shard_map/pallas_call | solution.py:143
  47.2 6.3 %all-to-all-start.2 = ((bf16[64,128,128]{2,1,0:T(8,128)(2,1)}), bf16[64,128,128]{2,1,0:T(8,128)(2,1)S(1)}, u32[]{:S(2)}, u32[]{:S(2)}) async-start(bf16[64,128,128]{2,1,0:T(8,128)(2,1)} %get-tuple-element.22), calls=%async_computation.2 | async-start | bytes 4194304 | tf_op jit(solution)/shard_map/all_to_all | solution.py:182
  53.5 4.3 %collective-permute-start.1 = (bf16[3,416,128]{2,1,0:T(8,128)(2,1)S(1)}, bf16[3,416,128]{2,1,0:T(8,128)(2,1)S(1)}, u32[]{:S(2)}, u32[]{:S(2)}) collective-permute-start(bf16[3,416,128]{2,1,0:T(8,128)(2,1)S(1)} %get-tuple-element.15), channel_id=1, source_target_pairs={{0,64},{64,128},{128,192},{192,256},{256,320},{320,384},{384,448},... | collective-permute-start | bytes 958472 | tf_op jit(solution)/shard_map/ppermute | solution.py:186
  57.8 12.2 %collective-permute-start.2 = (bf16[3,416,128]{2,1,0:T(8,128)(2,1)S(1)}, bf16[3,416,128]{2,1,0:T(8,128)(2,1)S(1)}, u32[]{:S(2)}, u32[]{:S(2)}) collective-permute-start(bf16[3,416,128]{2,1,0:T(8,128)(2,1)S(1)} %get-tuple-element.16), channel_id=1, source_target_pairs={{0,704},{64,0},{128,64},{192,128},{256,192},{320,256},{384,320},{4... | collective-permute-start | bytes 958472 | tf_op jit(solution)/shard_map/ppermute | solution.py:186
  70.0 1.9 %collective-permute-start.3 = (bf16[3,208,128]{2,1,0:T(8,128)(2,1)S(1)}, bf16[3,208,128]{2,1,0:T(8,128)(2,1)S(1)}, u32[]{:S(2)}, u32[]{:S(2)}) collective-permute-start(bf16[3,208,128]{2,1,0:T(8,128)(2,1)S(1)} %get-tuple-element.17), channel_id=1, source_target_pairs={{0,128},{64,192},{128,256},{192,320},{256,384},{320,448},{384,512}... | collective-permute-start | bytes 479240 | tf_op jit(solution)/shard_map/ppermute | solution.py:186
  71.9 6.0 %collective-permute-start.4 = (bf16[3,208,128]{2,1,0:T(8,128)(2,1)S(1)}, bf16[3,208,128]{2,1,0:T(8,128)(2,1)S(1)}, u32[]{:S(2)}, u32[]{:S(2)}) collective-permute-start(bf16[3,208,128]{2,1,0:T(8,128)(2,1)S(1)} %get-tuple-element.18), channel_id=1, source_target_pairs={{0,640},{64,704},{128,0},{192,64},{256,128},{320,192},{384,256},{4... | collective-permute-start | bytes 479240 | tf_op jit(solution)/shard_map/ppermute | solution.py:186
  78.0 4.3 %collective-permute-done.3.c_ref = bf16[3,208,128]{2,1,0:T(8,128)(2,1)S(1)} collective-permute-done((bf16[3,208,128]{2,1,0:T(8,128)(2,1)S(1)}, bf16[3,208,128]{2,1,0:T(8,128)(2,1)S(1)}, u32[]{:S(2)}, u32[]{:S(2)}) %collective-permute-start.3) | collective-permute-done | bytes 159776 | tf_op jit(solution)/shard_map/ppermute | solution.py:186
  82.2 2.2 %collective-permute-done.4.d_ref = bf16[3,208,128]{2,1,0:T(8,128)(2,1)S(1)} collective-permute-done((bf16[3,208,128]{2,1,0:T(8,128)(2,1)S(1)}, bf16[3,208,128]{2,1,0:T(8,128)(2,1)S(1)}, u32[]{:S(2)}, u32[]{:S(2)}) %collective-permute-start.4) | collective-permute-done | bytes 159776 | tf_op jit(solution)/shard_map/ppermute | solution.py:186
  84.4 0.0 collective-permute-done.1.a_ref
  84.4 0.0 collective-permute-done.2.b_ref
  84.4 0.2 shard_map.70
  84.5 5.1 %collective-permute-start.5 = (bf16[416,128]{1,0:T(8,128)(2,1)S(1)}, bf16[416,128]{1,0:T(8,128)(2,1)S(1)}, u32[]{:S(2)}, u32[]{:S(2)}) collective-permute-start(bf16[416,128]{1,0:T(8,128)(2,1)S(1)} %get-tuple-element.20), channel_id=1, source_target_pairs={{0,256},{64,320},{128,384},{192,448},{256,512},{320,576},{384,640}... | collective-permute-start | bytes 319496 | tf_op jit(solution)/shard_map/ppermute | solution.py:186
  89.6 4.7 %collective-permute-start.6 = (bf16[416,128]{1,0:T(8,128)(2,1)S(1)}, bf16[416,128]{1,0:T(8,128)(2,1)S(1)}, u32[]{:S(2)}, u32[]{:S(2)}) collective-permute-start(bf16[416,128]{1,0:T(8,128)(2,1)S(1)} %get-tuple-element.21), channel_id=1, source_target_pairs={{0,512},{64,576},{128,640},{192,704},{256,0},{320,64},{384,128},{4... | collective-permute-start | bytes 319496 | tf_op jit(solution)/shard_map/ppermute | solution.py:186
  94.3 4.2 %collective-permute-done.5.a_ref = bf16[416,128]{1,0:T(8,128)(2,1)S(1)} collective-permute-done((bf16[416,128]{1,0:T(8,128)(2,1)S(1)}, bf16[416,128]{1,0:T(8,128)(2,1)S(1)}, u32[]{:S(2)}, u32[]{:S(2)}) %collective-permute-start.5) | collective-permute-done | bytes 106528 | tf_op jit(solution)/shard_map/ppermute | solution.py:186
  98.5 3.9 %collective-permute-done.6.b_ref = bf16[416,128]{1,0:T(8,128)(2,1)S(1)} collective-permute-done((bf16[416,128]{1,0:T(8,128)(2,1)S(1)}, bf16[416,128]{1,0:T(8,128)(2,1)S(1)}, u32[]{:S(2)}, u32[]{:S(2)}) %collective-permute-start.6) | collective-permute-done | bytes 106528 | tf_op jit(solution)/shard_map/ppermute | solution.py:186
  102.5 24.5 %all-gather = bf16[1664,128]{1,0:T(8,128)(2,1)S(1)} all-gather(bf16[416,128]{1,0:T(8,128)(2,1)S(1)} %shard_map.71), channel_id=2, replica_groups={{0,192,384,576},{64,256,448,640},{128,320,512,704},{1,193,385,577},{65,..., dimensions={0}, use_global_device_ids=true | all-gather | bytes 532480 | tf_op jit(solution)/shard_map/all_gather | solution.py:197
  127.0 1.9 %collective-permute-start.8 = (bf16[4,416,128]{2,1,0:T(8,128)(2,1)S(1)}, bf16[4,416,128]{2,1,0:T(8,128)(2,1)S(1)}, u32[]{:S(2)}, u32[]{:S(2)}) collective-permute-start(bf16[4,416,128]{2,1,0:T(8,128)(2,1)S(1)} %bitcast.13), channel_id=1, source_target_pairs={{0,704},{64,0},{128,64},{192,128},{256,192},{320,256},{384,320},{4... | collective-permute-start | bytes 1277960 | tf_op jit(solution)/shard_map/ppermute | solution.py:186
  128.9 3.9 %collective-permute-start.7 = (bf16[4,416,128]{2,1,0:T(8,128)(2,1)S(1)}, bf16[4,416,128]{2,1,0:T(8,128)(2,1)S(1)}, u32[]{:S(2)}, u32[]{:S(2)}) collective-permute-start(bf16[4,416,128]{2,1,0:T(8,128)(2,1)S(1)} %bitcast.14), channel_id=1, source_target_pairs={{0,64},{64,128},{128,192},{192,256},{256,320},{320,384},{384,448},... | collective-permute-start | bytes 1277960 | tf_op jit(solution)/shard_map/ppermute | solution.py:186
  132.8 0.9 shard_map.72.after_ref
  133.8 4.2 %collective-permute-done.8.high_ref = bf16[4,416,128]{2,1,0:T(8,128)(2,1)S(1)} collective-permute-done((bf16[4,416,128]{2,1,0:T(8,128)(2,1)S(1)}, bf16[4,416,128]{2,1,0:T(8,128)(2,1)S(1)}, u32[]{:S(2)}, u32[]{:S(2)}) %collective-permute-start.8) | collective-permute-done | bytes 426016 | tf_op jit(solution)/shard_map/ppermute | solution.py:186
  138.0 3.1 %collective-permute-done.7.low_ref = bf16[4,416,128]{2,1,0:T(8,128)(2,1)S(1)} collective-permute-done((bf16[4,416,128]{2,1,0:T(8,128)(2,1)S(1)}, bf16[4,416,128]{2,1,0:T(8,128)(2,1)S(1)}, u32[]{:S(2)}, u32[]{:S(2)}) %collective-permute-start.7) | collective-permute-done | bytes 426016 | tf_op jit(solution)/shard_map/ppermute | solution.py:186
  141.1 0.8 copy-done
  142.0 2.2 %shard_map.73 = f32[4864,128]{1,0:T(8,128)} custom-call(s32[3]{0:T(128)S(1)} %and_select_fusion.place_ref, f32[128,128]{1,0:T(8,128)S(1)} %copy-done, bf16[4,416,128]{2,1,0:T(8,128)(2,1)S(1)} %collective-permute-done.7.low_ref, bf16[4,416,128]{2,1,0:T(8,128)(2,1)S(1)} %bitcast.16, bf16[4,416,128]{2,1,0:T(8,128)(2,1)S(1)} %collective-permute-done.8.high_ref), custom_call_target="tpu_custom_call" | custom-call | tf_op jit(solution)/shard_map/pallas_call | solution.py:143
  (13 shorter events, 0.1 us)
Async XLA Ops:
  0.6 0.8 copy-start.2
  1.5 37.9 %copy-start.3 = (s32[38,2]{0,1:T(2,128)S(1)}, s32[38,2]{0,1:T(2,128)}, u32[]{:S(2)}) copy-start(s32[38,2]{0,1:T(2,128)} %param.6) | copy-start | bytes 916
  21.3 20.7 %copy-start.1 = (f32[128,512]{1,0:T(8,128)S(1)}, f32[128,512]{1,0:T(8,128)}, u32[]{:S(2)}) copy-start(f32[128,512]{1,0:T(8,128)} %g_ref.1) | copy-start | bytes 786436
  21.3 16.2 %all-to-all-start.1 = ((bf16[4,8,128,128]{3,2,1,0:T(8,128)(2,1)}), bf16[4,8,128,128]{3,2,1,0:T(8,128)(2,1)S(1)}, u32[]{:S(2)}, u32[]{:S(2)}) async-start(bf16[4,8,128,128]{3,2,1,0:T(8,128)(2,1)} %shard_map.68), calls=%async_computation.1 | async-start | bytes 2097152 | tf_op jit(solution)/shard_map/all_to_all | solution.py:182
  37.4 4.5 %collective-permute-start = (bf16[32,128,128]{2,1,0:T(8,128)(2,1)S(1)}, bf16[32,128,128]{2,1,0:T(8,128)(2,1)S(1)}, u32[]{:S(2)}, u32[]{:S(2)}) collective-permute-start(bf16[32,128,128]{2,1,0:T(8,128)(2,1)S(1)} %bitcast.11), channel_id=1, source_target_pairs={{0,1},{1,0},{2,3},{3,2},{4,5},{5,4},{6,7},{7,6},{8,9},{9,8},{10,11... | collective-permute-start | bytes 3145736 | tf_op jit(solution)/shard_map/ppermute | solution.py:240
  47.2 85.7 %all-to-all-start.2 = ((bf16[64,128,128]{2,1,0:T(8,128)(2,1)}), bf16[64,128,128]{2,1,0:T(8,128)(2,1)S(1)}, u32[]{:S(2)}, u32[]{:S(2)}) async-start(bf16[64,128,128]{2,1,0:T(8,128)(2,1)} %get-tuple-element.22), calls=%async_computation.2 | async-start | bytes 4194304 | tf_op jit(solution)/shard_map/all_to_all | solution.py:182
  53.5 30.9 %collective-permute-start.1 = (bf16[3,416,128]{2,1,0:T(8,128)(2,1)S(1)}, bf16[3,416,128]{2,1,0:T(8,128)(2,1)S(1)}, u32[]{:S(2)}, u32[]{:S(2)}) collective-permute-start(bf16[3,416,128]{2,1,0:T(8,128)(2,1)S(1)} %get-tuple-element.15), channel_id=1, source_target_pairs={{0,64},{64,128},{128,192},{192,256},{256,320},{320,384},{384,448},... | collective-permute-start | bytes 958472 | tf_op jit(solution)/shard_map/ppermute | solution.py:186
  57.8 26.6 %collective-permute-start.2 = (bf16[3,416,128]{2,1,0:T(8,128)(2,1)S(1)}, bf16[3,416,128]{2,1,0:T(8,128)(2,1)S(1)}, u32[]{:S(2)}, u32[]{:S(2)}) collective-permute-start(bf16[3,416,128]{2,1,0:T(8,128)(2,1)S(1)} %get-tuple-element.16), channel_id=1, source_target_pairs={{0,704},{64,0},{128,64},{192,128},{256,192},{320,256},{384,320},{4... | collective-permute-start | bytes 958472 | tf_op jit(solution)/shard_map/ppermute | solution.py:186
  70.0 12.2 %collective-permute-start.3 = (bf16[3,208,128]{2,1,0:T(8,128)(2,1)S(1)}, bf16[3,208,128]{2,1,0:T(8,128)(2,1)S(1)}, u32[]{:S(2)}, u32[]{:S(2)}) collective-permute-start(bf16[3,208,128]{2,1,0:T(8,128)(2,1)S(1)} %get-tuple-element.17), channel_id=1, source_target_pairs={{0,128},{64,192},{128,256},{192,320},{256,384},{320,448},{384,512}... | collective-permute-start | bytes 479240 | tf_op jit(solution)/shard_map/ppermute | solution.py:186
  71.9 12.4 %collective-permute-start.4 = (bf16[3,208,128]{2,1,0:T(8,128)(2,1)S(1)}, bf16[3,208,128]{2,1,0:T(8,128)(2,1)S(1)}, u32[]{:S(2)}, u32[]{:S(2)}) collective-permute-start(bf16[3,208,128]{2,1,0:T(8,128)(2,1)S(1)} %get-tuple-element.18), channel_id=1, source_target_pairs={{0,640},{64,704},{128,0},{192,64},{256,128},{320,192},{384,256},{4... | collective-permute-start | bytes 479240 | tf_op jit(solution)/shard_map/ppermute | solution.py:186
  84.5 14.0 %collective-permute-start.5 = (bf16[416,128]{1,0:T(8,128)(2,1)S(1)}, bf16[416,128]{1,0:T(8,128)(2,1)S(1)}, u32[]{:S(2)}, u32[]{:S(2)}) collective-permute-start(bf16[416,128]{1,0:T(8,128)(2,1)S(1)} %get-tuple-element.20), channel_id=1, source_target_pairs={{0,256},{64,320},{128,384},{192,448},{256,512},{320,576},{384,640}... | collective-permute-start | bytes 319496 | tf_op jit(solution)/shard_map/ppermute | solution.py:186
  89.6 12.8 %collective-permute-start.6 = (bf16[416,128]{1,0:T(8,128)(2,1)S(1)}, bf16[416,128]{1,0:T(8,128)(2,1)S(1)}, u32[]{:S(2)}, u32[]{:S(2)}) collective-permute-start(bf16[416,128]{1,0:T(8,128)(2,1)S(1)} %get-tuple-element.21), channel_id=1, source_target_pairs={{0,512},{64,576},{128,640},{192,704},{256,0},{320,64},{384,128},{4... | collective-permute-start | bytes 319496 | tf_op jit(solution)/shard_map/ppermute | solution.py:186
  127.0 11.0 %collective-permute-start.8 = (bf16[4,416,128]{2,1,0:T(8,128)(2,1)S(1)}, bf16[4,416,128]{2,1,0:T(8,128)(2,1)S(1)}, u32[]{:S(2)}, u32[]{:S(2)}) collective-permute-start(bf16[4,416,128]{2,1,0:T(8,128)(2,1)S(1)} %bitcast.13), channel_id=1, source_target_pairs={{0,704},{64,0},{128,64},{192,128},{256,192},{320,256},{384,320},{4... | collective-permute-start | bytes 1277960 | tf_op jit(solution)/shard_map/ppermute | solution.py:186
  128.9 12.2 %collective-permute-start.7 = (bf16[4,416,128]{2,1,0:T(8,128)(2,1)S(1)}, bf16[4,416,128]{2,1,0:T(8,128)(2,1)S(1)}, u32[]{:S(2)}, u32[]{:S(2)}) collective-permute-start(bf16[4,416,128]{2,1,0:T(8,128)(2,1)S(1)} %bitcast.14), channel_id=1, source_target_pairs={{0,64},{64,128},{128,192},{192,256},{256,320},{320,384},{384,448},... | collective-permute-start | bytes 1277960 | tf_op jit(solution)/shard_map/ppermute | solution.py:186
  141.1 0.8 copy-start

commit v11 on v10

--- a/solution.py
+++ b/solution.py
@@ -15,7 +15,7 @@
 CHUNK = 416
 SPLIT = 208
 PIECES = 4
-Z_FAR = [[3 * i + r for i in range(4)] for r in range(3)]
+Z_EVEN_ODD = [[2 * i + r for i in range(6)] for r in range(2)]
 F32, BF16 = jnp.float32, jnp.bfloat16
 
 
@@ -94,27 +94,45 @@
     out_ref[...] = (stay_ref[...].astype(F32) + a_ref[...].astype(F32) + b_ref[...].astype(F32)).astype(BF16)
 
 
-def sum_kernel(after_ref, in_ref, out_ref):
+def sum_kernel(after_ref, in_ref, out_ref, token_ref):
     out_ref[...] = jnp.sum(in_ref[...].astype(F32), axis=0)
-
-
-def whole_kernel(place_ref, after_ref, low_ref, mid_ref, high_ref, out_ref, gw_ref, wide_ref, sems):
-    for i, part in enumerate((low_ref, mid_ref, high_ref)):
-        for b in range(4):
-            gw_ref[3 * b + place_ref[i]] = part[b]
+    token_ref[...] = jnp.zeros_like(token_ref)
+
+
+def halve_kernel(in_ref, low_ref, high_ref):
+    low_ref[...] = in_ref[:3]
+    high_ref[...] = in_ref[3:]
+
+
+def write_chunks(first, parts, out_ref, wide_ref, sems):
     rows = out_ref.shape[0]
-    copies = []
-    for j in range(NZ):
-        size = min(CHUNK, rows - j * CHUNK)
-        wide_ref[j, :size] = gw_ref[j, :size].astype(F32)
-        copies.append(
-            pltpu.make_async_copy(
-                wide_ref.at[j, pl.ds(0, size)], out_ref.at[pl.ds(j * CHUNK, size)], sems.at[j]
-            )
-        )
-        copies[-1].start()
-    for copy in copies:
-        copy.wait()
+    for i, part in enumerate(parts):
+        wide_ref[i] = part.astype(F32)
+    for parity in range(2):
+
+        @pl.when(first == parity)
+        def write():
+            copies = []
+            for i in range(len(parts)):
+                at = (2 * i + parity) * CHUNK
+                size = min(CHUNK, rows - at)
+                copies.append(
+                    pltpu.make_async_copy(
+                        wide_ref.at[i, pl.ds(0, size)], out_ref.at[pl.ds(at, size)], sems.at[i]
+                    )
+                )
+                copies[-1].start()
+            for copy in copies:
+                copy.wait()
+
+
+def own_parity_kernel(first_ref, token_ref, mid_ref, out_ref, wide_ref, sems):
+    write_chunks(first_ref[0], [mid_ref[i] for i in range(6)], out_ref, wide_ref, sems)
+
+
+def other_parity_kernel(first_ref, done_ref, low_ref, high_ref, out_ref, wide_ref, sems):
+    parts = [low_ref[i] for i in range(3)] + [high_ref[i] for i in range(3)]
+    write_chunks(1 - first_ref[0], parts, out_ref, wide_ref, sems)
 
 
 def first_spread_kernel(in_ref, out_ref):
@@ -139,14 +157,15 @@
 ORDER = pl.BlockSpec(memory_space=pl.ANY)
 
 
-def call(kernel, specs, ins, outs, scratch=(), out_specs=None):
+def call(kernel, specs, ins, outs, scratch=(), out_specs=None, aliases=None):
     return pl.pallas_call(
         kernel,
         out_shape=outs,
         in_specs=specs,
         out_specs=out_specs or jax.tree.map(lambda _: VMEM, outs),
         scratch_shapes=scratch,
-        compiler_params=pltpu.CompilerParams(vmem_limit_bytes=40 << 20),
+        input_output_aliases=aliases or {},
+        compiler_params=pltpu.CompilerParams(vmem_limit_bytes=20 << 20),
     )(*ins)
 
 
@@ -158,7 +177,7 @@
     slots = wb.shape[0]
     tokens, hidden = grad_act.shape
     cols = hidden // BS
-    full, half = array((3, CHUNK, BS)), array((3, SPLIT, BS))
+    full, half = pltpu.VMEM((3, CHUNK, BS), BF16), pltpu.VMEM((3, SPLIT, BS), BF16)
     return call(
         block_kernel,
         [SMEM] * 5 + [VMEM] * 4,
@@ -194,21 +213,25 @@
     stay, up, down = call(near_kernel, [VMEM] * 5, (keep, *parts), (one,) * 3)
     mine = call(far_kernel, [VMEM] * 3, (stay, shift(up, 4), shift(down, -4)), one)
 
-    mid = lax.all_gather(mine, "dp", axis_index_groups=Z_FAR)
-    grad_x = call(sum_kernel, [ORDER, VMEM], (mid, gx), array((tokens, BS), F32))
-    low, high = shift(mid, 1), shift(mid, -1)
-    place = (jnp.arange(3, dtype=jnp.int32) + lax.axis_index("dp") + 2) % 3
+    mid = lax.all_gather(mine, "dp", axis_index_groups=Z_EVEN_ODD)
+    full = pltpu.VMEM((3, CHUNK, BS), BF16)
+    low, high = call(halve_kernel, [VMEM], (mid,), (full, full))
+    low, high = shift(low, 1), shift(high, -1)
+    grad_x, token = call(
+        sum_kernel, [ORDER, VMEM], (mid, gx), (array((tokens, BS), F32), array((8, BS), F32))
+    )
+    first = (lax.axis_index("dp") % 2).astype(jnp.int32).reshape(1)
+    scratch = [pltpu.VMEM((6, CHUNK, BS), F32), pltpu.SemaphoreType.DMA((6,))]
+    result = pltpu.HBM((slots * BS, BS), F32)
+    grad_w = call(own_parity_kernel, [SMEM, VMEM, VMEM], (first, token, mid), result, scratch, HBM)
     grad_w = call(
-        whole_kernel,
-        [SMEM, ORDER] + [VMEM] * 3,
-        (place, grad_x, low, mid, high),
-        pltpu.HBM((slots * BS, BS), F32),
-        [
-            pltpu.VMEM((NZ, CHUNK, BS), BF16),
-            pltpu.VMEM((NZ, CHUNK, BS), F32),
-            pltpu.SemaphoreType.DMA((NZ,)),
-        ],
+        other_parity_kernel,
+        [SMEM, HBM, VMEM, VMEM],
+        (first, grad_w, low, high),
+        result,
+        scratch,
         HBM,
+        {1: 0},
     )
     return grad_x, grad_w.reshape(slots, BS, BS)
 

time: 145 us -> 149 us (1.028)
  waiting for transfers between devices: 31.3 us -> 28.2 us
  blocking collectives: 43.3 us -> 46.2 us
    ppermute x8, waiting for transfers between devices: 21.9 us -> 18.7 us  [shift(): return lax.ppermute(x, 'dp', [(i, (i + by) % NZ) for i in range(NZ)])]
    all_gather x1, blocking collectives: 24.5 us -> 27.4 us  [reduce_gradients(): mid = lax.all_gather(mine, 'dp', axis_index_groups=Z_EVEN_ODD)]
    pallas_call x7 -> x9, Pallas kernels: 9.53 us -> 10.5 us  [call(): pl.pallas_call(kernel, out_shape=outs, in_specs=specs, out_specs=out_spec...]
  transfers between devices with their start and end apart: 11 -> 11, of which waited for: 8 -> 8; matrix products, arithmetic and copies ran while one was open for 1% -> 1% of each run, Pallas kernels for 1% -> 2%
where the time goes in v11:
time: 149 us; the launch traced here: 147 us
  starting transfers between devices  56.8 us (38%)
  blocking collectives  46.2 us (31%)
  waiting for transfers between devices  28.2 us (19%)
  Pallas kernels  10.5 us (7%)
  local copies, waits for them, and re-layouts  2.22 us (1%)
  other arithmetic  2.01 us (1%)
    ppermute x8, starting transfers between devices, shift(): return lax.ppermute(x, 'dp', [(i, (i + by) % NZ) for i in range(NZ)])  41.2 us
    all_gather x1, blocking collectives, reduce_gradients(): mid = lax.all_gather(mine, 'dp', axis_index_groups=Z_EVEN_ODD)  27.4 us
    all_to_all x1, blocking collectives, swap(): return lax.all_to_all(x, axis, 0, 0, tiled=True, axis_index_groups=groups)  18.8 us
    ppermute x8, waiting for transfers between devices, shift(): return lax.ppermute(x, 'dp', [(i, (i + by) % NZ) for i in range(NZ)])  18.7 us
    all_to_all x2, starting transfers between devices, swap(): return lax.all_to_all(x, axis, 0, 0, tiled=True, axis_index_groups=groups)  13.7 us
    pallas_call x9, Pallas kernels, call(): pl.pallas_call(kernel, out_shape=outs, in_specs=specs, out_specs=out_spec...  10.5 us
    all_to_all x2, waiting for transfers between devices, swap(): return lax.all_to_all(x, axis, 0, 0, tiled=True, axis_index_groups=groups)  8.93 us
  transfers between devices with their start and end apart: 11, of which 8 were waited for; matrix products, arithmetic and copies ran while one was open for 1% of the time, Pallas kernels for 2%

profile of v11, /device:TPU:6, one launch (start us, length us, event | category | flops | bytes accessed | tf_op | source)
XLA Modules:
  0.0 146.8 jit_solution(9656182327519973633)
XLA Ops:
  0.6 0.8 copy-done.1
  1.5 18.8 %all_to_all.15.in_ref = bf16[8,128,128]{2,1,0:T(8,128)(2,1)S(1)} all-to-all(bf16[8,128,128]{2,1,0:T(8,128)(2,1)S(1)} %shard_map.67), channel_id=1, replica_groups={{0,8,16,24,32,40,48,56},{1,9,17,25,33,41,49,57},{2,10,18,26,34,42,50,58..., dimensions={0} | all-to-all | bytes 524288 | tf_op jit(solution)/shard_map/all_to_all | solution.py:201
  20.3 1.0 shard_map.68
  21.3 7.2 %all-to-all-start.1 = ((bf16[4,8,128,128]{3,2,1,0:T(8,128)(2,1)}), bf16[4,8,128,128]{3,2,1,0:T(8,128)(2,1)S(1)}, u32[]{:S(2)}, u32[]{:S(2)}) async-start(bf16[4,8,128,128]{3,2,1,0:T(8,128)(2,1)} %shard_map.68), calls=%async_computation.1 | async-start | bytes 2097152 | tf_op jit(solution)/shard_map/all_to_all | solution.py:201
  28.5 8.9 %all-to-all-done.1 = bf16[4,8,128,128]{3,2,1,0:T(8,128)(2,1)S(1)} async-done(((bf16[4,8,128,128]{3,2,1,0:T(8,128)(2,1)}), bf16[4,8,128,128]{3,2,1,0:T(8,128)(2,1)S(1)}, u32[]{:S(2)}, u32[]{:S(2)}) %all-to-all-start.1) | async-done | bytes 1048608 | tf_op jit(solution)/shard_map/all_to_all | solution.py:201
  37.4 1.9 %collective-permute-start = (bf16[32,128,128]{2,1,0:T(8,128)(2,1)S(1)}, bf16[32,128,128]{2,1,0:T(8,128)(2,1)S(1)}, u32[]{:S(2)}, u32[]{:S(2)}) collective-permute-start(bf16[32,128,128]{2,1,0:T(8,128)(2,1)S(1)} %bitcast.15), channel_id=1, source_target_pairs={{0,1},{1,0},{2,3},{3,2},{4,5},{5,4},{6,7},{7,6},{8,9},{9,8},{10,11... | collective-permute-start | bytes 3145736 | tf_op jit(solution)/shard_map/ppermute | solution.py:263
  39.4 2.0 %multiply_convert_fusion.w_ref = bf16[38,128,128]{2,1,0:T(8,128)(2,1)S(1)} fusion(f32[38,128,128]{2,1,0:T(8,128)} %param.5, f32[38]{0:T(128)S(1)} %fusion.3.live_ref), kind=kLoop, calls=%fused_computation | loop fusion | flops 1245184 | bytes 3735704 | tf_op jit(solution)/shard_map/convert_element_type | solution.py:249
  41.4 0.6 collective-permute-done.sib_ref
  42.0 5.2 %shard_map.69 = (f32[128,512]{1,0:T(8,128)}, bf16[64,128,128]{2,1,0:T(8,128)(2,1)}, bf16[3,416,128]{2,1,0:T(8,128)(2,1)S(1)}, bf16[3,416,128]{2,1,0:T(8,128)(2,1...) custom-call(s32[38]{0:T(128)S(1)} %fusion.5.idx_ref, ...), custom_call_target="tpu_custom_call" | custom-call | tf_op jit(solution)/shard_map/pallas_call | solution.py:161
  47.2 0.7 copy-done.2
  47.9 0.7 copy-done.4
  48.6 6.4 %all-to-all-start.2 = ((bf16[64,128,128]{2,1,0:T(8,128)(2,1)}), bf16[64,128,128]{2,1,0:T(8,128)(2,1)S(1)}, u32[]{:S(2)}, u32[]{:S(2)}) async-start(bf16[64,128,128]{2,1,0:T(8,128)(2,1)} %get-tuple-element.26), calls=%async_computation.2 | async-start | bytes 4194304 | tf_op jit(solution)/shard_map/all_to_all | solution.py:201
  55.0 4.3 %collective-permute-start.1 = (bf16[3,416,128]{2,1,0:T(8,128)(2,1)S(1)}, bf16[3,416,128]{2,1,0:T(8,128)(2,1)S(1)}, u32[]{:S(2)}, u32[]{:S(2)}) collective-permute-start(bf16[3,416,128]{2,1,0:T(8,128)(2,1)S(1)} %copy-done.3), channel_id=1, source_target_pairs={{0,64},{64,128},{128,192},{192,256},{256,320},{320,384},{384,448},... | collective-permute-start | bytes 958472 | tf_op jit(solution)/shard_map/ppermute | solution.py:205
  59.3 12.2 %collective-permute-start.2 = (bf16[3,416,128]{2,1,0:T(8,128)(2,1)S(1)}, bf16[3,416,128]{2,1,0:T(8,128)(2,1)S(1)}, u32[]{:S(2)}, u32[]{:S(2)}) collective-permute-start(bf16[3,416,128]{2,1,0:T(8,128)(2,1)S(1)} %get-tuple-element.20), channel_id=1, source_target_pairs={{0,704},{64,0},{128,64},{192,128},{256,192},{320,256},{384,320},{4... | collective-permute-start | bytes 958472 | tf_op jit(solution)/shard_map/ppermute | solution.py:205
  71.5 1.9 %collective-permute-start.3 = (bf16[3,208,128]{2,1,0:T(8,128)(2,1)S(1)}, bf16[3,208,128]{2,1,0:T(8,128)(2,1)S(1)}, u32[]{:S(2)}, u32[]{:S(2)}) collective-permute-start(bf16[3,208,128]{2,1,0:T(8,128)(2,1)S(1)} %copy-done.5), channel_id=1, source_target_pairs={{0,128},{64,192},{128,256},{192,320},{256,384},{320,448},{384,512}... | collective-permute-start | bytes 479240 | tf_op jit(solution)/shard_map/ppermute | solution.py:205
  73.5 6.0 %collective-permute-start.4 = (bf16[3,208,128]{2,1,0:T(8,128)(2,1)S(1)}, bf16[3,208,128]{2,1,0:T(8,128)(2,1)S(1)}, u32[]{:S(2)}, u32[]{:S(2)}) collective-permute-start(bf16[3,208,128]{2,1,0:T(8,128)(2,1)S(1)} %get-tuple-element.22), channel_id=1, source_target_pairs={{0,640},{64,704},{128,0},{192,64},{256,128},{320,192},{384,256},{4... | collective-permute-start | bytes 479240 | tf_op jit(solution)/shard_map/ppermute | solution.py:205
  79.5 4.2 %collective-permute-done.3.c_ref = bf16[3,208,128]{2,1,0:T(8,128)(2,1)S(1)} collective-permute-done((bf16[3,208,128]{2,1,0:T(8,128)(2,1)S(1)}, bf16[3,208,128]{2,1,0:T(8,128)(2,1)S(1)}, u32[]{:S(2)}, u32[]{:S(2)}) %collective-permute-start.3) | collective-permute-done | bytes 159776 | tf_op jit(solution)/shard_map/ppermute | solution.py:205
  83.7 2.2 %collective-permute-done.4.d_ref = bf16[3,208,128]{2,1,0:T(8,128)(2,1)S(1)} collective-permute-done((bf16[3,208,128]{2,1,0:T(8,128)(2,1)S(1)}, bf16[3,208,128]{2,1,0:T(8,128)(2,1)S(1)}, u32[]{:S(2)}, u32[]{:S(2)}) %collective-permute-start.4) | collective-permute-done | bytes 159776 | tf_op jit(solution)/shard_map/ppermute | solution.py:205
  85.9 0.2 shard_map.70
  86.1 5.1 %collective-permute-start.5 = (bf16[416,128]{1,0:T(8,128)(2,1)S(1)}, bf16[416,128]{1,0:T(8,128)(2,1)S(1)}, u32[]{:S(2)}, u32[]{:S(2)}) collective-permute-start(bf16[416,128]{1,0:T(8,128)(2,1)S(1)} %get-tuple-element.24), channel_id=1, source_target_pairs={{0,256},{64,320},{128,384},{192,448},{256,512},{320,576},{384,640}... | collective-permute-start | bytes 319496 | tf_op jit(solution)/shard_map/ppermute | solution.py:205
  91.2 4.7 %collective-permute-start.6 = (bf16[416,128]{1,0:T(8,128)(2,1)S(1)}, bf16[416,128]{1,0:T(8,128)(2,1)S(1)}, u32[]{:S(2)}, u32[]{:S(2)}) collective-permute-start(bf16[416,128]{1,0:T(8,128)(2,1)S(1)} %get-tuple-element.25), channel_id=1, source_target_pairs={{0,512},{64,576},{128,640},{192,704},{256,0},{320,64},{384,128},{4... | collective-permute-start | bytes 319496 | tf_op jit(solution)/shard_map/ppermute | solution.py:205
  95.8 4.2 %collective-permute-done.5.a_ref = bf16[416,128]{1,0:T(8,128)(2,1)S(1)} collective-permute-done((bf16[416,128]{1,0:T(8,128)(2,1)S(1)}, bf16[416,128]{1,0:T(8,128)(2,1)S(1)}, u32[]{:S(2)}, u32[]{:S(2)}) %collective-permute-start.5) | collective-permute-done | bytes 106528 | tf_op jit(solution)/shard_map/ppermute | solution.py:205
  100.1 3.9 %collective-permute-done.6.b_ref = bf16[416,128]{1,0:T(8,128)(2,1)S(1)} collective-permute-done((bf16[416,128]{1,0:T(8,128)(2,1)S(1)}, bf16[416,128]{1,0:T(8,128)(2,1)S(1)}, u32[]{:S(2)}, u32[]{:S(2)}) %collective-permute-start.6) | collective-permute-done | bytes 106528 | tf_op jit(solution)/shard_map/ppermute | solution.py:205
  104.0 27.4 %all-gather = bf16[2496,128]{1,0:T(8,128)(2,1)S(1)} all-gather(bf16[416,128]{1,0:T(8,128)(2,1)S(1)} %shard_map.71), channel_id=2, replica_groups={{0,128,256,384,512,640},{64,192,320,448,576,704},{1,129,257,385,513,641..., dimensions={0}, use_global_device_ids=true | all-gather | bytes 745472 | tf_op jit(solution)/shard_map/all_gather | solution.py:216
  131.4 0.9 shard_map.74
  132.3 1.9 %collective-permute-start.7 = (bf16[3,416,128]{2,1,0:T(8,128)(2,1)}, bf16[3,416,128]{2,1,0:T(8,128)(2,1)S(1)}, u32[]{:S(2)}, u32[]{:S(2)}) collective-permute-start(bf16[3,416,128]{2,1,0:T(8,128)(2,1)} %get-tuple-element.29), channel_id=1, source_target_pairs={{0,64},{64,128},{128,192},{192,256},{256,320},{320,384},{384,448},... | collective-permute-start | bytes 958472 | tf_op jit(solution)/shard_map/ppermute | solution.py:205
  134.2 5.1 %collective-permute-start.8 = (bf16[3,416,128]{2,1,0:T(8,128)(2,1)}, bf16[3,416,128]{2,1,0:T(8,128)(2,1)S(1)}, u32[]{:S(2)}, u32[]{:S(2)}) collective-permute-start(bf16[3,416,128]{2,1,0:T(8,128)(2,1)} %get-tuple-element.30), channel_id=1, source_target_pairs={{0,704},{64,0},{128,64},{192,128},{256,192},{320,256},{384,320},{4... | collective-permute-start | bytes 958472 | tf_op jit(solution)/shard_map/ppermute | solution.py:205
  139.4 0.9 shard_map.72
  140.4 1.2 shard_map.73.done_ref
  141.5 2.1 %collective-permute-done.7.low_ref = bf16[3,416,128]{2,1,0:T(8,128)(2,1)S(1)} collective-permute-done((bf16[3,416,128]{2,1,0:T(8,128)(2,1)}, bf16[3,416,128]{2,1,0:T(8,128)(2,1)S(1)}, u32[]{:S(2)}, u32[]{:S(2)}) %collective-permute-start.7) | collective-permute-done | bytes 319520 | tf_op jit(solution)/shard_map/ppermute | solution.py:205
  143.7 2.0 %collective-permute-done.8.high_ref = bf16[3,416,128]{2,1,0:T(8,128)(2,1)S(1)} collective-permute-done((bf16[3,416,128]{2,1,0:T(8,128)(2,1)}, bf16[3,416,128]{2,1,0:T(8,128)(2,1)S(1)}, u32[]{:S(2)}, u32[]{:S(2)}) %collective-permute-start.8) | collective-permute-done | bytes 319520 | tf_op jit(solution)/shard_map/ppermute | solution.py:205
  145.7 1.2 shard_map.75
  (20 shorter events, 0.1 us)
Async XLA Ops:
  0.6 0.8 copy-start.1
  1.5 37.9 %copy-start.6 = (s32[38,2]{0,1:T(2,128)S(1)}, s32[38,2]{0,1:T(2,128)}, u32[]{:S(2)}) copy-start(s32[38,2]{0,1:T(2,128)} %param.6) | copy-start | bytes 916
  21.3 20.7 %copy-start = (f32[128,512]{1,0:T(8,128)S(1)}, f32[128,512]{1,0:T(8,128)}, u32[]{:S(2)}) copy-start(f32[128,512]{1,0:T(8,128)} %g_ref.1) | copy-start | bytes 786436
  21.3 16.2 %all-to-all-start.1 = ((bf16[4,8,128,128]{3,2,1,0:T(8,128)(2,1)}), bf16[4,8,128,128]{3,2,1,0:T(8,128)(2,1)S(1)}, u32[]{:S(2)}, u32[]{:S(2)}) async-start(bf16[4,8,128,128]{3,2,1,0:T(8,128)(2,1)} %shard_map.68), calls=%async_computation.1 | async-start | bytes 2097152 | tf_op jit(solution)/shard_map/all_to_all | solution.py:201
  37.4 4.5 %collective-permute-start = (bf16[32,128,128]{2,1,0:T(8,128)(2,1)S(1)}, bf16[32,128,128]{2,1,0:T(8,128)(2,1)S(1)}, u32[]{:S(2)}, u32[]{:S(2)}) collective-permute-start(bf16[32,128,128]{2,1,0:T(8,128)(2,1)S(1)} %bitcast.15), channel_id=1, source_target_pairs={{0,1},{1,0},{2,3},{3,2},{4,5},{5,4},{6,7},{7,6},{8,9},{9,8},{10,11... | collective-permute-start | bytes 3145736 | tf_op jit(solution)/shard_map/ppermute | solution.py:263
  47.2 0.7 copy-start.2
  47.9 0.7 copy-start.4
  48.5 6.4 %copy-start.3 = (bf16[3,416,128]{2,1,0:T(8,128)(2,1)S(1)}, bf16[3,416,128]{2,1,0:T(8,128)(2,1)}, u32[]{:S(2)}) copy-start(bf16[3,416,128]{2,1,0:T(8,128)(2,1)} %copy-done.2) | copy-start | bytes 958468
  48.5 23.0 %copy-start.5 = (bf16[3,208,128]{2,1,0:T(8,128)(2,1)S(1)}, bf16[3,208,128]{2,1,0:T(8,128)(2,1)}, u32[]{:S(2)}) copy-start(bf16[3,208,128]{2,1,0:T(8,128)(2,1)} %copy-done.4) | copy-start | bytes 479236
  48.6 90.8 %all-to-all-start.2 = ((bf16[64,128,128]{2,1,0:T(8,128)(2,1)}), bf16[64,128,128]{2,1,0:T(8,128)(2,1)S(1)}, u32[]{:S(2)}, u32[]{:S(2)}) async-start(bf16[64,128,128]{2,1,0:T(8,128)(2,1)} %get-tuple-element.26), calls=%async_computation.2 | async-start | bytes 4194304 | tf_op jit(solution)/shard_map/all_to_all | solution.py:201
  55.0 30.9 %collective-permute-start.1 = (bf16[3,416,128]{2,1,0:T(8,128)(2,1)S(1)}, bf16[3,416,128]{2,1,0:T(8,128)(2,1)S(1)}, u32[]{:S(2)}, u32[]{:S(2)}) collective-permute-start(bf16[3,416,128]{2,1,0:T(8,128)(2,1)S(1)} %copy-done.3), channel_id=1, source_target_pairs={{0,64},{64,128},{128,192},{192,256},{256,320},{320,384},{384,448},... | collective-permute-start | bytes 958472 | tf_op jit(solution)/shard_map/ppermute | solution.py:205
  59.3 26.6 %collective-permute-start.2 = (bf16[3,416,128]{2,1,0:T(8,128)(2,1)S(1)}, bf16[3,416,128]{2,1,0:T(8,128)(2,1)S(1)}, u32[]{:S(2)}, u32[]{:S(2)}) collective-permute-start(bf16[3,416,128]{2,1,0:T(8,128)(2,1)S(1)} %get-tuple-element.20), channel_id=1, source_target_pairs={{0,704},{64,0},{128,64},{192,128},{256,192},{320,256},{384,320},{4... | collective-permute-start | bytes 958472 | tf_op jit(solution)/shard_map/ppermute | solution.py:205
  71.5 12.2 %collective-permute-start.3 = (bf16[3,208,128]{2,1,0:T(8,128)(2,1)S(1)}, bf16[3,208,128]{2,1,0:T(8,128)(2,1)S(1)}, u32[]{:S(2)}, u32[]{:S(2)}) collective-permute-start(bf16[3,208,128]{2,1,0:T(8,128)(2,1)S(1)} %copy-done.5), channel_id=1, source_target_pairs={{0,128},{64,192},{128,256},{192,320},{256,384},{320,448},{384,512}... | collective-permute-start | bytes 479240 | tf_op jit(solution)/shard_map/ppermute | solution.py:205
  73.5 12.4 %collective-permute-start.4 = (bf16[3,208,128]{2,1,0:T(8,128)(2,1)S(1)}, bf16[3,208,128]{2,1,0:T(8,128)(2,1)S(1)}, u32[]{:S(2)}, u32[]{:S(2)}) collective-permute-start(bf16[3,208,128]{2,1,0:T(8,128)(2,1)S(1)} %get-tuple-element.22), channel_id=1, source_target_pairs={{0,640},{64,704},{128,0},{192,64},{256,128},{320,192},{384,256},{4... | collective-permute-start | bytes 479240 | tf_op jit(solution)/shard_map/ppermute | solution.py:205
  86.1 14.0 %collective-permute-start.5 = (bf16[416,128]{1,0:T(8,128)(2,1)S(1)}, bf16[416,128]{1,0:T(8,128)(2,1)S(1)}, u32[]{:S(2)}, u32[]{:S(2)}) collective-permute-start(bf16[416,128]{1,0:T(8,128)(2,1)S(1)} %get-tuple-element.24), channel_id=1, source_target_pairs={{0,256},{64,320},{128,384},{192,448},{256,512},{320,576},{384,640}... | collective-permute-start | bytes 319496 | tf_op jit(solution)/shard_map/ppermute | solution.py:205
  91.2 12.8 %collective-permute-start.6 = (bf16[416,128]{1,0:T(8,128)(2,1)S(1)}, bf16[416,128]{1,0:T(8,128)(2,1)S(1)}, u32[]{:S(2)}, u32[]{:S(2)}) collective-permute-start(bf16[416,128]{1,0:T(8,128)(2,1)S(1)} %get-tuple-element.25), channel_id=1, source_target_pairs={{0,512},{64,576},{128,640},{192,704},{256,0},{320,64},{384,128},{4... | collective-permute-start | bytes 319496 | tf_op jit(solution)/shard_map/ppermute | solution.py:205
  132.3 11.3 %collective-permute-start.7 = (bf16[3,416,128]{2,1,0:T(8,128)(2,1)}, bf16[3,416,128]{2,1,0:T(8,128)(2,1)S(1)}, u32[]{:S(2)}, u32[]{:S(2)}) collective-permute-start(bf16[3,416,128]{2,1,0:T(8,128)(2,1)} %get-tuple-element.29), channel_id=1, source_target_pairs={{0,64},{64,128},{128,192},{192,256},{256,320},{320,384},{384,448},... | collective-permute-start | bytes 958472 | tf_op jit(solution)/shard_map/ppermute | solution.py:205
  134.2 11.4 %collective-permute-start.8 = (bf16[3,416,128]{2,1,0:T(8,128)(2,1)}, bf16[3,416,128]{2,1,0:T(8,128)(2,1)S(1)}, u32[]{:S(2)}, u32[]{:S(2)}) collective-permute-start(bf16[3,416,128]{2,1,0:T(8,128)(2,1)} %get-tuple-element.30), channel_id=1, source_target_pairs={{0,704},{64,0},{128,64},{192,128},{256,192},{320,256},{384,320},{4... | collective-permute-start | bytes 958472 | tf_op jit(solution)/shard_map/ppermute | solution.py:205

commit v12 on v11

--- a/solution.py
+++ b/solution.py
@@ -15,7 +15,7 @@
 CHUNK = 416
 SPLIT = 208
 PIECES = 4
-Z_EVEN_ODD = [[2 * i + r for i in range(6)] for r in range(2)]
+Z_FAR = [[3 * i + r for i in range(4)] for r in range(3)]
 F32, BF16 = jnp.float32, jnp.bfloat16
 
 
@@ -99,40 +99,38 @@
     token_ref[...] = jnp.zeros_like(token_ref)
 
 
-def halve_kernel(in_ref, low_ref, high_ref):
-    low_ref[...] = in_ref[:3]
-    high_ref[...] = in_ref[3:]
-
-
-def write_chunks(first, parts, out_ref, wide_ref, sems):
+def write_chunks(own, groups, out_ref, wide_ref, sems):
     rows = out_ref.shape[0]
-    for i, part in enumerate(parts):
-        wide_ref[i] = part.astype(F32)
-    for parity in range(2):
-
-        @pl.when(first == parity)
+    for g, (step, part_ref) in enumerate(groups):
+        for b in range(4):
+            wide_ref[4 * g + b] = part_ref[b].astype(F32)
+    for value in range(3):
+
+        @pl.when(own == value)
         def write():
             copies = []
-            for i in range(len(parts)):
-                at = (2 * i + parity) * CHUNK
-                size = min(CHUNK, rows - at)
-                copies.append(
-                    pltpu.make_async_copy(
-                        wide_ref.at[i, pl.ds(0, size)], out_ref.at[pl.ds(at, size)], sems.at[i]
+            for g, (step, part_ref) in enumerate(groups):
+                for b in range(4):
+                    at = (3 * b + (value + step) % 3) * CHUNK
+                    size = min(CHUNK, rows - at)
+                    copies.append(
+                        pltpu.make_async_copy(
+                            wide_ref.at[4 * g + b, pl.ds(0, size)],
+                            out_ref.at[pl.ds(at, size)],
+                            sems.at[4 * g + b],
+                        )
                     )
-                )
-                copies[-1].start()
+                    copies[-1].start()
             for copy in copies:
                 copy.wait()
 
 
-def own_parity_kernel(first_ref, token_ref, mid_ref, out_ref, wide_ref, sems):
-    write_chunks(first_ref[0], [mid_ref[i] for i in range(6)], out_ref, wide_ref, sems)
-
-
-def other_parity_kernel(first_ref, done_ref, low_ref, high_ref, out_ref, wide_ref, sems):
-    parts = [low_ref[i] for i in range(3)] + [high_ref[i] for i in range(3)]
-    write_chunks(1 - first_ref[0], parts, out_ref, wide_ref, sems)
+def own_kernel(own_ref, token_ref, mid_ref, out_ref, wide_ref, sems):
+    write_chunks(own_ref[0], [(0, mid_ref)], out_ref, wide_ref, sems)
+
+
+def rest_kernel(own_ref, done_ref, low_ref, high_ref, out_ref, wide_ref, sems):
+    write_chunks(own_ref[0], [(2, low_ref), (1, high_ref)], out_ref, wide_ref, sems)
 
 
 def first_spread_kernel(in_ref, out_ref):
@@ -165,7 +163,7 @@
         out_specs=out_specs or jax.tree.map(lambda _: VMEM, outs),
         scratch_shapes=scratch,
         input_output_aliases=aliases or {},
-        compiler_params=pltpu.CompilerParams(vmem_limit_bytes=20 << 20),
+        compiler_params=pltpu.CompilerParams(vmem_limit_bytes=40 << 20),
     )(*ins)
 
 
@@ -177,7 +175,7 @@
     slots = wb.shape[0]
     tokens, hidden = grad_act.shape
     cols = hidden // BS
-    full, half = pltpu.VMEM((3, CHUNK, BS), BF16), pltpu.VMEM((3, SPLIT, BS), BF16)
+    full, half = array((3, CHUNK, BS)), array((3, SPLIT, BS))
     return call(
         block_kernel,
         [SMEM] * 5 + [VMEM] * 4,
@@ -213,23 +211,27 @@
     stay, up, down = call(near_kernel, [VMEM] * 5, (keep, *parts), (one,) * 3)
     mine = call(far_kernel, [VMEM] * 3, (stay, shift(up, 4), shift(down, -4)), one)
 
-    mid = lax.all_gather(mine, "dp", axis_index_groups=Z_EVEN_ODD)
-    full = pltpu.VMEM((3, CHUNK, BS), BF16)
-    low, high = call(halve_kernel, [VMEM], (mid,), (full, full))
-    low, high = shift(low, 1), shift(high, -1)
+    mid = lax.all_gather(mine, "dp", axis_index_groups=Z_FAR)
     grad_x, token = call(
         sum_kernel, [ORDER, VMEM], (mid, gx), (array((tokens, BS), F32), array((8, BS), F32))
     )
-    first = (lax.axis_index("dp") % 2).astype(jnp.int32).reshape(1)
-    scratch = [pltpu.VMEM((6, CHUNK, BS), F32), pltpu.SemaphoreType.DMA((6,))]
+    low, high = shift(mid, 1), shift(mid, -1)
+    own = (lax.axis_index("dp") % 3).astype(jnp.int32).reshape(1)
     result = pltpu.HBM((slots * BS, BS), F32)
-    grad_w = call(own_parity_kernel, [SMEM, VMEM, VMEM], (first, token, mid), result, scratch, HBM)
     grad_w = call(
-        other_parity_kernel,
+        own_kernel,
+        [SMEM, VMEM, VMEM],
+        (own, token, mid),
+        result,
+        [pltpu.VMEM((4, CHUNK, BS), F32), pltpu.SemaphoreType.DMA((4,))],
+        HBM,
+    )
+    grad_w = call(
+        rest_kernel,
         [SMEM, HBM, VMEM, VMEM],
-        (first, grad_w, low, high),
+        (own, grad_w, low, high),
         result,
-        scratch,
+        [pltpu.VMEM((8, CHUNK, BS), F32), pltpu.SemaphoreType.DMA((8,))],
         HBM,
         {1: 0},
     )

time: 149 us -> 143 us (0.960); the launches traced: 147 us -> 142 us
  blocking collectives: 46.2 us -> 43.3 us
  waiting for transfers between devices: 28.2 us -> 30.4 us
    all_gather x1, blocking collectives: 27.4 us -> 24.5 us  [reduce_gradients(): mid = lax.all_gather(mine, 'dp', axis_index_groups=Z_FAR)]
    ppermute x8, waiting for transfers between devices: 18.7 us -> 20.9 us  [shift(): return lax.ppermute(x, 'dp', [(i, (i + by) % NZ) for i in range(NZ)])]
    pallas_call x9 -> x8, Pallas kernels: 10.5 us -> 9.67 us  [call(): pl.pallas_call(kernel, out_shape=outs, in_specs=specs, out_specs=out_spec...]
where the time goes in v12:
time: 143 us; the launch traced here: 142 us
  starting transfers between devices  55.5 us (39%)
  blocking collectives  43.3 us (30%)
  waiting for transfers between devices  30.4 us (21%)
  Pallas kernels  9.67 us (7%)
  other arithmetic  2.01 us (1%)
    ppermute x8, starting transfers between devices, shift(): return lax.ppermute(x, 'dp', [(i, (i + by) % NZ) for i in range(NZ)])  40 us
    all_gather x1, blocking collectives, reduce_gradients(): mid = lax.all_gather(mine, 'dp', axis_index_groups=Z_FAR)  24.5 us
    ppermute x8, waiting for transfers between devices, shift(): return lax.ppermute(x, 'dp', [(i, (i + by) % NZ) for i in range(NZ)])  20.9 us
    all_to_all x1, blocking collectives, swap(): return lax.all_to_all(x, axis, 0, 0, tiled=True, axis_index_groups=groups)  18.8 us
    all_to_all x2, starting transfers between devices, swap(): return lax.all_to_all(x, axis, 0, 0, tiled=True, axis_index_groups=groups)  13.5 us
    pallas_call x8, Pallas kernels, call(): pl.pallas_call(kernel, out_shape=outs, in_specs=specs, out_specs=out_spec...  9.67 us
    all_to_all x2, waiting for transfers between devices, swap(): return lax.all_to_all(x, axis, 0, 0, tiled=True, axis_index_groups=groups)  8.93 us
  transfers between devices with their start and end apart: 11, of which 8 were waited for; matrix products, arithmetic and copies ran while one was open for 1% of the time, Pallas kernels for 2%

profile of v12, /device:TPU:6, one launch (start us, length us, event | category | flops | bytes accessed | tf_op | source)
XLA Modules:
  0.0 142.5 jit_solution(1922311912337702795)
XLA Ops:
  0.6 0.8 copy-done.1
  1.5 18.8 %all_to_all.15.in_ref = bf16[8,128,128]{2,1,0:T(8,128)(2,1)S(1)} all-to-all(bf16[8,128,128]{2,1,0:T(8,128)(2,1)S(1)} %shard_map.67), channel_id=1, replica_groups={{0,8,16,24,32,40,48,56},{1,9,17,25,33,41,49,57},{2,10,18,26,34,42,50,58..., dimensions={0} | all-to-all | bytes 524288 | tf_op jit(solution)/shard_map/all_to_all | solution.py:199
  20.3 1.0 shard_map.68
  21.3 0.0 copy-start
  21.3 7.2 %all-to-all-start.1 = ((bf16[4,8,128,128]{3,2,1,0:T(8,128)(2,1)}), bf16[4,8,128,128]{3,2,1,0:T(8,128)(2,1)S(1)}, u32[]{:S(2)}, u32[]{:S(2)}) async-start(bf16[4,8,128,128]{3,2,1,0:T(8,128)(2,1)} %shard_map.68), calls=%async_computation.1 | async-start | bytes 2097152 | tf_op jit(solution)/shard_map/all_to_all | solution.py:199
  28.5 8.9 %all-to-all-done.1 = bf16[4,8,128,128]{3,2,1,0:T(8,128)(2,1)S(1)} async-done(((bf16[4,8,128,128]{3,2,1,0:T(8,128)(2,1)}), bf16[4,8,128,128]{3,2,1,0:T(8,128)(2,1)S(1)}, u32[]{:S(2)}, u32[]{:S(2)}) %all-to-all-start.1) | async-done | bytes 1048608 | tf_op jit(solution)/shard_map/all_to_all | solution.py:199
  37.4 1.9 %collective-permute-start = (bf16[32,128,128]{2,1,0:T(8,128)(2,1)S(1)}, bf16[32,128,128]{2,1,0:T(8,128)(2,1)S(1)}, u32[]{:S(2)}, u32[]{:S(2)}) collective-permute-start(bf16[32,128,128]{2,1,0:T(8,128)(2,1)S(1)} %bitcast.12), channel_id=1, source_target_pairs={{0,1},{1,0},{2,3},{3,2},{4,5},{5,4},{6,7},{7,6},{8,9},{9,8},{10,11... | collective-permute-start | bytes 3145736 | tf_op jit(solution)/shard_map/ppermute | solution.py:265
  39.4 2.0 %multiply_convert_fusion.w_ref = bf16[38,128,128]{2,1,0:T(8,128)(2,1)S(1)} fusion(f32[38,128,128]{2,1,0:T(8,128)} %param.5, f32[38]{0:T(128)S(1)} %fusion.3.live_ref), kind=kLoop, calls=%fused_computation | loop fusion | flops 1245184 | bytes 3735704 | tf_op jit(solution)/shard_map/convert_element_type | solution.py:251
  41.4 0.6 collective-permute-done.sib_ref
  42.0 5.2 %shard_map.69 = (f32[128,512]{1,0:T(8,128)}, bf16[64,128,128]{2,1,0:T(8,128)(2,1)}, bf16[3,416,128]{2,1,0:T(8,128)(2,1)S(1)}, bf16[3,416,128]{2,1,0:T(8,128)(2,1...) custom-call(s32[38]{0:T(128)S(1)} %fusion.5.idx_ref, ...), custom_call_target="tpu_custom_call" | custom-call | tf_op jit(solution)/shard_map/pallas_call | solution.py:159
  47.2 6.3 %all-to-all-start.2 = ((bf16[64,128,128]{2,1,0:T(8,128)(2,1)}), bf16[64,128,128]{2,1,0:T(8,128)(2,1)S(1)}, u32[]{:S(2)}, u32[]{:S(2)}) async-start(bf16[64,128,128]{2,1,0:T(8,128)(2,1)} %get-tuple-element.24), calls=%async_computation.2 | async-start | bytes 4194304 | tf_op jit(solution)/shard_map/all_to_all | solution.py:199
  53.5 4.3 %collective-permute-start.1 = (bf16[3,416,128]{2,1,0:T(8,128)(2,1)S(1)}, bf16[3,416,128]{2,1,0:T(8,128)(2,1)S(1)}, u32[]{:S(2)}, u32[]{:S(2)}) collective-permute-start(bf16[3,416,128]{2,1,0:T(8,128)(2,1)S(1)} %get-tuple-element.17), channel_id=1, source_target_pairs={{0,64},{64,128},{128,192},{192,256},{256,320},{320,384},{384,448},... | collective-permute-start | bytes 958472 | tf_op jit(solution)/shard_map/ppermute | solution.py:203
  57.8 12.2 %collective-permute-start.2 = (bf16[3,416,128]{2,1,0:T(8,128)(2,1)S(1)}, bf16[3,416,128]{2,1,0:T(8,128)(2,1)S(1)}, u32[]{:S(2)}, u32[]{:S(2)}) collective-permute-start(bf16[3,416,128]{2,1,0:T(8,128)(2,1)S(1)} %get-tuple-element.18), channel_id=1, source_target_pairs={{0,704},{64,0},{128,64},{192,128},{256,192},{320,256},{384,320},{4... | collective-permute-start | bytes 958472 | tf_op jit(solution)/shard_map/ppermute | solution.py:203
  70.0 1.9 %collective-permute-start.3 = (bf16[3,208,128]{2,1,0:T(8,128)(2,1)S(1)}, bf16[3,208,128]{2,1,0:T(8,128)(2,1)S(1)}, u32[]{:S(2)}, u32[]{:S(2)}) collective-permute-start(bf16[3,208,128]{2,1,0:T(8,128)(2,1)S(1)} %get-tuple-element.19), channel_id=1, source_target_pairs={{0,128},{64,192},{128,256},{192,320},{256,384},{320,448},{384,512}... | collective-permute-start | bytes 479240 | tf_op jit(solution)/shard_map/ppermute | solution.py:203
  71.9 6.0 %collective-permute-start.4 = (bf16[3,208,128]{2,1,0:T(8,128)(2,1)S(1)}, bf16[3,208,128]{2,1,0:T(8,128)(2,1)S(1)}, u32[]{:S(2)}, u32[]{:S(2)}) collective-permute-start(bf16[3,208,128]{2,1,0:T(8,128)(2,1)S(1)} %get-tuple-element.20), channel_id=1, source_target_pairs={{0,640},{64,704},{128,0},{192,64},{256,128},{320,192},{384,256},{4... | collective-permute-start | bytes 479240 | tf_op jit(solution)/shard_map/ppermute | solution.py:203
  78.0 4.3 %collective-permute-done.3.c_ref = bf16[3,208,128]{2,1,0:T(8,128)(2,1)S(1)} collective-permute-done((bf16[3,208,128]{2,1,0:T(8,128)(2,1)S(1)}, bf16[3,208,128]{2,1,0:T(8,128)(2,1)S(1)}, u32[]{:S(2)}, u32[]{:S(2)}) %collective-permute-start.3) | collective-permute-done | bytes 159776 | tf_op jit(solution)/shard_map/ppermute | solution.py:203
  82.2 2.2 %collective-permute-done.4.d_ref = bf16[3,208,128]{2,1,0:T(8,128)(2,1)S(1)} collective-permute-done((bf16[3,208,128]{2,1,0:T(8,128)(2,1)S(1)}, bf16[3,208,128]{2,1,0:T(8,128)(2,1)S(1)}, u32[]{:S(2)}, u32[]{:S(2)}) %collective-permute-start.4) | collective-permute-done | bytes 159776 | tf_op jit(solution)/shard_map/ppermute | solution.py:203
  84.4 0.0 collective-permute-done.1.a_ref
  84.4 0.0 collective-permute-done.2.b_ref
  84.4 0.2 shard_map.70
  84.5 5.1 %collective-permute-start.5 = (bf16[416,128]{1,0:T(8,128)(2,1)S(1)}, bf16[416,128]{1,0:T(8,128)(2,1)S(1)}, u32[]{:S(2)}, u32[]{:S(2)}) collective-permute-start(bf16[416,128]{1,0:T(8,128)(2,1)S(1)} %get-tuple-element.22), channel_id=1, source_target_pairs={{0,256},{64,320},{128,384},{192,448},{256,512},{320,576},{384,640}... | collective-permute-start | bytes 319496 | tf_op jit(solution)/shard_map/ppermute | solution.py:203
  89.6 4.7 %collective-permute-start.6 = (bf16[416,128]{1,0:T(8,128)(2,1)S(1)}, bf16[416,128]{1,0:T(8,128)(2,1)S(1)}, u32[]{:S(2)}, u32[]{:S(2)}) collective-permute-start(bf16[416,128]{1,0:T(8,128)(2,1)S(1)} %get-tuple-element.23), channel_id=1, source_target_pairs={{0,512},{64,576},{128,640},{192,704},{256,0},{320,64},{384,128},{4... | collective-permute-start | bytes 319496 | tf_op jit(solution)/shard_map/ppermute | solution.py:203
  94.3 4.2 %collective-permute-done.5.a_ref = bf16[416,128]{1,0:T(8,128)(2,1)S(1)} collective-permute-done((bf16[416,128]{1,0:T(8,128)(2,1)S(1)}, bf16[416,128]{1,0:T(8,128)(2,1)S(1)}, u32[]{:S(2)}, u32[]{:S(2)}) %collective-permute-start.5) | collective-permute-done | bytes 106528 | tf_op jit(solution)/shard_map/ppermute | solution.py:203
  98.5 3.9 %collective-permute-done.6.b_ref = bf16[416,128]{1,0:T(8,128)(2,1)S(1)} collective-permute-done((bf16[416,128]{1,0:T(8,128)(2,1)S(1)}, bf16[416,128]{1,0:T(8,128)(2,1)S(1)}, u32[]{:S(2)}, u32[]{:S(2)}) %collective-permute-start.6) | collective-permute-done | bytes 106528 | tf_op jit(solution)/shard_map/ppermute | solution.py:203
  102.5 24.5 %all-gather = bf16[1664,128]{1,0:T(8,128)(2,1)S(1)} all-gather(bf16[416,128]{1,0:T(8,128)(2,1)S(1)} %shard_map.71), channel_id=2, replica_groups={{0,192,384,576},{64,256,448,640},{128,320,512,704},{1,193,385,577},{65,..., dimensions={0}, use_global_device_ids=true | all-gather | bytes 532480 | tf_op jit(solution)/shard_map/all_gather | solution.py:214
  127.0 1.9 %collective-permute-start.8 = (bf16[4,416,128]{2,1,0:T(8,128)(2,1)S(1)}, bf16[4,416,128]{2,1,0:T(8,128)(2,1)S(1)}, u32[]{:S(2)}, u32[]{:S(2)}) collective-permute-start(bf16[4,416,128]{2,1,0:T(8,128)(2,1)S(1)} %bitcast.14), channel_id=1, source_target_pairs={{0,704},{64,0},{128,64},{192,128},{256,192},{320,256},{384,320},{4... | collective-permute-start | bytes 1277960 | tf_op jit(solution)/shard_map/ppermute | solution.py:203
  128.9 3.9 %collective-permute-start.7 = (bf16[4,416,128]{2,1,0:T(8,128)(2,1)S(1)}, bf16[4,416,128]{2,1,0:T(8,128)(2,1)S(1)}, u32[]{:S(2)}, u32[]{:S(2)}) collective-permute-start(bf16[4,416,128]{2,1,0:T(8,128)(2,1)S(1)} %bitcast.15), channel_id=1, source_target_pairs={{0,64},{64,128},{128,192},{192,256},{256,320},{320,384},{384,448},... | collective-permute-start | bytes 1277960 | tf_op jit(solution)/shard_map/ppermute | solution.py:203
  132.8 0.9 shard_map.72
  133.8 1.0 shard_map.73.done_ref
  134.8 3.2 %collective-permute-done.8.high_ref = bf16[4,416,128]{2,1,0:T(8,128)(2,1)S(1)} collective-permute-done((bf16[4,416,128]{2,1,0:T(8,128)(2,1)S(1)}, bf16[4,416,128]{2,1,0:T(8,128)(2,1)S(1)}, u32[]{:S(2)}, u32[]{:S(2)}) %collective-permute-start.8) | collective-permute-done | bytes 426016 | tf_op jit(solution)/shard_map/ppermute | solution.py:203
  138.0 3.1 %collective-permute-done.7.low_ref = bf16[4,416,128]{2,1,0:T(8,128)(2,1)S(1)} collective-permute-done((bf16[4,416,128]{2,1,0:T(8,128)(2,1)S(1)}, bf16[4,416,128]{2,1,0:T(8,128)(2,1)S(1)}, u32[]{:S(2)}, u32[]{:S(2)}) %collective-permute-start.7) | collective-permute-done | bytes 426016 | tf_op jit(solution)/shard_map/ppermute | solution.py:203
  141.1 1.3 shard_map.74
  (11 shorter events, 0.1 us)
Async XLA Ops:
  0.6 0.8 copy-start.1
  1.5 37.9 %copy-start.2 = (s32[38,2]{0,1:T(2,128)S(1)}, s32[38,2]{0,1:T(2,128)}, u32[]{:S(2)}) copy-start(s32[38,2]{0,1:T(2,128)} %param.6) | copy-start | bytes 916
  21.3 20.7 %copy-start = (f32[128,512]{1,0:T(8,128)S(1)}, f32[128,512]{1,0:T(8,128)}, u32[]{:S(2)}) copy-start(f32[128,512]{1,0:T(8,128)} %g_ref.1) | copy-start | bytes 786436
  21.3 16.2 %all-to-all-start.1 = ((bf16[4,8,128,128]{3,2,1,0:T(8,128)(2,1)}), bf16[4,8,128,128]{3,2,1,0:T(8,128)(2,1)S(1)}, u32[]{:S(2)}, u32[]{:S(2)}) async-start(bf16[4,8,128,128]{3,2,1,0:T(8,128)(2,1)} %shard_map.68), calls=%async_computation.1 | async-start | bytes 2097152 | tf_op jit(solution)/shard_map/all_to_all | solution.py:199
  37.4 4.5 %collective-permute-start = (bf16[32,128,128]{2,1,0:T(8,128)(2,1)S(1)}, bf16[32,128,128]{2,1,0:T(8,128)(2,1)S(1)}, u32[]{:S(2)}, u32[]{:S(2)}) collective-permute-start(bf16[32,128,128]{2,1,0:T(8,128)(2,1)S(1)} %bitcast.12), channel_id=1, source_target_pairs={{0,1},{1,0},{2,3},{3,2},{4,5},{5,4},{6,7},{7,6},{8,9},{9,8},{10,11... | collective-permute-start | bytes 3145736 | tf_op jit(solution)/shard_map/ppermute | solution.py:265
  47.2 85.6 %all-to-all-start.2 = ((bf16[64,128,128]{2,1,0:T(8,128)(2,1)}), bf16[64,128,128]{2,1,0:T(8,128)(2,1)S(1)}, u32[]{:S(2)}, u32[]{:S(2)}) async-start(bf16[64,128,128]{2,1,0:T(8,128)(2,1)} %get-tuple-element.24), calls=%async_computation.2 | async-start | bytes 4194304 | tf_op jit(solution)/shard_map/all_to_all | solution.py:199
  53.5 30.9 %collective-permute-start.1 = (bf16[3,416,128]{2,1,0:T(8,128)(2,1)S(1)}, bf16[3,416,128]{2,1,0:T(8,128)(2,1)S(1)}, u32[]{:S(2)}, u32[]{:S(2)}) collective-permute-start(bf16[3,416,128]{2,1,0:T(8,128)(2,1)S(1)} %get-tuple-element.17), channel_id=1, source_target_pairs={{0,64},{64,128},{128,192},{192,256},{256,320},{320,384},{384,448},... | collective-permute-start | bytes 958472 | tf_op jit(solution)/shard_map/ppermute | solution.py:203
  57.8 26.6 %collective-permute-start.2 = (bf16[3,416,128]{2,1,0:T(8,128)(2,1)S(1)}, bf16[3,416,128]{2,1,0:T(8,128)(2,1)S(1)}, u32[]{:S(2)}, u32[]{:S(2)}) collective-permute-start(bf16[3,416,128]{2,1,0:T(8,128)(2,1)S(1)} %get-tuple-element.18), channel_id=1, source_target_pairs={{0,704},{64,0},{128,64},{192,128},{256,192},{320,256},{384,320},{4... | collective-permute-start | bytes 958472 | tf_op jit(solution)/shard_map/ppermute | solution.py:203
  70.0 12.2 %collective-permute-start.3 = (bf16[3,208,128]{2,1,0:T(8,128)(2,1)S(1)}, bf16[3,208,128]{2,1,0:T(8,128)(2,1)S(1)}, u32[]{:S(2)}, u32[]{:S(2)}) collective-permute-start(bf16[3,208,128]{2,1,0:T(8,128)(2,1)S(1)} %get-tuple-element.19), channel_id=1, source_target_pairs={{0,128},{64,192},{128,256},{192,320},{256,384},{320,448},{384,512}... | collective-permute-start | bytes 479240 | tf_op jit(solution)/shard_map/ppermute | solution.py:203
  71.9 12.4 %collective-permute-start.4 = (bf16[3,208,128]{2,1,0:T(8,128)(2,1)S(1)}, bf16[3,208,128]{2,1,0:T(8,128)(2,1)S(1)}, u32[]{:S(2)}, u32[]{:S(2)}) collective-permute-start(bf16[3,208,128]{2,1,0:T(8,128)(2,1)S(1)} %get-tuple-element.20), channel_id=1, source_target_pairs={{0,640},{64,704},{128,0},{192,64},{256,128},{320,192},{384,256},{4... | collective-permute-start | bytes 479240 | tf_op jit(solution)/shard_map/ppermute | solution.py:203
  84.5 14.0 %collective-permute-start.5 = (bf16[416,128]{1,0:T(8,128)(2,1)S(1)}, bf16[416,128]{1,0:T(8,128)(2,1)S(1)}, u32[]{:S(2)}, u32[]{:S(2)}) collective-permute-start(bf16[416,128]{1,0:T(8,128)(2,1)S(1)} %get-tuple-element.22), channel_id=1, source_target_pairs={{0,256},{64,320},{128,384},{192,448},{256,512},{320,576},{384,640}... | collective-permute-start | bytes 319496 | tf_op jit(solution)/shard_map/ppermute | solution.py:203
  89.6 12.8 %collective-permute-start.6 = (bf16[416,128]{1,0:T(8,128)(2,1)S(1)}, bf16[416,128]{1,0:T(8,128)(2,1)S(1)}, u32[]{:S(2)}, u32[]{:S(2)}) collective-permute-start(bf16[416,128]{1,0:T(8,128)(2,1)S(1)} %get-tuple-element.23), channel_id=1, source_target_pairs={{0,512},{64,576},{128,640},{192,704},{256,0},{320,64},{384,128},{4... | collective-permute-start | bytes 319496 | tf_op jit(solution)/shard_map/ppermute | solution.py:203
  127.0 11.0 %collective-permute-start.8 = (bf16[4,416,128]{2,1,0:T(8,128)(2,1)S(1)}, bf16[4,416,128]{2,1,0:T(8,128)(2,1)S(1)}, u32[]{:S(2)}, u32[]{:S(2)}) collective-permute-start(bf16[4,416,128]{2,1,0:T(8,128)(2,1)S(1)} %bitcast.14), channel_id=1, source_target_pairs={{0,704},{64,0},{128,64},{192,128},{256,192},{320,256},{384,320},{4... | collective-permute-start | bytes 1277960 | tf_op jit(solution)/shard_map/ppermute | solution.py:203
  128.9 12.2 %collective-permute-start.7 = (bf16[4,416,128]{2,1,0:T(8,128)(2,1)S(1)}, bf16[4,416,128]{2,1,0:T(8,128)(2,1)S(1)}, u32[]{:S(2)}, u32[]{:S(2)}) collective-permute-start(bf16[4,416,128]{2,1,0:T(8,128)(2,1)S(1)} %bitcast.15), channel_id=1, source_target_pairs={{0,64},{64,128},{128,192},{192,256},{256,320},{320,384},{384,448},... | collective-permute-start | bytes 1277960 | tf_op jit(solution)/shard_map/ppermute | solution.py:203

commit v13 on v12

--- a/solution.py
+++ b/solution.py
@@ -14,7 +14,7 @@
 CORE_SWAP = [(i, i ^ 1) for i in range(HALF * NC)]
 CHUNK = 416
 SPLIT = 208
-PIECES = 4
+PIECES = 8
 Z_FAR = [[3 * i + r for i in range(4)] for r in range(3)]
 F32, BF16 = jnp.float32, jnp.bfloat16
 
@@ -35,7 +35,7 @@
 
 def block_kernel(idx_ref, out_idx_ref, col_ref, live_ref, rel_ref, own_ref, sib_ref, w_ref, g_ref,
                  act_ref, gx_out_ref, keep_ref, up1_ref, down1_ref, up2_ref, down2_ref,
-                 x_ref, prod_ref, pre_ref, dpre_ref, gx_ref, gw_ref, x_out_ref, sems):
+                 x_ref, prod_ref, pre_ref, dpre_ref, gx_ref, gw_ref, x_out_ref, act_v_ref, sems):
     slots = w_ref.shape[0]
     col_blocks = pre_ref.shape[0]
     x_ref[:HALF] = own_ref[...]
@@ -48,8 +48,10 @@
     for c in range(col_blocks):
         value, slope = gelu_parts(pre_ref[c])
         lanes = slice(c * BS, (c + 1) * BS)
-        act_ref[:, lanes] = value
+        act_v_ref[:, lanes] = value
         dpre_ref[c] = (g_ref[:, lanes] * slope).astype(BF16)
+    act_copy = pltpu.make_async_copy(act_v_ref, act_ref, sems.at[PIECES])
+    act_copy.start()
     for s in range(slots):
         wgrad = dot(x_ref[idx_ref[s]], dpre_ref[col_ref[s]], ((0,), (0,)))
         wgrad = (wgrad * live_ref[s]).astype(BF16)
@@ -72,7 +74,7 @@
         prod_ref[s] = dot(dpre_ref[col_ref[s]], w_ref[s], ((1,), (1,)))
     for s in range(slots):
         gx_ref[out_idx_ref[s]] += prod_ref[s]
-    copies = []
+    copies = [act_copy]
     size = gx_ref.shape[0] // PIECES
     for p in range(PIECES):
         part = pl.ds(p * size, size)
@@ -180,7 +182,7 @@
         block_kernel,
         [SMEM] * 5 + [VMEM] * 4,
         (idx, out_idx, col, live, rel, own, sib, wb, grad_act),
-        (array((tokens, hidden), F32), pltpu.HBM((2 * HALF, tokens, BS), BF16), full, full, full, half, half),
+        (pltpu.HBM((tokens, hidden), F32), pltpu.HBM((2 * HALF, tokens, BS), BF16), full, full, full, half, half),
         [
             pltpu.VMEM((2 * HALF, tokens, BS), BF16),
             pltpu.VMEM((slots, tokens, BS), F32),
@@ -189,9 +191,10 @@
             pltpu.VMEM((2 * HALF, tokens, BS), F32),
             pltpu.VMEM((NZ, CHUNK, BS), BF16),
             pltpu.VMEM((2 * HALF, tokens, BS), BF16),
-            pltpu.SemaphoreType.DMA((PIECES,)),
+            pltpu.VMEM((tokens, hidden), F32),
+            pltpu.SemaphoreType.DMA((PIECES + 1,)),
         ],
-        (VMEM, HBM) + (VMEM,) * 5,
+        (HBM, HBM) + (VMEM,) * 5,
     )
 
 

time: 143 us -> 142 us (level)
  no operation moved by 1% of the time
where the time goes in v13:
time: 142 us
  starting transfers between devices  55.5 us (39%)
  blocking collectives  42.6 us (30%)
  waiting for transfers between devices  31 us (22%)
  Pallas kernels  8.98 us (6%)
  other arithmetic  2.01 us (1%)
    ppermute x8, starting transfers between devices, shift(): return lax.ppermute(x, 'dp', [(i, (i + by) % NZ) for i in range(NZ)])  40 us
    all_gather x1, blocking collectives, reduce_gradients(): mid = lax.all_gather(mine, 'dp', axis_index_groups=Z_FAR)  23.8 us
    ppermute x8, waiting for transfers between devices, shift(): return lax.ppermute(x, 'dp', [(i, (i + by) % NZ) for i in range(NZ)])  21.5 us
    all_to_all x1, blocking collectives, swap(): return lax.all_to_all(x, axis, 0, 0, tiled=True, axis_index_groups=groups)  18.8 us
    all_to_all x2, starting transfers between devices, swap(): return lax.all_to_all(x, axis, 0, 0, tiled=True, axis_index_groups=groups)  13.5 us
    pallas_call x8, Pallas kernels, call(): pl.pallas_call(kernel, out_shape=outs, in_specs=specs, out_specs=out_spec...  8.98 us
    all_to_all x2, waiting for transfers between devices, swap(): return lax.all_to_all(x, axis, 0, 0, tiled=True, axis_index_groups=groups)  8.93 us
  transfers between devices with their start and end apart: 11, of which 8 were waited for; matrix products, arithmetic and copies ran while one was open for 1% of the time, Pallas kernels for 2%

profile of v13, /device:TPU:6, one launch (start us, length us, event | category | flops | bytes accessed | tf_op | source)
XLA Modules:
  0.0 141.7 jit_solution(16919916677728043327)
XLA Ops:
  0.6 0.8 copy-done.1
  1.5 18.8 %all_to_all.15.in_ref = bf16[8,128,128]{2,1,0:T(8,128)(2,1)S(1)} all-to-all(bf16[8,128,128]{2,1,0:T(8,128)(2,1)S(1)} %shard_map.67), channel_id=1, replica_groups={{0,8,16,24,32,40,48,56},{1,9,17,25,33,41,49,57},{2,10,18,26,34,42,50,58..., dimensions={0} | all-to-all | bytes 524288 | tf_op jit(solution)/shard_map/all_to_all | solution.py:202
  20.3 1.0 shard_map.68
  21.3 0.0 copy-start
  21.3 7.2 %all-to-all-start.1 = ((bf16[4,8,128,128]{3,2,1,0:T(8,128)(2,1)}), bf16[4,8,128,128]{3,2,1,0:T(8,128)(2,1)S(1)}, u32[]{:S(2)}, u32[]{:S(2)}) async-start(bf16[4,8,128,128]{3,2,1,0:T(8,128)(2,1)} %shard_map.68), calls=%async_computation.1 | async-start | bytes 2097152 | tf_op jit(solution)/shard_map/all_to_all | solution.py:202
  28.5 8.9 %all-to-all-done.1 = bf16[4,8,128,128]{3,2,1,0:T(8,128)(2,1)S(1)} async-done(((bf16[4,8,128,128]{3,2,1,0:T(8,128)(2,1)}), bf16[4,8,128,128]{3,2,1,0:T(8,128)(2,1)S(1)}, u32[]{:S(2)}, u32[]{:S(2)}) %all-to-all-start.1) | async-done | bytes 1048608 | tf_op jit(solution)/shard_map/all_to_all | solution.py:202
  37.4 1.9 %collective-permute-start = (bf16[32,128,128]{2,1,0:T(8,128)(2,1)S(1)}, bf16[32,128,128]{2,1,0:T(8,128)(2,1)S(1)}, u32[]{:S(2)}, u32[]{:S(2)}) collective-permute-start(bf16[32,128,128]{2,1,0:T(8,128)(2,1)S(1)} %bitcast.12), channel_id=1, source_target_pairs={{0,1},{1,0},{2,3},{3,2},{4,5},{5,4},{6,7},{7,6},{8,9},{9,8},{10,11... | collective-permute-start | bytes 3145736 | tf_op jit(solution)/shard_map/ppermute | solution.py:268
  39.4 2.0 %multiply_convert_fusion.w_ref = bf16[38,128,128]{2,1,0:T(8,128)(2,1)S(1)} fusion(f32[38,128,128]{2,1,0:T(8,128)} %param.5, f32[38]{0:T(128)S(1)} %fusion.3.live_ref), kind=kLoop, calls=%fused_computation | loop fusion | flops 1245184 | bytes 3735704 | tf_op jit(solution)/shard_map/convert_element_type | solution.py:254
  41.4 0.6 collective-permute-done.sib_ref
  42.0 4.5 %shard_map.69 = (f32[128,512]{1,0:T(8,128)}, bf16[64,128,128]{2,1,0:T(8,128)(2,1)}, bf16[3,416,128]{2,1,0:T(8,128)(2,1)S(1)}, bf16[3,416,128]{2,1,0:T(8,128)(2,1...) custom-call(s32[38]{0:T(128)S(1)} %fusion.5.idx_ref, ...), custom_call_target="tpu_custom_call" | custom-call | tf_op jit(solution)/shard_map/pallas_call | solution.py:161
  46.5 6.3 %all-to-all-start.2 = ((bf16[64,128,128]{2,1,0:T(8,128)(2,1)}), bf16[64,128,128]{2,1,0:T(8,128)(2,1)S(1)}, u32[]{:S(2)}, u32[]{:S(2)}) async-start(bf16[64,128,128]{2,1,0:T(8,128)(2,1)} %get-tuple-element.24), calls=%async_computation.2 | async-start | bytes 4194304 | tf_op jit(solution)/shard_map/all_to_all | solution.py:202
  52.8 4.3 %collective-permute-start.1 = (bf16[3,416,128]{2,1,0:T(8,128)(2,1)S(1)}, bf16[3,416,128]{2,1,0:T(8,128)(2,1)S(1)}, u32[]{:S(2)}, u32[]{:S(2)}) collective-permute-start(bf16[3,416,128]{2,1,0:T(8,128)(2,1)S(1)} %get-tuple-element.17), channel_id=1, source_target_pairs={{0,64},{64,128},{128,192},{192,256},{256,320},{320,384},{384,448},... | collective-permute-start | bytes 958472 | tf_op jit(solution)/shard_map/ppermute | solution.py:206
  57.1 12.2 %collective-permute-start.2 = (bf16[3,416,128]{2,1,0:T(8,128)(2,1)S(1)}, bf16[3,416,128]{2,1,0:T(8,128)(2,1)S(1)}, u32[]{:S(2)}, u32[]{:S(2)}) collective-permute-start(bf16[3,416,128]{2,1,0:T(8,128)(2,1)S(1)} %get-tuple-element.18), channel_id=1, source_target_pairs={{0,704},{64,0},{128,64},{192,128},{256,192},{320,256},{384,320},{4... | collective-permute-start | bytes 958472 | tf_op jit(solution)/shard_map/ppermute | solution.py:206
  69.3 1.9 %collective-permute-start.3 = (bf16[3,208,128]{2,1,0:T(8,128)(2,1)S(1)}, bf16[3,208,128]{2,1,0:T(8,128)(2,1)S(1)}, u32[]{:S(2)}, u32[]{:S(2)}) collective-permute-start(bf16[3,208,128]{2,1,0:T(8,128)(2,1)S(1)} %get-tuple-element.19), channel_id=1, source_target_pairs={{0,128},{64,192},{128,256},{192,320},{256,384},{320,448},{384,512}... | collective-permute-start | bytes 479240 | tf_op jit(solution)/shard_map/ppermute | solution.py:206
  71.2 6.0 %collective-permute-start.4 = (bf16[3,208,128]{2,1,0:T(8,128)(2,1)S(1)}, bf16[3,208,128]{2,1,0:T(8,128)(2,1)S(1)}, u32[]{:S(2)}, u32[]{:S(2)}) collective-permute-start(bf16[3,208,128]{2,1,0:T(8,128)(2,1)S(1)} %get-tuple-element.20), channel_id=1, source_target_pairs={{0,640},{64,704},{128,0},{192,64},{256,128},{320,192},{384,256},{4... | collective-permute-start | bytes 479240 | tf_op jit(solution)/shard_map/ppermute | solution.py:206
  77.3 4.2 %collective-permute-done.3.c_ref = bf16[3,208,128]{2,1,0:T(8,128)(2,1)S(1)} collective-permute-done((bf16[3,208,128]{2,1,0:T(8,128)(2,1)S(1)}, bf16[3,208,128]{2,1,0:T(8,128)(2,1)S(1)}, u32[]{:S(2)}, u32[]{:S(2)}) %collective-permute-start.3) | collective-permute-done | bytes 159776 | tf_op jit(solution)/shard_map/ppermute | solution.py:206
  81.5 2.2 %collective-permute-done.4.d_ref = bf16[3,208,128]{2,1,0:T(8,128)(2,1)S(1)} collective-permute-done((bf16[3,208,128]{2,1,0:T(8,128)(2,1)S(1)}, bf16[3,208,128]{2,1,0:T(8,128)(2,1)S(1)}, u32[]{:S(2)}, u32[]{:S(2)}) %collective-permute-start.4) | collective-permute-done | bytes 159776 | tf_op jit(solution)/shard_map/ppermute | solution.py:206
  83.7 0.0 collective-permute-done.1.a_ref
  83.7 0.0 collective-permute-done.2.b_ref
  83.7 0.2 shard_map.70
  83.9 5.1 %collective-permute-start.5 = (bf16[416,128]{1,0:T(8,128)(2,1)S(1)}, bf16[416,128]{1,0:T(8,128)(2,1)S(1)}, u32[]{:S(2)}, u32[]{:S(2)}) collective-permute-start(bf16[416,128]{1,0:T(8,128)(2,1)S(1)} %get-tuple-element.22), channel_id=1, source_target_pairs={{0,256},{64,320},{128,384},{192,448},{256,512},{320,576},{384,640}... | collective-permute-start | bytes 319496 | tf_op jit(solution)/shard_map/ppermute | solution.py:206
  89.0 4.7 %collective-permute-start.6 = (bf16[416,128]{1,0:T(8,128)(2,1)S(1)}, bf16[416,128]{1,0:T(8,128)(2,1)S(1)}, u32[]{:S(2)}, u32[]{:S(2)}) collective-permute-start(bf16[416,128]{1,0:T(8,128)(2,1)S(1)} %get-tuple-element.23), channel_id=1, source_target_pairs={{0,512},{64,576},{128,640},{192,704},{256,0},{320,64},{384,128},{4... | collective-permute-start | bytes 319496 | tf_op jit(solution)/shard_map/ppermute | solution.py:206
  93.6 4.2 %collective-permute-done.5.a_ref = bf16[416,128]{1,0:T(8,128)(2,1)S(1)} collective-permute-done((bf16[416,128]{1,0:T(8,128)(2,1)S(1)}, bf16[416,128]{1,0:T(8,128)(2,1)S(1)}, u32[]{:S(2)}, u32[]{:S(2)}) %collective-permute-start.5) | collective-permute-done | bytes 106528 | tf_op jit(solution)/shard_map/ppermute | solution.py:206
  97.8 3.9 %collective-permute-done.6.b_ref = bf16[416,128]{1,0:T(8,128)(2,1)S(1)} collective-permute-done((bf16[416,128]{1,0:T(8,128)(2,1)S(1)}, bf16[416,128]{1,0:T(8,128)(2,1)S(1)}, u32[]{:S(2)}, u32[]{:S(2)}) %collective-permute-start.6) | collective-permute-done | bytes 106528 | tf_op jit(solution)/shard_map/ppermute | solution.py:206
  101.8 23.8 %all-gather = bf16[1664,128]{1,0:T(8,128)(2,1)S(1)} all-gather(bf16[416,128]{1,0:T(8,128)(2,1)S(1)} %shard_map.71), channel_id=2, replica_groups={{0,192,384,576},{64,256,448,640},{128,320,512,704},{1,193,385,577},{65,..., dimensions={0}, use_global_device_ids=true | all-gather | bytes 532480 | tf_op jit(solution)/shard_map/all_gather | solution.py:217
  125.6 1.9 %collective-permute-start.8 = (bf16[4,416,128]{2,1,0:T(8,128)(2,1)S(1)}, bf16[4,416,128]{2,1,0:T(8,128)(2,1)S(1)}, u32[]{:S(2)}, u32[]{:S(2)}) collective-permute-start(bf16[4,416,128]{2,1,0:T(8,128)(2,1)S(1)} %bitcast.14), channel_id=1, source_target_pairs={{0,704},{64,0},{128,64},{192,128},{256,192},{320,256},{384,320},{4... | collective-permute-start | bytes 1277960 | tf_op jit(solution)/shard_map/ppermute | solution.py:206
  127.5 3.9 %collective-permute-start.7 = (bf16[4,416,128]{2,1,0:T(8,128)(2,1)S(1)}, bf16[4,416,128]{2,1,0:T(8,128)(2,1)S(1)}, u32[]{:S(2)}, u32[]{:S(2)}) collective-permute-start(bf16[4,416,128]{2,1,0:T(8,128)(2,1)S(1)} %bitcast.15), channel_id=1, source_target_pairs={{0,64},{64,128},{128,192},{192,256},{256,320},{320,384},{384,448},... | collective-permute-start | bytes 1277960 | tf_op jit(solution)/shard_map/ppermute | solution.py:206
  131.5 0.9 shard_map.72
  132.4 1.0 shard_map.73.done_ref
  133.4 3.8 %collective-permute-done.8.high_ref = bf16[4,416,128]{2,1,0:T(8,128)(2,1)S(1)} collective-permute-done((bf16[4,416,128]{2,1,0:T(8,128)(2,1)S(1)}, bf16[4,416,128]{2,1,0:T(8,128)(2,1)S(1)}, u32[]{:S(2)}, u32[]{:S(2)}) %collective-permute-start.8) | collective-permute-done | bytes 426016 | tf_op jit(solution)/shard_map/ppermute | solution.py:206
  137.2 3.1 %collective-permute-done.7.low_ref = bf16[4,416,128]{2,1,0:T(8,128)(2,1)S(1)} collective-permute-done((bf16[4,416,128]{2,1,0:T(8,128)(2,1)S(1)}, bf16[4,416,128]{2,1,0:T(8,128)(2,1)S(1)}, u32[]{:S(2)}, u32[]{:S(2)}) %collective-permute-start.7) | collective-permute-done | bytes 426016 | tf_op jit(solution)/shard_map/ppermute | solution.py:206
  140.4 1.3 shard_map.74
  (11 shorter events, 0.1 us)
Async XLA Ops:
  0.6 0.8 copy-start.1
  1.5 37.9 %copy-start.2 = (s32[38,2]{0,1:T(2,128)S(1)}, s32[38,2]{0,1:T(2,128)}, u32[]{:S(2)}) copy-start(s32[38,2]{0,1:T(2,128)} %param.6) | copy-start | bytes 916
  21.3 20.7 %copy-start = (f32[128,512]{1,0:T(8,128)S(1)}, f32[128,512]{1,0:T(8,128)}, u32[]{:S(2)}) copy-start(f32[128,512]{1,0:T(8,128)} %g_ref.1) | copy-start | bytes 786436
  21.3 16.2 %all-to-all-start.1 = ((bf16[4,8,128,128]{3,2,1,0:T(8,128)(2,1)}), bf16[4,8,128,128]{3,2,1,0:T(8,128)(2,1)S(1)}, u32[]{:S(2)}, u32[]{:S(2)}) async-start(bf16[4,8,128,128]{3,2,1,0:T(8,128)(2,1)} %shard_map.68), calls=%async_computation.1 | async-start | bytes 2097152 | tf_op jit(solution)/shard_map/all_to_all | solution.py:202
  37.4 4.5 %collective-permute-start = (bf16[32,128,128]{2,1,0:T(8,128)(2,1)S(1)}, bf16[32,128,128]{2,1,0:T(8,128)(2,1)S(1)}, u32[]{:S(2)}, u32[]{:S(2)}) collective-permute-start(bf16[32,128,128]{2,1,0:T(8,128)(2,1)S(1)} %bitcast.12), channel_id=1, source_target_pairs={{0,1},{1,0},{2,3},{3,2},{4,5},{5,4},{6,7},{7,6},{8,9},{9,8},{10,11... | collective-permute-start | bytes 3145736 | tf_op jit(solution)/shard_map/ppermute | solution.py:268
  46.5 85.0 %all-to-all-start.2 = ((bf16[64,128,128]{2,1,0:T(8,128)(2,1)}), bf16[64,128,128]{2,1,0:T(8,128)(2,1)S(1)}, u32[]{:S(2)}, u32[]{:S(2)}) async-start(bf16[64,128,128]{2,1,0:T(8,128)(2,1)} %get-tuple-element.24), calls=%async_computation.2 | async-start | bytes 4194304 | tf_op jit(solution)/shard_map/all_to_all | solution.py:202
  52.8 30.9 %collective-permute-start.1 = (bf16[3,416,128]{2,1,0:T(8,128)(2,1)S(1)}, bf16[3,416,128]{2,1,0:T(8,128)(2,1)S(1)}, u32[]{:S(2)}, u32[]{:S(2)}) collective-permute-start(bf16[3,416,128]{2,1,0:T(8,128)(2,1)S(1)} %get-tuple-element.17), channel_id=1, source_target_pairs={{0,64},{64,128},{128,192},{192,256},{256,320},{320,384},{384,448},... | collective-permute-start | bytes 958472 | tf_op jit(solution)/shard_map/ppermute | solution.py:206
  57.1 26.6 %collective-permute-start.2 = (bf16[3,416,128]{2,1,0:T(8,128)(2,1)S(1)}, bf16[3,416,128]{2,1,0:T(8,128)(2,1)S(1)}, u32[]{:S(2)}, u32[]{:S(2)}) collective-permute-start(bf16[3,416,128]{2,1,0:T(8,128)(2,1)S(1)} %get-tuple-element.18), channel_id=1, source_target_pairs={{0,704},{64,0},{128,64},{192,128},{256,192},{320,256},{384,320},{4... | collective-permute-start | bytes 958472 | tf_op jit(solution)/shard_map/ppermute | solution.py:206
  69.3 12.2 %collective-permute-start.3 = (bf16[3,208,128]{2,1,0:T(8,128)(2,1)S(1)}, bf16[3,208,128]{2,1,0:T(8,128)(2,1)S(1)}, u32[]{:S(2)}, u32[]{:S(2)}) collective-permute-start(bf16[3,208,128]{2,1,0:T(8,128)(2,1)S(1)} %get-tuple-element.19), channel_id=1, source_target_pairs={{0,128},{64,192},{128,256},{192,320},{256,384},{320,448},{384,512}... | collective-permute-start | bytes 479240 | tf_op jit(solution)/shard_map/ppermute | solution.py:206
  71.2 12.4 %collective-permute-start.4 = (bf16[3,208,128]{2,1,0:T(8,128)(2,1)S(1)}, bf16[3,208,128]{2,1,0:T(8,128)(2,1)S(1)}, u32[]{:S(2)}, u32[]{:S(2)}) collective-permute-start(bf16[3,208,128]{2,1,0:T(8,128)(2,1)S(1)} %get-tuple-element.20), channel_id=1, source_target_pairs={{0,640},{64,704},{128,0},{192,64},{256,128},{320,192},{384,256},{4... | collective-permute-start | bytes 479240 | tf_op jit(solution)/shard_map/ppermute | solution.py:206
  83.9 14.0 %collective-permute-start.5 = (bf16[416,128]{1,0:T(8,128)(2,1)S(1)}, bf16[416,128]{1,0:T(8,128)(2,1)S(1)}, u32[]{:S(2)}, u32[]{:S(2)}) collective-permute-start(bf16[416,128]{1,0:T(8,128)(2,1)S(1)} %get-tuple-element.22), channel_id=1, source_target_pairs={{0,256},{64,320},{128,384},{192,448},{256,512},{320,576},{384,640}... | collective-permute-start | bytes 319496 | tf_op jit(solution)/shard_map/ppermute | solution.py:206
  89.0 12.8 %collective-permute-start.6 = (bf16[416,128]{1,0:T(8,128)(2,1)S(1)}, bf16[416,128]{1,0:T(8,128)(2,1)S(1)}, u32[]{:S(2)}, u32[]{:S(2)}) collective-permute-start(bf16[416,128]{1,0:T(8,128)(2,1)S(1)} %get-tuple-element.23), channel_id=1, source_target_pairs={{0,512},{64,576},{128,640},{192,704},{256,0},{320,64},{384,128},{4... | collective-permute-start | bytes 319496 | tf_op jit(solution)/shard_map/ppermute | solution.py:206
  125.6 11.6 %collective-permute-start.8 = (bf16[4,416,128]{2,1,0:T(8,128)(2,1)S(1)}, bf16[4,416,128]{2,1,0:T(8,128)(2,1)S(1)}, u32[]{:S(2)}, u32[]{:S(2)}) collective-permute-start(bf16[4,416,128]{2,1,0:T(8,128)(2,1)S(1)} %bitcast.14), channel_id=1, source_target_pairs={{0,704},{64,0},{128,64},{192,128},{256,192},{320,256},{384,320},{4... | collective-permute-start | bytes 1277960 | tf_op jit(solution)/shard_map/ppermute | solution.py:206
  127.5 12.9 %collective-permute-start.7 = (bf16[4,416,128]{2,1,0:T(8,128)(2,1)S(1)}, bf16[4,416,128]{2,1,0:T(8,128)(2,1)S(1)}, u32[]{:S(2)}, u32[]{:S(2)}) collective-permute-start(bf16[4,416,128]{2,1,0:T(8,128)(2,1)S(1)} %bitcast.15), channel_id=1, source_target_pairs={{0,64},{64,128},{128,192},{192,256},{256,320},{320,384},{384,448},... | collective-permute-start | bytes 1277960 | tf_op jit(solution)/shard_map/ppermute | solution.py:206
